TPU v7x, 32 devices: a whole 2x2x4 slice. The times are simulated.
32 devices in a mesh: freq: 4 (over y, core), offset: 8 (over z, x).
Axes of the slice: x: 2, y: 2, z: 4, core: 2. Of those that a mesh axis runs over, the one named last changes fastest.
Arguments:
- raw_traces: bfloat16 [8192, 2048], P('offset', 'freq'), may hold values from -6 to 6
- trace_slot: int32 [32, 256], P(None, 'offset'), may hold values from 0 to 1023, as said below
- offset_index: int32 [256], replicated, may hold values from 1 to 1023
- slowness_index: int32 [256], replicated, may hold values from 0 to 511
Outputs:
- radon: float32 [256, 1024, 64], P('offset', 'freq')
Inputs may be any that keep to these rules, and one draw needn't show every extreme that they name: `trace_slot`: in every aligned block of 32 columns, the 32 x 32 entries name each of 0 to 1023 exactly once.
All inputs are finite; a program needn't handle non-finite values.
Results may differ from a plain program's by a relative error of at most 0.0046.
Values may be sent and summed in bfloat16 or wider, within the bound.
No kernel may reach another device: no remote copies, remote signals or barrier semaphores. Data moves between devices by JAX's collectives and lax.ppermute only.
A program may use at most 64 MiB of HBM per device.

v0:
```python
import math

import jax
import jax.numpy as jnp
from jax import lax
from jax.sharding import PartitionSpec as P

NF = 1024
NP = 256


APEX_TIME = 100.0
CURVATURE = 0.0003


def moveout(slowness, offset_grid):
    spread = (
        CURVATURE * slowness.astype(jnp.float32)[:, None] * offset_grid.astype(jnp.float32)[None, :]
    )
    return jnp.sqrt(APEX_TIME * APEX_TIME + spread * spread) - APEX_TIME


def whole_table(local_freqs, total_time):
    column_total = 2 * NF
    column = jnp.arange(column_total, dtype=jnp.int32)
    band_ids = column // (2 * local_freqs)
    within = column % (2 * local_freqs)
    freq_ids = band_ids * local_freqs + within % local_freqs
    shifts = jnp.where(within < local_freqs, 0, total_time // 2).astype(jnp.int32)
    odd_rates = 2 * freq_ids + 1
    fine_size = 64
    coarse_size = total_time // fine_size
    period = 2 * total_time
    coarse_ids = jnp.arange(coarse_size, dtype=jnp.int32)[:, None]
    fine_ids = jnp.arange(fine_size, dtype=jnp.int32)[:, None]
    coarse_turn = coarse_ids * fine_size % period * odd_rates[None, :] % period
    fine_turn = (fine_ids * odd_rates[None, :] + shifts[None, :]) % period
    coarse_angle = coarse_turn.astype(jnp.float32) * (math.pi / total_time)
    fine_angle = fine_turn.astype(jnp.float32) * (math.pi / total_time)
    coarse_cos = jnp.cos(coarse_angle)
    coarse_sin = jnp.sin(coarse_angle)
    fine_cos = jnp.cos(fine_angle)
    fine_sin = jnp.sin(fine_angle)
    values = (
        coarse_cos[:, None, :] * fine_cos[None, :, :]
        - coarse_sin[:, None, :] * fine_sin[None, :, :]
    )
    values = values.reshape(total_time, column_total)
    return (values * (1.0 / math.sqrt(total_time))).astype(jnp.bfloat16)


def local(raw_traces, trace_slot, offset_index, slowness_index):
    gathers, local_offsets = trace_slot.shape
    local_times = raw_traces.shape[1]
    freq_devices = lax.axis_size("freq")
    offset_devices = lax.axis_size("offset")
    total_time = local_times * freq_devices
    local_freqs = NF // freq_devices
    local_slows = NP // offset_devices
    trace_rows = gathers * local_offsets
    picked = raw_traces[trace_slot.reshape(-1)]
    grouped = picked.reshape(freq_devices, trace_rows // freq_devices, local_times)
    fourier_table = whole_table(local_freqs, total_time)
    series = lax.all_to_all(grouped, "freq", split_axis=0, concat_axis=2, tiled=True)
    flattened = series.reshape(series.shape[1], total_time)
    spectrum = jnp.dot(flattened, fourier_table, preferred_element_type=jnp.float32).astype(
        jnp.bfloat16
    )
    spectrum = jnp.transpose(
        spectrum.reshape(flattened.shape[0], freq_devices, 2 * local_freqs), (1, 0, 2)
    )
    assembled = lax.all_to_all(spectrum, "freq", split_axis=0, concat_axis=0, tiled=True)
    spectra = assembled.reshape(gathers, local_offsets, 2 * local_freqs)
    real_part = spectra[:, :, :local_freqs]
    imag_part = spectra[:, :, local_freqs:]
    freq_ids = lax.axis_index("freq") * local_freqs + jnp.arange(local_freqs, dtype=jnp.int32)
    angular = (2 * freq_ids + 1).astype(jnp.float32) * (math.pi / total_time)
    own_first = lax.axis_index("offset") * local_slows
    own_slowness = lax.dynamic_slice_in_dim(slowness_index, own_first, local_slows)
    real_in = lax.all_gather(real_part, "offset", axis=1, tiled=True)
    imag_in = lax.all_gather(imag_part, "offset", axis=1, tiled=True)
    delays = moveout(own_slowness, offset_index)
    phases = angular[:, None, None] * delays[None, :, :]
    cosine = jnp.cos(phases).astype(jnp.bfloat16)
    sines = jnp.sin(phases).astype(jnp.bfloat16)
    real_out = jnp.einsum(
        "fph,ghf->pfg", cosine, real_in, preferred_element_type=jnp.float32
    ) - jnp.einsum("fph,ghf->pfg", sines, imag_in, preferred_element_type=jnp.float32)
    imag_out = jnp.einsum(
        "fph,ghf->pfg", sines, real_in, preferred_element_type=jnp.float32
    ) + jnp.einsum("fph,ghf->pfg", cosine, imag_in, preferred_element_type=jnp.float32)
    summed = jnp.concatenate([real_out, imag_out], axis=2)
    return summed * (1.0 / math.sqrt(local_offsets * offset_devices))


def solution(mesh):
    placed = (P("offset", "freq"), P(None, "offset"), P(), P())
    return jax.shard_map(
        local, mesh=mesh, in_specs=placed, out_specs=P("offset", "freq", None), check_vma=False
    )
```

profile of v0, /device:TPU:0, one launch (start us, length us, event | category | flops | bytes accessed | tf_op | source)
XLA Modules:
  0.0 301.2 jit_solution(10427778525387622832)
XLA Ops:
  6.5 0.0 copy-start
  6.5 0.9 reshape.308
  7.4 0.3 copy-done
  7.8 4.0 %gather_fusion = bf16[1024,512]{1,0:T(8,128)(2,1)S(1)} fusion(bf16[1024,512]{1,0:T(8,128)(2,1)S(1)} %copy-done, s32[1024]{0:T(1024)S(1)} %broadcast_clamp_fusion), kind=kCustom, calls=%fused_computation | custom fusion | bytes 2101248 | tf_op jit(solution)/shard_map/gather | solution.py:61
  11.7 1.3 copy.21
  13.1 4.2 %all-to-all-start = ((bf16[4,256,512]{1,2,0:T(8,128)(2,1)}), bf16[4,256,512]{1,2,0:T(8,128)(2,1)S(1)}, u32[]{:S(2)}, u32[]{:S(2)}) async-start(bf16[4,256,512]{1,2,0:T(8,128)(2,1)} %copy.21), calls=%async_computation | async-start | bytes 2097152 | tf_op jit(solution)/shard_map/all_to_all | solution.py:64
  17.3 0.0 all-gather.3.cloned.1.call-start
  17.3 2.1 fusion.22
  19.4 1.1 fusion.27
  20.5 6.2 %multiply_convert_fusion = bf16[32,64,2048]{2,1,0:T(8,128)(2,1)} fusion(f32[64,2048]{1,0:T(8,128)S(1)} %get-tuple-element.8, f32[32,2048]{1,0:T(8,128)S(1)} %get-tuple-element.10, f32[64,2048]{1,0:T(8,128)S(1)} %get-tuple-element.7, f32[32,2048]{1,0:T(8,128)S(1)} %get-tuple-element.9), kind=kLoop, calls=%fused_computation.1 | loop fusion | flops 20971520 | bytes 9961472 | tf_op jit(solution)/shard_map/convert_element_type | solution.py:49
  26.7 5.1 %all-to-all-done = bf16[4,256,512]{1,2,0:T(8,128)(2,1)S(1)} async-done(((bf16[4,256,512]{1,2,0:T(8,128)(2,1)}), bf16[4,256,512]{1,2,0:T(8,128)(2,1)S(1)}, u32[]{:S(2)}, u32[]{:S(2)}) %all-to-all-start) | async-done | bytes 1048608 | tf_op jit(solution)/shard_map/all_to_all | solution.py:64
  31.8 5.7 %convolution_convert_fusion = bf16[256,2048]{1,0:T(8,128)(2,1)S(1)} fusion(bf16[256,2048]{0,1:T(8,128)(2,1)S(1)} %bitcast.27, bf16[2048,2048]{1,0:T(8,128)(2,1)} %bitcast.26), kind=kOutput, calls=%fused_computation.18 | convolution fusion | flops 2148007936 | bytes 10485760 | tf_op jit(solution)/shard_map/dot_general | solution.py:66
  37.5 0.1 copy.35
  37.6 0.0 copy-start.3
  37.6 0.0 copy-start.4
  37.6 16.9 %all_to_all.20 = bf16[4,256,512]{2,1,0:T(8,128)(2,1)S(1)} all-to-all(bf16[4,256,512]{2,1,0:T(8,128)(2,1)S(1)} %bitcast.31), channel_id=1, replica_groups=mesh['freq'=4,'offset'=8] {'freq'}, dimensions={0} | all-to-all | bytes 2097152 | tf_op jit(solution)/shard_map/all_to_all | solution.py:72
  54.5 0.1 fusion.43
  54.6 1.1 copy.23
  55.7 0.0 all-gather.3.cloned.1.call-update
  55.7 0.2 all-gather.5.cloned.1.call-start
  56.0 1.1 copy.25
  57.1 0.0 all-gather.5.cloned.1.call-update
  57.1 0.0 copy-done.3
  57.1 0.0 copy-done.4
  57.2 0.1 convert_multiply_fusion.1
  57.2 0.1 sqrt_add_fusion
  57.3 72.9 %all-gather.3.cloned.1.call-done = bf16[32,256,256]{2,0,1:T(8,128)(2,1)} async-done(((bf16[32,32,256]{2,0,1:T(8,128)(2,1)}), bf16[32,256,256]{2,0,1:T(8,128)(2,1)}) %all-gather.3.cloned.1.call-update) | async-done | bytes 4194320 | tf_op jit(solution)/shard_map/all_gather | solution.py:80
  130.3 8.5 %copy.24 = bf16[32,256,256]{1,0,2:T(8,128)(2,1)} copy(bf16[32,256,256]{2,0,1:T(8,128)(2,1)} %all-gather.3.cloned.1.call-done) | data formatting | bytes 8388608 | tf_op jit(solution)/shard_map/all_gather | solution.py:80
  138.8 0.0 copy-start.2
  138.8 30.7 %fusion.2 = f32[256,32,32]{1,2,0:T(8,128)} fusion(bf16[32,256,256]{1,0,2:T(8,128)(2,1)} %copy.24, f32[32,256]{1,0:T(8,128)S(1)} %sqrt_add_fusion, f32[256]{0:T(256)S(1)} %convert_multiply_fusion), kind=kOutput, calls=%fused_computation.6 | convolution fusion | flops 138412032 | bytes 5276672 | tf_op jit(solution)/shard_map/fph,ghf->pfg/dot_general | solution.py:89
  169.5 0.0 copy-done.2
  169.5 30.8 %fusion.8 = f32[256,32,32]{1,2,0:T(8,128)} fusion(bf16[32,256,256]{1,0,2:T(8,128)(2,1)S(1)} %copy-done.2, f32[32,256]{1,0:T(8,128)S(1)} %sqrt_add_fusion, f32[256]{0:T(256)S(1)} %convert_multiply_fusion), kind=kOutput, calls=%fused_computation.9 | convolution fusion | flops 138412032 | bytes 5276672 | tf_op jit(solution)/shard_map/fph,ghf->pfg/dot_general | solution.py:86
  200.3 3.9 %all-gather.5.cloned.1.call-done = bf16[32,256,256]{2,0,1:T(8,128)(2,1)} async-done(((bf16[32,32,256]{2,0,1:T(8,128)(2,1)}), bf16[32,256,256]{2,0,1:T(8,128)(2,1)}) %all-gather.5.cloned.1.call-update) | async-done | bytes 4194320 | tf_op jit(solution)/shard_map/all_gather | solution.py:81
  204.1 8.6 %copy.26 = bf16[32,256,256]{1,0,2:T(8,128)(2,1)} copy(bf16[32,256,256]{2,0,1:T(8,128)(2,1)} %all-gather.5.cloned.1.call-done) | data formatting | bytes 8388608 | tf_op jit(solution)/shard_map/all_gather | solution.py:81
  212.8 0.0 copy-start.1
  212.8 30.5 %fusion.6 = f32[256,32,32]{1,2,0:T(8,128)} fusion(bf16[32,256,256]{1,0,2:T(8,128)(2,1)} %copy.26, f32[32,256]{1,0:T(8,128)S(1)} %sqrt_add_fusion, f32[256]{0:T(256)S(1)} %convert_multiply_fusion), kind=kOutput, calls=%fused_computation.8 | convolution fusion | flops 138412032 | bytes 5276672 | tf_op jit(solution)/shard_map/fph,ghf->pfg/dot_general | solution.py:91
  243.2 0.0 copy-done.1
  243.2 31.1 %fusion.4 = f32[256,32,32]{1,2,0:T(8,128)} fusion(bf16[32,256,256]{1,0,2:T(8,128)(2,1)S(1)} %copy-done.1, f32[32,256]{1,0:T(8,128)S(1)} %sqrt_add_fusion, f32[256]{0:T(256)S(1)} %convert_multiply_fusion), kind=kOutput, calls=%fused_computation.7 | convolution fusion | flops 138412032 | bytes 5276672 | tf_op jit(solution)/shard_map/fph,ghf->pfg/dot_general | solution.py:88
  274.3 3.5 %copy.31 = f32[256,32,32]{0,1,2:T(8,128)S(1)} copy(f32[256,32,32]{1,2,0:T(8,128)} %fusion.2) | data formatting | bytes 2097152 | tf_op jit(solution)/shard_map/fph,ghf->pfg/dot_general | solution.py:89
  277.9 3.5 %copy.27 = f32[256,32,32]{0,1,2:T(8,128)S(1)} copy(f32[256,32,32]{1,2,0:T(8,128)} %fusion.8) | data formatting | bytes 2097152 | tf_op jit(solution)/shard_map/fph,ghf->pfg/dot_general | solution.py:86
  281.4 4.3 %copy.32 = f32[256,32,32]{0,1,2:T(8,128)} copy(f32[256,32,32]{1,2,0:T(8,128)} %fusion.6) | data formatting | bytes 2097152 | tf_op jit(solution)/shard_map/fph,ghf->pfg/dot_general | solution.py:91
  285.7 4.4 %copy.28 = f32[256,32,32]{0,1,2:T(8,128)} copy(f32[256,32,32]{1,2,0:T(8,128)} %fusion.4) | data formatting | bytes 2097152 | tf_op jit(solution)/shard_map/fph,ghf->pfg/dot_general | solution.py:88
  290.1 1.4 add_bitcast_fusion
  291.4 1.4 subtract_bitcast_fusion
  292.8 1.6 maximum_multiply_fusion
  (6 shorter events, 0.0 us)
Async XLA Ops:
  6.5 1.2 copy-start
  13.1 18.7 %all-to-all-start = ((bf16[4,256,512]{1,2,0:T(8,128)(2,1)}), bf16[4,256,512]{1,2,0:T(8,128)(2,1)S(1)}, u32[]{:S(2)}, u32[]{:S(2)}) async-start(bf16[4,256,512]{1,2,0:T(8,128)(2,1)} %copy.21), calls=%async_computation | async-start | bytes 2097152 | tf_op jit(solution)/shard_map/all_to_all | solution.py:64
  17.3 113.0 %all-gather.3.cloned.1.call-start = ((), (), s32[]{:S(2)}) async-start(), calls=%async_computation.2 | async-start | bytes 4718592 | tf_op jit(solution)/shard_map/all_gather | solution.py:80
  37.6 19.6 %copy-start.3 = (s32[256]{0:T(256)S(1)}, s32[256]{0:T(256)}, u32[]{:S(2)}) copy-start(s32[256]{0:T(256)} %param.6) | copy-start | bytes 3076
  37.6 19.6 %copy-start.4 = (s32[256]{0:T(256)S(1)}, s32[256]{0:T(256)}, u32[]{:S(2)}) copy-start(s32[256]{0:T(256)} %param.7) | copy-start | bytes 3076
  55.7 148.4 %all-gather.5.cloned.1.call-start = ((), (), s32[]{:S(2)}) async-start(), calls=%async_computation.3 | async-start | bytes 4718592 | tf_op jit(solution)/shard_map/all_gather | solution.py:81
  138.8 30.7 %copy-start.2 = (bf16[32,256,256]{1,0,2:T(8,128)(2,1)S(1)}, bf16[32,256,256]{1,0,2:T(8,128)(2,1)}, u32[]{:S(2)}) copy-start(bf16[32,256,256]{1,0,2:T(8,128)(2,1)} %copy.24) | copy-start | bytes 12582916
  212.8 30.5 %copy-start.1 = (bf16[32,256,256]{1,0,2:T(8,128)(2,1)S(1)}, bf16[32,256,256]{1,0,2:T(8,128)(2,1)}, u32[]{:S(2)}) copy-start(bf16[32,256,256]{1,0,2:T(8,128)(2,1)} %copy.26) | copy-start | bytes 12582916
Sparse Core Ops, SparseCore 0:
  55.8 74.3 all-gather.2
  132.4 71.7 all-gather.4
where the time goes:
time: 302 us; the launch traced here: 301 us
  matrix products  129 us (43%)
  waiting for transfers between devices  81.9 us (27%)
  local copies, waits for them, and re-layouts  41.8 us (14%)
  blocking collectives  16.9 us (6%)
  other arithmetic  13.9 us (5%)
  between operations  13.5 us (4%)
  starting transfers between devices  4.46 us (1%)
    all_gather x1, waiting for transfers between devices, local(): real_in = lax.all_gather(real_part, 'offset', axis=1, tiled=True)  72.9 us
    dot_general x1, matrix products, local(): jnp.einsum('fph,ghf->pfg', sines, imag_in, preferred_element_type=jnp.flo...  31.1 us
    dot_general x1, matrix products, local(): jnp.einsum('fph,ghf->pfg', cosine, real_in, preferred_element_type=jnp.fl...  30.8 us
    dot_general x1, matrix products, local(): jnp.einsum('fph,ghf->pfg', sines, real_in, preferred_element_type=jnp.flo...  30.7 us
    dot_general x1, matrix products, local(): jnp.einsum('fph,ghf->pfg', cosine, imag_in, preferred_element_type=jnp.fl...  30.5 us
    all_to_all x1, blocking collectives, local(): lax.all_to_all(spectrum, 'freq', split_axis=0, concat_axis=0, tiled=True)  16.9 us
    all_gather x1, local copies, waits for them, and re-layouts, local(): imag_in = lax.all_gather(imag_part, 'offset', axis=1, tiled=True)  8.61 us
    all_gather x1, local copies, waits for them, and re-layouts, local(): real_in = lax.all_gather(real_part, 'offset', axis=1, tiled=True)  8.54 us
  transfers between devices with their start and end apart: 3, of which 3 were waited for; matrix products, arithmetic and copies ran while one was open for 27% of the time, Pallas kernels for 0%

commit v1 on v0

v1 whole, which is shorter than its diff:
```python
import functools
import math

import jax
import jax.numpy as jnp
import ml_dtypes
import numpy as np
from jax import lax
from jax.experimental import pallas as pl
from jax.experimental.pallas import tpu as pltpu
from jax.sharding import PartitionSpec as P

NF = 1024
NP = 256
APEX_TIME = 100.0
CURVATURE = 0.0003
MIB = 1 << 20


def table_rows(total_time, freq_devices, offset_devices, halves, pairs):
    band = NF // freq_devices
    f, o, k, a = np.meshgrid(
        np.arange(freq_devices),
        np.arange(offset_devices),
        np.arange(pairs),
        np.arange(halves),
        indexing="ij",
    )
    freq_ids = (f * band + a * (band // halves) + o * pairs + k).reshape(-1)
    turns = (2 * freq_ids[:, None] + 1) * np.arange(total_time)[None, :] % (2 * total_time)
    angles = turns.astype(np.float32) * np.float32(math.pi / total_time)
    both = np.stack([np.cos(angles), -np.sin(angles)], axis=1).reshape(-1, total_time)
    return (both / np.float32(math.sqrt(total_time))).astype(ml_dtypes.bfloat16)


def transform_kernel(table_ref, series_ref, out_ref):
    blocks, _, local_times = series_ref.shape
    total = None
    for b in range(blocks):
        part = lax.dot_general(
            table_ref[:, b * local_times : (b + 1) * local_times],
            series_ref[b],
            (((1,), (1,)), ((), ())),
            preferred_element_type=jnp.float32,
        )
        total = part if total is None else total + part
    out_ref[...] = total.astype(out_ref.dtype)


def transform(table, series):
    columns, total_time = table.shape
    blocks, rows, local_times = series.shape
    step = min(columns, 256)
    return pl.pallas_call(
        transform_kernel,
        grid=(columns // step,),
        in_specs=[
            pl.BlockSpec((step, total_time), lambda i: (i, 0)),
            pl.BlockSpec((blocks, rows, local_times), lambda i: (0, 0, 0)),
        ],
        out_specs=pl.BlockSpec((step, rows), lambda i: (i, 0)),
        out_shape=jax.ShapeDtypeStruct((columns, rows), jnp.bfloat16),
        compiler_params=pltpu.CompilerParams(vmem_limit_bytes=32 * MIB),
    )(table, series)


def radon_kernel(shift, total_time, base_ref, slow_ref, offs_ref, data_ref, out_ref, cs, sn, tc, ts, held):
    pairs = data_ref.shape[0]
    slows = slow_ref.shape[0]
    half_lanes = data_ref.shape[2] // 2
    quarter = half_lanes // 2
    spread = CURVATURE * slow_ref[...] * offs_ref[...]
    delay = jnp.sqrt(APEX_TIME * APEX_TIME + spread * spread) - APEX_TIME
    phase = base_ref[0] * delay
    cs[0] = jnp.cos(phase)
    sn[0] = jnp.sin(phase)
    turn = delay * (2.0 * math.pi / total_time)
    tc[...] = jnp.cos(turn)
    ts[...] = jnp.sin(turn)
    far = delay * (2.0 * shift * math.pi / total_time)
    far_c = jnp.cos(far)
    far_s = jnp.sin(far)
    cs[1] = cs[0] * far_c - sn[0] * far_s
    sn[1] = sn[0] * far_c + cs[0] * far_s
    lane = lax.broadcasted_iota(jnp.int32, (1, data_ref.shape[2]), 1)
    first_half = lane < half_lanes
    real_lane = lane % half_lanes < quarter

    def step(k, carry):
        data = data_ref[k]
        wide = data.astype(jnp.float32)
        turned = jnp.where(
            real_lane,
            -pltpu.roll(wide, data_ref.shape[2] - quarter, 1),
            pltpu.roll(wide, quarter, 1),
        ).astype(jnp.bfloat16)
        results = []
        for a in range(2):
            c = cs[a]
            s = sn[a]
            results.append(
                jnp.dot(c.astype(jnp.bfloat16), data, preferred_element_type=jnp.float32)
                + jnp.dot(s.astype(jnp.bfloat16), turned, preferred_element_type=jnp.float32)
            )
            cs[a] = c * tc[...] - s * ts[...]
            sn[a] = s * tc[...] + c * ts[...]
        held[pl.ds(k, slows, stride=pairs), :] = jnp.where(first_half, results[0], results[1])
        return carry

    lax.fori_loop(0, pairs, step, 0)
    out_ref[...] = held[...].astype(out_ref.dtype)


def radon(base, slows, offs, data, shift, total_time):
    pairs, offsets, lanes = data.shape
    count = slows.shape[0]
    vmem = pl.BlockSpec(memory_space=pltpu.VMEM)
    return pl.pallas_call(
        functools.partial(radon_kernel, shift, total_time),
        in_specs=[pl.BlockSpec(memory_space=pltpu.SMEM), vmem, vmem, vmem],
        out_specs=vmem,
        out_shape=jax.ShapeDtypeStruct((count * pairs, lanes), jnp.bfloat16),
        scratch_shapes=[
            pltpu.VMEM((2, count, offsets), jnp.float32),
            pltpu.VMEM((2, count, offsets), jnp.float32),
            pltpu.VMEM((count, offsets), jnp.float32),
            pltpu.VMEM((count, offsets), jnp.float32),
            pltpu.VMEM((count * pairs, lanes), jnp.float32),
        ],
        compiler_params=pltpu.CompilerParams(vmem_limit_bytes=40 * MIB),
    )(base, slows, offs, data)


def finish_kernel(scale, in_ref, out_ref):
    devices, slows, pairs, lanes = in_ref.shape
    rows = devices * pairs
    for p in range(slows):
        block = in_ref[:, p].reshape(rows, lanes).astype(jnp.float32) * scale
        turned = block.T
        out_ref[p, :, :rows] = turned[: lanes // 2]
        out_ref[p, :, rows:] = turned[lanes // 2 :]


def finish(parts, scale):
    devices, slows, pairs, lanes = parts.shape
    rows = devices * pairs
    step = 8
    return pl.pallas_call(
        functools.partial(finish_kernel, scale),
        grid=(slows // step,),
        in_specs=[pl.BlockSpec((devices, step, pairs, lanes), lambda i: (0, i, 0, 0))],
        out_specs=pl.BlockSpec((step, lanes // 2, 2 * rows), lambda i: (i, 0, 0)),
        out_shape=jax.ShapeDtypeStruct((slows, lanes // 2, 2 * rows), jnp.float32),
        compiler_params=pltpu.CompilerParams(vmem_limit_bytes=32 * MIB),
    )(parts)


def local(raw_traces, trace_slot, offset_index, slowness_index):
    gathers, local_offsets = trace_slot.shape
    local_times = raw_traces.shape[1]
    freq_devices = lax.axis_size("freq")
    offset_devices = lax.axis_size("offset")
    devices = freq_devices * offset_devices
    total_time = local_times * freq_devices
    offsets = local_offsets * offset_devices
    band = NF // freq_devices
    own_freqs = NF // devices
    halves = 2
    pairs = own_freqs // halves
    own_offsets = local_offsets // freq_devices
    rows = own_offsets * gathers

    picked = raw_traces[trace_slot.T.reshape(-1)]
    series = lax.all_to_all(
        picked.reshape(freq_devices, rows, local_times), "freq", 0, 0, tiled=True
    )
    table = jnp.asarray(table_rows(total_time, freq_devices, offset_devices, halves, pairs))
    spectrum = transform(table, series).reshape(devices, 2 * own_freqs, rows)
    spectra = lax.all_to_all(spectrum, ("freq", "offset"), 0, 0, tiled=True)
    data = spectra.reshape(devices, pairs, 2 * halves, own_offsets, gathers)
    data = data.transpose(1, 0, 3, 2, 4).reshape(pairs, offsets, 2 * halves * gathers)

    offs = offset_index.reshape(offset_devices, freq_devices, own_offsets)
    offs = offs.transpose(1, 0, 2).reshape(1, offsets).astype(jnp.float32)
    slows = slowness_index.astype(jnp.float32)[:, None]
    first = lax.axis_index("freq") * band + lax.axis_index("offset") * pairs
    base = (2 * first + 1).astype(jnp.float32) * (math.pi / total_time)
    panel = radon(base.reshape(1), slows, offs, data, band // halves, total_time)
    panel = panel.reshape(offset_devices, NP // offset_devices, pairs, 2 * halves * gathers)
    parts = lax.all_to_all(panel, "offset", 0, 0, tiled=True)
    result = finish(parts, 1.0 / math.sqrt(offsets))
    return jnp.transpose(result, (0, 2, 1))


def solution(mesh):
    placed = (P("offset", "freq"), P(None, "offset"), P(), P())
    return jax.shard_map(
        local, mesh=mesh, in_specs=placed, out_specs=P("offset", "freq", None), check_vma=False
    )
```

time: 302 us -> 120 us (0.40)
  matrix products: 129 us -> 0 us
  waiting for transfers between devices: 81.9 us -> 27.2 us
  blocking collectives: 16.9 us -> 46.8 us
  local copies, waits for them, and re-layouts: 41.8 us -> 23.7 us
  Pallas kernels: 0 us -> 17 us
  other arithmetic: 13.9 us -> 0.02 us
  between operations: 13.5 us -> 0.12 us
    dot_general x5 -> x0, matrix products: 129 us -> none  [the longest x1 31.1 us: local(): jnp.einsum('fph,ghf->pfg', sines, imag_in, preferred_element_type=jnp.flo...]
    all_gather x2 -> x0, waiting for transfers between devices: 76.8 us -> none  [the longest x1 72.9 us: local(): real_in = lax.all_gather(real_part, 'offset', axis=1, tiled=True)]
    all_to_all x1 -> x2, blocking collectives: 16.9 us -> 46.8 us  [the longest x1 28.3 us: local(): parts = lax.all_to_all(panel, 'offset', 0, 0, tiled=True)]
    all_to_all x1, waiting for transfers between devices: 5.09 us -> 27.2 us  [local(): spectra = lax.all_to_all(spectrum, ('freq', 'offset'), 0, 0, tiled=True)]
    all_gather x2 -> x0, local copies, waits for them, and re-layouts: 17.1 us -> none  [the longest x1 8.61 us: local(): imag_in = lax.all_gather(imag_part, 'offset', axis=1, tiled=True)]
    pallas_call x0 -> x3, Pallas kernels: none -> 17 us  [the longest x1 9.75 us: radon(): pl.pallas_call(functools.partial(radon_kernel, shift, total_time), in_spe...]
    dot_general x4 -> x0, local copies, waits for them, and re-layouts: 15.7 us -> none  [the longest x1 4.35 us: local(): jnp.einsum('fph,ghf->pfg', sines, imag_in, preferred_element_type=jnp.flo...]
    transpose x0 -> x2, local copies, waits for them, and re-layouts: none -> 7.2 us  [the longest x1 6.32 us: local(): data.transpose(1, 0, 3, 2, 4).reshape(pairs, offsets, 2 * halves * gathers)]
  transfers between devices with their start and end apart: 3 -> 1, of which waited for: 3 -> 1; matrix products, arithmetic and copies ran while one was open for 27% -> 0% of each run, Pallas kernels for 0% -> 0%
where the time goes in v1:
time: 120 us
  blocking collectives  46.8 us (39%)
  waiting for transfers between devices  27.2 us (23%)
  local copies, waits for them, and re-layouts  23.7 us (20%)
  Pallas kernels  17 us (14%)
  starting transfers between devices  4.9 us (4%)
    all_to_all x1, blocking collectives, local(): parts = lax.all_to_all(panel, 'offset', 0, 0, tiled=True)  28.3 us
    all_to_all x1, waiting for transfers between devices, local(): spectra = lax.all_to_all(spectrum, ('freq', 'offset'), 0, 0, tiled=True)  27.2 us
    all_to_all x1, blocking collectives, local(): lax.all_to_all(picked.reshape(freq_devices, rows, local_times), 'freq', 0...  18.5 us
    pallas_call x1, Pallas kernels, radon(): pl.pallas_call(functools.partial(radon_kernel, shift, total_time), in_spe...  9.75 us
    transpose x1, local copies, waits for them, and re-layouts, local(): data.transpose(1, 0, 3, 2, 4).reshape(pairs, offsets, 2 * halves * gathers)  6.32 us
    reshape x1, local copies, waits for them, and re-layouts, local(): data.transpose(1, 0, 3, 2, 4).reshape(pairs, offsets, 2 * halves * gathers)  5.21 us
    pallas_call x1, Pallas kernels, transform(): pl.pallas_call(transform_kernel, grid=(columns // step,), in_specs=[pl.Bl...  4.98 us
    all_to_all x1, starting transfers between devices, local(): spectra = lax.all_to_all(spectrum, ('freq', 'offset'), 0, 0, tiled=True)  4.9 us
  transfers between devices with their start and end apart: 1, of which 1 were waited for; matrix products, arithmetic and copies ran while one was open for 0% of the time, Pallas kernels for 0%

profile of v1, /device:TPU:0, one launch (start us, length us, event | category | flops | bytes accessed | tf_op | source)
XLA Modules:
  0.0 119.8 jit_solution(17948677710992470464)
XLA Ops:
  0.0 0.0 copy-start
  0.0 0.9 copy.7
  0.9 0.1 reshape.66
  1.0 0.3 copy-done
  1.2 4.0 %gather_fusion = bf16[1024,512]{1,0:T(8,128)(2,1)S(1)} fusion(bf16[1024,512]{1,0:T(8,128)(2,1)S(1)} %copy-done, s32[1024]{0:T(1024)S(1)} %broadcast_clamp_fusion), kind=kCustom, calls=%fused_computation | custom fusion | bytes 2101248 | tf_op jit(solution)/shard_map/gather | solution.py:173
  5.2 18.5 %all_to_all.15.series_ref = bf16[4,256,512]{2,1,0:T(8,128)(2,1)S(1)} all-to-all(bf16[4,256,512]{2,1,0:T(8,128)(2,1)S(1)} %bitcast.12), channel_id=1, replica_groups=mesh['freq'=4,'offset'=8] {'freq'}, dimensions={0} | all-to-all | bytes 2097152 | tf_op jit(solution)/shard_map/all_to_all | solution.py:174
  23.7 0.0 copy-start.1
  23.7 3.4 %copy-done.1 = bf16[2048,2048]{1,0:T(8,128)(2,1)S(1)} copy-done((bf16[2048,2048]{1,0:T(8,128)(2,1)S(1)}, bf16[2048,2048]{1,0:T(8,128)(2,1)}, u32[]{:S(2)}) %copy-start.1) | copy-done | bytes 8388632
  27.1 0.0 copy-start.2
  27.1 0.0 copy-start.3
  27.1 5.0 %shard_map.55 = bf16[2048,256]{1,0:T(8,128)(2,1)} custom-call(bf16[2048,2048]{1,0:T(8,128)(2,1)S(1)} %copy-done.1, bf16[4,256,512]{2,1,0:T(8,128)(2,1)S(1)} %all_to_all.15.series_ref), custom_call_target="tpu_custom_call" | custom-call | tf_op jit(solution)/shard_map/pallas_call | solution.py:54
  32.1 4.9 %all-to-all-start.1 = ((bf16[32,64,256]{2,1,0:T(8,128)(2,1)}), bf16[32,64,256]{2,1,0:T(8,128)(2,1)S(1)}, u32[]{:S(2)}, u32[]{:S(2)}) async-start(bf16[32,64,256]{2,1,0:T(8,128)(2,1)} %bitcast.6), calls=%async_computation.1 | async-start | bytes 2097152 | tf_op jit(solution)/shard_map/all_to_all | solution.py:179
  37.0 0.0 copy-done.2
  37.0 0.1 copy.9.slow_ref
  37.2 0.0 copy-done.3
  37.2 0.1 convert_element_type.18
  37.3 0.1 convert_element_type.20.offs_ref
  37.4 27.2 %all-to-all-done.1 = bf16[32,64,256]{2,1,0:T(8,128)(2,1)S(1)} async-done(((bf16[32,64,256]{2,1,0:T(8,128)(2,1)}), bf16[32,64,256]{2,1,0:T(8,128)(2,1)S(1)}, u32[]{:S(2)}, u32[]{:S(2)}) %all-to-all-start.1) | async-done | bytes 1048608 | tf_op jit(solution)/shard_map/all_to_all | solution.py:179
  64.6 3.3 %reshape.69 = bf16[32,16,4,8,32]{4,3,2,1,0:T(8,128)(2,1)} reshape(bf16[32,64,256]{2,1,0:T(8,128)(2,1)S(1)} %all-to-all-done.1) | data formatting | bytes 2097152 | tf_op jit(solution)/shard_map/reshape | solution.py:180
  67.9 6.3 %copy.8 = bf16[16,32,8,4,32]{4,3,2,1,0:T(4,128)(2,1)} copy(bf16[16,32,8,4,32]{4,2,3,0,1:T(8,128)(2,1)} %bitcast.11) | data formatting | bytes 2097152 | tf_op jit(solution)/shard_map/transpose | solution.py:181
  74.2 5.2 %reshape.70.data_ref = bf16[16,256,128]{2,1,0:T(8,128)(2,1)S(1)} reshape(bf16[16,32,8,4,32]{4,3,2,1,0:T(4,128)(2,1)} %copy.8) | data formatting | bytes 2097152 | tf_op jit(solution)/shard_map/reshape | solution.py:181
  79.5 9.8 %shard_map.56 = bf16[4096,128]{1,0:T(8,128)(2,1)S(1)} custom-call(f32[1]{0:T(128)} %bitcast.base_ref, f32[256,1]{1,0:T(8,128)S(1)} %copy.9.slow_ref, f32[1,256]{1,0:T(1,128)S(1)} %convert_element_type.20.offs_ref, bf16[16,256,128]{2,1,0:T(8,128)(2,1)S(1)} %reshape.70.data_ref), custom_call_target="tpu_custom_call" | custom-call | tf_op jit(solution)/shard_map/pallas_call | solution.py:118
  89.2 28.3 %all_to_all.16.in_ref = bf16[8,32,16,128]{3,2,1,0:T(8,128)(2,1)S(1)} all-to-all(bf16[8,32,16,128]{3,2,1,0:T(8,128)(2,1)S(1)} %bitcast.10), channel_id=1, replica_groups=mesh['freq'=4,'offset'=8] {'offset'}, dimensions={0} | all-to-all | bytes 2097152 | tf_op jit(solution)/shard_map/all_to_all | solution.py:190
  117.5 2.3 %shard_map.57 = f32[32,64,256]{2,1,0:T(8,128)} custom-call(bf16[8,32,16,128]{3,2,1,0:T(8,128)(2,1)S(1)} %all_to_all.16.in_ref), custom_call_target="tpu_custom_call" | custom-call | tf_op jit(solution)/shard_map/pallas_call | solution.py:148
  (5 shorter events, 0.0 us)
Async XLA Ops:
  0.0 1.2 %copy-start = (bf16[1024,512]{1,0:T(8,128)(2,1)S(1)}, bf16[1024,512]{1,0:T(8,128)(2,1)}, u32[]{:S(2)}) copy-start(bf16[1024,512]{1,0:T(8,128)(2,1)} %param.5) | copy-start | bytes 3145732
  23.7 3.4 %copy-start.1 = (bf16[2048,2048]{1,0:T(8,128)(2,1)S(1)}, bf16[2048,2048]{1,0:T(8,128)(2,1)}, u32[]{:S(2)}) copy-start(bf16[2048,2048]{1,0:T(8,128)(2,1)} %constant.24.clone.table_ref) | copy-start | bytes 25165828
  27.1 9.9 %copy-start.2 = (s32[256]{0:T(256)S(1)}, s32[256]{0:T(256)}, u32[]{:S(2)}) copy-start(s32[256]{0:T(256)} %param.8) | copy-start | bytes 3076
  27.1 10.1 %copy-start.3 = (s32[256]{0:T(256)S(1)}, s32[256]{0:T(256)}, u32[]{:S(2)}) copy-start(s32[256]{0:T(256)} %param.7) | copy-start | bytes 3076
  32.1 32.5 %all-to-all-start.1 = ((bf16[32,64,256]{2,1,0:T(8,128)(2,1)}), bf16[32,64,256]{2,1,0:T(8,128)(2,1)S(1)}, u32[]{:S(2)}, u32[]{:S(2)}) async-start(bf16[32,64,256]{2,1,0:T(8,128)(2,1)} %bitcast.6), calls=%async_computation.1 | async-start | bytes 2097152 | tf_op jit(solution)/shard_map/all_to_all | solution.py:179

commit v2 on v1

v2 whole, which is shorter than its diff:
```python
import functools
import math

import jax
import jax.numpy as jnp
import ml_dtypes
import numpy as np
from jax import lax
from jax.experimental import pallas as pl
from jax.experimental.pallas import tpu as pltpu
from jax.sharding import PartitionSpec as P

NF = 1024
NP = 256
APEX_TIME = 100.0
CURVATURE = 0.0003
MIB = 1 << 20


def table_rows(total_time, freq_devices, offset_devices, halves, pairs):
    band = NF // freq_devices
    f, o, a, k = np.meshgrid(
        np.arange(freq_devices),
        np.arange(offset_devices),
        np.arange(halves),
        np.arange(pairs),
        indexing="ij",
    )
    freq_ids = (f * band + a * (band // halves) + o * pairs + k).reshape(-1, pairs)
    turns = (2 * freq_ids[..., None] + 1) * np.arange(total_time) % (2 * total_time)
    angles = turns.astype(np.float32) * np.float32(math.pi / total_time)
    both = np.stack([np.cos(angles), -np.sin(angles)], axis=1).reshape(-1, total_time)
    return (both / np.float32(math.sqrt(total_time))).astype(ml_dtypes.bfloat16)


def transform_kernel(table_ref, series_ref, out_ref, held, sems):
    blocks, _, local_times = series_ref.shape
    chunks, step, _ = held.shape
    copies = [
        pltpu.make_async_copy(table_ref.at[pl.ds(i * step, step)], held.at[i], sems.at[i])
        for i in range(chunks)
    ]
    for copy in copies:
        copy.start()
    for i in range(chunks):
        copies[i].wait()
        total = None
        for b in range(blocks):
            part = lax.dot_general(
                held[i, :, b * local_times : (b + 1) * local_times],
                series_ref[b],
                (((1,), (1,)), ((), ())),
                preferred_element_type=jnp.float32,
            )
            total = part if total is None else total + part
        out_ref[i * step : (i + 1) * step] = total.astype(out_ref.dtype)


def transform(table, series):
    columns, total_time = table.shape
    blocks, rows, local_times = series.shape
    chunks = 4
    vmem = pl.BlockSpec(memory_space=pltpu.VMEM)
    return pl.pallas_call(
        transform_kernel,
        in_specs=[pl.BlockSpec(memory_space=pltpu.HBM), vmem],
        out_specs=vmem,
        out_shape=jax.ShapeDtypeStruct((columns, rows), jnp.bfloat16),
        scratch_shapes=[
            pltpu.VMEM((chunks, columns // chunks, total_time), jnp.bfloat16),
            pltpu.SemaphoreType.DMA((chunks,)),
        ],
        compiler_params=pltpu.CompilerParams(vmem_limit_bytes=32 * MIB),
    )(table, series)


def moveout_kernel(shift, total_time, base_ref, slow_ref, offs_ref, out_ref, cs, sn, tc, ts):
    @pl.when(pl.program_id(0) == 0)
    def start():
        spread = CURVATURE * slow_ref[...] * offs_ref[...]
        delay = jnp.sqrt(APEX_TIME * APEX_TIME + spread * spread) - APEX_TIME
        phase = base_ref[0] * delay
        cs[0] = jnp.cos(phase)
        sn[0] = jnp.sin(phase)
        turn = delay * (2.0 * math.pi / total_time)
        tc[...] = jnp.cos(turn)
        ts[...] = jnp.sin(turn)
        far = delay * (2.0 * shift * math.pi / total_time)
        far_c = jnp.cos(far)
        far_s = jnp.sin(far)
        cs[1] = cs[0] * far_c - sn[0] * far_s
        sn[1] = sn[0] * far_c + cs[0] * far_s

    for a in range(2):
        c = cs[a]
        s = sn[a]
        out_ref[0, 2 * a] = c.astype(out_ref.dtype)
        out_ref[0, 2 * a + 1] = s.astype(out_ref.dtype)
        cs[a] = c * tc[...] - s * ts[...]
        sn[a] = s * tc[...] + c * ts[...]


def moveout(base, slows, offs, pairs, shift, total_time):
    count = slows.shape[0]
    offsets = offs.shape[1]
    return pl.pallas_call(
        functools.partial(moveout_kernel, shift, total_time),
        grid=(pairs,),
        in_specs=[
            pl.BlockSpec(memory_space=pltpu.SMEM),
            pl.BlockSpec((count, 1), lambda k: (0, 0)),
            pl.BlockSpec((1, offsets), lambda k: (0, 0)),
        ],
        out_specs=pl.BlockSpec((1, 4, count, offsets), lambda k: (k, 0, 0, 0)),
        out_shape=jax.ShapeDtypeStruct((pairs, 4, count, offsets), jnp.bfloat16),
        scratch_shapes=[
            pltpu.VMEM((2, count, offsets), jnp.float32),
            pltpu.VMEM((2, count, offsets), jnp.float32),
            pltpu.VMEM((count, offsets), jnp.float32),
            pltpu.VMEM((count, offsets), jnp.float32),
        ],
        compiler_params=pltpu.CompilerParams(vmem_limit_bytes=24 * MIB),
        cost_estimate=pl.CostEstimate(
            flops=pairs * 40 * count * offsets,
            bytes_accessed=pairs * 8 * count * offsets,
            transcendentals=6 * count * offsets,
        ),
    )(base, slows, offs)


def regroup(data_ref, wide, gathers):
    devices, blocks, pairs, rows = data_ref.shape
    lanes = blocks * gathers
    own_offsets = rows // gathers

    def exact(d, carry):
        for h in range(own_offsets):
            cut = [
                data_ref[d, c, :, h * gathers : (h + 1) * gathers].astype(jnp.float32)
                for c in range(blocks)
            ]
            start = pl.multiple_of((d * own_offsets + h) * pairs, pairs)
            wide[pl.ds(start, pairs), :] = jnp.concatenate(cut, axis=1)
        return carry

    lane = lax.broadcasted_iota(jnp.int32, (1, lanes), 1)
    low_half = lane < 2 * gathers
    low_part = lane % (2 * gathers) < gathers

    def rolled(d, carry):
        for q in range(rows // lanes):
            x = [
                data_ref[d, c, :, q * lanes : (q + 1) * lanes].astype(jnp.float32)
                for c in range(blocks)
            ]
            for top in range(2):
                pair = []
                for part in range(2):
                    a, b = x[part], x[2 + part]
                    if top == 0:
                        pair.append(jnp.where(low_half, a, pltpu.roll(b, 2 * gathers, 1)))
                    else:
                        pair.append(jnp.where(low_half, pltpu.roll(a, 2 * gathers, 1), b))
                outs = (
                    jnp.where(low_part, pair[0], pltpu.roll(pair[1], gathers, 1)),
                    jnp.where(low_part, pltpu.roll(pair[0], lanes - gathers, 1), pair[1]),
                )
                for bit in range(2):
                    h = 4 * q + 2 * top + bit
                    start = pl.multiple_of((d * own_offsets + h) * pairs, pairs)
                    wide[pl.ds(start, pairs), :] = outs[bit]
        return carry

    lax.fori_loop(0, devices, rolled if rows % lanes == 0 else exact, 0, unroll=2)


def radon_kernel(gathers, turn_ref, data_ref, out_ref, wide, held):
    k = pl.program_id(0)
    pairs = data_ref.shape[2]
    lanes = wide.shape[1]
    offsets = wide.shape[0] // pairs
    slows = turn_ref.shape[2]

    @pl.when(k == 0)
    def start():
        regroup(data_ref, wide, gathers)

    lane = lax.broadcasted_iota(jnp.int32, (1, lanes), 1)
    first_half = lane < 2 * gathers
    real_lane = lane % (2 * gathers) < gathers
    block = wide[pl.ds(k, offsets, stride=pairs), :]
    turned = jnp.where(
        real_lane, -pltpu.roll(block, lanes - gathers, 1), pltpu.roll(block, gathers, 1)
    ).astype(jnp.bfloat16)
    data = block.astype(jnp.bfloat16)
    results = [
        jnp.dot(turn_ref[0, 2 * a], data, preferred_element_type=jnp.float32)
        + jnp.dot(turn_ref[0, 2 * a + 1], turned, preferred_element_type=jnp.float32)
        for a in range(2)
    ]
    held[pl.ds(k, slows, stride=pairs), :] = jnp.where(first_half, results[0], results[1])

    @pl.when(k == pairs - 1)
    def end():
        out_ref[...] = held[...].astype(out_ref.dtype)


def radon(turns, data, gathers):
    pairs, parts, count, offsets = turns.shape
    lanes = parts * gathers
    return pl.pallas_call(
        functools.partial(radon_kernel, gathers),
        grid=(pairs,),
        in_specs=[
            pl.BlockSpec((1, parts, count, offsets), lambda k: (k, 0, 0, 0)),
            pl.BlockSpec(data.shape, lambda k: (0, 0, 0, 0)),
        ],
        out_specs=pl.BlockSpec((count * pairs, lanes), lambda k: (0, 0)),
        out_shape=jax.ShapeDtypeStruct((count * pairs, lanes), jnp.bfloat16),
        scratch_shapes=[
            pltpu.VMEM((offsets * pairs, lanes), jnp.float32),
            pltpu.VMEM((count * pairs, lanes), jnp.float32),
        ],
        compiler_params=pltpu.CompilerParams(vmem_limit_bytes=24 * MIB),
    )(turns, data)


def finish_kernel(scale, in_ref, out_ref):
    devices, slows, pairs, lanes = in_ref.shape
    rows = devices * pairs
    for p in range(slows):
        block = in_ref[:, p].reshape(rows, lanes).astype(jnp.float32) * scale
        turned = block.T
        out_ref[p, :, :rows] = turned[: lanes // 2]
        out_ref[p, :, rows:] = turned[lanes // 2 :]


def finish(parts, scale):
    devices, slows, pairs, lanes = parts.shape
    rows = devices * pairs
    step = 8
    return pl.pallas_call(
        functools.partial(finish_kernel, scale),
        grid=(slows // step,),
        in_specs=[pl.BlockSpec((devices, step, pairs, lanes), lambda i: (0, i, 0, 0))],
        out_specs=pl.BlockSpec((step, lanes // 2, 2 * rows), lambda i: (i, 0, 0)),
        out_shape=jax.ShapeDtypeStruct((slows, lanes // 2, 2 * rows), jnp.float32),
        compiler_params=pltpu.CompilerParams(vmem_limit_bytes=32 * MIB),
    )(parts)


def local(raw_traces, trace_slot, offset_index, slowness_index):
    gathers, local_offsets = trace_slot.shape
    local_times = raw_traces.shape[1]
    freq_devices = lax.axis_size("freq")
    offset_devices = lax.axis_size("offset")
    devices = freq_devices * offset_devices
    total_time = local_times * freq_devices
    offsets = local_offsets * offset_devices
    band = NF // freq_devices
    own_freqs = NF // devices
    halves = 2
    pairs = own_freqs // halves
    own_offsets = local_offsets // freq_devices
    rows = own_offsets * gathers

    picked = raw_traces[trace_slot.T.reshape(-1)]
    series = lax.all_to_all(
        picked.reshape(freq_devices, rows, local_times), "freq", 0, 0, tiled=True
    )
    table = jnp.asarray(table_rows(total_time, freq_devices, offset_devices, halves, pairs))
    spectrum = transform(table, series).reshape(devices, 2 * own_freqs, rows)
    spectra = lax.all_to_all(spectrum, ("freq", "offset"), 0, 0, tiled=True)
    data = spectra.reshape(devices, 2 * halves, pairs, rows)

    offs = offset_index.reshape(offset_devices, freq_devices, own_offsets)
    offs = offs.transpose(1, 0, 2).reshape(1, offsets).astype(jnp.float32)
    slows = slowness_index.astype(jnp.float32)[:, None]
    first = lax.axis_index("freq") * band + lax.axis_index("offset") * pairs
    base = (2 * first + 1).astype(jnp.float32) * (math.pi / total_time)
    turns = moveout(base.reshape(1), slows, offs, pairs, band // halves, total_time)
    panel = radon(turns, data, gathers)
    panel = panel.reshape(offset_devices, NP // offset_devices, pairs, 2 * halves * gathers)
    parts = lax.all_to_all(panel, "offset", 0, 0, tiled=True)
    result = finish(parts, 1.0 / math.sqrt(offsets))
    return jnp.transpose(result, (0, 2, 1))


def solution(mesh):
    placed = (P("offset", "freq"), P(None, "offset"), P(), P())
    return jax.shard_map(
        local, mesh=mesh, in_specs=placed, out_specs=P("offset", "freq", None), check_vma=False
    )
```

time: 120 us -> 110 us (0.917)
  waiting for transfers between devices: 27.2 us -> 16.7 us
  Pallas kernels: 17 us -> 25.7 us
  local copies, waits for them, and re-layouts: 23.7 us -> 15.5 us
    all_to_all x1, waiting for transfers between devices: 27.2 us -> 16.7 us  [local(): spectra = lax.all_to_all(spectrum, ('freq', 'offset'), 0, 0, tiled=True)]
    pallas_call x2 -> x3, Pallas kernels: 14.7 us -> 23.4 us  [the longest x1 9.53 us: radon(): pl.pallas_call(functools.partial(radon_kernel, gathers), grid=(pairs,), i...]
    reshape x2 -> x0, local copies, waits for them, and re-layouts: 8.55 us -> none  [the longest x1 5.21 us: local(): data.transpose(1, 0, 3, 2, 4).reshape(pairs, offsets, 2 * halves * gathers)]
    unnamed x8 -> x12, local copies, waits for them, and re-layouts: 3.64 us -> 10.3 us
    transpose x1 -> x0, local copies, waits for them, and re-layouts: 6.32 us -> none  [local(): data.transpose(1, 0, 3, 2, 4).reshape(pairs, offsets, 2 * halves * gathers)]
  transfers between devices with their start and end apart: 1 -> 1, of which waited for: 1 -> 1; matrix products, arithmetic and copies ran while one was open for 0% -> 0% of each run, Pallas kernels for 0% -> 7%
where the time goes in v2:
time: 110 us
  blocking collectives  46.8 us (43%)
  Pallas kernels  25.7 us (23%)
  waiting for transfers between devices  16.7 us (15%)
  local copies, waits for them, and re-layouts  15.5 us (14%)
  starting transfers between devices  4.9 us (4%)
    all_to_all x1, blocking collectives, local(): parts = lax.all_to_all(panel, 'offset', 0, 0, tiled=True)  28.3 us
    all_to_all x1, blocking collectives, local(): lax.all_to_all(picked.reshape(freq_devices, rows, local_times), 'freq', 0...  18.5 us
    all_to_all x1, waiting for transfers between devices, local(): spectra = lax.all_to_all(spectrum, ('freq', 'offset'), 0, 0, tiled=True)  16.7 us
    unnamed x12, local copies, waits for them, and re-layouts  10.3 us
    pallas_call x1, Pallas kernels, radon(): pl.pallas_call(functools.partial(radon_kernel, gathers), grid=(pairs,), i...  9.53 us
    pallas_call x1, Pallas kernels, moveout(): pl.pallas_call(functools.partial(moveout_kernel, shift, total_time), grid...  7.29 us
    pallas_call x1, Pallas kernels, transform(): pl.pallas_call(transform_kernel, in_specs=[pl.BlockSpec(memory_space=pltp...  6.61 us
    all_to_all x1, starting transfers between devices, local(): spectra = lax.all_to_all(spectrum, ('freq', 'offset'), 0, 0, tiled=True)  4.9 us
  transfers between devices with their start and end apart: 1, of which 1 were waited for; matrix products, arithmetic and copies ran while one was open for 0% of the time, Pallas kernels for 7%

profile of v2, /device:TPU:0, one launch (start us, length us, event | category | flops | bytes accessed | tf_op | source)
XLA Modules:
  0.0 109.7 jit_solution(14395096742471716566)
XLA Ops:
  0.0 0.0 copy-start
  0.0 0.9 copy.8
  0.9 0.1 reshape.63
  1.0 0.3 copy-done
  1.2 4.0 %gather_fusion = bf16[1024,512]{1,0:T(8,128)(2,1)S(1)} fusion(bf16[1024,512]{1,0:T(8,128)(2,1)S(1)} %copy-done, s32[1024]{0:T(1024)S(1)} %broadcast_clamp_fusion), kind=kCustom, calls=%fused_computation | custom fusion | bytes 2101248 | tf_op jit(solution)/shard_map/gather | solution.py:267
  5.2 0.0 copy-start.4
  5.2 0.0 copy-start.5
  5.2 18.5 %all_to_all.15.series_ref = bf16[4,256,512]{2,1,0:T(8,128)(2,1)S(1)} all-to-all(bf16[4,256,512]{2,1,0:T(8,128)(2,1)S(1)} %bitcast.12), channel_id=1, replica_groups=mesh['freq'=4,'offset'=8] {'freq'}, dimensions={0} | all-to-all | bytes 2097152 | tf_op jit(solution)/shard_map/all_to_all | solution.py:268
  23.7 0.0 copy-start.3
  23.7 3.4 %copy-done.3 = bf16[2048,2048]{1,0:T(8,128)(2,1)S(1)} copy-done((bf16[2048,2048]{1,0:T(8,128)(2,1)S(1)}, bf16[2048,2048]{1,0:T(8,128)(2,1)}, u32[]{:S(2)}) %copy-start.3) | copy-done | bytes 8388632
  27.1 6.6 %shard_map.56 = bf16[2048,256]{1,0:T(8,128)(2,1)} custom-call(bf16[2048,2048]{1,0:T(8,128)(2,1)S(1)} %copy-done.3, bf16[4,256,512]{2,1,0:T(8,128)(2,1)S(1)} %all_to_all.15.series_ref), custom_call_target="tpu_custom_call" | custom-call | tf_op jit(solution)/shard_map/pallas_call | solution.py:64
  33.7 4.9 %all-to-all-start.1 = ((bf16[32,64,256]{2,1,0:T(8,128)(2,1)}), bf16[32,64,256]{2,1,0:T(8,128)(2,1)S(1)}, u32[]{:S(2)}, u32[]{:S(2)}) async-start(bf16[32,64,256]{2,1,0:T(8,128)(2,1)} %bitcast.6), calls=%async_computation.1 | async-start | bytes 2097152 | tf_op jit(solution)/shard_map/all_to_all | solution.py:273
  38.7 0.0 copy-done.4
  38.7 0.0 copy-done.5
  38.7 0.1 convert_element_type.18
  38.8 0.1 convert_element_type.20.offs_ref
  38.9 0.1 copy.7.slow_ref
  39.0 7.3 %shard_map.55.turn_ref = bf16[16,4,256,256]{3,2,1,0:T(8,128)(2,1)S(1)} custom-call(f32[1]{0:T(128)} %bitcast.base_ref, f32[256,1]{1,0:T(8,128)S(1)} %copy.7.slow_ref, f32[1,256]{1,0:T(1,128)S(1)} %convert_element_type.20.offs_ref), custom_call_target="tpu_custom_call" | custom-call | flops 41943040 | bytes 8388608 | tf_op jit(solution)/shard_map/pallas_call | solution.py:106
  46.3 0.0 copy-start.1
  46.4 3.2 %copy-done.1 = bf16[16,4,256,256]{3,2,1,0:T(8,128)(2,1)} copy-done((bf16[16,4,256,256]{3,2,1,0:T(8,128)(2,1)}, bf16[16,4,256,256]{3,2,1,0:T(8,128)(2,1)S(1)}, u32[]{:S(2)}) %copy-start.1) | copy-done | bytes 8388632
  49.6 16.7 %all-to-all-done.1 = bf16[32,64,256]{2,1,0:T(8,128)(2,1)S(1)} async-done(((bf16[32,64,256]{2,1,0:T(8,128)(2,1)}), bf16[32,64,256]{2,1,0:T(8,128)(2,1)S(1)}, u32[]{:S(2)}, u32[]{:S(2)}) %all-to-all-start.1) | async-done | bytes 1048608 | tf_op jit(solution)/shard_map/all_to_all | solution.py:273
  66.2 0.0 copy-start.2
  66.2 3.4 %copy-done.2 = bf16[16,4,256,256]{3,2,1,0:T(8,128)(2,1)S(1)} copy-done((bf16[16,4,256,256]{3,2,1,0:T(8,128)(2,1)S(1)}, bf16[16,4,256,256]{3,2,1,0:T(8,128)(2,1)}, u32[]{:S(2)}) %copy-start.2) | copy-done | bytes 8388632
  69.6 9.5 %shard_map.57 = bf16[4096,128]{1,0:T(8,128)(2,1)S(1)} custom-call(bf16[16,4,256,256]{3,2,1,0:T(8,128)(2,1)S(1)} %copy-done.2, bf16[32,4,16,256]{3,2,1,0:T(8,128)(2,1)S(1)} %bitcast.10), custom_call_target="tpu_custom_call" | custom-call | tf_op jit(solution)/shard_map/pallas_call | solution.py:211
  79.2 28.3 %all_to_all.16.in_ref = bf16[8,32,16,128]{3,2,1,0:T(8,128)(2,1)S(1)} all-to-all(bf16[8,32,16,128]{3,2,1,0:T(8,128)(2,1)S(1)} %bitcast.11), channel_id=1, replica_groups=mesh['freq'=4,'offset'=8] {'offset'}, dimensions={0} | all-to-all | bytes 2097152 | tf_op jit(solution)/shard_map/all_to_all | solution.py:284
  107.5 2.3 %shard_map.58 = f32[32,64,256]{2,1,0:T(8,128)} custom-call(bf16[8,32,16,128]{3,2,1,0:T(8,128)(2,1)S(1)} %all_to_all.16.in_ref), custom_call_target="tpu_custom_call" | custom-call | tf_op jit(solution)/shard_map/pallas_call | solution.py:242
  (5 shorter events, 0.0 us)
Async XLA Ops:
  0.0 1.2 %copy-start = (bf16[1024,512]{1,0:T(8,128)(2,1)S(1)}, bf16[1024,512]{1,0:T(8,128)(2,1)}, u32[]{:S(2)}) copy-start(bf16[1024,512]{1,0:T(8,128)(2,1)} %param.5) | copy-start | bytes 3145732
  5.2 33.5 %copy-start.4 = (s32[256]{0:T(256)S(1)}, s32[256]{0:T(256)}, u32[]{:S(2)}) copy-start(s32[256]{0:T(256)} %param.7) | copy-start | bytes 3076
  5.2 33.5 %copy-start.5 = (s32[256]{0:T(256)S(1)}, s32[256]{0:T(256)}, u32[]{:S(2)}) copy-start(s32[256]{0:T(256)} %param.8) | copy-start | bytes 3076
  23.7 3.4 %copy-start.3 = (bf16[2048,2048]{1,0:T(8,128)(2,1)S(1)}, bf16[2048,2048]{1,0:T(8,128)(2,1)}, u32[]{:S(2)}) copy-start(bf16[2048,2048]{1,0:T(8,128)(2,1)} %constant.24.clone.table_ref) | copy-start | bytes 25165828
  33.7 32.5 %all-to-all-start.1 = ((bf16[32,64,256]{2,1,0:T(8,128)(2,1)}), bf16[32,64,256]{2,1,0:T(8,128)(2,1)S(1)}, u32[]{:S(2)}, u32[]{:S(2)}) async-start(bf16[32,64,256]{2,1,0:T(8,128)(2,1)} %bitcast.6), calls=%async_computation.1 | async-start | bytes 2097152 | tf_op jit(solution)/shard_map/all_to_all | solution.py:273
  46.3 3.2 %copy-start.1 = (bf16[16,4,256,256]{3,2,1,0:T(8,128)(2,1)}, bf16[16,4,256,256]{3,2,1,0:T(8,128)(2,1)S(1)}, u32[]{:S(2)}) copy-start(bf16[16,4,256,256]{3,2,1,0:T(8,128)(2,1)S(1)} %shard_map.55.turn_ref) | copy-start | bytes 25165828
  66.2 3.4 %copy-start.2 = (bf16[16,4,256,256]{3,2,1,0:T(8,128)(2,1)S(1)}, bf16[16,4,256,256]{3,2,1,0:T(8,128)(2,1)}, u32[]{:S(2)}) copy-start(bf16[16,4,256,256]{3,2,1,0:T(8,128)(2,1)} %copy-done.1) | copy-start | bytes 25165828

commit v3 on v2

--- a/solution.py
+++ b/solution.py
@@ -33,8 +33,57 @@
     return (both / np.float32(math.sqrt(total_time))).astype(ml_dtypes.bfloat16)
 
 
-def transform_kernel(table_ref, series_ref, out_ref, held, sems):
-    blocks, _, local_times = series_ref.shape
+def pick_kernel(slot_ref, raw_ref, out_ref):
+    gathers = slot_ref.shape[0]
+    groups, rows, _ = out_ref.shape
+    own_offsets = rows // gathers
+    lane = lax.broadcasted_iota(jnp.int32, (gathers, raw_ref.shape[0]), 1)
+    for f in range(groups):
+        picks = [
+            jnp.where(lane == slot_ref[:, h : h + 1], 1.0, 0.0).astype(jnp.bfloat16)
+            for h in range(f * own_offsets, (f + 1) * own_offsets)
+        ]
+        out_ref[f] = jnp.dot(
+            jnp.concatenate(picks, axis=0), raw_ref[...], preferred_element_type=jnp.float32
+        ).astype(out_ref.dtype)
+
+
+def pick(trace_slot, raw_traces, groups):
+    gathers, local_offsets = trace_slot.shape
+    rows = gathers * local_offsets // groups
+    vmem = pl.BlockSpec(memory_space=pltpu.VMEM)
+    return pl.pallas_call(
+        pick_kernel,
+        in_specs=[vmem, vmem],
+        out_specs=vmem,
+        out_shape=jax.ShapeDtypeStruct((groups, rows, raw_traces.shape[1]), raw_traces.dtype),
+        compiler_params=pltpu.CompilerParams(vmem_limit_bytes=32 * MIB),
+    )(trace_slot, raw_traces)
+
+
+def regroup(total, pairs, gathers):
+    lanes = 4 * gathers
+    lane = lax.broadcasted_iota(jnp.int32, (1, lanes), 1)
+    low_half = lane < 2 * gathers
+    low_part = lane % (2 * gathers) < gathers
+    found = []
+    for q in range(total.shape[1] // lanes):
+        x = [total[c * pairs : (c + 1) * pairs, q * lanes : (q + 1) * lanes] for c in range(4)]
+        for top in range(2):
+            pair = []
+            for part in range(2):
+                a, b = x[part], x[2 + part]
+                if top == 0:
+                    pair.append(jnp.where(low_half, a, pltpu.roll(b, 2 * gathers, 1)))
+                else:
+                    pair.append(jnp.where(low_half, pltpu.roll(a, 2 * gathers, 1), b))
+            found.append(jnp.where(low_part, pair[0], pltpu.roll(pair[1], gathers, 1)))
+            found.append(jnp.where(low_part, pltpu.roll(pair[0], lanes - gathers, 1), pair[1]))
+    return found
+
+
+def transform_kernel(pairs, gathers, table_ref, series_ref, out_ref, held, sems):
+    blocks, rows, local_times = series_ref.shape
     chunks, step, _ = held.shape
     copies = [
         pltpu.make_async_copy(table_ref.at[pl.ds(i * step, step)], held.at[i], sems.at[i])
@@ -53,25 +102,39 @@
                 preferred_element_type=jnp.float32,
             )
             total = part if total is None else total + part
-        out_ref[i * step : (i + 1) * step] = total.astype(out_ref.dtype)
-
-
-def transform(table, series):
+        if len(out_ref.shape) == 2:
+            out_ref[i * step : (i + 1) * step] = total.astype(out_ref.dtype)
+            continue
+        targets = step // (4 * pairs)
+        for d in range(targets):
+            found = regroup(total[d * 4 * pairs : (d + 1) * 4 * pairs], pairs, gathers)
+            for h, value in enumerate(found):
+                out_ref[i * targets + d, h] = value.astype(out_ref.dtype)
+
+
+def transform(table, series, pairs, gathers):
     columns, total_time = table.shape
     blocks, rows, local_times = series.shape
+    devices = columns // (4 * pairs)
+    final = (devices, rows // gathers, pairs, 4 * gathers)
     chunks = 4
+    aligned = rows % (4 * gathers) == 0 and pairs % 8 == 0 and devices % chunks == 0
     vmem = pl.BlockSpec(memory_space=pltpu.VMEM)
-    return pl.pallas_call(
-        transform_kernel,
-        in_specs=[pl.BlockSpec(memory_space=pltpu.HBM), vmem],
+    out = pl.pallas_call(
+        functools.partial(transform_kernel, pairs, gathers),
+        in_specs=[pl.BlockSpec(memory_space=pl.ANY), vmem],
         out_specs=vmem,
-        out_shape=jax.ShapeDtypeStruct((columns, rows), jnp.bfloat16),
+        out_shape=jax.ShapeDtypeStruct(final if aligned else (columns, rows), jnp.bfloat16),
         scratch_shapes=[
             pltpu.VMEM((chunks, columns // chunks, total_time), jnp.bfloat16),
             pltpu.SemaphoreType.DMA((chunks,)),
         ],
-        compiler_params=pltpu.CompilerParams(vmem_limit_bytes=32 * MIB),
+        compiler_params=pltpu.CompilerParams(vmem_limit_bytes=56 * MIB),
     )(table, series)
+    if aligned:
+        return out
+    out = out.reshape(devices, 4, pairs, rows // gathers, gathers)
+    return out.transpose(0, 3, 2, 1, 4).reshape(final)
 
 
 def moveout_kernel(shift, total_time, base_ref, slow_ref, offs_ref, out_ref, cs, sn, tc, ts):
@@ -94,8 +157,8 @@
     for a in range(2):
         c = cs[a]
         s = sn[a]
-        out_ref[0, 2 * a] = c.astype(out_ref.dtype)
-        out_ref[0, 2 * a + 1] = s.astype(out_ref.dtype)
+        out_ref[0, a] = c.astype(out_ref.dtype)
+        out_ref[0, 2 + a] = s.astype(out_ref.dtype)
         cs[a] = c * tc[...] - s * ts[...]
         sn[a] = s * tc[...] + c * ts[...]
 
@@ -119,7 +182,7 @@
             pltpu.VMEM((count, offsets), jnp.float32),
             pltpu.VMEM((count, offsets), jnp.float32),
         ],
-        compiler_params=pltpu.CompilerParams(vmem_limit_bytes=24 * MIB),
+        compiler_params=pltpu.CompilerParams(vmem_limit_bytes=56 * MIB),
         cost_estimate=pl.CostEstimate(
             flops=pairs * 40 * count * offsets,
             bytes_accessed=pairs * 8 * count * offsets,
@@ -128,79 +191,34 @@
     )(base, slows, offs)
 
 
-def regroup(data_ref, wide, gathers):
-    devices, blocks, pairs, rows = data_ref.shape
-    lanes = blocks * gathers
-    own_offsets = rows // gathers
-
-    def exact(d, carry):
-        for h in range(own_offsets):
-            cut = [
-                data_ref[d, c, :, h * gathers : (h + 1) * gathers].astype(jnp.float32)
-                for c in range(blocks)
-            ]
-            start = pl.multiple_of((d * own_offsets + h) * pairs, pairs)
-            wide[pl.ds(start, pairs), :] = jnp.concatenate(cut, axis=1)
-        return carry
-
-    lane = lax.broadcasted_iota(jnp.int32, (1, lanes), 1)
-    low_half = lane < 2 * gathers
-    low_part = lane % (2 * gathers) < gathers
-
-    def rolled(d, carry):
-        for q in range(rows // lanes):
-            x = [
-                data_ref[d, c, :, q * lanes : (q + 1) * lanes].astype(jnp.float32)
-                for c in range(blocks)
-            ]
-            for top in range(2):
-                pair = []
-                for part in range(2):
-                    a, b = x[part], x[2 + part]
-                    if top == 0:
-                        pair.append(jnp.where(low_half, a, pltpu.roll(b, 2 * gathers, 1)))
-                    else:
-                        pair.append(jnp.where(low_half, pltpu.roll(a, 2 * gathers, 1), b))
-                outs = (
-                    jnp.where(low_part, pair[0], pltpu.roll(pair[1], gathers, 1)),
-                    jnp.where(low_part, pltpu.roll(pair[0], lanes - gathers, 1), pair[1]),
-                )
-                for bit in range(2):
-                    h = 4 * q + 2 * top + bit
-                    start = pl.multiple_of((d * own_offsets + h) * pairs, pairs)
-                    wide[pl.ds(start, pairs), :] = outs[bit]
-        return carry
-
-    lax.fori_loop(0, devices, rolled if rows % lanes == 0 else exact, 0, unroll=2)
-
-
 def radon_kernel(gathers, turn_ref, data_ref, out_ref, wide, held):
-    k = pl.program_id(0)
-    pairs = data_ref.shape[2]
-    lanes = wide.shape[1]
-    offsets = wide.shape[0] // pairs
-    slows = turn_ref.shape[2]
-
-    @pl.when(k == 0)
+    step = pl.program_id(0)
+    devices, own_offsets, pairs, lanes = data_ref.shape
+    offsets = devices * own_offsets
+    group, _, slows, _ = turn_ref.shape
+
+    @pl.when(step == 0)
     def start():
-        regroup(data_ref, wide, gathers)
+        wide[...] = data_ref[...].reshape(offsets * pairs, lanes).astype(jnp.float32)
 
     lane = lax.broadcasted_iota(jnp.int32, (1, lanes), 1)
     first_half = lane < 2 * gathers
     real_lane = lane % (2 * gathers) < gathers
-    block = wide[pl.ds(k, offsets, stride=pairs), :]
-    turned = jnp.where(
-        real_lane, -pltpu.roll(block, lanes - gathers, 1), pltpu.roll(block, gathers, 1)
-    ).astype(jnp.bfloat16)
-    data = block.astype(jnp.bfloat16)
-    results = [
-        jnp.dot(turn_ref[0, 2 * a], data, preferred_element_type=jnp.float32)
-        + jnp.dot(turn_ref[0, 2 * a + 1], turned, preferred_element_type=jnp.float32)
-        for a in range(2)
-    ]
-    held[pl.ds(k, slows, stride=pairs), :] = jnp.where(first_half, results[0], results[1])
-
-    @pl.when(k == pairs - 1)
+    for i in range(group):
+        k = step * group + i
+        block = wide[pl.ds(k, offsets, stride=pairs), :]
+        turned = jnp.where(
+            real_lane, -pltpu.roll(block, lanes - gathers, 1), pltpu.roll(block, gathers, 1)
+        ).astype(jnp.bfloat16)
+        data = block.astype(jnp.bfloat16)
+        cosine = turn_ref[i, :2].reshape(2 * slows, offsets)
+        sines = turn_ref[i, 2:].reshape(2 * slows, offsets)
+        both = jnp.dot(cosine, data, preferred_element_type=jnp.float32) + jnp.dot(
+            sines, turned, preferred_element_type=jnp.float32
+        )
+        held[pl.ds(k, slows, stride=pairs), :] = jnp.where(first_half, both[:slows], both[slows:])
+
+    @pl.when(step == pairs // group - 1)
     def end():
         out_ref[...] = held[...].astype(out_ref.dtype)
 
@@ -208,11 +226,12 @@
 def radon(turns, data, gathers):
     pairs, parts, count, offsets = turns.shape
     lanes = parts * gathers
+    group = 2 if pairs % 2 == 0 else 1
     return pl.pallas_call(
         functools.partial(radon_kernel, gathers),
-        grid=(pairs,),
+        grid=(pairs // group,),
         in_specs=[
-            pl.BlockSpec((1, parts, count, offsets), lambda k: (k, 0, 0, 0)),
+            pl.BlockSpec((group, parts, count, offsets), lambda k: (k, 0, 0, 0)),
             pl.BlockSpec(data.shape, lambda k: (0, 0, 0, 0)),
         ],
         out_specs=pl.BlockSpec((count * pairs, lanes), lambda k: (0, 0)),
@@ -221,7 +240,7 @@
             pltpu.VMEM((offsets * pairs, lanes), jnp.float32),
             pltpu.VMEM((count * pairs, lanes), jnp.float32),
         ],
-        compiler_params=pltpu.CompilerParams(vmem_limit_bytes=24 * MIB),
+        compiler_params=pltpu.CompilerParams(vmem_limit_bytes=56 * MIB),
     )(turns, data)
 
 
@@ -262,16 +281,12 @@
     halves = 2
     pairs = own_freqs // halves
     own_offsets = local_offsets // freq_devices
-    rows = own_offsets * gathers
-
-    picked = raw_traces[trace_slot.T.reshape(-1)]
-    series = lax.all_to_all(
-        picked.reshape(freq_devices, rows, local_times), "freq", 0, 0, tiled=True
-    )
+
+    picked = pick(trace_slot, raw_traces, freq_devices)
+    series = lax.all_to_all(picked, "freq", 0, 0, tiled=True)
     table = jnp.asarray(table_rows(total_time, freq_devices, offset_devices, halves, pairs))
-    spectrum = transform(table, series).reshape(devices, 2 * own_freqs, rows)
-    spectra = lax.all_to_all(spectrum, ("freq", "offset"), 0, 0, tiled=True)
-    data = spectra.reshape(devices, 2 * halves, pairs, rows)
+    spectrum = transform(table, series, pairs, gathers)
+    data = lax.all_to_all(spectrum, ("freq", "offset"), 0, 0, tiled=True)
 
     offs = offset_index.reshape(offset_devices, freq_devices, own_offsets)
     offs = offs.transpose(1, 0, 2).reshape(1, offsets).astype(jnp.float32)

time: 110 us -> 107 us (0.973)
  local copies, waits for them, and re-layouts: 15.5 us -> 4.47 us
  Pallas kernels: 25.7 us -> 34.1 us
  waiting for transfers between devices: 16.7 us -> 14.7 us
  blocking collectives: 46.8 us -> 47.9 us
    unnamed x12 -> x10, local copies, waits for them, and re-layouts: 10.3 us -> 2.92 us
    pallas_call x2 -> x3, Pallas kernels: 16.1 us -> 20.6 us  [the longest x1 9.83 us: radon(): pl.pallas_call(functools.partial(radon_kernel, gathers), grid=(pairs // g...]
    pallas_call x1, Pallas kernels: 7.29 us -> 11.3 us  [moveout(): pl.pallas_call(functools.partial(moveout_kernel, shift, total_time), grid...]
    gather x1 -> x0, local copies, waits for them, and re-layouts: 3.96 us -> none  [local(): picked = raw_traces[trace_slot.T.reshape(-1)]]
    all_to_all x1, waiting for transfers between devices: 16.7 us -> 14.7 us  [local(): data = lax.all_to_all(spectrum, ('freq', 'offset'), 0, 0, tiled=True)]
  transfers between devices with their start and end apart: 1 -> 1, of which waited for: 1 -> 1; matrix products, arithmetic and copies ran while one was open for 0% -> 1% of each run, Pallas kernels for 7% -> 11%
where the time goes in v3:
time: 107 us
  blocking collectives  47.9 us (45%)
  Pallas kernels  34.1 us (32%)
  waiting for transfers between devices  14.7 us (14%)
  starting transfers between devices  5.34 us (5%)
  local copies, waits for them, and re-layouts  4.47 us (4%)
    all_to_all x1, blocking collectives, local(): parts = lax.all_to_all(panel, 'offset', 0, 0, tiled=True)  29.3 us
    all_to_all x1, blocking collectives, local(): series = lax.all_to_all(picked, 'freq', 0, 0, tiled=True)  18.6 us
    all_to_all x1, waiting for transfers between devices, local(): data = lax.all_to_all(spectrum, ('freq', 'offset'), 0, 0, tiled=True)  14.7 us
    pallas_call x1, Pallas kernels, moveout(): pl.pallas_call(functools.partial(moveout_kernel, shift, total_time), grid...  11.3 us
    pallas_call x1, Pallas kernels, radon(): pl.pallas_call(functools.partial(radon_kernel, gathers), grid=(pairs // g...  9.83 us
    pallas_call x1, Pallas kernels, transform(): pl.pallas_call(functools.partial(transform_kernel, pairs, gathers), in_sp...  9.45 us
    all_to_all x1, starting transfers between devices, local(): data = lax.all_to_all(spectrum, ('freq', 'offset'), 0, 0, tiled=True)  5.34 us
    unnamed x10, local copies, waits for them, and re-layouts  2.92 us
  transfers between devices with their start and end apart: 1, of which 1 were waited for; matrix products, arithmetic and copies ran while one was open for 1% of the time, Pallas kernels for 11%

profile of v3, /device:TPU:0, one launch (start us, length us, event | category | flops | bytes accessed | tf_op | source)
XLA Modules:
  0.0 106.6 jit_solution(5498953489898288100)
XLA Ops:
  0.0 0.0 copy-start
  0.0 1.2 %copy-done = bf16[1024,512]{1,0:T(8,128)(2,1)S(1)} copy-done((bf16[1024,512]{1,0:T(8,128)(2,1)S(1)}, bf16[1024,512]{1,0:T(8,128)(2,1)}, u32[]{:S(2)}) %copy-start) | copy-done | bytes 1048600
  1.2 0.0 copy-start.1
  1.2 0.7 copy-done.1
  1.9 0.0 copy-start.3
  1.9 0.0 copy-start.4
  1.9 1.3 %shard_map.56 = bf16[4,256,512]{2,1,0:T(8,128)(2,1)S(1)} custom-call(s32[32,32]{1,0:T(8,128)S(1)} %copy-done.1, bf16[1024,512]{1,0:T(8,128)(2,1)S(1)} %copy-done), custom_call_target="tpu_custom_call" | custom-call | tf_op jit(solution)/shard_map/pallas_call | solution.py:55
  3.2 18.6 %all_to_all.15.series_ref = bf16[4,256,512]{2,1,0:T(8,128)(2,1)} all-to-all(bf16[4,256,512]{2,1,0:T(8,128)(2,1)S(1)} %shard_map.56), channel_id=1, replica_groups=mesh['freq'=4,'offset'=8] {'freq'}, dimensions={0} | all-to-all | bytes 2097152 | tf_op jit(solution)/shard_map/all_to_all | solution.py:286
  21.8 9.5 %shard_map.57 = bf16[32,8,16,128]{3,2,1,0:T(8,128)(2,1)} custom-call(bf16[2048,2048]{1,0:T(8,128)(2,1)} %constant.20.clone.table_ref, bf16[4,256,512]{2,1,0:T(8,128)(2,1)} %all_to_all.15.series_ref), custom_call_target="tpu_custom_call" | custom-call | tf_op jit(solution)/shard_map/pallas_call | solution.py:123
  31.3 5.3 %all-to-all-start.1 = ((bf16[32,8,16,128]{3,2,1,0:T(8,128)(2,1)}), bf16[32,8,16,128]{3,2,1,0:T(8,128)(2,1)S(1)}, u32[]{:S(2)}, u32[]{:S(2)}) async-start(bf16[32,8,16,128]{3,2,1,0:T(8,128)(2,1)} %shard_map.57), calls=%async_computation.1 | async-start | bytes 2097152 | tf_op jit(solution)/shard_map/all_to_all | solution.py:289
  36.7 0.0 copy-done.3
  36.7 0.0 copy-done.4
  36.7 0.1 convert_element_type.18
  36.8 0.7 convert_element_type.20.offs_ref
  37.5 0.8 copy.7.slow_ref
  38.3 11.3 %shard_map.55.turn_ref = bf16[16,4,256,256]{3,2,1,0:T(8,128)(2,1)} custom-call(f32[1]{0:T(128)} %bitcast.base_ref, f32[256,1]{1,0:T(8,128)} %copy.7.slow_ref, f32[1,256]{1,0:T(1,128)} %convert_element_type.20.offs_ref), custom_call_target="tpu_custom_call" | custom-call | flops 41943040 | bytes 8388608 | tf_op jit(solution)/shard_map/pallas_call | solution.py:169
  49.6 14.7 %all-to-all-done.1.data_ref = bf16[32,8,16,128]{3,2,1,0:T(8,128)(2,1)S(1)} async-done(((bf16[32,8,16,128]{3,2,1,0:T(8,128)(2,1)}), bf16[32,8,16,128]{3,2,1,0:T(8,128)(2,1)S(1)}, u32[]{:S(2)}, u32[]{:S(2)}) %all-to-all-start.1) | async-done | bytes 1048608 | tf_op jit(solution)/shard_map/all_to_all | solution.py:289
  64.2 0.0 copy-start.2
  64.2 1.0 copy-done.2
  65.2 9.8 %shard_map.58 = bf16[4096,128]{1,0:T(8,128)(2,1)} custom-call(bf16[16,4,256,256]{3,2,1,0:T(8,128)(2,1)} %shard_map.55.turn_ref, bf16[32,8,16,128]{3,2,1,0:T(8,128)(2,1)} %copy-done.2), custom_call_target="tpu_custom_call" | custom-call | tf_op jit(solution)/shard_map/pallas_call | solution.py:230
  75.0 29.3 %all_to_all.16.in_ref = bf16[8,32,16,128]{3,2,1,0:T(8,128)(2,1)S(1)} all-to-all(bf16[8,32,16,128]{3,2,1,0:T(8,128)(2,1)} %bitcast.5), channel_id=1, replica_groups=mesh['freq'=4,'offset'=8] {'offset'}, dimensions={0} | all-to-all | bytes 2097152 | tf_op jit(solution)/shard_map/all_to_all | solution.py:299
  104.4 2.3 %shard_map.59 = f32[32,64,256]{2,1,0:T(8,128)} custom-call(bf16[8,32,16,128]{3,2,1,0:T(8,128)(2,1)S(1)} %all_to_all.16.in_ref), custom_call_target="tpu_custom_call" | custom-call | tf_op jit(solution)/shard_map/pallas_call | solution.py:261
  (3 shorter events, 0.0 us)
Async XLA Ops:
  0.0 1.2 %copy-start = (bf16[1024,512]{1,0:T(8,128)(2,1)S(1)}, bf16[1024,512]{1,0:T(8,128)(2,1)}, u32[]{:S(2)}) copy-start(bf16[1024,512]{1,0:T(8,128)(2,1)} %raw_ref.1) | copy-start | bytes 3145732
  1.2 0.7 copy-start.1
  1.9 34.7 %copy-start.3 = (s32[256]{0:T(256)S(1)}, s32[256]{0:T(256)}, u32[]{:S(2)}) copy-start(s32[256]{0:T(256)} %param.7) | copy-start | bytes 3076
  1.9 34.7 %copy-start.4 = (s32[256]{0:T(256)S(1)}, s32[256]{0:T(256)}, u32[]{:S(2)}) copy-start(s32[256]{0:T(256)} %param.8) | copy-start | bytes 3076
  31.3 32.9 %all-to-all-start.1 = ((bf16[32,8,16,128]{3,2,1,0:T(8,128)(2,1)}), bf16[32,8,16,128]{3,2,1,0:T(8,128)(2,1)S(1)}, u32[]{:S(2)}, u32[]{:S(2)}) async-start(bf16[32,8,16,128]{3,2,1,0:T(8,128)(2,1)} %shard_map.57), calls=%async_computation.1 | async-start | bytes 2097152 | tf_op jit(solution)/shard_map/all_to_all | solution.py:289
  64.2 1.0 copy-start.2

commit v4 on v3

--- a/solution.py
+++ b/solution.py
@@ -57,7 +57,7 @@
         in_specs=[vmem, vmem],
         out_specs=vmem,
         out_shape=jax.ShapeDtypeStruct((groups, rows, raw_traces.shape[1]), raw_traces.dtype),
-        compiler_params=pltpu.CompilerParams(vmem_limit_bytes=32 * MIB),
+        compiler_params=pltpu.CompilerParams(vmem_limit_bytes=63 * MIB),
     )(trace_slot, raw_traces)
 
 
@@ -82,7 +82,7 @@
     return found
 
 
-def transform_kernel(pairs, gathers, table_ref, series_ref, out_ref, held, sems):
+def transform_kernel(pairs, gathers, table_ref, series_ref, out_ref, held, turned, sems):
     blocks, rows, local_times = series_ref.shape
     chunks, step, _ = held.shape
     copies = [
@@ -91,17 +91,11 @@
     ]
     for copy in copies:
         copy.start()
+    for b in range(blocks):
+        turned[b * local_times : (b + 1) * local_times] = series_ref[b].T
     for i in range(chunks):
         copies[i].wait()
-        total = None
-        for b in range(blocks):
-            part = lax.dot_general(
-                held[i, :, b * local_times : (b + 1) * local_times],
-                series_ref[b],
-                (((1,), (1,)), ((), ())),
-                preferred_element_type=jnp.float32,
-            )
-            total = part if total is None else total + part
+        total = jnp.dot(held[i], turned[...], preferred_element_type=jnp.float32)
         if len(out_ref.shape) == 2:
             out_ref[i * step : (i + 1) * step] = total.astype(out_ref.dtype)
             continue
@@ -127,6 +121,7 @@
         out_shape=jax.ShapeDtypeStruct(final if aligned else (columns, rows), jnp.bfloat16),
         scratch_shapes=[
             pltpu.VMEM((chunks, columns // chunks, total_time), jnp.bfloat16),
+            pltpu.VMEM((total_time, rows), jnp.bfloat16),
             pltpu.SemaphoreType.DMA((chunks,)),
         ],
         compiler_params=pltpu.CompilerParams(vmem_limit_bytes=56 * MIB),
@@ -191,36 +186,62 @@
     )(base, slows, offs)
 
 
-def radon_kernel(gathers, turn_ref, data_ref, out_ref, wide, held):
+def one_hot(rows, columns, source):
+    row = lax.broadcasted_iota(jnp.int32, (rows, columns), 0)
+    column = lax.broadcasted_iota(jnp.int32, (rows, columns), 1)
+    return jnp.where(column == source(row), 1.0, 0.0).astype(jnp.bfloat16)
+
+
+def radon_kernel(gathers, turn_ref, data_ref, out_ref, plain, turned, held):
     step = pl.program_id(0)
     devices, own_offsets, pairs, lanes = data_ref.shape
     offsets = devices * own_offsets
     group, _, slows, _ = turn_ref.shape
+    tile = 16
 
     @pl.when(step == 0)
     def start():
-        wide[...] = data_ref[...].reshape(offsets * pairs, lanes).astype(jnp.float32)
-
-    lane = lax.broadcasted_iota(jnp.int32, (1, lanes), 1)
-    first_half = lane < 2 * gathers
-    real_lane = lane % (2 * gathers) < gathers
+        size = tile * pairs
+        together = tile // own_offsets
+        swap = one_hot(size, size, lambda r: r % tile * pairs + r // tile)
+        for d in range(devices // together):
+            block = data_ref[d * together : (d + 1) * together].reshape(size, lanes)
+            if pairs > 1:
+                block = jnp.dot(swap, block, preferred_element_type=jnp.float32)
+                block = block.astype(jnp.bfloat16)
+            plain[:, d * tile : (d + 1) * tile] = block.reshape(pairs, tile, lanes)
+        row = lax.broadcasted_iota(jnp.int32, (lanes, lanes), 0)
+        column = lax.broadcasted_iota(jnp.int32, (lanes, lanes), 1)
+        real_lane = column % (2 * gathers) < gathers
+        quarter = jnp.where(
+            real_lane,
+            jnp.where(row == column + gathers, -1.0, 0.0),
+            jnp.where(row == column - gathers, 1.0, 0.0),
+        ).astype(jnp.bfloat16)
+        for k in range(pairs):
+            turned[k] = jnp.dot(plain[k], quarter, preferred_element_type=jnp.float32).astype(
+                jnp.bfloat16
+            )
+
+    first_half = lax.broadcasted_iota(jnp.int32, (1, lanes), 1) < 2 * gathers
     for i in range(group):
         k = step * group + i
-        block = wide[pl.ds(k, offsets, stride=pairs), :]
-        turned = jnp.where(
-            real_lane, -pltpu.roll(block, lanes - gathers, 1), pltpu.roll(block, gathers, 1)
-        ).astype(jnp.bfloat16)
-        data = block.astype(jnp.bfloat16)
         cosine = turn_ref[i, :2].reshape(2 * slows, offsets)
         sines = turn_ref[i, 2:].reshape(2 * slows, offsets)
-        both = jnp.dot(cosine, data, preferred_element_type=jnp.float32) + jnp.dot(
-            sines, turned, preferred_element_type=jnp.float32
+        both = jnp.dot(cosine, plain[k], preferred_element_type=jnp.float32) + jnp.dot(
+            sines, turned[k], preferred_element_type=jnp.float32
         )
-        held[pl.ds(k, slows, stride=pairs), :] = jnp.where(first_half, both[:slows], both[slows:])
+        held[k] = jnp.where(first_half, both[:slows], both[slows:]).astype(jnp.bfloat16)
 
     @pl.when(step == pairs // group - 1)
     def end():
-        out_ref[...] = held[...].astype(out_ref.dtype)
+        size = tile * pairs
+        swap = one_hot(size, size, lambda r: r % pairs * tile + r // pairs)
+        for p in range(slows // tile):
+            block = held[:, p * tile : (p + 1) * tile].reshape(size, lanes)
+            if pairs > 1:
+                block = jnp.dot(swap, block, preferred_element_type=jnp.float32)
+            out_ref[p * size : (p + 1) * size] = block.astype(out_ref.dtype)
 
 
 def radon(turns, data, gathers):
@@ -237,10 +258,11 @@
         out_specs=pl.BlockSpec((count * pairs, lanes), lambda k: (0, 0)),
         out_shape=jax.ShapeDtypeStruct((count * pairs, lanes), jnp.bfloat16),
         scratch_shapes=[
-            pltpu.VMEM((offsets * pairs, lanes), jnp.float32),
-            pltpu.VMEM((count * pairs, lanes), jnp.float32),
-        ],
-        compiler_params=pltpu.CompilerParams(vmem_limit_bytes=56 * MIB),
+            pltpu.VMEM((pairs, offsets, lanes), jnp.bfloat16),
+            pltpu.VMEM((pairs, offsets, lanes), jnp.bfloat16),
+            pltpu.VMEM((pairs, count, lanes), jnp.bfloat16),
+        ],
+        compiler_params=pltpu.CompilerParams(vmem_limit_bytes=63 * MIB),
     )(turns, data)
 
 

time: 107 us -> 108 us (level)
  local copies, waits for them, and re-layouts: 4.47 us -> 1.57 us
  Pallas kernels: 34.1 us -> 36.8 us
    unnamed x10 -> x4, local copies, waits for them, and re-layouts: 2.92 us -> 0.01 us
    pallas_call x1, Pallas kernels: 1.28 us -> 3.53 us  [pick(): pl.pallas_call(pick_kernel, in_specs=[vmem, vmem], out_specs=vmem, out_sh...]
  transfers between devices with their start and end apart: 1 -> 1, of which waited for: 1 -> 1; matrix products, arithmetic and copies ran while one was open for 1% -> 1% of each run, Pallas kernels for 11% -> 10%
where the time goes in v4:
time: 108 us
  blocking collectives  48.7 us (45%)
  Pallas kernels  36.8 us (34%)
  waiting for transfers between devices  14.7 us (14%)
  starting transfers between devices  5.83 us (5%)
  local copies, waits for them, and re-layouts  1.57 us (1%)
    all_to_all x1, blocking collectives, local(): parts = lax.all_to_all(panel, 'offset', 0, 0, tiled=True)  29.3 us
    all_to_all x1, blocking collectives, local(): series = lax.all_to_all(picked, 'freq', 0, 0, tiled=True)  19.4 us
    all_to_all x1, waiting for transfers between devices, local(): data = lax.all_to_all(spectrum, ('freq', 'offset'), 0, 0, tiled=True)  14.7 us
    pallas_call x1, Pallas kernels, moveout(): pl.pallas_call(functools.partial(moveout_kernel, shift, total_time), grid...  11.3 us
    pallas_call x1, Pallas kernels, radon(): pl.pallas_call(functools.partial(radon_kernel, gathers), grid=(pairs // g...  10.4 us
    pallas_call x1, Pallas kernels, transform(): pl.pallas_call(functools.partial(transform_kernel, pairs, gathers), in_sp...  9.33 us
    all_to_all x1, starting transfers between devices, local(): data = lax.all_to_all(spectrum, ('freq', 'offset'), 0, 0, tiled=True)  5.83 us
    pallas_call x1, Pallas kernels, pick(): pl.pallas_call(pick_kernel, in_specs=[vmem, vmem], out_specs=vmem, out_sh...  3.53 us
  transfers between devices with their start and end apart: 1, of which 1 were waited for; matrix products, arithmetic and copies ran while one was open for 1% of the time, Pallas kernels for 10%

profile of v4, /device:TPU:0, one launch (start us, length us, event | category | flops | bytes accessed | tf_op | source)
XLA Modules:
  0.0 107.7 jit_solution(6987761547202461803)
XLA Ops:
  0.0 0.0 copy-start
  0.0 0.0 copy-start.1
  0.0 3.5 %shard_map.56 = bf16[4,256,512]{2,1,0:T(8,128)(2,1)} custom-call(s32[32,32]{1,0:T(8,128)} %slot_ref.1, bf16[1024,512]{1,0:T(8,128)(2,1)} %raw_ref.1), custom_call_target="tpu_custom_call" | custom-call | tf_op jit(solution)/shard_map/pallas_call | solution.py:55
  3.5 19.4 %all_to_all.15.series_ref = bf16[4,256,512]{2,1,0:T(8,128)(2,1)} all-to-all(bf16[4,256,512]{2,1,0:T(8,128)(2,1)} %shard_map.56), channel_id=1, replica_groups=mesh['freq'=4,'offset'=8] {'freq'}, dimensions={0} | all-to-all | bytes 2097152 | tf_op jit(solution)/shard_map/all_to_all | solution.py:308
  22.9 9.3 %shard_map.57 = bf16[32,8,16,128]{3,2,1,0:T(8,128)(2,1)} custom-call(bf16[2048,2048]{1,0:T(8,128)(2,1)} %constant.20.clone.table_ref, bf16[4,256,512]{2,1,0:T(8,128)(2,1)} %all_to_all.15.series_ref), custom_call_target="tpu_custom_call" | custom-call | tf_op jit(solution)/shard_map/pallas_call | solution.py:117
  32.3 5.8 %all-to-all-start.1 = ((bf16[32,8,16,128]{3,2,1,0:T(8,128)(2,1)}), bf16[32,8,16,128]{3,2,1,0:T(8,128)(2,1)}, u32[]{:S(2)}, u32[]{:S(2)}) async-start(bf16[32,8,16,128]{3,2,1,0:T(8,128)(2,1)} %shard_map.57), calls=%async_computation.1 | async-start | bytes 2097152 | tf_op jit(solution)/shard_map/all_to_all | solution.py:311
  38.1 0.0 copy-done
  38.1 0.0 copy-done.1
  38.2 0.1 convert_element_type.18
  38.3 0.7 convert_element_type.20.offs_ref
  38.9 0.8 copy.7.slow_ref
  39.7 11.3 %shard_map.55.turn_ref = bf16[16,4,256,256]{3,2,1,0:T(8,128)(2,1)} custom-call(f32[1]{0:T(128)} %bitcast.base_ref, f32[256,1]{1,0:T(8,128)} %copy.7.slow_ref, f32[1,256]{1,0:T(1,128)} %convert_element_type.20.offs_ref), custom_call_target="tpu_custom_call" | custom-call | flops 41943040 | bytes 8388608 | tf_op jit(solution)/shard_map/pallas_call | solution.py:164
  51.0 14.7 %all-to-all-done.1.data_ref = bf16[32,8,16,128]{3,2,1,0:T(8,128)(2,1)} async-done(((bf16[32,8,16,128]{3,2,1,0:T(8,128)(2,1)}), bf16[32,8,16,128]{3,2,1,0:T(8,128)(2,1)}, u32[]{:S(2)}, u32[]{:S(2)}) %all-to-all-start.1) | async-done | bytes 1048608 | tf_op jit(solution)/shard_map/all_to_all | solution.py:311
  65.7 10.4 %shard_map.58 = bf16[4096,128]{1,0:T(8,128)(2,1)} custom-call(bf16[16,4,256,256]{3,2,1,0:T(8,128)(2,1)} %shard_map.55.turn_ref, bf16[32,8,16,128]{3,2,1,0:T(8,128)(2,1)} %all-to-all-done.1.data_ref), custom_call_target="tpu_custom_call" | custom-call | tf_op jit(solution)/shard_map/pallas_call | solution.py:251
  76.1 29.3 %all_to_all.16.in_ref = bf16[8,32,16,128]{3,2,1,0:T(8,128)(2,1)S(1)} all-to-all(bf16[8,32,16,128]{3,2,1,0:T(8,128)(2,1)} %bitcast.5), channel_id=1, replica_groups=mesh['freq'=4,'offset'=8] {'offset'}, dimensions={0} | all-to-all | bytes 2097152 | tf_op jit(solution)/shard_map/all_to_all | solution.py:321
  105.4 2.3 %shard_map.59 = f32[32,64,256]{2,1,0:T(8,128)} custom-call(bf16[8,32,16,128]{3,2,1,0:T(8,128)(2,1)S(1)} %all_to_all.16.in_ref), custom_call_target="tpu_custom_call" | custom-call | tf_op jit(solution)/shard_map/pallas_call | solution.py:283
  (3 shorter events, 0.0 us)
Async XLA Ops:
  0.0 38.1 %copy-start = (s32[256]{0:T(256)S(1)}, s32[256]{0:T(256)}, u32[]{:S(2)}) copy-start(s32[256]{0:T(256)} %param.7) | copy-start | bytes 3076
  0.0 38.1 %copy-start.1 = (s32[256]{0:T(256)S(1)}, s32[256]{0:T(256)}, u32[]{:S(2)}) copy-start(s32[256]{0:T(256)} %param.8) | copy-start | bytes 3076
  32.3 33.4 %all-to-all-start.1 = ((bf16[32,8,16,128]{3,2,1,0:T(8,128)(2,1)}), bf16[32,8,16,128]{3,2,1,0:T(8,128)(2,1)}, u32[]{:S(2)}, u32[]{:S(2)}) async-start(bf16[32,8,16,128]{3,2,1,0:T(8,128)(2,1)} %shard_map.57), calls=%async_computation.1 | async-start | bytes 2097152 | tf_op jit(solution)/shard_map/all_to_all | solution.py:311

commit v5 on v4

--- a/solution.py
+++ b/solution.py
@@ -20,14 +20,15 @@
 def table_rows(total_time, freq_devices, offset_devices, halves, pairs):
     band = NF // freq_devices
     f, o, a, k = np.meshgrid(
-        np.arange(freq_devices),
+        np.arange(freq_devices // 2),
         np.arange(offset_devices),
         np.arange(halves),
         np.arange(pairs),
         indexing="ij",
     )
     freq_ids = (f * band + a * (band // halves) + o * pairs + k).reshape(-1, pairs)
-    turns = (2 * freq_ids[..., None] + 1) * np.arange(total_time) % (2 * total_time)
+    times = np.concatenate([np.arange(0, total_time, 2), np.arange(1, total_time, 2)])
+    turns = (2 * freq_ids[..., None] + 1) * times % (2 * total_time)
     angles = turns.astype(np.float32) * np.float32(math.pi / total_time)
     both = np.stack([np.cos(angles), -np.sin(angles)], axis=1).reshape(-1, total_time)
     return (both / np.float32(math.sqrt(total_time))).astype(ml_dtypes.bfloat16)
@@ -37,6 +38,13 @@
     gathers = slot_ref.shape[0]
     groups, rows, _ = out_ref.shape
     own_offsets = rows // gathers
+    times = raw_ref.shape[1]
+    half = times // 2
+    row = lax.broadcasted_iota(jnp.int32, (times, times), 0)
+    column = lax.broadcasted_iota(jnp.int32, (times, times), 1)
+    source = jnp.where(column < half, 2 * column, 2 * (column - half) + 1)
+    split = jnp.where(row == source, 1.0, 0.0).astype(jnp.bfloat16)
+    raw = jnp.dot(raw_ref[...], split, preferred_element_type=jnp.float32).astype(jnp.bfloat16)
     lane = lax.broadcasted_iota(jnp.int32, (gathers, raw_ref.shape[0]), 1)
     for f in range(groups):
         picks = [
@@ -44,7 +52,7 @@
             for h in range(f * own_offsets, (f + 1) * own_offsets)
         ]
         out_ref[f] = jnp.dot(
-            jnp.concatenate(picks, axis=0), raw_ref[...], preferred_element_type=jnp.float32
+            jnp.concatenate(picks, axis=0), raw, preferred_element_type=jnp.float32
         ).astype(out_ref.dtype)
 
 
@@ -57,18 +65,18 @@
         in_specs=[vmem, vmem],
         out_specs=vmem,
         out_shape=jax.ShapeDtypeStruct((groups, rows, raw_traces.shape[1]), raw_traces.dtype),
-        compiler_params=pltpu.CompilerParams(vmem_limit_bytes=63 * MIB),
+        compiler_params=pltpu.CompilerParams(vmem_limit_bytes=61 * MIB),
     )(trace_slot, raw_traces)
 
 
-def regroup(total, pairs, gathers):
+def regroup(parts, gathers):
     lanes = 4 * gathers
     lane = lax.broadcasted_iota(jnp.int32, (1, lanes), 1)
     low_half = lane < 2 * gathers
     low_part = lane % (2 * gathers) < gathers
     found = []
-    for q in range(total.shape[1] // lanes):
-        x = [total[c * pairs : (c + 1) * pairs, q * lanes : (q + 1) * lanes] for c in range(4)]
+    for q in range(parts[0].shape[1] // lanes):
+        x = [part[:, q * lanes : (q + 1) * lanes] for part in parts]
         for top in range(2):
             pair = []
             for part in range(2):
@@ -82,9 +90,10 @@
     return found
 
 
-def transform_kernel(pairs, gathers, table_ref, series_ref, out_ref, held, turned, sems):
+def transform_kernel(pairs, gathers, table_ref, series_ref, out_ref, held, even, odd, sems):
     blocks, rows, local_times = series_ref.shape
     chunks, step, _ = held.shape
+    half = local_times // 2
     copies = [
         pltpu.make_async_copy(table_ref.at[pl.ds(i * step, step)], held.at[i], sems.at[i])
         for i in range(chunks)
@@ -92,44 +101,62 @@
     for copy in copies:
         copy.start()
     for b in range(blocks):
-        turned[b * local_times : (b + 1) * local_times] = series_ref[b].T
+        turned = series_ref[b].T
+        even[b * half : (b + 1) * half] = turned[:half]
+        odd[b * half : (b + 1) * half] = turned[half:]
+    depth = blocks * half
     for i in range(chunks):
         copies[i].wait()
-        total = jnp.dot(held[i], turned[...], preferred_element_type=jnp.float32)
-        if len(out_ref.shape) == 2:
-            out_ref[i * step : (i + 1) * step] = total.astype(out_ref.dtype)
+        evens = jnp.dot(held[i, :, :depth], even[...], preferred_element_type=jnp.float32)
+        odds = jnp.dot(held[i, :, depth:], odd[...], preferred_element_type=jnp.float32)
+        low = evens + odds
+        high = evens - odds
+        if len(out_ref.shape) == 3:
+            row = lax.broadcasted_iota(jnp.int32, (step, 1), 0)
+            out_ref[0, i * step : (i + 1) * step] = low.astype(out_ref.dtype)
+            out_ref[1, i * step : (i + 1) * step] = jnp.where(
+                row // pairs % 2 == 0, high, -high
+            ).astype(out_ref.dtype)
             continue
         targets = step // (4 * pairs)
+        devices = out_ref.shape[0]
         for d in range(targets):
-            found = regroup(total[d * 4 * pairs : (d + 1) * 4 * pairs], pairs, gathers)
-            for h, value in enumerate(found):
-                out_ref[i * targets + d, h] = value.astype(out_ref.dtype)
+            cuts = [slice((4 * d + c) * pairs, (4 * d + c + 1) * pairs) for c in range(4)]
+            place = i * targets + d
+            for h, value in enumerate(regroup([low[cut] for cut in cuts], gathers)):
+                out_ref[place, h] = value.astype(out_ref.dtype)
+            mirrored = [high[cuts[2]], -high[cuts[3]], high[cuts[0]], -high[cuts[1]]]
+            for h, value in enumerate(regroup(mirrored, gathers)):
+                out_ref[devices - 1 - place, h] = value.astype(out_ref.dtype)
 
 
 def transform(table, series, pairs, gathers):
     columns, total_time = table.shape
     blocks, rows, local_times = series.shape
-    devices = columns // (4 * pairs)
-    final = (devices, rows // gathers, pairs, 4 * gathers)
+    own_offsets = rows // gathers
+    devices = columns // (2 * pairs)
+    final = (devices, own_offsets, pairs, 4 * gathers)
     chunks = 4
-    aligned = rows % (4 * gathers) == 0 and pairs % 8 == 0 and devices % chunks == 0
+    aligned = rows % (4 * gathers) == 0 and pairs % 8 == 0 and devices % (2 * chunks) == 0
     vmem = pl.BlockSpec(memory_space=pltpu.VMEM)
     out = pl.pallas_call(
         functools.partial(transform_kernel, pairs, gathers),
         in_specs=[pl.BlockSpec(memory_space=pl.ANY), vmem],
         out_specs=vmem,
-        out_shape=jax.ShapeDtypeStruct(final if aligned else (columns, rows), jnp.bfloat16),
+        out_shape=jax.ShapeDtypeStruct(final if aligned else (2, columns, rows), jnp.bfloat16),
         scratch_shapes=[
             pltpu.VMEM((chunks, columns // chunks, total_time), jnp.bfloat16),
-            pltpu.VMEM((total_time, rows), jnp.bfloat16),
+            pltpu.VMEM((total_time // 2, rows), jnp.bfloat16),
+            pltpu.VMEM((total_time // 2, rows), jnp.bfloat16),
             pltpu.SemaphoreType.DMA((chunks,)),
         ],
-        compiler_params=pltpu.CompilerParams(vmem_limit_bytes=56 * MIB),
+        compiler_params=pltpu.CompilerParams(vmem_limit_bytes=61 * MIB),
     )(table, series)
     if aligned:
         return out
-    out = out.reshape(devices, 4, pairs, rows // gathers, gathers)
-    return out.transpose(0, 3, 2, 1, 4).reshape(final)
+    out = out.reshape(2, devices // 2, 2, 2, pairs, own_offsets, gathers)
+    out = jnp.concatenate([out[0], jnp.flip(out[1], (0, 1))], axis=0)
+    return out.transpose(0, 4, 3, 1, 2, 5).reshape(final)
 
 
 def moveout_kernel(shift, total_time, base_ref, slow_ref, offs_ref, out_ref, cs, sn, tc, ts):
@@ -177,7 +204,7 @@
             pltpu.VMEM((count, offsets), jnp.float32),
             pltpu.VMEM((count, offsets), jnp.float32),
         ],
-        compiler_params=pltpu.CompilerParams(vmem_limit_bytes=56 * MIB),
+        compiler_params=pltpu.CompilerParams(vmem_limit_bytes=61 * MIB),
         cost_estimate=pl.CostEstimate(
             flops=pairs * 40 * count * offsets,
             bytes_accessed=pairs * 8 * count * offsets,
@@ -192,78 +219,83 @@
     return jnp.where(column == source(row), 1.0, 0.0).astype(jnp.bfloat16)
 
 
-def radon_kernel(gathers, turn_ref, data_ref, out_ref, plain, turned, held):
-    step = pl.program_id(0)
+def radon_kernel(gathers, down_ref, turn_ref, data_ref, out_ref, turns, plain, turned, held, sems):
     devices, own_offsets, pairs, lanes = data_ref.shape
     offsets = devices * own_offsets
-    group, _, slows, _ = turn_ref.shape
+    slows = turn_ref.shape[2]
     tile = 16
-
-    @pl.when(step == 0)
-    def start():
-        size = tile * pairs
-        together = tile // own_offsets
-        swap = one_hot(size, size, lambda r: r % tile * pairs + r // tile)
-        for d in range(devices // together):
-            block = data_ref[d * together : (d + 1) * together].reshape(size, lanes)
-            if pairs > 1:
-                block = jnp.dot(swap, block, preferred_element_type=jnp.float32)
-                block = block.astype(jnp.bfloat16)
-            plain[:, d * tile : (d + 1) * tile] = block.reshape(pairs, tile, lanes)
-        row = lax.broadcasted_iota(jnp.int32, (lanes, lanes), 0)
-        column = lax.broadcasted_iota(jnp.int32, (lanes, lanes), 1)
-        real_lane = column % (2 * gathers) < gathers
-        quarter = jnp.where(
-            real_lane,
-            jnp.where(row == column + gathers, -1.0, 0.0),
-            jnp.where(row == column - gathers, 1.0, 0.0),
-        ).astype(jnp.bfloat16)
-        for k in range(pairs):
-            turned[k] = jnp.dot(plain[k], quarter, preferred_element_type=jnp.float32).astype(
-                jnp.bfloat16
-            )
+    size = tile * pairs
+    copies = [
+        pltpu.make_async_copy(turn_ref.at[k], turns.at[k], sems.at[k]) for k in range(pairs)
+    ]
+    for copy in copies:
+        copy.start()
+
+    together = tile // own_offsets
+    down = down_ref[0]
+
+    def received(r):
+        k = r // tile
+        return r % tile * pairs + k + down * (pairs - 1 - 2 * k)
+
+    swap = one_hot(size, size, received)
+    for d in range(devices // together):
+        block = data_ref[d * together : (d + 1) * together].reshape(size, lanes)
+        if pairs > 1:
+            block = jnp.dot(swap, block, preferred_element_type=jnp.float32).astype(jnp.bfloat16)
+        plain[:, d * tile : (d + 1) * tile] = block.reshape(pairs, tile, lanes)
+    row = lax.broadcasted_iota(jnp.int32, (lanes, lanes), 0)
+    column = lax.broadcasted_iota(jnp.int32, (lanes, lanes), 1)
+    quarter = jnp.where(
+        column % (2 * gathers) < gathers,
+        jnp.where(row == column + gathers, -1.0, 0.0),
+        jnp.where(row == column - gathers, 1.0, 0.0),
+    ).astype(jnp.bfloat16)
+    for k in range(pairs):
+        turned[k] = jnp.dot(plain[k], quarter, preferred_element_type=jnp.float32).astype(
+            jnp.bfloat16
+        )
 
     first_half = lax.broadcasted_iota(jnp.int32, (1, lanes), 1) < 2 * gathers
-    for i in range(group):
-        k = step * group + i
-        cosine = turn_ref[i, :2].reshape(2 * slows, offsets)
-        sines = turn_ref[i, 2:].reshape(2 * slows, offsets)
+    for k in range(pairs):
+        copies[k].wait()
+        cosine = turns[k, :2].reshape(2 * slows, offsets)
+        sines = turns[k, 2:].reshape(2 * slows, offsets)
         both = jnp.dot(cosine, plain[k], preferred_element_type=jnp.float32) + jnp.dot(
             sines, turned[k], preferred_element_type=jnp.float32
         )
         held[k] = jnp.where(first_half, both[:slows], both[slows:]).astype(jnp.bfloat16)
 
-    @pl.when(step == pairs // group - 1)
-    def end():
-        size = tile * pairs
-        swap = one_hot(size, size, lambda r: r % pairs * tile + r // pairs)
-        for p in range(slows // tile):
-            block = held[:, p * tile : (p + 1) * tile].reshape(size, lanes)
-            if pairs > 1:
-                block = jnp.dot(swap, block, preferred_element_type=jnp.float32)
-            out_ref[p * size : (p + 1) * size] = block.astype(out_ref.dtype)
-
-
-def radon(turns, data, gathers):
+    swap = one_hot(size, size, lambda r: r % pairs * tile + r // pairs)
+    for p in range(slows // tile):
+        block = held[:, p * tile : (p + 1) * tile].reshape(size, lanes)
+        if pairs > 1:
+            block = jnp.dot(swap, block, preferred_element_type=jnp.float32)
+        out_ref[p * size : (p + 1) * size] = block.astype(out_ref.dtype)
+
+
+def radon(down, turns, data, gathers):
     pairs, parts, count, offsets = turns.shape
     lanes = parts * gathers
-    group = 2 if pairs % 2 == 0 else 1
+    vmem = pl.BlockSpec(memory_space=pltpu.VMEM)
     return pl.pallas_call(
         functools.partial(radon_kernel, gathers),
-        grid=(pairs // group,),
         in_specs=[
-            pl.BlockSpec((group, parts, count, offsets), lambda k: (k, 0, 0, 0)),
-            pl.BlockSpec(data.shape, lambda k: (0, 0, 0, 0)),
-        ],
-        out_specs=pl.BlockSpec((count * pairs, lanes), lambda k: (0, 0)),
+            pl.BlockSpec(memory_space=pltpu.SMEM),
+            pl.BlockSpec(memory_space=pl.ANY),
+            vmem,
+        ],
+        out_specs=vmem,
         out_shape=jax.ShapeDtypeStruct((count * pairs, lanes), jnp.bfloat16),
         scratch_shapes=[
+            pltpu.VMEM(turns.shape, jnp.bfloat16),
             pltpu.VMEM((pairs, offsets, lanes), jnp.bfloat16),
             pltpu.VMEM((pairs, offsets, lanes), jnp.bfloat16),
             pltpu.VMEM((pairs, count, lanes), jnp.bfloat16),
-        ],
-        compiler_params=pltpu.CompilerParams(vmem_limit_bytes=63 * MIB),
-    )(turns, data)
+            pltpu.SemaphoreType.DMA((pairs,)),
+        ],
+        compiler_params=pltpu.CompilerParams(vmem_limit_bytes=61 * MIB),
+    )(down, turns, data)
 
 
 def finish_kernel(scale, in_ref, out_ref):
@@ -316,7 +348,8 @@
     first = lax.axis_index("freq") * band + lax.axis_index("offset") * pairs
     base = (2 * first + 1).astype(jnp.float32) * (math.pi / total_time)
     turns = moveout(base.reshape(1), slows, offs, pairs, band // halves, total_time)
-    panel = radon(turns, data, gathers)
+    down = (2 * lax.axis_index("freq") // freq_devices).astype(jnp.int32).reshape(1)
+    panel = radon(down, turns, data, gathers)
     panel = panel.reshape(offset_devices, NP // offset_devices, pairs, 2 * halves * gathers)
     parts = lax.all_to_all(panel, "offset", 0, 0, tiled=True)
     result = finish(parts, 1.0 / math.sqrt(offsets))

time: 108 us -> 106 us (0.981)
  Pallas kernels: 36.8 us -> 34.3 us
    pallas_call x1, Pallas kernels: 9.33 us -> 5.83 us  [transform(): pl.pallas_call(functools.partial(transform_kernel, pairs, gathers), in_sp...]
  transfers between devices with their start and end apart: 1 -> 1, of which waited for: 1 -> 1; matrix products, arithmetic and copies ran while one was open for 1% -> 1% of each run, Pallas kernels for 10% -> 11%
where the time goes in v5:
time: 106 us
  blocking collectives  48.7 us (46%)
  Pallas kernels  34.3 us (32%)
  waiting for transfers between devices  14.5 us (14%)
  starting transfers between devices  5.88 us (6%)
  local copies, waits for them, and re-layouts  2.55 us (2%)
    all_to_all x1, blocking collectives, local(): parts = lax.all_to_all(panel, 'offset', 0, 0, tiled=True)  29.3 us
    all_to_all x1, blocking collectives, local(): series = lax.all_to_all(picked, 'freq', 0, 0, tiled=True)  19.4 us
    all_to_all x1, waiting for transfers between devices, local(): data = lax.all_to_all(spectrum, ('freq', 'offset'), 0, 0, tiled=True)  14.5 us
    pallas_call x1, Pallas kernels, moveout(): pl.pallas_call(functools.partial(moveout_kernel, shift, total_time), grid...  11.3 us
    pallas_call x1, Pallas kernels, radon(): pl.pallas_call(functools.partial(radon_kernel, gathers), in_specs=[pl.Blo...  10.8 us
    all_to_all x1, starting transfers between devices, local(): data = lax.all_to_all(spectrum, ('freq', 'offset'), 0, 0, tiled=True)  5.88 us
    pallas_call x1, Pallas kernels, transform(): pl.pallas_call(functools.partial(transform_kernel, pairs, gathers), in_sp...  5.83 us
    pallas_call x1, Pallas kernels, pick(): pl.pallas_call(pick_kernel, in_specs=[vmem, vmem], out_specs=vmem, out_sh...  4.1 us
  transfers between devices with their start and end apart: 1, of which 1 were waited for; matrix products, arithmetic and copies ran while one was open for 1% of the time, Pallas kernels for 11%

profile of v5, /device:TPU:0, one launch (start us, length us, event | category | flops | bytes accessed | tf_op | source)
XLA Modules:
  0.0 106.0 jit_solution(13015303598569148166)
XLA Ops:
  0.0 4.1 %shard_map.56 = bf16[4,256,512]{2,1,0:T(8,128)(2,1)} custom-call(s32[32,32]{1,0:T(8,128)} %slot_ref.1, bf16[1024,512]{1,0:T(8,128)(2,1)} %raw_ref.1), custom_call_target="tpu_custom_call" | custom-call | tf_op jit(solution)/shard_map/pallas_call | solution.py:63
  4.1 19.4 %all_to_all.15.series_ref = bf16[4,256,512]{2,1,0:T(8,128)(2,1)} all-to-all(bf16[4,256,512]{2,1,0:T(8,128)(2,1)} %shard_map.56), channel_id=1, replica_groups=mesh['freq'=4,'offset'=8] {'freq'}, dimensions={0} | all-to-all | bytes 2097152 | tf_op jit(solution)/shard_map/all_to_all | solution.py:340
  23.5 0.0 copy-start.1
  23.5 0.0 copy-start.2
  23.5 5.8 %shard_map.57 = bf16[32,8,16,128]{3,2,1,0:T(8,128)(2,1)} custom-call(bf16[1024,2048]{1,0:T(8,128)(2,1)} %constant.34.clone.table_ref, bf16[4,256,512]{2,1,0:T(8,128)(2,1)} %all_to_all.15.series_ref), custom_call_target="tpu_custom_call" | custom-call | tf_op jit(solution)/shard_map/pallas_call | solution.py:142
  29.4 5.9 %all-to-all-start.1 = ((bf16[32,8,16,128]{3,2,1,0:T(8,128)(2,1)}), bf16[32,8,16,128]{3,2,1,0:T(8,128)(2,1)S(1)}, u32[]{:S(2)}, u32[]{:S(2)}) async-start(bf16[32,8,16,128]{3,2,1,0:T(8,128)(2,1)} %shard_map.57), calls=%async_computation.1 | async-start | bytes 2097152 | tf_op jit(solution)/shard_map/all_to_all | solution.py:343
  35.3 0.0 copy-done.1
  35.3 0.0 copy-done.2
  35.3 0.1 convert_element_type.18
  35.4 0.7 convert_element_type.20.offs_ref
  36.1 0.8 copy.7.slow_ref
  36.9 11.3 %shard_map.55.turn_ref = bf16[16,4,256,256]{3,2,1,0:T(8,128)(2,1)} custom-call(f32[1]{0:T(128)} %bitcast.1.base_ref, f32[256,1]{1,0:T(8,128)} %copy.7.slow_ref, f32[1,256]{1,0:T(1,128)} %convert_element_type.20.offs_ref), custom_call_target="tpu_custom_call" | custom-call | flops 41943040 | bytes 8388608 | tf_op jit(solution)/shard_map/pallas_call | solution.py:191
  48.2 14.5 %all-to-all-done.1.data_ref = bf16[32,8,16,128]{3,2,1,0:T(8,128)(2,1)S(1)} async-done(((bf16[32,8,16,128]{3,2,1,0:T(8,128)(2,1)}), bf16[32,8,16,128]{3,2,1,0:T(8,128)(2,1)S(1)}, u32[]{:S(2)}, u32[]{:S(2)}) %all-to-all-start.1) | async-done | bytes 1048608 | tf_op jit(solution)/shard_map/all_to_all | solution.py:343
  62.6 0.0 copy-start
  62.7 1.0 copy-done
  63.6 10.8 %shard_map.58 = bf16[4096,128]{1,0:T(8,128)(2,1)} custom-call(s32[1]{0:T(128)} %bitcast.down_ref, bf16[16,4,256,256]{3,2,1,0:T(8,128)(2,1)} %shard_map.55.turn_ref, bf16[32,8,16,128]{3,2,1,0:T(8,128)(2,1)} %copy-done), custom_call_target="tpu_custom_call" | custom-call | tf_op jit(solution)/shard_map/pallas_call | solution.py:281
  74.4 29.3 %all_to_all.16.in_ref = bf16[8,32,16,128]{3,2,1,0:T(8,128)(2,1)S(1)} all-to-all(bf16[8,32,16,128]{3,2,1,0:T(8,128)(2,1)} %bitcast.6), channel_id=1, replica_groups=mesh['freq'=4,'offset'=8] {'offset'}, dimensions={0} | all-to-all | bytes 2097152 | tf_op jit(solution)/shard_map/all_to_all | solution.py:354
  103.8 2.3 %shard_map.59 = f32[32,64,256]{2,1,0:T(8,128)} custom-call(bf16[8,32,16,128]{3,2,1,0:T(8,128)(2,1)S(1)} %all_to_all.16.in_ref), custom_call_target="tpu_custom_call" | custom-call | tf_op jit(solution)/shard_map/pallas_call | solution.py:315
  (3 shorter events, 0.0 us)
Async XLA Ops:
  23.5 11.7 %copy-start.1 = (s32[256]{0:T(256)S(1)}, s32[256]{0:T(256)}, u32[]{:S(2)}) copy-start(s32[256]{0:T(256)} %param.7) | copy-start | bytes 3076
  23.5 11.8 %copy-start.2 = (s32[256]{0:T(256)S(1)}, s32[256]{0:T(256)}, u32[]{:S(2)}) copy-start(s32[256]{0:T(256)} %param.8) | copy-start | bytes 3076
  29.4 33.3 %all-to-all-start.1 = ((bf16[32,8,16,128]{3,2,1,0:T(8,128)(2,1)}), bf16[32,8,16,128]{3,2,1,0:T(8,128)(2,1)S(1)}, u32[]{:S(2)}, u32[]{:S(2)}) async-start(bf16[32,8,16,128]{3,2,1,0:T(8,128)(2,1)} %shard_map.57), calls=%async_computation.1 | async-start | bytes 2097152 | tf_op jit(solution)/shard_map/all_to_all | solution.py:343
  62.6 1.0 copy-start

commit v6 on v5

--- a/solution.py
+++ b/solution.py
@@ -65,7 +65,7 @@
         in_specs=[vmem, vmem],
         out_specs=vmem,
         out_shape=jax.ShapeDtypeStruct((groups, rows, raw_traces.shape[1]), raw_traces.dtype),
-        compiler_params=pltpu.CompilerParams(vmem_limit_bytes=61 * MIB),
+        compiler_params=pltpu.CompilerParams(vmem_limit_bytes=24 * MIB),
     )(trace_slot, raw_traces)
 
 
@@ -90,31 +90,25 @@
     return found
 
 
-def transform_kernel(pairs, gathers, table_ref, series_ref, out_ref, held, even, odd, sems):
+def transform_kernel(pairs, gathers, chunks, table_ref, series_ref, out_ref, even, odd):
     blocks, rows, local_times = series_ref.shape
-    chunks, step, _ = held.shape
+    step = table_ref.shape[0] // chunks
     half = local_times // 2
-    copies = [
-        pltpu.make_async_copy(table_ref.at[pl.ds(i * step, step)], held.at[i], sems.at[i])
-        for i in range(chunks)
-    ]
-    for copy in copies:
-        copy.start()
     for b in range(blocks):
         turned = series_ref[b].T
         even[b * half : (b + 1) * half] = turned[:half]
         odd[b * half : (b + 1) * half] = turned[half:]
     depth = blocks * half
     for i in range(chunks):
-        copies[i].wait()
-        evens = jnp.dot(held[i, :, :depth], even[...], preferred_element_type=jnp.float32)
-        odds = jnp.dot(held[i, :, depth:], odd[...], preferred_element_type=jnp.float32)
+        own = slice(i * step, (i + 1) * step)
+        evens = jnp.dot(table_ref[own, :depth], even[...], preferred_element_type=jnp.float32)
+        odds = jnp.dot(table_ref[own, depth:], odd[...], preferred_element_type=jnp.float32)
         low = evens + odds
         high = evens - odds
         if len(out_ref.shape) == 3:
             row = lax.broadcasted_iota(jnp.int32, (step, 1), 0)
-            out_ref[0, i * step : (i + 1) * step] = low.astype(out_ref.dtype)
-            out_ref[1, i * step : (i + 1) * step] = jnp.where(
+            out_ref[0, own] = low.astype(out_ref.dtype)
+            out_ref[1, own] = jnp.where(
                 row // pairs % 2 == 0, high, -high
             ).astype(out_ref.dtype)
             continue
@@ -140,17 +134,15 @@
     aligned = rows % (4 * gathers) == 0 and pairs % 8 == 0 and devices % (2 * chunks) == 0
     vmem = pl.BlockSpec(memory_space=pltpu.VMEM)
     out = pl.pallas_call(
-        functools.partial(transform_kernel, pairs, gathers),
-        in_specs=[pl.BlockSpec(memory_space=pl.ANY), vmem],
+        functools.partial(transform_kernel, pairs, gathers, chunks),
+        in_specs=[vmem, vmem],
         out_specs=vmem,
         out_shape=jax.ShapeDtypeStruct(final if aligned else (2, columns, rows), jnp.bfloat16),
         scratch_shapes=[
-            pltpu.VMEM((chunks, columns // chunks, total_time), jnp.bfloat16),
             pltpu.VMEM((total_time // 2, rows), jnp.bfloat16),
             pltpu.VMEM((total_time // 2, rows), jnp.bfloat16),
-            pltpu.SemaphoreType.DMA((chunks,)),
         ],
-        compiler_params=pltpu.CompilerParams(vmem_limit_bytes=61 * MIB),
+        compiler_params=pltpu.CompilerParams(vmem_limit_bytes=24 * MIB),
     )(table, series)
     if aligned:
         return out
@@ -159,84 +151,77 @@
     return out.transpose(0, 4, 3, 1, 2, 5).reshape(final)
 
 
-def moveout_kernel(shift, total_time, base_ref, slow_ref, offs_ref, out_ref, cs, sn, tc, ts):
-    @pl.when(pl.program_id(0) == 0)
-    def start():
-        spread = CURVATURE * slow_ref[...] * offs_ref[...]
-        delay = jnp.sqrt(APEX_TIME * APEX_TIME + spread * spread) - APEX_TIME
-        phase = base_ref[0] * delay
-        cs[0] = jnp.cos(phase)
-        sn[0] = jnp.sin(phase)
-        turn = delay * (2.0 * math.pi / total_time)
-        tc[...] = jnp.cos(turn)
-        ts[...] = jnp.sin(turn)
-        far = delay * (2.0 * shift * math.pi / total_time)
-        far_c = jnp.cos(far)
-        far_s = jnp.sin(far)
-        cs[1] = cs[0] * far_c - sn[0] * far_s
-        sn[1] = sn[0] * far_c + cs[0] * far_s
-
-    for a in range(2):
-        c = cs[a]
-        s = sn[a]
-        out_ref[0, a] = c.astype(out_ref.dtype)
-        out_ref[0, 2 + a] = s.astype(out_ref.dtype)
-        cs[a] = c * tc[...] - s * ts[...]
-        sn[a] = s * tc[...] + c * ts[...]
-
-
-def moveout(base, slows, offs, pairs, shift, total_time):
+def moveout_kernel(shift, total_time, base_ref, slow_ref, offs_ref, out_ref):
+    spread = CURVATURE * slow_ref[...] * offs_ref[...]
+    delay = jnp.sqrt(APEX_TIME * APEX_TIME + spread * spread) - APEX_TIME
+    phase = base_ref[0] * delay
+    c = jnp.cos(phase)
+    s = jnp.sin(phase)
+    far = delay * (2.0 * shift * math.pi / total_time)
+    far_c = jnp.cos(far)
+    far_s = jnp.sin(far)
+    turn = delay * (2.0 * math.pi / total_time)
+    out_ref[0] = c
+    out_ref[1] = c * far_c - s * far_s
+    out_ref[2] = s
+    out_ref[3] = s * far_c + c * far_s
+    out_ref[4] = jnp.cos(turn)
+    out_ref[5] = jnp.sin(turn)
+
+
+def moveout(base, slows, offs, shift, total_time):
     count = slows.shape[0]
     offsets = offs.shape[1]
+    rows = min(count, 64)
     return pl.pallas_call(
         functools.partial(moveout_kernel, shift, total_time),
-        grid=(pairs,),
+        grid=(count // rows,),
         in_specs=[
             pl.BlockSpec(memory_space=pltpu.SMEM),
-            pl.BlockSpec((count, 1), lambda k: (0, 0)),
-            pl.BlockSpec((1, offsets), lambda k: (0, 0)),
+            pl.BlockSpec((rows, 1), lambda i: (i, 0)),
+            pl.BlockSpec((1, offsets), lambda i: (0, 0)),
         ],
-        out_specs=pl.BlockSpec((1, 4, count, offsets), lambda k: (k, 0, 0, 0)),
-        out_shape=jax.ShapeDtypeStruct((pairs, 4, count, offsets), jnp.bfloat16),
-        scratch_shapes=[
-            pltpu.VMEM((2, count, offsets), jnp.float32),
-            pltpu.VMEM((2, count, offsets), jnp.float32),
-            pltpu.VMEM((count, offsets), jnp.float32),
-            pltpu.VMEM((count, offsets), jnp.float32),
-        ],
-        compiler_params=pltpu.CompilerParams(vmem_limit_bytes=61 * MIB),
+        out_specs=pl.BlockSpec((6, rows, offsets), lambda i: (0, i, 0)),
+        out_shape=jax.ShapeDtypeStruct((6, count, offsets), jnp.float32),
+        compiler_params=pltpu.CompilerParams(vmem_limit_bytes=24 * MIB),
         cost_estimate=pl.CostEstimate(
-            flops=pairs * 40 * count * offsets,
-            bytes_accessed=pairs * 8 * count * offsets,
+            flops=300 * count * offsets,
+            bytes_accessed=24 * count * offsets,
             transcendentals=6 * count * offsets,
         ),
     )(base, slows, offs)
 
 
+def quotient(value, divisor):
+    if divisor & (divisor - 1):
+        return value // divisor
+    return lax.shift_right_logical(value, jnp.int32(divisor.bit_length() - 1))
+
+
+def remainder(value, divisor):
+    if divisor & (divisor - 1):
+        return value % divisor
+    return value & (divisor - 1)
+
+
 def one_hot(rows, columns, source):
-    row = lax.broadcasted_iota(jnp.int32, (rows, columns), 0)
+    row = lax.broadcasted_iota(jnp.int32, (rows, 1), 0)
     column = lax.broadcasted_iota(jnp.int32, (rows, columns), 1)
     return jnp.where(column == source(row), 1.0, 0.0).astype(jnp.bfloat16)
 
 
-def radon_kernel(gathers, down_ref, turn_ref, data_ref, out_ref, turns, plain, turned, held, sems):
+def radon_kernel(gathers, down_ref, state_ref, data_ref, out_ref, turns, plain, turned, held):
     devices, own_offsets, pairs, lanes = data_ref.shape
     offsets = devices * own_offsets
-    slows = turn_ref.shape[2]
+    slows = state_ref.shape[1]
     tile = 16
     size = tile * pairs
-    copies = [
-        pltpu.make_async_copy(turn_ref.at[k], turns.at[k], sems.at[k]) for k in range(pairs)
-    ]
-    for copy in copies:
-        copy.start()
-
     together = tile // own_offsets
     down = down_ref[0]
 
     def received(r):
-        k = r // tile
-        return r % tile * pairs + k + down * (pairs - 1 - 2 * k)
+        k = quotient(r, tile)
+        return remainder(r, tile) * pairs + k + down * (pairs - 1 - 2 * k)
 
     swap = one_hot(size, size, received)
     for d in range(devices // together):
@@ -247,7 +232,7 @@
     row = lax.broadcasted_iota(jnp.int32, (lanes, lanes), 0)
     column = lax.broadcasted_iota(jnp.int32, (lanes, lanes), 1)
     quarter = jnp.where(
-        column % (2 * gathers) < gathers,
+        remainder(column, 2 * gathers) < gathers,
         jnp.where(row == column + gathers, -1.0, 0.0),
         jnp.where(row == column - gathers, 1.0, 0.0),
     ).astype(jnp.bfloat16)
@@ -256,9 +241,24 @@
             jnp.bfloat16
         )
 
+    def fill(t, carry):
+        own = pl.ds(pl.multiple_of(t * tile, tile), tile)
+        step_c = state_ref[4, own]
+        step_s = state_ref[5, own]
+        twice = 2.0 * step_c
+        now = [state_ref[i, own] for i in range(4)]
+        past = [now[a] * step_c + now[2 + a] * step_s for a in range(2)]
+        past += [now[2 + a] * step_c - now[a] * step_s for a in range(2)]
+        for k in range(pairs):
+            for i in range(4):
+                turns[k, i, own] = now[i].astype(jnp.bfloat16)
+                now[i], past[i] = twice * now[i] - past[i], now[i]
+        return carry
+
+    lax.fori_loop(0, slows // tile, fill, 0)
+
     first_half = lax.broadcasted_iota(jnp.int32, (1, lanes), 1) < 2 * gathers
     for k in range(pairs):
-        copies[k].wait()
         cosine = turns[k, :2].reshape(2 * slows, offsets)
         sines = turns[k, 2:].reshape(2 * slows, offsets)
         both = jnp.dot(cosine, plain[k], preferred_element_type=jnp.float32) + jnp.dot(
@@ -266,7 +266,7 @@
         )
         held[k] = jnp.where(first_half, both[:slows], both[slows:]).astype(jnp.bfloat16)
 
-    swap = one_hot(size, size, lambda r: r % pairs * tile + r // pairs)
+    swap = one_hot(size, size, lambda r: remainder(r, pairs) * tile + quotient(r, pairs))
     for p in range(slows // tile):
         block = held[:, p * tile : (p + 1) * tile].reshape(size, lanes)
         if pairs > 1:
@@ -274,28 +274,23 @@
         out_ref[p * size : (p + 1) * size] = block.astype(out_ref.dtype)
 
 
-def radon(down, turns, data, gathers):
-    pairs, parts, count, offsets = turns.shape
-    lanes = parts * gathers
+def radon(down, state, data, gathers):
+    _, count, offsets = state.shape
+    pairs, lanes = data.shape[2:]
     vmem = pl.BlockSpec(memory_space=pltpu.VMEM)
     return pl.pallas_call(
         functools.partial(radon_kernel, gathers),
-        in_specs=[
-            pl.BlockSpec(memory_space=pltpu.SMEM),
-            pl.BlockSpec(memory_space=pl.ANY),
-            vmem,
-        ],
+        in_specs=[pl.BlockSpec(memory_space=pltpu.SMEM), vmem, vmem],
         out_specs=vmem,
         out_shape=jax.ShapeDtypeStruct((count * pairs, lanes), jnp.bfloat16),
         scratch_shapes=[
-            pltpu.VMEM(turns.shape, jnp.bfloat16),
+            pltpu.VMEM((pairs, 4, count, offsets), jnp.bfloat16),
             pltpu.VMEM((pairs, offsets, lanes), jnp.bfloat16),
             pltpu.VMEM((pairs, offsets, lanes), jnp.bfloat16),
             pltpu.VMEM((pairs, count, lanes), jnp.bfloat16),
-            pltpu.SemaphoreType.DMA((pairs,)),
         ],
-        compiler_params=pltpu.CompilerParams(vmem_limit_bytes=61 * MIB),
-    )(down, turns, data)
+        compiler_params=pltpu.CompilerParams(vmem_limit_bytes=24 * MIB),
+    )(down, state, data)
 
 
 def finish_kernel(scale, in_ref, out_ref):
@@ -347,9 +342,9 @@
     slows = slowness_index.astype(jnp.float32)[:, None]
     first = lax.axis_index("freq") * band + lax.axis_index("offset") * pairs
     base = (2 * first + 1).astype(jnp.float32) * (math.pi / total_time)
-    turns = moveout(base.reshape(1), slows, offs, pairs, band // halves, total_time)
+    state = moveout(base.reshape(1), slows, offs, band // halves, total_time)
     down = (2 * lax.axis_index("freq") // freq_devices).astype(jnp.int32).reshape(1)
-    panel = radon(down, turns, data, gathers)
+    panel = radon(down, state, data, gathers)
     panel = panel.reshape(offset_devices, NP // offset_devices, pairs, 2 * halves * gathers)
     parts = lax.all_to_all(panel, "offset", 0, 0, tiled=True)
     result = finish(parts, 1.0 / math.sqrt(offsets))

time: 106 us -> 94.1 us (0.89)
  Pallas kernels: 34.3 us -> 15.6 us
  waiting for transfers between devices: 14.5 us -> 23.7 us
  blocking collectives: 48.7 us -> 46.8 us
    all_to_all x1, waiting for transfers between devices: 14.5 us -> 23.7 us  [local(): data = lax.all_to_all(spectrum, ('freq', 'offset'), 0, 0, tiled=True)]
    pallas_call x1, Pallas kernels: 11.3 us -> 3.43 us  [moveout(): pl.pallas_call(functools.partial(moveout_kernel, shift, total_time), grid...]
    pallas_call x1, Pallas kernels: 10.8 us -> 5.51 us  [radon(): pl.pallas_call(functools.partial(radon_kernel, gathers), in_specs=[pl.Blo...]
    pallas_call x1, Pallas kernels: 5.83 us -> 2.48 us  [transform(): pl.pallas_call(functools.partial(transform_kernel, pairs, gathers, chunks...]
    pallas_call x1, Pallas kernels: 4.1 us -> 1.88 us  [pick(): pl.pallas_call(pick_kernel, in_specs=[vmem, vmem], out_specs=vmem, out_sh...]
    unnamed x6 -> x10, local copies, waits for them, and re-layouts: 0.98 us -> 2.3 us
  transfers between devices with their start and end apart: 1 -> 1, of which waited for: 1 -> 1; matrix products, arithmetic and copies ran while one was open for 1% -> 0% of each run, Pallas kernels for 11% -> 4%
where the time goes in v6:
time: 94.1 us; the launch traced here: 93.8 us
  blocking collectives  46.8 us (50%)
  waiting for transfers between devices  23.7 us (25%)
  Pallas kernels  15.6 us (17%)
  starting transfers between devices  4.89 us (5%)
  local copies, waits for them, and re-layouts  2.62 us (3%)
    all_to_all x1, blocking collectives, local(): parts = lax.all_to_all(panel, 'offset', 0, 0, tiled=True)  28.3 us
    all_to_all x1, waiting for transfers between devices, local(): data = lax.all_to_all(spectrum, ('freq', 'offset'), 0, 0, tiled=True)  23.7 us
    all_to_all x1, blocking collectives, local(): series = lax.all_to_all(picked, 'freq', 0, 0, tiled=True)  18.5 us
    pallas_call x1, Pallas kernels, radon(): pl.pallas_call(functools.partial(radon_kernel, gathers), in_specs=[pl.Blo...  5.51 us
    all_to_all x1, starting transfers between devices, local(): data = lax.all_to_all(spectrum, ('freq', 'offset'), 0, 0, tiled=True)  4.89 us
    pallas_call x1, Pallas kernels, moveout(): pl.pallas_call(functools.partial(moveout_kernel, shift, total_time), grid...  3.43 us
    pallas_call x1, Pallas kernels, transform(): pl.pallas_call(functools.partial(transform_kernel, pairs, gathers, chunks...  2.48 us
    unnamed x10, local copies, waits for them, and re-layouts  2.3 us
  transfers between devices with their start and end apart: 1, of which 1 were waited for; matrix products, arithmetic and copies ran while one was open for 0% of the time, Pallas kernels for 4%

profile of v6, /device:TPU:0, one launch (start us, length us, event | category | flops | bytes accessed | tf_op | source)
XLA Modules:
  0.0 93.8 jit_solution(7266443538888956306)
XLA Ops:
  0.0 0.0 copy-start
  0.0 0.0 copy-start.1
  0.0 1.4 %copy-done.1 = bf16[1024,512]{1,0:T(8,128)(2,1)S(1)} copy-done((bf16[1024,512]{1,0:T(8,128)(2,1)S(1)}, bf16[1024,512]{1,0:T(8,128)(2,1)}, u32[]{:S(2)}) %copy-start.1) | copy-done | bytes 1048600
  1.4 0.0 copy-start.2
  1.4 0.9 copy-done.2
  2.3 1.9 %shard_map.56 = bf16[4,256,512]{2,1,0:T(8,128)(2,1)S(1)} custom-call(s32[32,32]{1,0:T(8,128)S(1)} %copy-done.2, bf16[1024,512]{1,0:T(8,128)(2,1)S(1)} %copy-done.1), custom_call_target="tpu_custom_call" | custom-call | tf_op jit(solution)/shard_map/pallas_call | solution.py:63
  4.2 18.5 %all_to_all.15.series_ref = bf16[4,256,512]{2,1,0:T(8,128)(2,1)S(1)} all-to-all(bf16[4,256,512]{2,1,0:T(8,128)(2,1)S(1)} %shard_map.56), channel_id=1, replica_groups=mesh['freq'=4,'offset'=8] {'freq'}, dimensions={0} | all-to-all | bytes 2097152 | tf_op jit(solution)/shard_map/all_to_all | solution.py:335
  22.7 0.0 copy-done
  22.7 2.5 %shard_map.57 = bf16[32,8,16,128]{3,2,1,0:T(8,128)(2,1)} custom-call(bf16[1024,2048]{1,0:T(8,128)(2,1)S(1)} %copy-done, bf16[4,256,512]{2,1,0:T(8,128)(2,1)S(1)} %all_to_all.15.series_ref), custom_call_target="tpu_custom_call" | custom-call | tf_op jit(solution)/shard_map/pallas_call | solution.py:136
  25.2 0.0 copy-start.3
  25.2 0.0 copy-start.4
  25.2 4.9 %all-to-all-start.1 = ((bf16[32,8,16,128]{3,2,1,0:T(8,128)(2,1)}), bf16[32,8,16,128]{3,2,1,0:T(8,128)(2,1)S(1)}, u32[]{:S(2)}, u32[]{:S(2)}) async-start(bf16[32,8,16,128]{3,2,1,0:T(8,128)(2,1)} %shard_map.57), calls=%async_computation.1 | async-start | bytes 2097152 | tf_op jit(solution)/shard_map/all_to_all | solution.py:338
  30.1 0.0 copy-done.3
  30.1 0.0 copy-done.4
  30.1 0.1 convert_element_type.18
  30.2 0.1 convert_element_type.20.offs_ref
  30.3 0.1 copy.7.slow_ref
  30.5 3.4 %shard_map.55.state_ref = f32[6,256,256]{2,1,0:T(8,128)S(1)} custom-call(f32[1]{0:T(128)} %bitcast.1.base_ref, f32[256,1]{1,0:T(8,128)S(1)} %copy.7.slow_ref, f32[1,256]{1,0:T(1,128)S(1)} %convert_element_type.20.offs_ref), custom_call_target="tpu_custom_call" | custom-call | flops 19660800 | bytes 1572864 | tf_op jit(solution)/shard_map/pallas_call | solution.py:176
  33.9 23.7 %all-to-all-done.1.data_ref = bf16[32,8,16,128]{3,2,1,0:T(8,128)(2,1)S(1)} async-done(((bf16[32,8,16,128]{3,2,1,0:T(8,128)(2,1)}), bf16[32,8,16,128]{3,2,1,0:T(8,128)(2,1)S(1)}, u32[]{:S(2)}, u32[]{:S(2)}) %all-to-all-start.1) | async-done | bytes 1048608 | tf_op jit(solution)/shard_map/all_to_all | solution.py:338
  57.7 5.5 %shard_map.58 = bf16[4096,128]{1,0:T(8,128)(2,1)S(1)} custom-call(s32[1]{0:T(128)} %bitcast.down_ref, f32[6,256,256]{2,1,0:T(8,128)S(1)} %shard_map.55.state_ref, bf16[32,8,16,128]{3,2,1,0:T(8,128)(2,1)S(1)} %all-to-all-done.1.data_ref), custom_call_target="tpu_custom_call" | custom-call | tf_op jit(solution)/shard_map/pallas_call | solution.py:281
  63.2 28.3 %all_to_all.16.in_ref = bf16[8,32,16,128]{3,2,1,0:T(8,128)(2,1)S(1)} all-to-all(bf16[8,32,16,128]{3,2,1,0:T(8,128)(2,1)S(1)} %bitcast.6), channel_id=1, replica_groups=mesh['freq'=4,'offset'=8] {'offset'}, dimensions={0} | all-to-all | bytes 2097152 | tf_op jit(solution)/shard_map/all_to_all | solution.py:349
  91.5 2.3 %shard_map.59 = f32[32,64,256]{2,1,0:T(8,128)} custom-call(bf16[8,32,16,128]{3,2,1,0:T(8,128)(2,1)S(1)} %all_to_all.16.in_ref), custom_call_target="tpu_custom_call" | custom-call | tf_op jit(solution)/shard_map/pallas_call | solution.py:310
  (3 shorter events, 0.0 us)
Async XLA Ops:
  0.0 22.7 %copy-start = (bf16[1024,2048]{1,0:T(8,128)(2,1)S(1)}, bf16[1024,2048]{1,0:T(8,128)(2,1)}, u32[]{:S(2)}) copy-start(bf16[1024,2048]{1,0:T(8,128)(2,1)} %constant.34.clone.table_ref) | copy-start | bytes 12582916
  0.0 1.4 %copy-start.1 = (bf16[1024,512]{1,0:T(8,128)(2,1)S(1)}, bf16[1024,512]{1,0:T(8,128)(2,1)}, u32[]{:S(2)}) copy-start(bf16[1024,512]{1,0:T(8,128)(2,1)} %raw_ref.1) | copy-start | bytes 3145732
  1.4 0.9 copy-start.2
  25.2 4.9 %copy-start.3 = (s32[256]{0:T(256)S(1)}, s32[256]{0:T(256)}, u32[]{:S(2)}) copy-start(s32[256]{0:T(256)} %param.7) | copy-start | bytes 3076
  25.2 4.9 %copy-start.4 = (s32[256]{0:T(256)S(1)}, s32[256]{0:T(256)}, u32[]{:S(2)}) copy-start(s32[256]{0:T(256)} %param.8) | copy-start | bytes 3076
  25.2 32.5 %all-to-all-start.1 = ((bf16[32,8,16,128]{3,2,1,0:T(8,128)(2,1)}), bf16[32,8,16,128]{3,2,1,0:T(8,128)(2,1)S(1)}, u32[]{:S(2)}, u32[]{:S(2)}) async-start(bf16[32,8,16,128]{3,2,1,0:T(8,128)(2,1)} %shard_map.57), calls=%async_computation.1 | async-start | bytes 2097152 | tf_op jit(solution)/shard_map/all_to_all | solution.py:338

commit v7 on v6

--- a/solution.py
+++ b/solution.py
@@ -34,10 +34,9 @@
     return (both / np.float32(math.sqrt(total_time))).astype(ml_dtypes.bfloat16)
 
 
-def pick_kernel(slot_ref, raw_ref, out_ref):
-    gathers = slot_ref.shape[0]
-    groups, rows, _ = out_ref.shape
-    own_offsets = rows // gathers
+def pick_kernel(me_ref, slot_ref, raw_ref, *out_refs):
+    gathers, local_offsets = slot_ref.shape
+    own_offsets = local_offsets // len(out_refs)
     times = raw_ref.shape[1]
     half = times // 2
     row = lax.broadcasted_iota(jnp.int32, (times, times), 0)
@@ -46,27 +45,33 @@
     split = jnp.where(row == source, 1.0, 0.0).astype(jnp.bfloat16)
     raw = jnp.dot(raw_ref[...], split, preferred_element_type=jnp.float32).astype(jnp.bfloat16)
     lane = lax.broadcasted_iota(jnp.int32, (gathers, raw_ref.shape[0]), 1)
-    for f in range(groups):
-        picks = [
-            jnp.where(lane == slot_ref[:, h : h + 1], 1.0, 0.0).astype(jnp.bfloat16)
-            for h in range(f * own_offsets, (f + 1) * own_offsets)
-        ]
-        out_ref[f] = jnp.dot(
+    slot = slot_ref[...]
+    place = lax.broadcasted_iota(jnp.int32, slot.shape, 1)
+    for s, out_ref in enumerate(out_refs):
+        first = (me_ref[0] ^ s) * own_offsets
+        picks = []
+        for h in range(own_offsets):
+            wanted = jnp.sum(jnp.where(place == first + h, slot, 0.0), axis=1, keepdims=True)
+            picks.append(
+                jnp.where(lane == wanted.astype(jnp.int32), 1.0, 0.0).astype(jnp.bfloat16)
+            )
+        out_ref[...] = jnp.dot(
             jnp.concatenate(picks, axis=0), raw, preferred_element_type=jnp.float32
         ).astype(out_ref.dtype)
 
 
-def pick(trace_slot, raw_traces, groups):
+def pick(me, trace_slot, raw_traces, groups):
     gathers, local_offsets = trace_slot.shape
     rows = gathers * local_offsets // groups
     vmem = pl.BlockSpec(memory_space=pltpu.VMEM)
+    block = jax.ShapeDtypeStruct((rows, raw_traces.shape[1]), raw_traces.dtype)
     return pl.pallas_call(
         pick_kernel,
-        in_specs=[vmem, vmem],
-        out_specs=vmem,
-        out_shape=jax.ShapeDtypeStruct((groups, rows, raw_traces.shape[1]), raw_traces.dtype),
+        in_specs=[pl.BlockSpec(memory_space=pltpu.SMEM), vmem, vmem],
+        out_specs=[vmem] * groups,
+        out_shape=[block] * groups,
         compiler_params=pltpu.CompilerParams(vmem_limit_bytes=24 * MIB),
-    )(trace_slot, raw_traces)
+    )(me, trace_slot, raw_traces)
 
 
 def regroup(parts, gathers):
@@ -90,14 +95,17 @@
     return found
 
 
-def transform_kernel(pairs, gathers, chunks, table_ref, series_ref, out_ref, even, odd):
-    blocks, rows, local_times = series_ref.shape
+def transform_kernel(pairs, gathers, chunks, me_ref, table_ref, *refs):
+    *series_refs, out_ref, even, odd = refs
+    blocks = len(series_refs)
+    _, local_times = series_refs[0].shape
     step = table_ref.shape[0] // chunks
     half = local_times // 2
-    for b in range(blocks):
-        turned = series_ref[b].T
-        even[b * half : (b + 1) * half] = turned[:half]
-        odd[b * half : (b + 1) * half] = turned[half:]
+    for s, series_ref in enumerate(series_refs):
+        turned = series_ref[...].T
+        place = pl.ds(pl.multiple_of((me_ref[0] ^ s) * half, half), half)
+        even[place] = turned[:half]
+        odd[place] = turned[half:]
     depth = blocks * half
     for i in range(chunks):
         own = slice(i * step, (i + 1) * step)
@@ -124,9 +132,9 @@
                 out_ref[devices - 1 - place, h] = value.astype(out_ref.dtype)
 
 
-def transform(table, series, pairs, gathers):
+def transform(me, table, series, pairs, gathers):
     columns, total_time = table.shape
-    blocks, rows, local_times = series.shape
+    rows = series[0].shape[0]
     own_offsets = rows // gathers
     devices = columns // (2 * pairs)
     final = (devices, own_offsets, pairs, 4 * gathers)
@@ -135,7 +143,7 @@
     vmem = pl.BlockSpec(memory_space=pltpu.VMEM)
     out = pl.pallas_call(
         functools.partial(transform_kernel, pairs, gathers, chunks),
-        in_specs=[vmem, vmem],
+        in_specs=[pl.BlockSpec(memory_space=pltpu.SMEM)] + [vmem] * (1 + len(series)),
         out_specs=vmem,
         out_shape=jax.ShapeDtypeStruct(final if aligned else (2, columns, rows), jnp.bfloat16),
         scratch_shapes=[
@@ -143,7 +151,7 @@
             pltpu.VMEM((total_time // 2, rows), jnp.bfloat16),
         ],
         compiler_params=pltpu.CompilerParams(vmem_limit_bytes=24 * MIB),
-    )(table, series)
+    )(me, table, *series)
     if aligned:
         return out
     out = out.reshape(2, devices // 2, 2, 2, pairs, own_offsets, gathers)
@@ -331,10 +339,13 @@
     pairs = own_freqs // halves
     own_offsets = local_offsets // freq_devices
 
-    picked = pick(trace_slot, raw_traces, freq_devices)
-    series = lax.all_to_all(picked, "freq", 0, 0, tiled=True)
+    me = lax.axis_index("freq").astype(jnp.int32).reshape(1)
+    series = list(pick(me, trace_slot.astype(jnp.float32), raw_traces, freq_devices))
+    for s in range(1, freq_devices):
+        swaps = [(f, f ^ s) for f in range(freq_devices)]
+        series[s] = lax.ppermute(series[s], "freq", swaps)
     table = jnp.asarray(table_rows(total_time, freq_devices, offset_devices, halves, pairs))
-    spectrum = transform(table, series, pairs, gathers)
+    spectrum = transform(me, table, series, pairs, gathers)
     data = lax.all_to_all(spectrum, ("freq", "offset"), 0, 0, tiled=True)
 
     offs = offset_index.reshape(offset_devices, freq_devices, own_offsets)

time: 94.1 us -> 94.2 us (level)
  blocking collectives: 46.8 us -> 28.3 us
  waiting for transfers between devices: 23.7 us -> 35.9 us
  starting transfers between devices: 4.89 us -> 9.07 us
  local copies, waits for them, and re-layouts: 2.62 us -> 3.74 us
    all_to_all x1 -> x0, blocking collectives: 18.5 us -> none  [local(): series = lax.all_to_all(picked, 'freq', 0, 0, tiled=True)]
    ppermute x0 -> x3, waiting for transfers between devices: none -> 12.2 us  [local(): series[s] = lax.ppermute(series[s], 'freq', swaps)]
    ppermute x0 -> x3, starting transfers between devices: none -> 3.18 us  [local(): series[s] = lax.ppermute(series[s], 'freq', swaps)]
    unnamed x10 -> x8, local copies, waits for them, and re-layouts: 2.3 us -> 3.42 us
    all_to_all x1, starting transfers between devices: 4.89 us -> 5.89 us  [local(): data = lax.all_to_all(spectrum, ('freq', 'offset'), 0, 0, tiled=True)]
  transfers between devices with their start and end apart: 1 -> 4, of which waited for: 1 -> 3; matrix products, arithmetic and copies ran while one was open for 0% -> 0% of each run, Pallas kernels for 4% -> 4%
where the time goes in v7:
time: 94.2 us; the launch traced here: 93.8 us
  waiting for transfers between devices  35.9 us (38%)
  blocking collectives  28.3 us (30%)
  Pallas kernels  16 us (17%)
  starting transfers between devices  9.07 us (10%)
  local copies, waits for them, and re-layouts  3.74 us (4%)
    all_to_all x1, blocking collectives, local(): parts = lax.all_to_all(panel, 'offset', 0, 0, tiled=True)  28.3 us
    all_to_all x1, waiting for transfers between devices, local(): data = lax.all_to_all(spectrum, ('freq', 'offset'), 0, 0, tiled=True)  23.7 us
    ppermute x3, waiting for transfers between devices, local(): series[s] = lax.ppermute(series[s], 'freq', swaps)  12.2 us
    all_to_all x1, starting transfers between devices, local(): data = lax.all_to_all(spectrum, ('freq', 'offset'), 0, 0, tiled=True)  5.89 us
    pallas_call x1, Pallas kernels, radon(): pl.pallas_call(functools.partial(radon_kernel, gathers), in_specs=[pl.Blo...  5.51 us
    pallas_call x1, Pallas kernels, moveout(): pl.pallas_call(functools.partial(moveout_kernel, shift, total_time), grid...  3.43 us
    unnamed x8, local copies, waits for them, and re-layouts  3.42 us
    ppermute x3, starting transfers between devices, local(): series[s] = lax.ppermute(series[s], 'freq', swaps)  3.18 us
  transfers between devices with their start and end apart: 4, of which 3 were waited for; matrix products, arithmetic and copies ran while one was open for 0% of the time, Pallas kernels for 4%

profile of v7, /device:TPU:0, one launch (start us, length us, event | category | flops | bytes accessed | tf_op | source)
XLA Modules:
  0.0 93.8 jit_solution(8335069673337808471)
XLA Ops:
  0.0 0.7 convert_element_type.24.slot_ref
  0.7 0.0 copy-start.1
  0.7 1.2 %copy-done.1 = bf16[1024,512]{1,0:T(8,128)(2,1)S(1)} copy-done((bf16[1024,512]{1,0:T(8,128)(2,1)S(1)}, bf16[1024,512]{1,0:T(8,128)(2,1)}, u32[]{:S(2)}) %copy-start.1) | copy-done | bytes 1048600
  1.9 2.0 %shard_map.56 = (bf16[256,512]{1,0:T(8,128)(2,1)S(1)}, bf16[256,512]{1,0:T(8,128)(2,1)S(1)}, bf16[256,512]{1,0:T(8,128)(2,1)S(1)}, bf16[256,512]{1,0:T(8,128)(2,1)S(1)}) custom-call(s32[1]{0:T(128)} %bitcast.4.me_ref, f32[32,32]{1,0:T(8,128)S(1)} %convert_element_type.24.slot_ref, bf16[1024,512]{1,0:T(8,128)(2,1)S(1)} %copy-done.1), custom_call_target="tpu_custom_call" | custom-call | tf_op jit(solution)/shard_map/pallas_call | solution.py:68
  3.9 0.5 collective-permute-start
  4.4 2.6 %collective-permute-start.1 = (bf16[256,512]{1,0:T(8,128)(2,1)S(1)}, bf16[256,512]{1,0:T(8,128)(2,1)S(1)}, u32[]{:S(2)}, u32[]{:S(2)}) collective-permute-start(bf16[256,512]{1,0:T(8,128)(2,1)S(1)} %get-tuple-element.11), channel_id=1, source_target_pairs={{0,16},{8,24},{16,0},{24,8},{1,17},{9,25},{17,1},{25,9},{2,18},{10... | collective-permute-start | bytes 786440 | tf_op jit(solution)/shard_map/ppermute | solution.py:346
  7.0 0.1 collective-permute-start.2
  7.1 0.0 collective-permute-done.refs_1_
  7.1 7.1 %collective-permute-done.1.refs_2_ = bf16[256,512]{1,0:T(8,128)(2,1)S(1)} collective-permute-done((bf16[256,512]{1,0:T(8,128)(2,1)S(1)}, bf16[256,512]{1,0:T(8,128)(2,1)S(1)}, u32[]{:S(2)}, u32[]{:S(2)}) %collective-permute-start.1) | collective-permute-done | bytes 262176 | tf_op jit(solution)/shard_map/ppermute | solution.py:346
  14.2 5.1 %collective-permute-done.2.refs_3_ = bf16[256,512]{1,0:T(8,128)(2,1)S(1)} collective-permute-done((bf16[256,512]{1,0:T(8,128)(2,1)S(1)}, bf16[256,512]{1,0:T(8,128)(2,1)S(1)}, u32[]{:S(2)}, u32[]{:S(2)}) %collective-permute-start.2) | collective-permute-done | bytes 262176 | tf_op jit(solution)/shard_map/ppermute | solution.py:346
  19.3 0.0 copy-start
  19.3 2.2 %copy-done = bf16[1024,2048]{1,0:T(8,128)(2,1)S(1)} copy-done((bf16[1024,2048]{1,0:T(8,128)(2,1)S(1)}, bf16[1024,2048]{1,0:T(8,128)(2,1)}, u32[]{:S(2)}) %copy-start) | copy-done | bytes 4194328
  21.5 2.8 %shard_map.57 = bf16[32,8,16,128]{3,2,1,0:T(8,128)(2,1)} custom-call(s32[1]{0:T(128)} %bitcast.4.me_ref, bf16[1024,2048]{1,0:T(8,128)(2,1)S(1)} %copy-done, bf16[256,512]{1,0:T(8,128)(2,1)S(1)} %get-tuple-element.9.refs_0_, bf16[256,512]{1,0:T(8,128)(2,1)S(1)} %collective-permute-done.refs_1_, bf16[256,512]{1,0:T(8,128)(2,1)S(1)} %collective-permute-done.1.refs_2_, ...), custom_call_target="tpu_custom_call" | custom-call | tf_op jit(solution)/shard_map/pallas_call | solution.py:144
  24.3 0.0 copy-start.2
  24.3 0.0 copy-start.3
  24.3 5.9 %all-to-all-start = ((bf16[32,8,16,128]{3,2,1,0:T(8,128)(2,1)}), bf16[32,8,16,128]{3,2,1,0:T(8,128)(2,1)S(1)}, u32[]{:S(2)}, u32[]{:S(2)}) async-start(bf16[32,8,16,128]{3,2,1,0:T(8,128)(2,1)} %shard_map.57), calls=%async_computation | async-start | bytes 2097152 | tf_op jit(solution)/shard_map/all_to_all | solution.py:349
  30.2 0.0 copy-done.2
  30.2 0.0 copy-done.3
  30.2 0.1 convert_element_type.21
  30.3 0.1 convert_element_type.23.offs_ref
  30.4 0.1 copy.7.slow_ref
  30.6 3.4 %shard_map.55.state_ref = f32[6,256,256]{2,1,0:T(8,128)S(1)} custom-call(f32[1]{0:T(128)} %bitcast.1.base_ref, f32[256,1]{1,0:T(8,128)S(1)} %copy.7.slow_ref, f32[1,256]{1,0:T(1,128)S(1)} %convert_element_type.23.offs_ref), custom_call_target="tpu_custom_call" | custom-call | flops 19660800 | bytes 1572864 | tf_op jit(solution)/shard_map/pallas_call | solution.py:184
  34.0 23.7 %all-to-all-done.data_ref = bf16[32,8,16,128]{3,2,1,0:T(8,128)(2,1)S(1)} async-done(((bf16[32,8,16,128]{3,2,1,0:T(8,128)(2,1)}), bf16[32,8,16,128]{3,2,1,0:T(8,128)(2,1)S(1)}, u32[]{:S(2)}, u32[]{:S(2)}) %all-to-all-start) | async-done | bytes 1048608 | tf_op jit(solution)/shard_map/all_to_all | solution.py:349
  57.8 5.5 %shard_map.58 = bf16[4096,128]{1,0:T(8,128)(2,1)S(1)} custom-call(s32[1]{0:T(128)} %bitcast.down_ref, f32[6,256,256]{2,1,0:T(8,128)S(1)} %shard_map.55.state_ref, bf16[32,8,16,128]{3,2,1,0:T(8,128)(2,1)S(1)} %all-to-all-done.data_ref), custom_call_target="tpu_custom_call" | custom-call | tf_op jit(solution)/shard_map/pallas_call | solution.py:289
  63.3 28.3 %all_to_all.10.in_ref = bf16[8,32,16,128]{3,2,1,0:T(8,128)(2,1)S(1)} all-to-all(bf16[8,32,16,128]{3,2,1,0:T(8,128)(2,1)S(1)} %bitcast.7), channel_id=1, replica_groups=mesh['freq'=4,'offset'=8] {'offset'}, dimensions={0} | all-to-all | bytes 2097152 | tf_op jit(solution)/shard_map/all_to_all | solution.py:360
  91.6 2.3 %shard_map.59 = f32[32,64,256]{2,1,0:T(8,128)} custom-call(bf16[8,32,16,128]{3,2,1,0:T(8,128)(2,1)S(1)} %all_to_all.10.in_ref), custom_call_target="tpu_custom_call" | custom-call | tf_op jit(solution)/shard_map/pallas_call | solution.py:318
  (3 shorter events, 0.0 us)
Async XLA Ops:
  0.7 1.2 %copy-start.1 = (bf16[1024,512]{1,0:T(8,128)(2,1)S(1)}, bf16[1024,512]{1,0:T(8,128)(2,1)}, u32[]{:S(2)}) copy-start(bf16[1024,512]{1,0:T(8,128)(2,1)} %raw_ref.1) | copy-start | bytes 3145732
  3.9 3.2 %collective-permute-start = (bf16[256,512]{1,0:T(8,128)(2,1)S(1)}, bf16[256,512]{1,0:T(8,128)(2,1)S(1)}, u32[]{:S(2)}, u32[]{:S(2)}) collective-permute-start(bf16[256,512]{1,0:T(8,128)(2,1)S(1)} %get-tuple-element.10), channel_id=1, source_target_pairs={{0,8},{8,0},{16,24},{24,16},{1,9},{9,1},{17,25},{25,17},{2,10},{10... | collective-permute-start | bytes 786440 | tf_op jit(solution)/shard_map/ppermute | solution.py:346
  4.4 9.8 %collective-permute-start.1 = (bf16[256,512]{1,0:T(8,128)(2,1)S(1)}, bf16[256,512]{1,0:T(8,128)(2,1)S(1)}, u32[]{:S(2)}, u32[]{:S(2)}) collective-permute-start(bf16[256,512]{1,0:T(8,128)(2,1)S(1)} %get-tuple-element.11), channel_id=1, source_target_pairs={{0,16},{8,24},{16,0},{24,8},{1,17},{9,25},{17,1},{25,9},{2,18},{10... | collective-permute-start | bytes 786440 | tf_op jit(solution)/shard_map/ppermute | solution.py:346
  7.0 12.3 %collective-permute-start.2 = (bf16[256,512]{1,0:T(8,128)(2,1)S(1)}, bf16[256,512]{1,0:T(8,128)(2,1)S(1)}, u32[]{:S(2)}, u32[]{:S(2)}) collective-permute-start(bf16[256,512]{1,0:T(8,128)(2,1)S(1)} %get-tuple-element.12), channel_id=1, source_target_pairs={{0,24},{8,16},{16,8},{24,0},{1,25},{9,17},{17,9},{25,1},{2,26},{10... | collective-permute-start | bytes 786440 | tf_op jit(solution)/shard_map/ppermute | solution.py:346
  19.3 2.2 %copy-start = (bf16[1024,2048]{1,0:T(8,128)(2,1)S(1)}, bf16[1024,2048]{1,0:T(8,128)(2,1)}, u32[]{:S(2)}) copy-start(bf16[1024,2048]{1,0:T(8,128)(2,1)} %constant.34.clone.table_ref) | copy-start | bytes 12582916
  24.3 5.9 %copy-start.2 = (s32[256]{0:T(256)S(1)}, s32[256]{0:T(256)}, u32[]{:S(2)}) copy-start(s32[256]{0:T(256)} %param.7) | copy-start | bytes 3076
  24.3 5.9 %copy-start.3 = (s32[256]{0:T(256)S(1)}, s32[256]{0:T(256)}, u32[]{:S(2)}) copy-start(s32[256]{0:T(256)} %param.8) | copy-start | bytes 3076
  24.3 33.5 %all-to-all-start = ((bf16[32,8,16,128]{3,2,1,0:T(8,128)(2,1)}), bf16[32,8,16,128]{3,2,1,0:T(8,128)(2,1)S(1)}, u32[]{:S(2)}, u32[]{:S(2)}) async-start(bf16[32,8,16,128]{3,2,1,0:T(8,128)(2,1)} %shard_map.57), calls=%async_computation | async-start | bytes 2097152 | tf_op jit(solution)/shard_map/all_to_all | solution.py:349

commit v8 on v6

--- a/solution.py
+++ b/solution.py
@@ -48,7 +48,7 @@
     lane = lax.broadcasted_iota(jnp.int32, (gathers, raw_ref.shape[0]), 1)
     for f in range(groups):
         picks = [
-            jnp.where(lane == slot_ref[:, h : h + 1], 1.0, 0.0).astype(jnp.bfloat16)
+            jnp.where(lane == slot_ref[:, h : h + 1].astype(jnp.int32), 1.0, 0.0).astype(jnp.bfloat16)
             for h in range(f * own_offsets, (f + 1) * own_offsets)
         ]
         out_ref[f] = jnp.dot(
@@ -210,25 +210,24 @@
     return jnp.where(column == source(row), 1.0, 0.0).astype(jnp.bfloat16)
 
 
-def radon_kernel(gathers, down_ref, state_ref, data_ref, out_ref, turns, plain, turned, held):
+TILE = 16
+
+
+def prepare(gathers, down, data_ref, plain, turned):
     devices, own_offsets, pairs, lanes = data_ref.shape
-    offsets = devices * own_offsets
-    slows = state_ref.shape[1]
-    tile = 16
-    size = tile * pairs
-    together = tile // own_offsets
-    down = down_ref[0]
+    size = TILE * pairs
+    together = TILE // own_offsets
 
     def received(r):
-        k = quotient(r, tile)
-        return remainder(r, tile) * pairs + k + down * (pairs - 1 - 2 * k)
+        k = quotient(r, TILE)
+        return remainder(r, TILE) * pairs + k + down * (pairs - 1 - 2 * k)
 
     swap = one_hot(size, size, received)
     for d in range(devices // together):
         block = data_ref[d * together : (d + 1) * together].reshape(size, lanes)
         if pairs > 1:
             block = jnp.dot(swap, block, preferred_element_type=jnp.float32).astype(jnp.bfloat16)
-        plain[:, d * tile : (d + 1) * tile] = block.reshape(pairs, tile, lanes)
+        plain[:, d * TILE : (d + 1) * TILE] = block.reshape(pairs, TILE, lanes)
     row = lax.broadcasted_iota(jnp.int32, (lanes, lanes), 0)
     column = lax.broadcasted_iota(jnp.int32, (lanes, lanes), 1)
     quarter = jnp.where(
@@ -241,12 +240,18 @@
             jnp.bfloat16
         )
 
+
+def sum_offsets(gathers, first, state_ref, plain, turned, turns, held):
+    pairs, slows, lanes = held.shape
+    offsets = plain.shape[1]
+
     def fill(t, carry):
-        own = pl.ds(pl.multiple_of(t * tile, tile), tile)
-        step_c = state_ref[4, own]
-        step_s = state_ref[5, own]
+        source = pl.ds(pl.multiple_of(first + t * TILE, TILE), TILE)
+        own = pl.ds(pl.multiple_of(t * TILE, TILE), TILE)
+        step_c = state_ref[4, source]
+        step_s = state_ref[5, source]
         twice = 2.0 * step_c
-        now = [state_ref[i, own] for i in range(4)]
+        now = [state_ref[i, source] for i in range(4)]
         past = [now[a] * step_c + now[2 + a] * step_s for a in range(2)]
         past += [now[2 + a] * step_c - now[a] * step_s for a in range(2)]
         for k in range(pairs):
@@ -255,8 +260,7 @@
                 now[i], past[i] = twice * now[i] - past[i], now[i]
         return carry
 
-    lax.fori_loop(0, slows // tile, fill, 0)
-
+    lax.fori_loop(0, slows // TILE, fill, 0)
     first_half = lax.broadcasted_iota(jnp.int32, (1, lanes), 1) < 2 * gathers
     for k in range(pairs):
         cosine = turns[k, :2].reshape(2 * slows, offsets)
@@ -266,12 +270,25 @@
         )
         held[k] = jnp.where(first_half, both[:slows], both[slows:]).astype(jnp.bfloat16)
 
-    swap = one_hot(size, size, lambda r: remainder(r, pairs) * tile + quotient(r, pairs))
-    for p in range(slows // tile):
-        block = held[:, p * tile : (p + 1) * tile].reshape(size, lanes)
+
+def deal(held, first, out_ref):
+    pairs, _, lanes = held.shape
+    size = TILE * pairs
+    swap = one_hot(size, size, lambda r: remainder(r, pairs) * TILE + quotient(r, pairs))
+    for p in range(out_ref.shape[0] // size):
+        start = first + p * TILE
+        if not isinstance(start, int):
+            start = pl.multiple_of(start, TILE)
+        block = held[:, pl.ds(start, TILE)].reshape(size, lanes)
         if pairs > 1:
             block = jnp.dot(swap, block, preferred_element_type=jnp.float32)
         out_ref[p * size : (p + 1) * size] = block.astype(out_ref.dtype)
+
+
+def radon_kernel(gathers, down_ref, state_ref, data_ref, out_ref, turns, plain, turned, held):
+    prepare(gathers, down_ref[0], data_ref, plain, turned)
+    sum_offsets(gathers, 0, state_ref, plain, turned, turns, held)
+    deal(held, 0, out_ref)
 
 
 def radon(down, state, data, gathers):
@@ -293,6 +310,116 @@
     )(down, state, data)
 
 
+def deal_half(held, me, first, out_refs):
+    half = len(out_refs)
+    each = held.shape[1] // half
+    for s, out_ref in enumerate(out_refs):
+        deal(held, remainder(me ^ (first + s), half) * each, out_ref)
+
+
+def far_kernel(gathers, half, place_ref, state_ref, data_ref, plain, turned, *refs):
+    *out_refs, turns, held = refs
+    me = place_ref[1]
+    prepare(gathers, place_ref[0], data_ref, plain, turned)
+    other = (1 - quotient(me, half)) * held.shape[1]
+    sum_offsets(gathers, other, state_ref, plain, turned, turns, held)
+    deal_half(held, me, half, out_refs)
+
+
+def near_kernel(gathers, half, place_ref, state_ref, plain, turned, *refs):
+    *out_refs, turns, held = refs
+    me = place_ref[1]
+    own = quotient(me, half) * held.shape[1]
+    sum_offsets(gathers, own, state_ref, plain, turned, turns, held)
+    deal_half(held, me, 0, out_refs)
+
+
+def radon_swapped(place, state, data, gathers, offset_devices):
+    _, count, offsets = state.shape
+    pairs, lanes = data.shape[2:]
+    half = offset_devices // 2
+    vmem = pl.BlockSpec(memory_space=pltpu.VMEM)
+    smem = pl.BlockSpec(memory_space=pltpu.SMEM)
+    block = jax.ShapeDtypeStruct((count // offset_devices * pairs, lanes), jnp.bfloat16)
+    spectra = jax.ShapeDtypeStruct((pairs, offsets, lanes), jnp.bfloat16)
+    scratch = [
+        pltpu.VMEM((pairs, 4, count // 2, offsets), jnp.bfloat16),
+        pltpu.VMEM((pairs, count // 2, lanes), jnp.bfloat16),
+    ]
+    cost = pl.CostEstimate(
+        flops=8 * count * offsets * pairs * lanes,
+        bytes_accessed=8 * count * offsets,
+        transcendentals=0,
+    )
+    plain, turned, *far = pl.pallas_call(
+        functools.partial(far_kernel, gathers, half),
+        in_specs=[smem, vmem, vmem],
+        out_specs=[vmem] * (2 + half),
+        out_shape=[spectra, spectra] + [block] * half,
+        scratch_shapes=scratch,
+        compiler_params=pltpu.CompilerParams(vmem_limit_bytes=20 * MIB),
+        cost_estimate=cost,
+    )(place, state, data)
+    near = pl.pallas_call(
+        functools.partial(near_kernel, gathers, half),
+        in_specs=[smem, vmem, vmem, vmem],
+        out_specs=[vmem] * half,
+        out_shape=[block] * half,
+        scratch_shapes=scratch,
+        compiler_params=pltpu.CompilerParams(vmem_limit_bytes=20 * MIB),
+        cost_estimate=cost,
+    )(place, state, plain, turned)
+    blocks = list(near) + list(far)
+    for s in reversed(range(1, offset_devices)):
+        swaps = [(o, o ^ s) for o in range(offset_devices)]
+        blocks[s] = lax.ppermute(blocks[s], "offset", swaps)
+    return blocks
+
+
+def join_kernel(scale, place_ref, *refs):
+    *parts, out_ref, wide, ready, sems = refs
+    groups, step, half_lanes, _ = ready.shape
+    rows = wide.shape[1]
+    pairs = rows // len(parts)
+    copies = []
+    for g in range(groups):
+        for s, part in enumerate(parts):
+            own = pl.ds(pl.multiple_of((place_ref[1] ^ s) * pairs, pairs), pairs)
+            for i in range(step):
+                p = g * step + i
+                wide[p, own] = part[p * pairs : (p + 1) * pairs].astype(jnp.float32) * scale
+        for i in range(step):
+            block = wide[g * step + i].T
+            ready[g, i, :, :rows] = block[:half_lanes]
+            ready[g, i, :, rows:] = block[half_lanes:]
+        copies.append(
+            pltpu.make_async_copy(ready.at[g], out_ref.at[pl.ds(g * step, step)], sems.at[g])
+        )
+        copies[-1].start()
+    for copy in copies:
+        copy.wait()
+
+
+def join(place, parts, slows, scale):
+    pairs = parts[0].shape[0] // slows
+    lanes = parts[0].shape[1]
+    rows = len(parts) * pairs
+    step = 4
+    vmem = pl.BlockSpec(memory_space=pltpu.VMEM)
+    return pl.pallas_call(
+        functools.partial(join_kernel, scale),
+        in_specs=[pl.BlockSpec(memory_space=pltpu.SMEM)] + [vmem] * len(parts),
+        out_specs=pl.BlockSpec(memory_space=pl.ANY),
+        out_shape=jax.ShapeDtypeStruct((slows, lanes // 2, 2 * rows), jnp.float32),
+        scratch_shapes=[
+            pltpu.VMEM((slows, rows, lanes), jnp.float32),
+            pltpu.VMEM((slows // step, step, lanes // 2, 2 * rows), jnp.float32),
+            pltpu.SemaphoreType.DMA((slows // step,)),
+        ],
+        compiler_params=pltpu.CompilerParams(vmem_limit_bytes=16 * MIB),
+    )(place, *parts)
+
+
 def finish_kernel(scale, in_ref, out_ref):
     devices, slows, pairs, lanes = in_ref.shape
     rows = devices * pairs
@@ -331,7 +458,7 @@
     pairs = own_freqs // halves
     own_offsets = local_offsets // freq_devices
 
-    picked = pick(trace_slot, raw_traces, freq_devices)
+    picked = pick(trace_slot.astype(jnp.float32), raw_traces, freq_devices)
     series = lax.all_to_all(picked, "freq", 0, 0, tiled=True)
     table = jnp.asarray(table_rows(total_time, freq_devices, offset_devices, halves, pairs))
     spectrum = transform(table, series, pairs, gathers)
@@ -343,11 +470,17 @@
     first = lax.axis_index("freq") * band + lax.axis_index("offset") * pairs
     base = (2 * first + 1).astype(jnp.float32) * (math.pi / total_time)
     state = moveout(base.reshape(1), slows, offs, band // halves, total_time)
-    down = (2 * lax.axis_index("freq") // freq_devices).astype(jnp.int32).reshape(1)
-    panel = radon(down, state, data, gathers)
-    panel = panel.reshape(offset_devices, NP // offset_devices, pairs, 2 * halves * gathers)
-    parts = lax.all_to_all(panel, "offset", 0, 0, tiled=True)
-    result = finish(parts, 1.0 / math.sqrt(offsets))
+    down = (2 * lax.axis_index("freq") // freq_devices).astype(jnp.int32)
+    place = jnp.stack([down, lax.axis_index("offset").astype(jnp.int32)])
+    slows_each = NP // offset_devices
+    scale = 1.0 / math.sqrt(offsets)
+    if slows_each % TILE == 0:
+        blocks = radon_swapped(place, state, data, gathers, offset_devices)
+        result = join(place, blocks, slows_each, scale)
+    else:
+        panel = radon(place, state, data, gathers)
+        panel = panel.reshape(offset_devices, slows_each, pairs, 2 * halves * gathers)
+        result = finish(lax.all_to_all(panel, "offset", 0, 0, tiled=True), scale)
     return jnp.transpose(result, (0, 2, 1))
 
 

time: 94.1 us -> 93.2 us (level)
  the two profiles are of different devices: /device:TPU:0 before, /device:TPU:8 now
where the time goes in v8:
time: 93.2 us; the launch traced here: 92.9 us
  waiting for transfers between devices  42.3 us (45%)
  blocking collectives  17.1 us (18%)
  Pallas kernels  16.8 us (18%)
  starting transfers between devices  14.2 us (15%)
  local copies, waits for them, and re-layouts  1.55 us (2%)
    all_to_all x1, waiting for transfers between devices, local(): data = lax.all_to_all(spectrum, ('freq', 'offset'), 0, 0, tiled=True)  22 us
    ppermute x7, waiting for transfers between devices, radon_swapped(): blocks[s] = lax.ppermute(blocks[s], 'offset', swaps)  20.3 us
    all_to_all x1, blocking collectives, local(): series = lax.all_to_all(picked, 'freq', 0, 0, tiled=True)  17.1 us
    ppermute x7, starting transfers between devices, radon_swapped(): blocks[s] = lax.ppermute(blocks[s], 'offset', swaps)  9.1 us
    all_to_all x1, starting transfers between devices, local(): data = lax.all_to_all(spectrum, ('freq', 'offset'), 0, 0, tiled=True)  5.09 us
    pallas_call x1, Pallas kernels, radon_swapped(): pl.pallas_call(functools.partial(far_kernel, gathers, half), in_specs=[sm...  3.98 us
    pallas_call x1, Pallas kernels, moveout(): pl.pallas_call(functools.partial(moveout_kernel, shift, total_time), grid...  3.43 us
    pallas_call x1, Pallas kernels, radon_swapped(): pl.pallas_call(functools.partial(near_kernel, gathers, half), in_specs=[s...  2.95 us
  transfers between devices with their start and end apart: 8, of which 6 were waited for; matrix products, arithmetic and copies ran while one was open for 0% of the time, Pallas kernels for 4%

profile of v8, /device:TPU:8, one launch (start us, length us, event | category | flops | bytes accessed | tf_op | source)
XLA Modules:
  0.0 92.9 jit_solution(3211620224611979627)
XLA Ops:
  0.0 0.7 convert_element_type.24.slot_ref
  0.7 0.0 copy-start.1
  0.7 1.2 %copy-done.1 = bf16[1024,512]{1,0:T(8,128)(2,1)S(1)} copy-done((bf16[1024,512]{1,0:T(8,128)(2,1)S(1)}, bf16[1024,512]{1,0:T(8,128)(2,1)}, u32[]{:S(2)}) %copy-start.1) | copy-done | bytes 1048600
  1.9 0.0 copy-start
  1.9 1.9 %shard_map.56 = bf16[4,256,512]{2,1,0:T(8,128)(2,1)S(1)} custom-call(f32[32,32]{1,0:T(8,128)S(1)} %convert_element_type.24.slot_ref, bf16[1024,512]{1,0:T(8,128)(2,1)S(1)} %copy-done.1), custom_call_target="tpu_custom_call" | custom-call | tf_op jit(solution)/shard_map/pallas_call | solution.py:63
  3.8 17.1 %all_to_all.10.series_ref = bf16[4,256,512]{2,1,0:T(8,128)(2,1)S(1)} all-to-all(bf16[4,256,512]{2,1,0:T(8,128)(2,1)S(1)} %shard_map.56), channel_id=1, replica_groups=mesh['freq'=4,'offset'=8] {'freq'}, dimensions={0} | all-to-all | bytes 2097152 | tf_op jit(solution)/shard_map/all_to_all | solution.py:462
  20.9 0.0 copy-done
  20.9 2.5 %shard_map.57 = bf16[32,8,16,128]{3,2,1,0:T(8,128)(2,1)} custom-call(bf16[1024,2048]{1,0:T(8,128)(2,1)S(1)} %copy-done, bf16[4,256,512]{2,1,0:T(8,128)(2,1)S(1)} %all_to_all.10.series_ref), custom_call_target="tpu_custom_call" | custom-call | tf_op jit(solution)/shard_map/pallas_call | solution.py:136
  23.4 0.0 copy-start.2
  23.4 0.0 copy-start.3
  23.4 5.1 %all-to-all-start.1 = ((bf16[32,8,16,128]{3,2,1,0:T(8,128)(2,1)}), bf16[32,8,16,128]{3,2,1,0:T(8,128)(2,1)S(1)}, u32[]{:S(2)}, u32[]{:S(2)}) async-start(bf16[32,8,16,128]{3,2,1,0:T(8,128)(2,1)} %shard_map.57), calls=%async_computation.1 | async-start | bytes 2097152 | tf_op jit(solution)/shard_map/all_to_all | solution.py:465
  28.5 0.0 copy-done.2
  28.5 0.0 copy-done.3
  28.5 0.1 convert_element_type.21
  28.6 0.1 convert_element_type.23.offs_ref
  28.7 0.1 copy.7.slow_ref
  28.9 3.4 %shard_map.55.state_ref = f32[6,256,256]{2,1,0:T(8,128)S(1)} custom-call(f32[1]{0:T(128)} %bitcast.2.base_ref, f32[256,1]{1,0:T(8,128)S(1)} %copy.7.slow_ref, f32[1,256]{1,0:T(1,128)S(1)} %convert_element_type.23.offs_ref), custom_call_target="tpu_custom_call" | custom-call | flops 19660800 | bytes 1572864 | tf_op jit(solution)/shard_map/pallas_call | solution.py:176
  32.3 0.1 pad_add_fusion.place_ref
  32.4 22.0 %all-to-all-done.1.data_ref = bf16[32,8,16,128]{3,2,1,0:T(8,128)(2,1)S(1)} async-done(((bf16[32,8,16,128]{3,2,1,0:T(8,128)(2,1)}), bf16[32,8,16,128]{3,2,1,0:T(8,128)(2,1)S(1)}, u32[]{:S(2)}, u32[]{:S(2)}) %all-to-all-start.1) | async-done | bytes 1048608 | tf_op jit(solution)/shard_map/all_to_all | solution.py:465
  54.4 4.0 %shard_map.58 = (bf16[16,256,128]{2,1,0:T(8,128)(2,1)S(1)}, bf16[16,256,128]{2,1,0:T(8,128)(2,1)S(1)}, bf16[512,128]{1,0:T(8,128)(2,1)S(1)}, bf16[512,128]{1,0:T...) custom-call(s32[2]{0:T(128)S(1)} %pad_add_fusion.place_ref, ...), custom_call_target="tpu_custom_call" | custom-call | flops 1073741824 | bytes 524288 | tf_op jit(solution)/shard_map/pallas_call | solution.py:354
  58.4 2.9 %shard_map.59 = (bf16[512,128]{1,0:T(8,128)(2,1)S(1)}, bf16[512,128]{1,0:T(8,128)(2,1)S(1)}, bf16[512,128]{1,0:T(8,128)(2,1)S(1)}, bf16[512,128]{1,0:T(8,128)(2,1)S(1)}) custom-call(s32[2]{0:T(128)S(1)} %pad_add_fusion.place_ref, f32[6,256,256]{2,1,0:T(8,128)S(1)} %shard_map.55.state_ref, bf16[16,256,128]{2,1,0:T(8,128)(2,1)S(1)} %get-tuple-element.15.plain, ...), custom_call_target="tpu_custom_call" | custom-call | flops 1073741824 | bytes 524288 | tf_op jit(solution)/shard_map/pallas_call | solution.py:363
  61.3 0.1 collective-permute-start
  61.4 2.6 %collective-permute-start.1 = (bf16[512,128]{1,0:T(8,128)(2,1)S(1)}, bf16[512,128]{1,0:T(8,128)(2,1)S(1)}, u32[]{:S(2)}, u32[]{:S(2)}) collective-permute-start(bf16[512,128]{1,0:T(8,128)(2,1)S(1)} %get-tuple-element.19), channel_id=1, source_target_pairs={{0,2},{1,3},{2,0},{3,1},{4,6},{5,7},{6,4},{7,5},{8,10},{9,11},{10,... | collective-permute-start | bytes 393224 | tf_op jit(solution)/shard_map/ppermute | solution.py:375
  64.0 0.9 collective-permute-start.2
  64.9 1.5 %collective-permute-start.3 = (bf16[512,128]{1,0:T(8,128)(2,1)S(1)}, bf16[512,128]{1,0:T(8,128)(2,1)S(1)}, u32[]{:S(2)}, u32[]{:S(2)}) collective-permute-start(bf16[512,128]{1,0:T(8,128)(2,1)S(1)} %get-tuple-element.21), channel_id=1, source_target_pairs={{0,4},{1,5},{2,6},{3,7},{4,0},{5,1},{6,2},{7,3},{8,12},{9,13},{10,... | collective-permute-start | bytes 393224 | tf_op jit(solution)/shard_map/ppermute | solution.py:375
  66.4 1.4 %collective-permute-start.4 = (bf16[512,128]{1,0:T(8,128)(2,1)S(1)}, bf16[512,128]{1,0:T(8,128)(2,1)S(1)}, u32[]{:S(2)}, u32[]{:S(2)}) collective-permute-start(bf16[512,128]{1,0:T(8,128)(2,1)S(1)} %get-tuple-element.22), channel_id=1, source_target_pairs={{0,5},{1,4},{2,7},{3,6},{4,1},{5,0},{6,3},{7,2},{8,13},{9,12},{10,... | collective-permute-start | bytes 393224 | tf_op jit(solution)/shard_map/ppermute | solution.py:375
  67.8 0.0 collective-permute-done.refs_1_
  67.8 0.6 collective-permute-start.5
  68.4 1.8 %collective-permute-done.1.refs_2_ = bf16[512,128]{1,0:T(8,128)(2,1)S(1)} collective-permute-done((bf16[512,128]{1,0:T(8,128)(2,1)S(1)}, bf16[512,128]{1,0:T(8,128)(2,1)S(1)}, u32[]{:S(2)}, u32[]{:S(2)}) %collective-permute-start.1) | collective-permute-done | bytes 131104 | tf_op jit(solution)/shard_map/ppermute | solution.py:375
  70.2 2.1 %collective-permute-start.6 = (bf16[512,128]{1,0:T(8,128)(2,1)S(1)}, bf16[512,128]{1,0:T(8,128)(2,1)S(1)}, u32[]{:S(2)}, u32[]{:S(2)}) collective-permute-start(bf16[512,128]{1,0:T(8,128)(2,1)S(1)} %get-tuple-element.24), channel_id=1, source_target_pairs={{0,7},{1,6},{2,5},{3,4},{4,3},{5,2},{6,1},{7,0},{8,15},{9,14},{10,... | collective-permute-start | bytes 393224 | tf_op jit(solution)/shard_map/ppermute | solution.py:375
  72.2 0.0 collective-permute-done.2.refs_3_
  72.2 9.3 %collective-permute-done.3.refs_4_ = bf16[512,128]{1,0:T(8,128)(2,1)S(1)} collective-permute-done((bf16[512,128]{1,0:T(8,128)(2,1)S(1)}, bf16[512,128]{1,0:T(8,128)(2,1)S(1)}, u32[]{:S(2)}, u32[]{:S(2)}) %collective-permute-start.3) | collective-permute-done | bytes 131104 | tf_op jit(solution)/shard_map/ppermute | solution.py:375
  81.5 2.8 %collective-permute-done.4.refs_5_ = bf16[512,128]{1,0:T(8,128)(2,1)S(1)} collective-permute-done((bf16[512,128]{1,0:T(8,128)(2,1)S(1)}, bf16[512,128]{1,0:T(8,128)(2,1)S(1)}, u32[]{:S(2)}, u32[]{:S(2)}) %collective-permute-start.4) | collective-permute-done | bytes 131104 | tf_op jit(solution)/shard_map/ppermute | solution.py:375
  84.3 4.4 %collective-permute-done.5.refs_6_ = bf16[512,128]{1,0:T(8,128)(2,1)S(1)} collective-permute-done((bf16[512,128]{1,0:T(8,128)(2,1)S(1)}, bf16[512,128]{1,0:T(8,128)(2,1)S(1)}, u32[]{:S(2)}, u32[]{:S(2)}) %collective-permute-start.5) | collective-permute-done | bytes 131104 | tf_op jit(solution)/shard_map/ppermute | solution.py:375
  88.8 2.0 %collective-permute-done.6.refs_7_ = bf16[512,128]{1,0:T(8,128)(2,1)S(1)} collective-permute-done((bf16[512,128]{1,0:T(8,128)(2,1)S(1)}, bf16[512,128]{1,0:T(8,128)(2,1)S(1)}, u32[]{:S(2)}, u32[]{:S(2)}) %collective-permute-start.6) | collective-permute-done | bytes 131104 | tf_op jit(solution)/shard_map/ppermute | solution.py:375
  90.8 2.1 %shard_map.60 = f32[32,64,256]{2,1,0:T(8,128)} custom-call(s32[2]{0:T(128)S(1)} %pad_add_fusion.place_ref, bf16[512,128]{1,0:T(8,128)(2,1)S(1)} %get-tuple-element.17.refs_0_, bf16[512,128]{1,0:T(8,128)(2,1)S(1)} %collective-permute-done.refs_1_, bf16[512,128]{1,0:T(8,128)(2,1)S(1)} %collective-permute-done.1.refs_2_, ...), custom_call_target="tpu_custom_call" | custom-call | tf_op jit(solution)/shard_map/pallas_call | solution.py:409
  (3 shorter events, 0.0 us)
Async XLA Ops:
  0.7 1.2 %copy-start.1 = (bf16[1024,512]{1,0:T(8,128)(2,1)S(1)}, bf16[1024,512]{1,0:T(8,128)(2,1)}, u32[]{:S(2)}) copy-start(bf16[1024,512]{1,0:T(8,128)(2,1)} %raw_ref.1) | copy-start | bytes 3145732
  1.9 19.0 %copy-start = (bf16[1024,2048]{1,0:T(8,128)(2,1)S(1)}, bf16[1024,2048]{1,0:T(8,128)(2,1)}, u32[]{:S(2)}) copy-start(bf16[1024,2048]{1,0:T(8,128)(2,1)} %constant.34.clone.table_ref) | copy-start | bytes 12582916
  23.4 5.1 %copy-start.2 = (s32[256]{0:T(256)S(1)}, s32[256]{0:T(256)}, u32[]{:S(2)}) copy-start(s32[256]{0:T(256)} %param.7) | copy-start | bytes 3076
  23.4 5.1 %copy-start.3 = (s32[256]{0:T(256)S(1)}, s32[256]{0:T(256)}, u32[]{:S(2)}) copy-start(s32[256]{0:T(256)} %param.8) | copy-start | bytes 3076
  23.4 31.0 %all-to-all-start.1 = ((bf16[32,8,16,128]{3,2,1,0:T(8,128)(2,1)}), bf16[32,8,16,128]{3,2,1,0:T(8,128)(2,1)S(1)}, u32[]{:S(2)}, u32[]{:S(2)}) async-start(bf16[32,8,16,128]{3,2,1,0:T(8,128)(2,1)} %shard_map.57), calls=%async_computation.1 | async-start | bytes 2097152 | tf_op jit(solution)/shard_map/all_to_all | solution.py:465
  61.3 6.5 %collective-permute-start = (bf16[512,128]{1,0:T(8,128)(2,1)S(1)}, bf16[512,128]{1,0:T(8,128)(2,1)S(1)}, u32[]{:S(2)}, u32[]{:S(2)}) collective-permute-start(bf16[512,128]{1,0:T(8,128)(2,1)S(1)} %get-tuple-element.18), channel_id=1, source_target_pairs={{0,1},{1,0},{2,3},{3,2},{4,5},{5,4},{6,7},{7,6},{8,9},{9,8},{10,11... | collective-permute-start | bytes 393224 | tf_op jit(solution)/shard_map/ppermute | solution.py:375
  61.4 8.8 %collective-permute-start.1 = (bf16[512,128]{1,0:T(8,128)(2,1)S(1)}, bf16[512,128]{1,0:T(8,128)(2,1)S(1)}, u32[]{:S(2)}, u32[]{:S(2)}) collective-permute-start(bf16[512,128]{1,0:T(8,128)(2,1)S(1)} %get-tuple-element.19), channel_id=1, source_target_pairs={{0,2},{1,3},{2,0},{3,1},{4,6},{5,7},{6,4},{7,5},{8,10},{9,11},{10,... | collective-permute-start | bytes 393224 | tf_op jit(solution)/shard_map/ppermute | solution.py:375
  64.0 8.2 %collective-permute-start.2 = (bf16[512,128]{1,0:T(8,128)(2,1)S(1)}, bf16[512,128]{1,0:T(8,128)(2,1)S(1)}, u32[]{:S(2)}, u32[]{:S(2)}) collective-permute-start(bf16[512,128]{1,0:T(8,128)(2,1)S(1)} %get-tuple-element.20), channel_id=1, source_target_pairs={{0,3},{1,2},{2,1},{3,0},{4,7},{5,6},{6,5},{7,4},{8,11},{9,10},{10,... | collective-permute-start | bytes 393224 | tf_op jit(solution)/shard_map/ppermute | solution.py:375
  64.9 16.6 %collective-permute-start.3 = (bf16[512,128]{1,0:T(8,128)(2,1)S(1)}, bf16[512,128]{1,0:T(8,128)(2,1)S(1)}, u32[]{:S(2)}, u32[]{:S(2)}) collective-permute-start(bf16[512,128]{1,0:T(8,128)(2,1)S(1)} %get-tuple-element.21), channel_id=1, source_target_pairs={{0,4},{1,5},{2,6},{3,7},{4,0},{5,1},{6,2},{7,3},{8,12},{9,13},{10,... | collective-permute-start | bytes 393224 | tf_op jit(solution)/shard_map/ppermute | solution.py:375
  66.4 17.9 %collective-permute-start.4 = (bf16[512,128]{1,0:T(8,128)(2,1)S(1)}, bf16[512,128]{1,0:T(8,128)(2,1)S(1)}, u32[]{:S(2)}, u32[]{:S(2)}) collective-permute-start(bf16[512,128]{1,0:T(8,128)(2,1)S(1)} %get-tuple-element.22), channel_id=1, source_target_pairs={{0,5},{1,4},{2,7},{3,6},{4,1},{5,0},{6,3},{7,2},{8,13},{9,12},{10,... | collective-permute-start | bytes 393224 | tf_op jit(solution)/shard_map/ppermute | solution.py:375
  67.8 20.9 %collective-permute-start.5 = (bf16[512,128]{1,0:T(8,128)(2,1)S(1)}, bf16[512,128]{1,0:T(8,128)(2,1)S(1)}, u32[]{:S(2)}, u32[]{:S(2)}) collective-permute-start(bf16[512,128]{1,0:T(8,128)(2,1)S(1)} %get-tuple-element.23), channel_id=1, source_target_pairs={{0,6},{1,7},{2,4},{3,5},{4,2},{5,3},{6,0},{7,1},{8,14},{9,15},{10,... | collective-permute-start | bytes 393224 | tf_op jit(solution)/shard_map/ppermute | solution.py:375
  70.2 20.6 %collective-permute-start.6 = (bf16[512,128]{1,0:T(8,128)(2,1)S(1)}, bf16[512,128]{1,0:T(8,128)(2,1)S(1)}, u32[]{:S(2)}, u32[]{:S(2)}) collective-permute-start(bf16[512,128]{1,0:T(8,128)(2,1)S(1)} %get-tuple-element.24), channel_id=1, source_target_pairs={{0,7},{1,6},{2,5},{3,4},{4,3},{5,2},{6,1},{7,0},{8,15},{9,14},{10,... | collective-permute-start | bytes 393224 | tf_op jit(solution)/shard_map/ppermute | solution.py:375

commit v9 on v8

--- a/solution.py
+++ b/solution.py
@@ -369,21 +369,22 @@
         compiler_params=pltpu.CompilerParams(vmem_limit_bytes=20 * MIB),
         cost_estimate=cost,
     )(place, state, plain, turned)
-    blocks = list(near) + list(far)
-    for s in reversed(range(1, offset_devices)):
+    order = list(range(half, offset_devices)) + list(range(half))
+    blocks = []
+    for s, part in zip(order, list(far) + list(near)):
         swaps = [(o, o ^ s) for o in range(offset_devices)]
-        blocks[s] = lax.ppermute(blocks[s], "offset", swaps)
-    return blocks
-
-
-def join_kernel(scale, place_ref, *refs):
+        blocks.append(lax.ppermute(part, "offset", swaps) if s else part)
+    return order, blocks
+
+
+def join_kernel(scale, order, place_ref, *refs):
     *parts, out_ref, wide, ready, sems = refs
     groups, step, half_lanes, _ = ready.shape
     rows = wide.shape[1]
     pairs = rows // len(parts)
     copies = []
     for g in range(groups):
-        for s, part in enumerate(parts):
+        for s, part in zip(order, parts):
             own = pl.ds(pl.multiple_of((place_ref[1] ^ s) * pairs, pairs), pairs)
             for i in range(step):
                 p = g * step + i
@@ -400,14 +401,14 @@
         copy.wait()
 
 
-def join(place, parts, slows, scale):
+def join(place, order, parts, slows, scale):
     pairs = parts[0].shape[0] // slows
     lanes = parts[0].shape[1]
     rows = len(parts) * pairs
     step = 4
     vmem = pl.BlockSpec(memory_space=pltpu.VMEM)
     return pl.pallas_call(
-        functools.partial(join_kernel, scale),
+        functools.partial(join_kernel, scale, order),
         in_specs=[pl.BlockSpec(memory_space=pltpu.SMEM)] + [vmem] * len(parts),
         out_specs=pl.BlockSpec(memory_space=pl.ANY),
         out_shape=jax.ShapeDtypeStruct((slows, lanes // 2, 2 * rows), jnp.float32),
@@ -475,8 +476,8 @@
     slows_each = NP // offset_devices
     scale = 1.0 / math.sqrt(offsets)
     if slows_each % TILE == 0:
-        blocks = radon_swapped(place, state, data, gathers, offset_devices)
-        result = join(place, blocks, slows_each, scale)
+        order, blocks = radon_swapped(place, state, data, gathers, offset_devices)
+        result = join(place, order, blocks, slows_each, scale)
     else:
         panel = radon(place, state, data, gathers)
         panel = panel.reshape(offset_devices, slows_each, pairs, 2 * halves * gathers)

time: 93.2 us -> 89 us (0.955)
  the two profiles are of different devices: /device:TPU:8 before, /device:TPU:0 now
where the time goes in v9:
time: 89 us; the launch traced here: 88.7 us
  waiting for transfers between devices  37.4 us (42%)
  blocking collectives  18.5 us (21%)
  Pallas kernels  16.8 us (19%)
  starting transfers between devices  13.5 us (15%)
  local copies, waits for them, and re-layouts  1.55 us (2%)
    all_to_all x1, waiting for transfers between devices, local(): data = lax.all_to_all(spectrum, ('freq', 'offset'), 0, 0, tiled=True)  23.6 us
    all_to_all x1, blocking collectives, local(): series = lax.all_to_all(picked, 'freq', 0, 0, tiled=True)  18.5 us
    ppermute x7, waiting for transfers between devices, radon_swapped(): blocks.append(lax.ppermute(part, 'offset', swaps) if s else part)  13.7 us
    ppermute x7, starting transfers between devices, radon_swapped(): blocks.append(lax.ppermute(part, 'offset', swaps) if s else part)  8.58 us
    all_to_all x1, starting transfers between devices, local(): data = lax.all_to_all(spectrum, ('freq', 'offset'), 0, 0, tiled=True)  4.9 us
    pallas_call x1, Pallas kernels, radon_swapped(): pl.pallas_call(functools.partial(far_kernel, gathers, half), in_specs=[sm...  3.97 us
    pallas_call x1, Pallas kernels, moveout(): pl.pallas_call(functools.partial(moveout_kernel, shift, total_time), grid...  3.43 us
    pallas_call x1, Pallas kernels, radon_swapped(): pl.pallas_call(functools.partial(near_kernel, gathers, half), in_specs=[s...  2.95 us
  transfers between devices with their start and end apart: 8, of which 5 were waited for; matrix products, arithmetic and copies ran while one was open for 0% of the time, Pallas kernels for 7%

profile of v9, /device:TPU:0, one launch (start us, length us, event | category | flops | bytes accessed | tf_op | source)
XLA Modules:
  0.0 88.7 jit_solution(7417487219438820219)
XLA Ops:
  0.0 0.7 convert_element_type.24.slot_ref
  0.7 0.0 copy-start.1
  0.7 1.2 %copy-done.1 = bf16[1024,512]{1,0:T(8,128)(2,1)S(1)} copy-done((bf16[1024,512]{1,0:T(8,128)(2,1)S(1)}, bf16[1024,512]{1,0:T(8,128)(2,1)}, u32[]{:S(2)}) %copy-start.1) | copy-done | bytes 1048600
  1.9 0.0 copy-start
  1.9 1.9 %shard_map.56 = bf16[4,256,512]{2,1,0:T(8,128)(2,1)S(1)} custom-call(f32[32,32]{1,0:T(8,128)S(1)} %convert_element_type.24.slot_ref, bf16[1024,512]{1,0:T(8,128)(2,1)S(1)} %copy-done.1), custom_call_target="tpu_custom_call" | custom-call | tf_op jit(solution)/shard_map/pallas_call | solution.py:63
  3.8 18.5 %all_to_all.10.series_ref = bf16[4,256,512]{2,1,0:T(8,128)(2,1)S(1)} all-to-all(bf16[4,256,512]{2,1,0:T(8,128)(2,1)S(1)} %shard_map.56), channel_id=1, replica_groups=mesh['freq'=4,'offset'=8] {'freq'}, dimensions={0} | all-to-all | bytes 2097152 | tf_op jit(solution)/shard_map/all_to_all | solution.py:463
  22.3 0.0 copy-done
  22.3 2.5 %shard_map.57 = bf16[32,8,16,128]{3,2,1,0:T(8,128)(2,1)} custom-call(bf16[1024,2048]{1,0:T(8,128)(2,1)S(1)} %copy-done, bf16[4,256,512]{2,1,0:T(8,128)(2,1)S(1)} %all_to_all.10.series_ref), custom_call_target="tpu_custom_call" | custom-call | tf_op jit(solution)/shard_map/pallas_call | solution.py:136
  24.8 0.0 copy-start.2
  24.8 0.0 copy-start.3
  24.8 4.9 %all-to-all-start.1 = ((bf16[32,8,16,128]{3,2,1,0:T(8,128)(2,1)}), bf16[32,8,16,128]{3,2,1,0:T(8,128)(2,1)S(1)}, u32[]{:S(2)}, u32[]{:S(2)}) async-start(bf16[32,8,16,128]{3,2,1,0:T(8,128)(2,1)} %shard_map.57), calls=%async_computation.1 | async-start | bytes 2097152 | tf_op jit(solution)/shard_map/all_to_all | solution.py:466
  29.7 0.0 copy-done.2
  29.8 0.0 copy-done.3
  29.8 0.1 convert_element_type.21
  29.9 0.1 convert_element_type.23.offs_ref
  30.0 0.1 copy.7.slow_ref
  30.1 3.4 %shard_map.55.state_ref = f32[6,256,256]{2,1,0:T(8,128)S(1)} custom-call(f32[1]{0:T(128)} %bitcast.2.base_ref, f32[256,1]{1,0:T(8,128)S(1)} %copy.7.slow_ref, f32[1,256]{1,0:T(1,128)S(1)} %convert_element_type.23.offs_ref), custom_call_target="tpu_custom_call" | custom-call | flops 19660800 | bytes 1572864 | tf_op jit(solution)/shard_map/pallas_call | solution.py:176
  33.6 0.1 pad_add_fusion.place_ref
  33.7 23.6 %all-to-all-done.1.data_ref = bf16[32,8,16,128]{3,2,1,0:T(8,128)(2,1)S(1)} async-done(((bf16[32,8,16,128]{3,2,1,0:T(8,128)(2,1)}), bf16[32,8,16,128]{3,2,1,0:T(8,128)(2,1)S(1)}, u32[]{:S(2)}, u32[]{:S(2)}) %all-to-all-start.1) | async-done | bytes 1048608 | tf_op jit(solution)/shard_map/all_to_all | solution.py:466
  57.3 4.0 %shard_map.58 = (bf16[16,256,128]{2,1,0:T(8,128)(2,1)S(1)}, bf16[16,256,128]{2,1,0:T(8,128)(2,1)S(1)}, bf16[512,128]{1,0:T(8,128)(2,1)S(1)}, bf16[512,128]{1,0:T...) custom-call(s32[2]{0:T(128)S(1)} %pad_add_fusion.place_ref, ...), custom_call_target="tpu_custom_call" | custom-call | flops 1073741824 | bytes 524288 | tf_op jit(solution)/shard_map/pallas_call | solution.py:354
  61.3 0.1 collective-permute-start
  61.4 3.0 %collective-permute-start.1 = (bf16[512,128]{1,0:T(8,128)(2,1)S(1)}, bf16[512,128]{1,0:T(8,128)(2,1)S(1)}, u32[]{:S(2)}, u32[]{:S(2)}) collective-permute-start(bf16[512,128]{1,0:T(8,128)(2,1)S(1)} %get-tuple-element.16), channel_id=1, source_target_pairs={{0,5},{1,4},{2,7},{3,6},{4,1},{5,0},{6,3},{7,2},{8,13},{9,12},{10,... | collective-permute-start | bytes 393224 | tf_op jit(solution)/shard_map/ppermute | solution.py:376
  64.4 1.3 %collective-permute-start.2 = (bf16[512,128]{1,0:T(8,128)(2,1)S(1)}, bf16[512,128]{1,0:T(8,128)(2,1)S(1)}, u32[]{:S(2)}, u32[]{:S(2)}) collective-permute-start(bf16[512,128]{1,0:T(8,128)(2,1)S(1)} %get-tuple-element.17), channel_id=1, source_target_pairs={{0,6},{1,7},{2,4},{3,5},{4,2},{5,3},{6,0},{7,1},{8,14},{9,15},{10,... | collective-permute-start | bytes 393224 | tf_op jit(solution)/shard_map/ppermute | solution.py:376
  65.7 3.3 %collective-permute-start.3 = (bf16[512,128]{1,0:T(8,128)(2,1)S(1)}, bf16[512,128]{1,0:T(8,128)(2,1)S(1)}, u32[]{:S(2)}, u32[]{:S(2)}) collective-permute-start(bf16[512,128]{1,0:T(8,128)(2,1)S(1)} %get-tuple-element.18), channel_id=1, source_target_pairs={{0,7},{1,6},{2,5},{3,4},{4,3},{5,2},{6,1},{7,0},{8,15},{9,14},{10,... | collective-permute-start | bytes 393224 | tf_op jit(solution)/shard_map/ppermute | solution.py:376
  69.0 2.9 %shard_map.59 = (bf16[512,128]{1,0:T(8,128)(2,1)S(1)}, bf16[512,128]{1,0:T(8,128)(2,1)S(1)}, bf16[512,128]{1,0:T(8,128)(2,1)S(1)}, bf16[512,128]{1,0:T(8,128)(2,1)S(1)}) custom-call(s32[2]{0:T(128)S(1)} %pad_add_fusion.place_ref, f32[6,256,256]{2,1,0:T(8,128)S(1)} %shard_map.55.state_ref, bf16[16,256,128]{2,1,0:T(8,128)(2,1)S(1)} %get-tuple-element.19.plain, ...), custom_call_target="tpu_custom_call" | custom-call | flops 1073741824 | bytes 524288 | tf_op jit(solution)/shard_map/pallas_call | solution.py:363
  72.0 0.7 collective-permute-start.4
  72.7 6.3 %collective-permute-done.refs_0_ = bf16[512,128]{1,0:T(8,128)(2,1)S(1)} collective-permute-done((bf16[512,128]{1,0:T(8,128)(2,1)S(1)}, bf16[512,128]{1,0:T(8,128)(2,1)S(1)}, u32[]{:S(2)}, u32[]{:S(2)}) %collective-permute-start) | collective-permute-done | bytes 131104 | tf_op jit(solution)/shard_map/ppermute | solution.py:376
  79.1 0.0 collective-permute-start.5
  79.1 1.3 %collective-permute-done.1.refs_1_ = bf16[512,128]{1,0:T(8,128)(2,1)S(1)} collective-permute-done((bf16[512,128]{1,0:T(8,128)(2,1)S(1)}, bf16[512,128]{1,0:T(8,128)(2,1)S(1)}, u32[]{:S(2)}, u32[]{:S(2)}) %collective-permute-start.1) | collective-permute-done | bytes 131104 | tf_op jit(solution)/shard_map/ppermute | solution.py:376
  80.4 0.1 collective-permute-start.6
  80.5 0.0 collective-permute-done.2.refs_2_
  80.5 0.0 collective-permute-done.3.refs_3_
  80.5 0.0 collective-permute-done.4.refs_5_
  80.5 3.7 %collective-permute-done.5.refs_6_ = bf16[512,128]{1,0:T(8,128)(2,1)S(1)} collective-permute-done((bf16[512,128]{1,0:T(8,128)(2,1)S(1)}, bf16[512,128]{1,0:T(8,128)(2,1)S(1)}, u32[]{:S(2)}, u32[]{:S(2)}) %collective-permute-start.5) | collective-permute-done | bytes 131104 | tf_op jit(solution)/shard_map/ppermute | solution.py:376
  84.2 2.3 %collective-permute-done.6.refs_7_ = bf16[512,128]{1,0:T(8,128)(2,1)S(1)} collective-permute-done((bf16[512,128]{1,0:T(8,128)(2,1)S(1)}, bf16[512,128]{1,0:T(8,128)(2,1)S(1)}, u32[]{:S(2)}, u32[]{:S(2)}) %collective-permute-start.6) | collective-permute-done | bytes 131104 | tf_op jit(solution)/shard_map/ppermute | solution.py:376
  86.6 2.1 %shard_map.60 = f32[32,64,256]{2,1,0:T(8,128)} custom-call(s32[2]{0:T(128)S(1)} %pad_add_fusion.place_ref, bf16[512,128]{1,0:T(8,128)(2,1)S(1)} %collective-permute-done.refs_0_, bf16[512,128]{1,0:T(8,128)(2,1)S(1)} %collective-permute-done.1.refs_1_, bf16[512,128]{1,0:T(8,128)(2,1)S(1)} %collective-permute-done.2.refs_2_, ...), custom_call_target="tpu_custom_call" | custom-call | tf_op jit(solution)/shard_map/pallas_call | solution.py:410
  (3 shorter events, 0.0 us)
Async XLA Ops:
  0.7 1.2 %copy-start.1 = (bf16[1024,512]{1,0:T(8,128)(2,1)S(1)}, bf16[1024,512]{1,0:T(8,128)(2,1)}, u32[]{:S(2)}) copy-start(bf16[1024,512]{1,0:T(8,128)(2,1)} %raw_ref.1) | copy-start | bytes 3145732
  1.9 20.4 %copy-start = (bf16[1024,2048]{1,0:T(8,128)(2,1)S(1)}, bf16[1024,2048]{1,0:T(8,128)(2,1)}, u32[]{:S(2)}) copy-start(bf16[1024,2048]{1,0:T(8,128)(2,1)} %constant.34.clone.table_ref) | copy-start | bytes 12582916
  24.8 4.9 %copy-start.2 = (s32[256]{0:T(256)S(1)}, s32[256]{0:T(256)}, u32[]{:S(2)}) copy-start(s32[256]{0:T(256)} %param.7) | copy-start | bytes 3076
  24.8 4.9 %copy-start.3 = (s32[256]{0:T(256)S(1)}, s32[256]{0:T(256)}, u32[]{:S(2)}) copy-start(s32[256]{0:T(256)} %param.8) | copy-start | bytes 3076
  24.8 32.5 %all-to-all-start.1 = ((bf16[32,8,16,128]{3,2,1,0:T(8,128)(2,1)}), bf16[32,8,16,128]{3,2,1,0:T(8,128)(2,1)S(1)}, u32[]{:S(2)}, u32[]{:S(2)}) async-start(bf16[32,8,16,128]{3,2,1,0:T(8,128)(2,1)} %shard_map.57), calls=%async_computation.1 | async-start | bytes 2097152 | tf_op jit(solution)/shard_map/all_to_all | solution.py:466
  61.3 17.8 %collective-permute-start = (bf16[512,128]{1,0:T(8,128)(2,1)S(1)}, bf16[512,128]{1,0:T(8,128)(2,1)S(1)}, u32[]{:S(2)}, u32[]{:S(2)}) collective-permute-start(bf16[512,128]{1,0:T(8,128)(2,1)S(1)} %get-tuple-element.15), channel_id=1, source_target_pairs={{0,4},{1,5},{2,6},{3,7},{4,0},{5,1},{6,2},{7,3},{8,12},{9,13},{10,... | collective-permute-start | bytes 393224 | tf_op jit(solution)/shard_map/ppermute | solution.py:376
  61.4 19.0 %collective-permute-start.1 = (bf16[512,128]{1,0:T(8,128)(2,1)S(1)}, bf16[512,128]{1,0:T(8,128)(2,1)S(1)}, u32[]{:S(2)}, u32[]{:S(2)}) collective-permute-start(bf16[512,128]{1,0:T(8,128)(2,1)S(1)} %get-tuple-element.16), channel_id=1, source_target_pairs={{0,5},{1,4},{2,7},{3,6},{4,1},{5,0},{6,3},{7,2},{8,13},{9,12},{10,... | collective-permute-start | bytes 393224 | tf_op jit(solution)/shard_map/ppermute | solution.py:376
  64.4 16.1 %collective-permute-start.2 = (bf16[512,128]{1,0:T(8,128)(2,1)S(1)}, bf16[512,128]{1,0:T(8,128)(2,1)S(1)}, u32[]{:S(2)}, u32[]{:S(2)}) collective-permute-start(bf16[512,128]{1,0:T(8,128)(2,1)S(1)} %get-tuple-element.17), channel_id=1, source_target_pairs={{0,6},{1,7},{2,4},{3,5},{4,2},{5,3},{6,0},{7,1},{8,14},{9,15},{10,... | collective-permute-start | bytes 393224 | tf_op jit(solution)/shard_map/ppermute | solution.py:376
  65.7 14.8 %collective-permute-start.3 = (bf16[512,128]{1,0:T(8,128)(2,1)S(1)}, bf16[512,128]{1,0:T(8,128)(2,1)S(1)}, u32[]{:S(2)}, u32[]{:S(2)}) collective-permute-start(bf16[512,128]{1,0:T(8,128)(2,1)S(1)} %get-tuple-element.18), channel_id=1, source_target_pairs={{0,7},{1,6},{2,5},{3,4},{4,3},{5,2},{6,1},{7,0},{8,15},{9,14},{10,... | collective-permute-start | bytes 393224 | tf_op jit(solution)/shard_map/ppermute | solution.py:376
  72.0 8.6 %collective-permute-start.4 = (bf16[512,128]{1,0:T(8,128)(2,1)S(1)}, bf16[512,128]{1,0:T(8,128)(2,1)S(1)}, u32[]{:S(2)}, u32[]{:S(2)}) collective-permute-start(bf16[512,128]{1,0:T(8,128)(2,1)S(1)} %get-tuple-element.22), channel_id=1, source_target_pairs={{0,1},{1,0},{2,3},{3,2},{4,5},{5,4},{6,7},{7,6},{8,9},{9,8},{10,11... | collective-permute-start | bytes 393224 | tf_op jit(solution)/shard_map/ppermute | solution.py:376
  79.1 5.2 %collective-permute-start.5 = (bf16[512,128]{1,0:T(8,128)(2,1)S(1)}, bf16[512,128]{1,0:T(8,128)(2,1)S(1)}, u32[]{:S(2)}, u32[]{:S(2)}) collective-permute-start(bf16[512,128]{1,0:T(8,128)(2,1)S(1)} %get-tuple-element.23), channel_id=1, source_target_pairs={{0,2},{1,3},{2,0},{3,1},{4,6},{5,7},{6,4},{7,5},{8,10},{9,11},{10,... | collective-permute-start | bytes 393224 | tf_op jit(solution)/shard_map/ppermute | solution.py:376
  80.4 6.2 %collective-permute-start.6 = (bf16[512,128]{1,0:T(8,128)(2,1)S(1)}, bf16[512,128]{1,0:T(8,128)(2,1)S(1)}, u32[]{:S(2)}, u32[]{:S(2)}) collective-permute-start(bf16[512,128]{1,0:T(8,128)(2,1)S(1)} %get-tuple-element.24), channel_id=1, source_target_pairs={{0,3},{1,2},{2,1},{3,0},{4,7},{5,6},{6,5},{7,4},{8,11},{9,10},{10,... | collective-permute-start | bytes 393224 | tf_op jit(solution)/shard_map/ppermute | solution.py:376

commit v10 on v8

--- a/solution.py
+++ b/solution.py
@@ -310,28 +310,21 @@
     )(down, state, data)
 
 
-def deal_half(held, me, first, out_refs):
-    half = len(out_refs)
-    each = held.shape[1] // half
-    for s, out_ref in enumerate(out_refs):
-        deal(held, remainder(me ^ (first + s), half) * each, out_ref)
-
-
 def far_kernel(gathers, half, place_ref, state_ref, data_ref, plain, turned, *refs):
     *out_refs, turns, held = refs
     me = place_ref[1]
     prepare(gathers, place_ref[0], data_ref, plain, turned)
     other = (1 - quotient(me, half)) * held.shape[1]
     sum_offsets(gathers, other, state_ref, plain, turned, turns, held)
-    deal_half(held, me, half, out_refs)
-
-
-def near_kernel(gathers, half, place_ref, state_ref, plain, turned, *refs):
-    *out_refs, turns, held = refs
-    me = place_ref[1]
-    own = quotient(me, half) * held.shape[1]
+    for s, out_ref in enumerate(out_refs):
+        deal(held, remainder(me ^ s, half) * (held.shape[1] // half), out_ref)
+
+
+def near_kernel(gathers, half, place_ref, state_ref, plain, turned, out_ref, turns, held):
+    own = quotient(place_ref[1], half) * held.shape[1]
     sum_offsets(gathers, own, state_ref, plain, turned, turns, held)
-    deal_half(held, me, 0, out_refs)
+    for b in range(half):
+        deal(held, b * (held.shape[1] // half), out_ref.at[b])
 
 
 def radon_swapped(place, state, data, gathers, offset_devices):
@@ -363,28 +356,34 @@
     near = pl.pallas_call(
         functools.partial(near_kernel, gathers, half),
         in_specs=[smem, vmem, vmem, vmem],
-        out_specs=[vmem] * half,
-        out_shape=[block] * half,
+        out_specs=vmem,
+        out_shape=jax.ShapeDtypeStruct((half,) + block.shape, block.dtype),
         scratch_shapes=scratch,
         compiler_params=pltpu.CompilerParams(vmem_limit_bytes=20 * MIB),
         cost_estimate=cost,
     )(place, state, plain, turned)
-    blocks = list(near) + list(far)
-    for s in reversed(range(1, offset_devices)):
-        swaps = [(o, o ^ s) for o in range(offset_devices)]
-        blocks[s] = lax.ppermute(blocks[s], "offset", swaps)
+    blocks = []
+    for s, part in enumerate(far):
+        swaps = [(o, o ^ (half + s)) for o in range(offset_devices)]
+        blocks.append(lax.ppermute(part, "offset", swaps))
+    sides = [list(range(half)), list(range(half, offset_devices))]
+    blocks.append(lax.all_to_all(near, "offset", 0, 0, axis_index_groups=sides, tiled=True))
     return blocks
 
 
 def join_kernel(scale, place_ref, *refs):
-    *parts, out_ref, wide, ready, sems = refs
+    *far, near, out_ref, wide, ready, sems = refs
+    half = len(far)
+    me = place_ref[1]
+    parts = [(me ^ (half + s), part) for s, part in enumerate(far)]
+    parts += [(quotient(me, half) * half + b, near.at[b]) for b in range(half)]
     groups, step, half_lanes, _ = ready.shape
     rows = wide.shape[1]
     pairs = rows // len(parts)
     copies = []
     for g in range(groups):
-        for s, part in enumerate(parts):
-            own = pl.ds(pl.multiple_of((place_ref[1] ^ s) * pairs, pairs), pairs)
+        for source, part in parts:
+            own = pl.ds(pl.multiple_of(source * pairs, pairs), pairs)
             for i in range(step):
                 p = g * step + i
                 wide[p, own] = part[p * pairs : (p + 1) * pairs].astype(jnp.float32) * scale
@@ -403,7 +402,7 @@
 def join(place, parts, slows, scale):
     pairs = parts[0].shape[0] // slows
     lanes = parts[0].shape[1]
-    rows = len(parts) * pairs
+    rows = 2 * (len(parts) - 1) * pairs
     step = 4
     vmem = pl.BlockSpec(memory_space=pltpu.VMEM)
     return pl.pallas_call(

time: 93.2 us -> 95.4 us (1.024)
  starting transfers between devices: 14.2 us -> 16.3 us
    all_to_all x0 -> x1, starting transfers between devices: none -> 5.36 us  [radon_swapped(): lax.all_to_all(near, 'offset', 0, 0, axis_index_groups=sides, tiled=True)]
    ppermute x7 -> x4, starting transfers between devices: 9.1 us -> 5.85 us  [radon_swapped(): blocks.append(lax.ppermute(part, 'offset', swaps))]
    ppermute x7 -> x4, waiting for transfers between devices: 20.3 us -> 19.5 us  [radon_swapped(): blocks.append(lax.ppermute(part, 'offset', swaps))]
  transfers between devices with their start and end apart: 8 -> 6, of which waited for: 6 -> 5; matrix products, arithmetic and copies ran while one was open for 0% -> 0% of each run, Pallas kernels for 4% -> 4%
where the time goes in v10:
time: 95.4 us; the launch traced here: 95 us
  waiting for transfers between devices  41.5 us (44%)
  Pallas kernels  17.6 us (18%)
  blocking collectives  17.1 us (18%)
  starting transfers between devices  16.3 us (17%)
  local copies, waits for them, and re-layouts  1.55 us (2%)
    all_to_all x1, waiting for transfers between devices, local(): data = lax.all_to_all(spectrum, ('freq', 'offset'), 0, 0, tiled=True)  22 us
    ppermute x4, waiting for transfers between devices, radon_swapped(): blocks.append(lax.ppermute(part, 'offset', swaps))  19.5 us
    all_to_all x1, blocking collectives, local(): series = lax.all_to_all(picked, 'freq', 0, 0, tiled=True)  17.1 us
    ppermute x4, starting transfers between devices, radon_swapped(): blocks.append(lax.ppermute(part, 'offset', swaps))  5.85 us
    all_to_all x1, starting transfers between devices, radon_swapped(): lax.all_to_all(near, 'offset', 0, 0, axis_index_groups=sides, tiled=True)  5.36 us
    all_to_all x1, starting transfers between devices, local(): data = lax.all_to_all(spectrum, ('freq', 'offset'), 0, 0, tiled=True)  5.09 us
    pallas_call x1, Pallas kernels, radon_swapped(): pl.pallas_call(functools.partial(far_kernel, gathers, half), in_specs=[sm...  3.99 us
    pallas_call x1, Pallas kernels, radon_swapped(): pl.pallas_call(functools.partial(near_kernel, gathers, half), in_specs=[s...  3.73 us
  transfers between devices with their start and end apart: 6, of which 5 were waited for; matrix products, arithmetic and copies ran while one was open for 0% of the time, Pallas kernels for 4%

profile of v10, /device:TPU:8, one launch (start us, length us, event | category | flops | bytes accessed | tf_op | source)
XLA Modules:
  0.0 95.0 jit_solution(6911322919438072445)
XLA Ops:
  0.0 0.7 convert_element_type.24.slot_ref
  0.7 0.0 copy-start.1
  0.7 1.2 %copy-done.1 = bf16[1024,512]{1,0:T(8,128)(2,1)S(1)} copy-done((bf16[1024,512]{1,0:T(8,128)(2,1)S(1)}, bf16[1024,512]{1,0:T(8,128)(2,1)}, u32[]{:S(2)}) %copy-start.1) | copy-done | bytes 1048600
  1.9 0.0 copy-start
  1.9 1.9 %shard_map.56 = bf16[4,256,512]{2,1,0:T(8,128)(2,1)S(1)} custom-call(f32[32,32]{1,0:T(8,128)S(1)} %convert_element_type.24.slot_ref, bf16[1024,512]{1,0:T(8,128)(2,1)S(1)} %copy-done.1), custom_call_target="tpu_custom_call" | custom-call | tf_op jit(solution)/shard_map/pallas_call | solution.py:63
  3.8 17.1 %all_to_all.15.series_ref = bf16[4,256,512]{2,1,0:T(8,128)(2,1)S(1)} all-to-all(bf16[4,256,512]{2,1,0:T(8,128)(2,1)S(1)} %shard_map.56), channel_id=1, replica_groups=mesh['freq'=4,'offset'=8] {'freq'}, dimensions={0} | all-to-all | bytes 2097152 | tf_op jit(solution)/shard_map/all_to_all | solution.py:461
  20.9 0.0 copy-done
  20.9 2.5 %shard_map.57 = bf16[32,8,16,128]{3,2,1,0:T(8,128)(2,1)} custom-call(bf16[1024,2048]{1,0:T(8,128)(2,1)S(1)} %copy-done, bf16[4,256,512]{2,1,0:T(8,128)(2,1)S(1)} %all_to_all.15.series_ref), custom_call_target="tpu_custom_call" | custom-call | tf_op jit(solution)/shard_map/pallas_call | solution.py:136
  23.4 0.0 copy-start.2
  23.4 0.0 copy-start.3
  23.4 5.1 %all-to-all-start.1 = ((bf16[32,8,16,128]{3,2,1,0:T(8,128)(2,1)}), bf16[32,8,16,128]{3,2,1,0:T(8,128)(2,1)S(1)}, u32[]{:S(2)}, u32[]{:S(2)}) async-start(bf16[32,8,16,128]{3,2,1,0:T(8,128)(2,1)} %shard_map.57), calls=%async_computation.1 | async-start | bytes 2097152 | tf_op jit(solution)/shard_map/all_to_all | solution.py:464
  28.5 0.0 copy-done.2
  28.5 0.0 copy-done.3
  28.5 0.1 convert_element_type.21
  28.6 0.1 convert_element_type.23.offs_ref
  28.7 0.1 copy.7.slow_ref
  28.9 3.4 %shard_map.55.state_ref = f32[6,256,256]{2,1,0:T(8,128)S(1)} custom-call(f32[1]{0:T(128)} %bitcast.2.base_ref, f32[256,1]{1,0:T(8,128)S(1)} %copy.7.slow_ref, f32[1,256]{1,0:T(1,128)S(1)} %convert_element_type.23.offs_ref), custom_call_target="tpu_custom_call" | custom-call | flops 19660800 | bytes 1572864 | tf_op jit(solution)/shard_map/pallas_call | solution.py:176
  32.3 0.1 pad_add_fusion.place_ref
  32.4 22.0 %all-to-all-done.1.data_ref = bf16[32,8,16,128]{3,2,1,0:T(8,128)(2,1)S(1)} async-done(((bf16[32,8,16,128]{3,2,1,0:T(8,128)(2,1)}), bf16[32,8,16,128]{3,2,1,0:T(8,128)(2,1)S(1)}, u32[]{:S(2)}, u32[]{:S(2)}) %all-to-all-start.1) | async-done | bytes 1048608 | tf_op jit(solution)/shard_map/all_to_all | solution.py:464
  54.4 4.0 %shard_map.58 = (bf16[16,256,128]{2,1,0:T(8,128)(2,1)S(1)}, bf16[16,256,128]{2,1,0:T(8,128)(2,1)S(1)}, bf16[512,128]{1,0:T(8,128)(2,1)S(1)}, bf16[512,128]{1,0:T...) custom-call(s32[2]{0:T(128)S(1)} %pad_add_fusion.place_ref, ...), custom_call_target="tpu_custom_call" | custom-call | flops 1073741824 | bytes 524288 | tf_op jit(solution)/shard_map/pallas_call | solution.py:347
  58.4 3.7 %shard_map.59 = bf16[4,512,128]{2,1,0:T(8,128)(2,1)} custom-call(s32[2]{0:T(128)S(1)} %pad_add_fusion.place_ref, f32[6,256,256]{2,1,0:T(8,128)S(1)} %shard_map.55.state_ref, bf16[16,256,128]{2,1,0:T(8,128)(2,1)S(1)} %get-tuple-element.15.plain, bf16[16,256,128]{2,1,0:T(8,128)(2,1)S(1)} %get-tuple-element.16.turned), custom_call_target="tpu_custom_call" | custom-call | flops 1073741824 | bytes 524288 | tf_op jit(solution)/shard_map/pallas_call | solution.py:356
  62.1 5.4 %all-to-all-start.2 = ((bf16[4,512,128]{2,1,0:T(8,128)(2,1)}), bf16[4,512,128]{2,1,0:T(8,128)(2,1)S(1)}, u32[]{:S(2)}, u32[]{:S(2)}) async-start(bf16[4,512,128]{2,1,0:T(8,128)(2,1)} %shard_map.59), calls=%async_computation.2 | async-start | bytes 1048576 | tf_op jit(solution)/shard_map/all_to_all | solution.py:370
  67.5 0.0 collective-permute-start
  67.5 3.8 %collective-permute-start.1 = (bf16[512,128]{1,0:T(8,128)(2,1)S(1)}, bf16[512,128]{1,0:T(8,128)(2,1)S(1)}, u32[]{:S(2)}, u32[]{:S(2)}) collective-permute-start(bf16[512,128]{1,0:T(8,128)(2,1)S(1)} %get-tuple-element.12), channel_id=1, source_target_pairs={{0,5},{1,4},{2,7},{3,6},{4,1},{5,0},{6,3},{7,2},{8,13},{9,12},{10,... | collective-permute-start | bytes 393224 | tf_op jit(solution)/shard_map/ppermute | solution.py:368
  71.3 0.0 collective-permute-start.2
  71.3 2.0 %collective-permute-start.3 = (bf16[512,128]{1,0:T(8,128)(2,1)S(1)}, bf16[512,128]{1,0:T(8,128)(2,1)S(1)}, u32[]{:S(2)}, u32[]{:S(2)}) collective-permute-start(bf16[512,128]{1,0:T(8,128)(2,1)S(1)} %get-tuple-element.14), channel_id=1, source_target_pairs={{0,7},{1,6},{2,5},{3,4},{4,3},{5,2},{6,1},{7,0},{8,15},{9,14},{10,... | collective-permute-start | bytes 393224 | tf_op jit(solution)/shard_map/ppermute | solution.py:368
  73.3 4.2 %collective-permute-done.refs_0_ = bf16[512,128]{1,0:T(8,128)(2,1)S(1)} collective-permute-done((bf16[512,128]{1,0:T(8,128)(2,1)S(1)}, bf16[512,128]{1,0:T(8,128)(2,1)S(1)}, u32[]{:S(2)}, u32[]{:S(2)}) %collective-permute-start) | collective-permute-done | bytes 131104 | tf_op jit(solution)/shard_map/ppermute | solution.py:368
  77.6 8.6 %collective-permute-done.1.refs_1_ = bf16[512,128]{1,0:T(8,128)(2,1)S(1)} collective-permute-done((bf16[512,128]{1,0:T(8,128)(2,1)S(1)}, bf16[512,128]{1,0:T(8,128)(2,1)S(1)}, u32[]{:S(2)}, u32[]{:S(2)}) %collective-permute-start.1) | collective-permute-done | bytes 131104 | tf_op jit(solution)/shard_map/ppermute | solution.py:368
  86.2 4.1 %collective-permute-done.2.refs_2_ = bf16[512,128]{1,0:T(8,128)(2,1)S(1)} collective-permute-done((bf16[512,128]{1,0:T(8,128)(2,1)S(1)}, bf16[512,128]{1,0:T(8,128)(2,1)S(1)}, u32[]{:S(2)}, u32[]{:S(2)}) %collective-permute-start.2) | collective-permute-done | bytes 131104 | tf_op jit(solution)/shard_map/ppermute | solution.py:368
  90.3 2.6 %collective-permute-done.3.refs_3_ = bf16[512,128]{1,0:T(8,128)(2,1)S(1)} collective-permute-done((bf16[512,128]{1,0:T(8,128)(2,1)S(1)}, bf16[512,128]{1,0:T(8,128)(2,1)S(1)}, u32[]{:S(2)}, u32[]{:S(2)}) %collective-permute-start.3) | collective-permute-done | bytes 131104 | tf_op jit(solution)/shard_map/ppermute | solution.py:368
  92.9 0.0 all-to-all-done.2.refs_4_
  92.9 2.1 %shard_map.60 = f32[32,64,256]{2,1,0:T(8,128)} custom-call(s32[2]{0:T(128)S(1)} %pad_add_fusion.place_ref, bf16[512,128]{1,0:T(8,128)(2,1)S(1)} %collective-permute-done.refs_0_, bf16[512,128]{1,0:T(8,128)(2,1)S(1)} %collective-permute-done.1.refs_1_, bf16[512,128]{1,0:T(8,128)(2,1)S(1)} %collective-permute-done.2.refs_2_, ...), custom_call_target="tpu_custom_call" | custom-call | tf_op jit(solution)/shard_map/pallas_call | solution.py:408
  (3 shorter events, 0.0 us)
Async XLA Ops:
  0.7 1.2 %copy-start.1 = (bf16[1024,512]{1,0:T(8,128)(2,1)S(1)}, bf16[1024,512]{1,0:T(8,128)(2,1)}, u32[]{:S(2)}) copy-start(bf16[1024,512]{1,0:T(8,128)(2,1)} %raw_ref.1) | copy-start | bytes 3145732
  1.9 19.0 %copy-start = (bf16[1024,2048]{1,0:T(8,128)(2,1)S(1)}, bf16[1024,2048]{1,0:T(8,128)(2,1)}, u32[]{:S(2)}) copy-start(bf16[1024,2048]{1,0:T(8,128)(2,1)} %constant.34.clone.table_ref) | copy-start | bytes 12582916
  23.4 5.1 %copy-start.2 = (s32[256]{0:T(256)S(1)}, s32[256]{0:T(256)}, u32[]{:S(2)}) copy-start(s32[256]{0:T(256)} %param.7) | copy-start | bytes 3076
  23.4 5.1 %copy-start.3 = (s32[256]{0:T(256)S(1)}, s32[256]{0:T(256)}, u32[]{:S(2)}) copy-start(s32[256]{0:T(256)} %param.8) | copy-start | bytes 3076
  23.4 31.0 %all-to-all-start.1 = ((bf16[32,8,16,128]{3,2,1,0:T(8,128)(2,1)}), bf16[32,8,16,128]{3,2,1,0:T(8,128)(2,1)S(1)}, u32[]{:S(2)}, u32[]{:S(2)}) async-start(bf16[32,8,16,128]{3,2,1,0:T(8,128)(2,1)} %shard_map.57), calls=%async_computation.1 | async-start | bytes 2097152 | tf_op jit(solution)/shard_map/all_to_all | solution.py:464
  62.1 30.8 %all-to-all-start.2 = ((bf16[4,512,128]{2,1,0:T(8,128)(2,1)}), bf16[4,512,128]{2,1,0:T(8,128)(2,1)S(1)}, u32[]{:S(2)}, u32[]{:S(2)}) async-start(bf16[4,512,128]{2,1,0:T(8,128)(2,1)} %shard_map.59), calls=%async_computation.2 | async-start | bytes 1048576 | tf_op jit(solution)/shard_map/all_to_all | solution.py:370
  67.5 10.1 %collective-permute-start = (bf16[512,128]{1,0:T(8,128)(2,1)S(1)}, bf16[512,128]{1,0:T(8,128)(2,1)S(1)}, u32[]{:S(2)}, u32[]{:S(2)}) collective-permute-start(bf16[512,128]{1,0:T(8,128)(2,1)S(1)} %get-tuple-element.11), channel_id=1, source_target_pairs={{0,4},{1,5},{2,6},{3,7},{4,0},{5,1},{6,2},{7,3},{8,12},{9,13},{10,... | collective-permute-start | bytes 393224 | tf_op jit(solution)/shard_map/ppermute | solution.py:368
  67.5 18.7 %collective-permute-start.1 = (bf16[512,128]{1,0:T(8,128)(2,1)S(1)}, bf16[512,128]{1,0:T(8,128)(2,1)S(1)}, u32[]{:S(2)}, u32[]{:S(2)}) collective-permute-start(bf16[512,128]{1,0:T(8,128)(2,1)S(1)} %get-tuple-element.12), channel_id=1, source_target_pairs={{0,5},{1,4},{2,7},{3,6},{4,1},{5,0},{6,3},{7,2},{8,13},{9,12},{10,... | collective-permute-start | bytes 393224 | tf_op jit(solution)/shard_map/ppermute | solution.py:368
  71.3 19.0 %collective-permute-start.2 = (bf16[512,128]{1,0:T(8,128)(2,1)S(1)}, bf16[512,128]{1,0:T(8,128)(2,1)S(1)}, u32[]{:S(2)}, u32[]{:S(2)}) collective-permute-start(bf16[512,128]{1,0:T(8,128)(2,1)S(1)} %get-tuple-element.13), channel_id=1, source_target_pairs={{0,6},{1,7},{2,4},{3,5},{4,2},{5,3},{6,0},{7,1},{8,14},{9,15},{10,... | collective-permute-start | bytes 393224 | tf_op jit(solution)/shard_map/ppermute | solution.py:368
  71.3 21.6 %collective-permute-start.3 = (bf16[512,128]{1,0:T(8,128)(2,1)S(1)}, bf16[512,128]{1,0:T(8,128)(2,1)S(1)}, u32[]{:S(2)}, u32[]{:S(2)}) collective-permute-start(bf16[512,128]{1,0:T(8,128)(2,1)S(1)} %get-tuple-element.14), channel_id=1, source_target_pairs={{0,7},{1,6},{2,5},{3,4},{4,3},{5,2},{6,1},{7,0},{8,15},{9,14},{10,... | collective-permute-start | bytes 393224 | tf_op jit(solution)/shard_map/ppermute | solution.py:368

commit v11 on v9

--- a/solution.py
+++ b/solution.py
@@ -369,9 +369,12 @@
         compiler_params=pltpu.CompilerParams(vmem_limit_bytes=20 * MIB),
         cost_estimate=cost,
     )(place, state, plain, turned)
-    order = list(range(half, offset_devices)) + list(range(half))
+    crossing = list(range(half, offset_devices))
+    order = crossing[:-1] + list(range(2, half)) + crossing[-1:] + list(range(min(2, half)))[::-1]
+    parts = list(near) + list(far)
     blocks = []
-    for s, part in zip(order, list(far) + list(near)):
+    for s in order:
+        part = parts[s]
         swaps = [(o, o ^ s) for o in range(offset_devices)]
         blocks.append(lax.ppermute(part, "offset", swaps) if s else part)
     return order, blocks

time: 89 us -> 89.3 us (level)
  starting transfers between devices: 13.5 us -> 15.3 us
  waiting for transfers between devices: 37.4 us -> 35.9 us
    ppermute x7, starting transfers between devices: 8.58 us -> 10.4 us  [radon_swapped(): blocks.append(lax.ppermute(part, 'offset', swaps) if s else part)]
    ppermute x7, waiting for transfers between devices: 13.7 us -> 12.2 us  [radon_swapped(): blocks.append(lax.ppermute(part, 'offset', swaps) if s else part)]
  transfers between devices with their start and end apart: 8 -> 8, of which waited for: 5 -> 6; matrix products, arithmetic and copies ran while one was open for 0% -> 0% of each run, Pallas kernels for 7% -> 7%
where the time goes in v11:
time: 89.3 us; the launch traced here: 89 us
  waiting for transfers between devices  35.9 us (40%)
  blocking collectives  18.5 us (21%)
  Pallas kernels  16.8 us (19%)
  starting transfers between devices  15.3 us (17%)
  local copies, waits for them, and re-layouts  1.55 us (2%)
    all_to_all x1, waiting for transfers between devices, local(): data = lax.all_to_all(spectrum, ('freq', 'offset'), 0, 0, tiled=True)  23.6 us
    all_to_all x1, blocking collectives, local(): series = lax.all_to_all(picked, 'freq', 0, 0, tiled=True)  18.5 us
    ppermute x7, waiting for transfers between devices, radon_swapped(): blocks.append(lax.ppermute(part, 'offset', swaps) if s else part)  12.2 us
    ppermute x7, starting transfers between devices, radon_swapped(): blocks.append(lax.ppermute(part, 'offset', swaps) if s else part)  10.4 us
    all_to_all x1, starting transfers between devices, local(): data = lax.all_to_all(spectrum, ('freq', 'offset'), 0, 0, tiled=True)  4.9 us
    pallas_call x1, Pallas kernels, radon_swapped(): pl.pallas_call(functools.partial(far_kernel, gathers, half), in_specs=[sm...  3.97 us
    pallas_call x1, Pallas kernels, moveout(): pl.pallas_call(functools.partial(moveout_kernel, shift, total_time), grid...  3.43 us
    pallas_call x1, Pallas kernels, radon_swapped(): pl.pallas_call(functools.partial(near_kernel, gathers, half), in_specs=[s...  2.95 us
  transfers between devices with their start and end apart: 8, of which 6 were waited for; matrix products, arithmetic and copies ran while one was open for 0% of the time, Pallas kernels for 7%

profile of v11, /device:TPU:0, one launch (start us, length us, event | category | flops | bytes accessed | tf_op | source)
XLA Modules:
  0.0 89.0 jit_solution(5398719559992658734)
XLA Ops:
  0.0 0.7 convert_element_type.24.slot_ref
  0.7 0.0 copy-start.1
  0.7 1.2 %copy-done.1 = bf16[1024,512]{1,0:T(8,128)(2,1)S(1)} copy-done((bf16[1024,512]{1,0:T(8,128)(2,1)S(1)}, bf16[1024,512]{1,0:T(8,128)(2,1)}, u32[]{:S(2)}) %copy-start.1) | copy-done | bytes 1048600
  1.9 0.0 copy-start
  1.9 1.9 %shard_map.56 = bf16[4,256,512]{2,1,0:T(8,128)(2,1)S(1)} custom-call(f32[32,32]{1,0:T(8,128)S(1)} %convert_element_type.24.slot_ref, bf16[1024,512]{1,0:T(8,128)(2,1)S(1)} %copy-done.1), custom_call_target="tpu_custom_call" | custom-call | tf_op jit(solution)/shard_map/pallas_call | solution.py:63
  3.8 18.5 %all_to_all.10.series_ref = bf16[4,256,512]{2,1,0:T(8,128)(2,1)S(1)} all-to-all(bf16[4,256,512]{2,1,0:T(8,128)(2,1)S(1)} %shard_map.56), channel_id=1, replica_groups=mesh['freq'=4,'offset'=8] {'freq'}, dimensions={0} | all-to-all | bytes 2097152 | tf_op jit(solution)/shard_map/all_to_all | solution.py:466
  22.3 0.0 copy-done
  22.3 2.5 %shard_map.57 = bf16[32,8,16,128]{3,2,1,0:T(8,128)(2,1)} custom-call(bf16[1024,2048]{1,0:T(8,128)(2,1)S(1)} %copy-done, bf16[4,256,512]{2,1,0:T(8,128)(2,1)S(1)} %all_to_all.10.series_ref), custom_call_target="tpu_custom_call" | custom-call | tf_op jit(solution)/shard_map/pallas_call | solution.py:136
  24.8 0.0 copy-start.2
  24.8 0.0 copy-start.3
  24.8 4.9 %all-to-all-start.1 = ((bf16[32,8,16,128]{3,2,1,0:T(8,128)(2,1)}), bf16[32,8,16,128]{3,2,1,0:T(8,128)(2,1)S(1)}, u32[]{:S(2)}, u32[]{:S(2)}) async-start(bf16[32,8,16,128]{3,2,1,0:T(8,128)(2,1)} %shard_map.57), calls=%async_computation.1 | async-start | bytes 2097152 | tf_op jit(solution)/shard_map/all_to_all | solution.py:469
  29.7 0.0 copy-done.2
  29.8 0.0 copy-done.3
  29.8 0.1 convert_element_type.21
  29.9 0.1 convert_element_type.23.offs_ref
  30.0 0.1 copy.7.slow_ref
  30.1 3.4 %shard_map.55.state_ref = f32[6,256,256]{2,1,0:T(8,128)S(1)} custom-call(f32[1]{0:T(128)} %bitcast.2.base_ref, f32[256,1]{1,0:T(8,128)S(1)} %copy.7.slow_ref, f32[1,256]{1,0:T(1,128)S(1)} %convert_element_type.23.offs_ref), custom_call_target="tpu_custom_call" | custom-call | flops 19660800 | bytes 1572864 | tf_op jit(solution)/shard_map/pallas_call | solution.py:176
  33.6 0.1 pad_add_fusion.place_ref
  33.7 23.6 %all-to-all-done.1.data_ref = bf16[32,8,16,128]{3,2,1,0:T(8,128)(2,1)S(1)} async-done(((bf16[32,8,16,128]{3,2,1,0:T(8,128)(2,1)}), bf16[32,8,16,128]{3,2,1,0:T(8,128)(2,1)S(1)}, u32[]{:S(2)}, u32[]{:S(2)}) %all-to-all-start.1) | async-done | bytes 1048608 | tf_op jit(solution)/shard_map/all_to_all | solution.py:469
  57.3 4.0 %shard_map.58 = (bf16[16,256,128]{2,1,0:T(8,128)(2,1)S(1)}, bf16[16,256,128]{2,1,0:T(8,128)(2,1)S(1)}, bf16[512,128]{1,0:T(8,128)(2,1)S(1)}, bf16[512,128]{1,0:T...) custom-call(s32[2]{0:T(128)S(1)} %pad_add_fusion.place_ref, ...), custom_call_target="tpu_custom_call" | custom-call | flops 1073741824 | bytes 524288 | tf_op jit(solution)/shard_map/pallas_call | solution.py:354
  61.3 0.1 collective-permute-start
  61.4 3.0 %collective-permute-start.1 = (bf16[512,128]{1,0:T(8,128)(2,1)S(1)}, bf16[512,128]{1,0:T(8,128)(2,1)S(1)}, u32[]{:S(2)}, u32[]{:S(2)}) collective-permute-start(bf16[512,128]{1,0:T(8,128)(2,1)S(1)} %get-tuple-element.16), channel_id=1, source_target_pairs={{0,5},{1,4},{2,7},{3,6},{4,1},{5,0},{6,3},{7,2},{8,13},{9,12},{10,... | collective-permute-start | bytes 393224 | tf_op jit(solution)/shard_map/ppermute | solution.py:379
  64.4 1.3 %collective-permute-start.2 = (bf16[512,128]{1,0:T(8,128)(2,1)S(1)}, bf16[512,128]{1,0:T(8,128)(2,1)S(1)}, u32[]{:S(2)}, u32[]{:S(2)}) collective-permute-start(bf16[512,128]{1,0:T(8,128)(2,1)S(1)} %get-tuple-element.17), channel_id=1, source_target_pairs={{0,6},{1,7},{2,4},{3,5},{4,2},{5,3},{6,0},{7,1},{8,14},{9,15},{10,... | collective-permute-start | bytes 393224 | tf_op jit(solution)/shard_map/ppermute | solution.py:379
  65.7 2.9 %shard_map.59 = (bf16[512,128]{1,0:T(8,128)(2,1)S(1)}, bf16[512,128]{1,0:T(8,128)(2,1)S(1)}, bf16[512,128]{1,0:T(8,128)(2,1)S(1)}, bf16[512,128]{1,0:T(8,128)(2,1)S(1)}) custom-call(s32[2]{0:T(128)S(1)} %pad_add_fusion.place_ref, f32[6,256,256]{2,1,0:T(8,128)S(1)} %shard_map.55.state_ref, bf16[16,256,128]{2,1,0:T(8,128)(2,1)S(1)} %get-tuple-element.18.plain, ...), custom_call_target="tpu_custom_call" | custom-call | flops 1073741824 | bytes 524288 | tf_op jit(solution)/shard_map/pallas_call | solution.py:363
  68.6 0.1 collective-permute-start.3
  68.7 2.6 %collective-permute-start.4 = (bf16[512,128]{1,0:T(8,128)(2,1)S(1)}, bf16[512,128]{1,0:T(8,128)(2,1)S(1)}, u32[]{:S(2)}, u32[]{:S(2)}) collective-permute-start(bf16[512,128]{1,0:T(8,128)(2,1)S(1)} %get-tuple-element.21), channel_id=1, source_target_pairs={{0,3},{1,2},{2,1},{3,0},{4,7},{5,6},{6,5},{7,4},{8,11},{9,10},{10,... | collective-permute-start | bytes 393224 | tf_op jit(solution)/shard_map/ppermute | solution.py:379
  71.3 5.0 %collective-permute-done.refs_0_ = bf16[512,128]{1,0:T(8,128)(2,1)S(1)} collective-permute-done((bf16[512,128]{1,0:T(8,128)(2,1)S(1)}, bf16[512,128]{1,0:T(8,128)(2,1)S(1)}, u32[]{:S(2)}, u32[]{:S(2)}) %collective-permute-start) | collective-permute-done | bytes 131104 | tf_op jit(solution)/shard_map/ppermute | solution.py:379
  76.3 0.0 collective-permute-start.6
  76.3 1.2 %collective-permute-done.1.refs_1_ = bf16[512,128]{1,0:T(8,128)(2,1)S(1)} collective-permute-done((bf16[512,128]{1,0:T(8,128)(2,1)S(1)}, bf16[512,128]{1,0:T(8,128)(2,1)S(1)}, u32[]{:S(2)}, u32[]{:S(2)}) %collective-permute-start.1) | collective-permute-done | bytes 131104 | tf_op jit(solution)/shard_map/ppermute | solution.py:379
  77.5 3.3 %collective-permute-start.5 = (bf16[512,128]{1,0:T(8,128)(2,1)S(1)}, bf16[512,128]{1,0:T(8,128)(2,1)S(1)}, u32[]{:S(2)}, u32[]{:S(2)}) collective-permute-start(bf16[512,128]{1,0:T(8,128)(2,1)S(1)} %get-tuple-element.22), channel_id=1, source_target_pairs={{0,7},{1,6},{2,5},{3,4},{4,3},{5,2},{6,1},{7,0},{8,15},{9,14},{10,... | collective-permute-start | bytes 393224 | tf_op jit(solution)/shard_map/ppermute | solution.py:379
  80.9 0.0 collective-permute-done.2.refs_2_
  80.9 0.7 collective-permute-done.3.refs_3_
  81.5 4.4 %collective-permute-done.4.refs_4_ = bf16[512,128]{1,0:T(8,128)(2,1)S(1)} collective-permute-done((bf16[512,128]{1,0:T(8,128)(2,1)S(1)}, bf16[512,128]{1,0:T(8,128)(2,1)S(1)}, u32[]{:S(2)}, u32[]{:S(2)}) %collective-permute-start.4) | collective-permute-done | bytes 131104 | tf_op jit(solution)/shard_map/ppermute | solution.py:379
  85.9 1.0 %collective-permute-done.6.refs_6_ = bf16[512,128]{1,0:T(8,128)(2,1)S(1)} collective-permute-done((bf16[512,128]{1,0:T(8,128)(2,1)S(1)}, bf16[512,128]{1,0:T(8,128)(2,1)S(1)}, u32[]{:S(2)}, u32[]{:S(2)}) %collective-permute-start.6) | collective-permute-done | bytes 131104 | tf_op jit(solution)/shard_map/ppermute | solution.py:379
  86.9 0.0 collective-permute-done.5.refs_5_
  86.9 2.1 %shard_map.60 = f32[32,64,256]{2,1,0:T(8,128)} custom-call(s32[2]{0:T(128)S(1)} %pad_add_fusion.place_ref, bf16[512,128]{1,0:T(8,128)(2,1)S(1)} %collective-permute-done.refs_0_, bf16[512,128]{1,0:T(8,128)(2,1)S(1)} %collective-permute-done.1.refs_1_, bf16[512,128]{1,0:T(8,128)(2,1)S(1)} %collective-permute-done.2.refs_2_, ...), custom_call_target="tpu_custom_call" | custom-call | tf_op jit(solution)/shard_map/pallas_call | solution.py:413
  (3 shorter events, 0.0 us)
Async XLA Ops:
  0.7 1.2 %copy-start.1 = (bf16[1024,512]{1,0:T(8,128)(2,1)S(1)}, bf16[1024,512]{1,0:T(8,128)(2,1)}, u32[]{:S(2)}) copy-start(bf16[1024,512]{1,0:T(8,128)(2,1)} %raw_ref.1) | copy-start | bytes 3145732
  1.9 20.4 %copy-start = (bf16[1024,2048]{1,0:T(8,128)(2,1)S(1)}, bf16[1024,2048]{1,0:T(8,128)(2,1)}, u32[]{:S(2)}) copy-start(bf16[1024,2048]{1,0:T(8,128)(2,1)} %constant.34.clone.table_ref) | copy-start | bytes 12582916
  24.8 4.9 %copy-start.2 = (s32[256]{0:T(256)S(1)}, s32[256]{0:T(256)}, u32[]{:S(2)}) copy-start(s32[256]{0:T(256)} %param.7) | copy-start | bytes 3076
  24.8 4.9 %copy-start.3 = (s32[256]{0:T(256)S(1)}, s32[256]{0:T(256)}, u32[]{:S(2)}) copy-start(s32[256]{0:T(256)} %param.8) | copy-start | bytes 3076
  24.8 32.5 %all-to-all-start.1 = ((bf16[32,8,16,128]{3,2,1,0:T(8,128)(2,1)}), bf16[32,8,16,128]{3,2,1,0:T(8,128)(2,1)S(1)}, u32[]{:S(2)}, u32[]{:S(2)}) async-start(bf16[32,8,16,128]{3,2,1,0:T(8,128)(2,1)} %shard_map.57), calls=%async_computation.1 | async-start | bytes 2097152 | tf_op jit(solution)/shard_map/all_to_all | solution.py:469
  61.3 15.0 %collective-permute-start = (bf16[512,128]{1,0:T(8,128)(2,1)S(1)}, bf16[512,128]{1,0:T(8,128)(2,1)S(1)}, u32[]{:S(2)}, u32[]{:S(2)}) collective-permute-start(bf16[512,128]{1,0:T(8,128)(2,1)S(1)} %get-tuple-element.15), channel_id=1, source_target_pairs={{0,4},{1,5},{2,6},{3,7},{4,0},{5,1},{6,2},{7,3},{8,12},{9,13},{10,... | collective-permute-start | bytes 393224 | tf_op jit(solution)/shard_map/ppermute | solution.py:379
  61.4 16.1 %collective-permute-start.1 = (bf16[512,128]{1,0:T(8,128)(2,1)S(1)}, bf16[512,128]{1,0:T(8,128)(2,1)S(1)}, u32[]{:S(2)}, u32[]{:S(2)}) collective-permute-start(bf16[512,128]{1,0:T(8,128)(2,1)S(1)} %get-tuple-element.16), channel_id=1, source_target_pairs={{0,5},{1,4},{2,7},{3,6},{4,1},{5,0},{6,3},{7,2},{8,13},{9,12},{10,... | collective-permute-start | bytes 393224 | tf_op jit(solution)/shard_map/ppermute | solution.py:379
  64.4 16.5 %collective-permute-start.2 = (bf16[512,128]{1,0:T(8,128)(2,1)S(1)}, bf16[512,128]{1,0:T(8,128)(2,1)S(1)}, u32[]{:S(2)}, u32[]{:S(2)}) collective-permute-start(bf16[512,128]{1,0:T(8,128)(2,1)S(1)} %get-tuple-element.17), channel_id=1, source_target_pairs={{0,6},{1,7},{2,4},{3,5},{4,2},{5,3},{6,0},{7,1},{8,14},{9,15},{10,... | collective-permute-start | bytes 393224 | tf_op jit(solution)/shard_map/ppermute | solution.py:379
  68.6 12.9 %collective-permute-start.3 = (bf16[512,128]{1,0:T(8,128)(2,1)S(1)}, bf16[512,128]{1,0:T(8,128)(2,1)S(1)}, u32[]{:S(2)}, u32[]{:S(2)}) collective-permute-start(bf16[512,128]{1,0:T(8,128)(2,1)S(1)} %get-tuple-element.20), channel_id=1, source_target_pairs={{0,2},{1,3},{2,0},{3,1},{4,6},{5,7},{6,4},{7,5},{8,10},{9,11},{10,... | collective-permute-start | bytes 393224 | tf_op jit(solution)/shard_map/ppermute | solution.py:379
  68.7 17.2 %collective-permute-start.4 = (bf16[512,128]{1,0:T(8,128)(2,1)S(1)}, bf16[512,128]{1,0:T(8,128)(2,1)S(1)}, u32[]{:S(2)}, u32[]{:S(2)}) collective-permute-start(bf16[512,128]{1,0:T(8,128)(2,1)S(1)} %get-tuple-element.21), channel_id=1, source_target_pairs={{0,3},{1,2},{2,1},{3,0},{4,7},{5,6},{6,5},{7,4},{8,11},{9,10},{10,... | collective-permute-start | bytes 393224 | tf_op jit(solution)/shard_map/ppermute | solution.py:379
  76.3 10.6 %collective-permute-start.6 = (bf16[512,128]{1,0:T(8,128)(2,1)S(1)}, bf16[512,128]{1,0:T(8,128)(2,1)S(1)}, u32[]{:S(2)}, u32[]{:S(2)}) collective-permute-start(bf16[512,128]{1,0:T(8,128)(2,1)S(1)} %get-tuple-element.23), channel_id=1, source_target_pairs={{0,1},{1,0},{2,3},{3,2},{4,5},{5,4},{6,7},{7,6},{8,9},{9,8},{10,11... | collective-permute-start | bytes 393224 | tf_op jit(solution)/shard_map/ppermute | solution.py:379
  77.5 9.4 %collective-permute-start.5 = (bf16[512,128]{1,0:T(8,128)(2,1)S(1)}, bf16[512,128]{1,0:T(8,128)(2,1)S(1)}, u32[]{:S(2)}, u32[]{:S(2)}) collective-permute-start(bf16[512,128]{1,0:T(8,128)(2,1)S(1)} %get-tuple-element.22), channel_id=1, source_target_pairs={{0,7},{1,6},{2,5},{3,4},{4,3},{5,2},{6,1},{7,0},{8,15},{9,14},{10,... | collective-permute-start | bytes 393224 | tf_op jit(solution)/shard_map/ppermute | solution.py:379

commit v12 on v11

--- a/solution.py
+++ b/solution.py
@@ -34,10 +34,9 @@
     return (both / np.float32(math.sqrt(total_time))).astype(ml_dtypes.bfloat16)
 
 
-def pick_kernel(slot_ref, raw_ref, out_ref):
-    gathers = slot_ref.shape[0]
-    groups, rows, _ = out_ref.shape
-    own_offsets = rows // gathers
+def pick_kernel(me_ref, slot_ref, raw_ref, *out_refs):
+    gathers, local_offsets = slot_ref.shape
+    own_offsets = local_offsets // len(out_refs)
     times = raw_ref.shape[1]
     half = times // 2
     row = lax.broadcasted_iota(jnp.int32, (times, times), 0)
@@ -46,27 +45,33 @@
     split = jnp.where(row == source, 1.0, 0.0).astype(jnp.bfloat16)
     raw = jnp.dot(raw_ref[...], split, preferred_element_type=jnp.float32).astype(jnp.bfloat16)
     lane = lax.broadcasted_iota(jnp.int32, (gathers, raw_ref.shape[0]), 1)
-    for f in range(groups):
-        picks = [
-            jnp.where(lane == slot_ref[:, h : h + 1].astype(jnp.int32), 1.0, 0.0).astype(jnp.bfloat16)
-            for h in range(f * own_offsets, (f + 1) * own_offsets)
-        ]
-        out_ref[f] = jnp.dot(
+    slot = slot_ref[...]
+    place = lax.broadcasted_iota(jnp.int32, slot.shape, 1)
+    for s, out_ref in enumerate(out_refs):
+        first = (me_ref[0] ^ s) * own_offsets
+        picks = []
+        for h in range(own_offsets):
+            wanted = jnp.sum(jnp.where(place == first + h, slot, 0.0), axis=1, keepdims=True)
+            picks.append(
+                jnp.where(lane == wanted.astype(jnp.int32), 1.0, 0.0).astype(jnp.bfloat16)
+            )
+        out_ref[...] = jnp.dot(
             jnp.concatenate(picks, axis=0), raw, preferred_element_type=jnp.float32
         ).astype(out_ref.dtype)
 
 
-def pick(trace_slot, raw_traces, groups):
+def pick(me, trace_slot, raw_traces, groups):
     gathers, local_offsets = trace_slot.shape
     rows = gathers * local_offsets // groups
     vmem = pl.BlockSpec(memory_space=pltpu.VMEM)
+    block = jax.ShapeDtypeStruct((rows, raw_traces.shape[1]), raw_traces.dtype)
     return pl.pallas_call(
         pick_kernel,
-        in_specs=[vmem, vmem],
-        out_specs=vmem,
-        out_shape=jax.ShapeDtypeStruct((groups, rows, raw_traces.shape[1]), raw_traces.dtype),
+        in_specs=[pl.BlockSpec(memory_space=pltpu.SMEM), vmem, vmem],
+        out_specs=[vmem] * groups,
+        out_shape=[block] * groups,
         compiler_params=pltpu.CompilerParams(vmem_limit_bytes=24 * MIB),
-    )(trace_slot, raw_traces)
+    )(me, trace_slot, raw_traces)
 
 
 def regroup(parts, gathers):
@@ -90,27 +95,64 @@
     return found
 
 
-def transform_kernel(pairs, gathers, chunks, table_ref, series_ref, out_ref, even, odd):
-    blocks, rows, local_times = series_ref.shape
+def time_sums(me, first, table_ref, series_refs, even, odd, own):
+    half = even.shape[1] // 2
+    depth = table_ref.shape[1] // 2
+    evens = odds = None
+    for r in range(len(series_refs) // 2):
+        start = (quotient(me, 2) ^ (first + r)) * 2 * half
+        even_part = jnp.dot(
+            table_ref[own, pl.ds(pl.multiple_of(start, 2 * half), 2 * half)],
+            even[r],
+            preferred_element_type=jnp.float32,
+        )
+        odd_part = jnp.dot(
+            table_ref[own, pl.ds(pl.multiple_of(depth + start, 2 * half), 2 * half)],
+            odd[r],
+            preferred_element_type=jnp.float32,
+        )
+        evens = even_part if evens is None else evens + even_part
+        odds = odd_part if odds is None else odds + odd_part
+    return evens, odds
+
+
+def turn_series(me, series_refs, even, odd):
+    half = even.shape[1] // 2
+    for s, series_ref in enumerate(series_refs):
+        turned = series_ref[...].T
+        place = pl.ds(pl.multiple_of(((me ^ s) & 1) * half, half), half)
+        even[s // 2, place] = turned[:half]
+        odd[s // 2, place] = turned[half:]
+
+
+def begin_kernel(chunks, me_ref, table_ref, *refs):
+    *series_refs, out_ref, even, odd = refs
+    me = me_ref[0]
+    turn_series(me, series_refs, even, odd)
     step = table_ref.shape[0] // chunks
-    half = local_times // 2
-    for b in range(blocks):
-        turned = series_ref[b].T
-        even[b * half : (b + 1) * half] = turned[:half]
-        odd[b * half : (b + 1) * half] = turned[half:]
-    depth = blocks * half
     for i in range(chunks):
         own = slice(i * step, (i + 1) * step)
-        evens = jnp.dot(table_ref[own, :depth], even[...], preferred_element_type=jnp.float32)
-        odds = jnp.dot(table_ref[own, depth:], odd[...], preferred_element_type=jnp.float32)
+        out_ref[0, own], out_ref[1, own] = time_sums(
+            me, 0, table_ref, series_refs, even, odd, own
+        )
+
+
+def transform_kernel(pairs, gathers, chunks, me_ref, table_ref, begun_ref, *refs):
+    *series_refs, out_ref, even, odd = refs
+    me = me_ref[0]
+    turn_series(me, series_refs, even, odd)
+    step = table_ref.shape[0] // chunks
+    for i in range(chunks):
+        own = slice(i * step, (i + 1) * step)
+        evens, odds = time_sums(me, 1, table_ref, series_refs, even, odd, own)
+        evens = evens + begun_ref[0, own]
+        odds = odds + begun_ref[1, own]
         low = evens + odds
         high = evens - odds
         if len(out_ref.shape) == 3:
             row = lax.broadcasted_iota(jnp.int32, (step, 1), 0)
             out_ref[0, own] = low.astype(out_ref.dtype)
-            out_ref[1, own] = jnp.where(
-                row // pairs % 2 == 0, high, -high
-            ).astype(out_ref.dtype)
+            out_ref[1, own] = jnp.where(row // pairs % 2 == 0, high, -high).astype(out_ref.dtype)
             continue
         targets = step // (4 * pairs)
         devices = out_ref.shape[0]
@@ -124,26 +166,43 @@
                 out_ref[devices - 1 - place, h] = value.astype(out_ref.dtype)
 
 
-def transform(table, series, pairs, gathers):
+def transform(me, table, series, pairs, gathers):
     columns, total_time = table.shape
-    blocks, rows, local_times = series.shape
+    rows, local_times = series[0].shape
     own_offsets = rows // gathers
     devices = columns // (2 * pairs)
     final = (devices, own_offsets, pairs, 4 * gathers)
     chunks = 4
     aligned = rows % (4 * gathers) == 0 and pairs % 8 == 0 and devices % (2 * chunks) == 0
     vmem = pl.BlockSpec(memory_space=pltpu.VMEM)
+    smem = pl.BlockSpec(memory_space=pltpu.SMEM)
+    early, late = series[:2], series[2:]
+
+    def scratch(blocks):
+        return [pltpu.VMEM((len(blocks) // 2, local_times, rows), jnp.bfloat16)] * 2
+
+    params = pltpu.CompilerParams(vmem_limit_bytes=24 * MIB)
+    begun = pl.pallas_call(
+        functools.partial(begin_kernel, chunks),
+        in_specs=[smem] + [vmem] * (1 + len(early)),
+        out_specs=vmem,
+        out_shape=jax.ShapeDtypeStruct((2, columns, rows), jnp.float32),
+        scratch_shapes=scratch(early),
+        compiler_params=params,
+        cost_estimate=pl.CostEstimate(
+            flops=columns * total_time * rows,
+            bytes_accessed=2 * columns * total_time,
+            transcendentals=0,
+        ),
+    )(me, table, *early)
     out = pl.pallas_call(
         functools.partial(transform_kernel, pairs, gathers, chunks),
-        in_specs=[vmem, vmem],
+        in_specs=[smem] + [vmem] * (2 + len(late)),
         out_specs=vmem,
         out_shape=jax.ShapeDtypeStruct(final if aligned else (2, columns, rows), jnp.bfloat16),
-        scratch_shapes=[
-            pltpu.VMEM((total_time // 2, rows), jnp.bfloat16),
-            pltpu.VMEM((total_time // 2, rows), jnp.bfloat16),
-        ],
-        compiler_params=pltpu.CompilerParams(vmem_limit_bytes=24 * MIB),
-    )(table, series)
+        scratch_shapes=scratch(late),
+        compiler_params=params,
+    )(me, table, begun, *late)
     if aligned:
         return out
     out = out.reshape(2, devices // 2, 2, 2, pairs, own_offsets, gathers)
@@ -462,10 +521,13 @@
     pairs = own_freqs // halves
     own_offsets = local_offsets // freq_devices
 
-    picked = pick(trace_slot.astype(jnp.float32), raw_traces, freq_devices)
-    series = lax.all_to_all(picked, "freq", 0, 0, tiled=True)
+    me = lax.axis_index("freq").astype(jnp.int32).reshape(1)
+    series = list(pick(me, trace_slot.astype(jnp.float32), raw_traces, freq_devices))
+    for s in list(range(2, freq_devices)) + [1]:
+        swaps = [(f, f ^ s) for f in range(freq_devices)]
+        series[s] = lax.ppermute(series[s], "freq", swaps)
     table = jnp.asarray(table_rows(total_time, freq_devices, offset_devices, halves, pairs))
-    spectrum = transform(table, series, pairs, gathers)
+    spectrum = transform(me, table, series, pairs, gathers)
     data = lax.all_to_all(spectrum, ("freq", "offset"), 0, 0, tiled=True)
 
     offs = offset_index.reshape(offset_devices, freq_devices, own_offsets)

time: 89.3 us -> 90.9 us (1.018)
  the two profiles are of different devices: /device:TPU:0 before, /device:TPU:8 now
where the time goes in v12:
time: 90.9 us; the launch traced here: 90.6 us
  waiting for transfers between devices  52.4 us (58%)
  Pallas kernels  17.6 us (19%)
  starting transfers between devices  15.9 us (17%)
  local copies, waits for them, and re-layouts  3.74 us (4%)
    all_to_all x1, waiting for transfers between devices, local(): data = lax.all_to_all(spectrum, ('freq', 'offset'), 0, 0, tiled=True)  22 us
    ppermute x7, waiting for transfers between devices, radon_swapped(): blocks.append(lax.ppermute(part, 'offset', swaps) if s else part)  21.5 us
    ppermute x3, waiting for transfers between devices, local(): series[s] = lax.ppermute(series[s], 'freq', swaps)  8.92 us
    ppermute x7, starting transfers between devices, radon_swapped(): blocks.append(lax.ppermute(part, 'offset', swaps) if s else part)  7.93 us
    all_to_all x1, starting transfers between devices, local(): data = lax.all_to_all(spectrum, ('freq', 'offset'), 0, 0, tiled=True)  6.03 us
    pallas_call x1, Pallas kernels, radon_swapped(): pl.pallas_call(functools.partial(far_kernel, gathers, half), in_specs=[sm...  3.97 us
    pallas_call x1, Pallas kernels, moveout(): pl.pallas_call(functools.partial(moveout_kernel, shift, total_time), grid...  3.43 us
    unnamed x10, local copies, waits for them, and re-layouts  3.42 us
  transfers between devices with their start and end apart: 11, of which 9 were waited for; matrix products, arithmetic and copies ran while one was open for 0% of the time, Pallas kernels for 5%

profile of v12, /device:TPU:8, one launch (start us, length us, event | category | flops | bytes accessed | tf_op | source)
XLA Modules:
  0.0 90.6 jit_solution(11106080486031645878)
XLA Ops:
  0.0 0.7 convert_element_type.24.slot_ref
  0.7 0.0 copy-start.2
  0.7 1.2 %copy-done.2 = bf16[1024,512]{1,0:T(8,128)(2,1)S(1)} copy-done((bf16[1024,512]{1,0:T(8,128)(2,1)S(1)}, bf16[1024,512]{1,0:T(8,128)(2,1)}, u32[]{:S(2)}) %copy-start.2) | copy-done | bytes 1048600
  1.9 2.0 %shard_map.56 = (bf16[256,512]{1,0:T(8,128)(2,1)S(1)}, bf16[256,512]{1,0:T(8,128)(2,1)S(1)}, bf16[256,512]{1,0:T(8,128)(2,1)S(1)}, bf16[256,512]{1,0:T(8,128)(2,1)S(1)}) custom-call(s32[1]{0:T(128)} %bitcast.5.me_ref, f32[32,32]{1,0:T(8,128)S(1)} %convert_element_type.24.slot_ref, bf16[1024,512]{1,0:T(8,128)(2,1)S(1)} %copy-done.2), custom_call_target="tpu_custom_call" | custom-call | tf_op jit(solution)/shard_map/pallas_call | solution.py:68
  3.9 0.1 collective-permute-start
  4.0 1.6 %collective-permute-start.1 = (bf16[256,512]{1,0:T(8,128)(2,1)S(1)}, bf16[256,512]{1,0:T(8,128)(2,1)S(1)}, u32[]{:S(2)}, u32[]{:S(2)}) collective-permute-start(bf16[256,512]{1,0:T(8,128)(2,1)S(1)} %get-tuple-element.21), channel_id=1, source_target_pairs={{0,16},{8,24},{16,0},{24,8},{1,17},{9,25},{17,1},{25,9},{2,18},{10... | collective-permute-start | bytes 786440 | tf_op jit(solution)/shard_map/ppermute | solution.py:528
  5.6 0.3 collective-permute-start.2
  5.9 0.0 collective-permute-done.refs_1_
  5.9 0.0 copy-start
  5.9 2.2 %copy-done = bf16[1024,2048]{1,0:T(8,128)(2,1)S(1)} copy-done((bf16[1024,2048]{1,0:T(8,128)(2,1)S(1)}, bf16[1024,2048]{1,0:T(8,128)(2,1)}, u32[]{:S(2)}) %copy-start) | copy-done | bytes 4194328
  8.1 0.0 copy-start.1
  8.1 0.9 shard_map.57.begun_ref
  9.0 4.2 %collective-permute-done.1.refs_0_ = bf16[256,512]{1,0:T(8,128)(2,1)S(1)} collective-permute-done((bf16[256,512]{1,0:T(8,128)(2,1)S(1)}, bf16[256,512]{1,0:T(8,128)(2,1)S(1)}, u32[]{:S(2)}, u32[]{:S(2)}) %collective-permute-start.1) | collective-permute-done | bytes 262176 | tf_op jit(solution)/shard_map/ppermute | solution.py:528
  13.2 4.7 %collective-permute-done.2.refs_1_ = bf16[256,512]{1,0:T(8,128)(2,1)S(1)} collective-permute-done((bf16[256,512]{1,0:T(8,128)(2,1)S(1)}, bf16[256,512]{1,0:T(8,128)(2,1)S(1)}, u32[]{:S(2)}, u32[]{:S(2)}) %collective-permute-start.2) | collective-permute-done | bytes 262176 | tf_op jit(solution)/shard_map/ppermute | solution.py:528
  17.9 0.0 copy-done.1
  17.9 2.2 %shard_map.58 = bf16[32,8,16,128]{3,2,1,0:T(8,128)(2,1)} custom-call(s32[1]{0:T(128)} %bitcast.5.me_ref, bf16[1024,2048]{1,0:T(8,128)(2,1)S(1)} %copy-done.1, f32[2,1024,256]{2,1,0:T(8,128)S(1)} %shard_map.57.begun_ref, bf16[256,512]{1,0:T(8,128)(2,1)S(1)} %collective-permute-done.1.refs_0_, bf16[256,512]{1,0:T(8,128)(2,1)S(1)} %collective-permute-done.2.refs_1_), custom_call_target="tpu_custom_call" | custom-call | tf_op jit(solution)/shard_map/pallas_call | solution.py:198
  20.1 0.0 copy-start.3
  20.1 0.0 copy-start.4
  20.1 6.0 %all-to-all-start = ((bf16[32,8,16,128]{3,2,1,0:T(8,128)(2,1)}), bf16[32,8,16,128]{3,2,1,0:T(8,128)(2,1)S(1)}, u32[]{:S(2)}, u32[]{:S(2)}) async-start(bf16[32,8,16,128]{3,2,1,0:T(8,128)(2,1)} %shard_map.58), calls=%async_computation | async-start | bytes 2097152 | tf_op jit(solution)/shard_map/all_to_all | solution.py:531
  26.2 0.0 copy-done.3
  26.2 0.1 copy.7.slow_ref
  26.4 0.0 copy-done.4
  26.4 0.1 convert_element_type.21
  26.5 0.1 convert_element_type.23.offs_ref
  26.6 3.4 %shard_map.55.state_ref = f32[6,256,256]{2,1,0:T(8,128)S(1)} custom-call(f32[1]{0:T(128)} %bitcast.2.base_ref, f32[256,1]{1,0:T(8,128)S(1)} %copy.7.slow_ref, f32[1,256]{1,0:T(1,128)S(1)} %convert_element_type.23.offs_ref), custom_call_target="tpu_custom_call" | custom-call | flops 19660800 | bytes 1572864 | tf_op jit(solution)/shard_map/pallas_call | solution.py:235
  30.0 0.1 pad_add_fusion.place_ref
  30.1 22.0 %all-to-all-done.data_ref = bf16[32,8,16,128]{3,2,1,0:T(8,128)(2,1)S(1)} async-done(((bf16[32,8,16,128]{3,2,1,0:T(8,128)(2,1)}), bf16[32,8,16,128]{3,2,1,0:T(8,128)(2,1)S(1)}, u32[]{:S(2)}, u32[]{:S(2)}) %all-to-all-start) | async-done | bytes 1048608 | tf_op jit(solution)/shard_map/all_to_all | solution.py:531
  52.1 4.0 %shard_map.59 = (bf16[16,256,128]{2,1,0:T(8,128)(2,1)S(1)}, bf16[16,256,128]{2,1,0:T(8,128)(2,1)S(1)}, bf16[512,128]{1,0:T(8,128)(2,1)S(1)}, bf16[512,128]{1,0:T...) custom-call(s32[2]{0:T(128)S(1)} %pad_add_fusion.place_ref, ...), custom_call_target="tpu_custom_call" | custom-call | flops 1073741824 | bytes 524288 | tf_op jit(solution)/shard_map/pallas_call | solution.py:413
  56.1 2.9 %shard_map.60 = (bf16[512,128]{1,0:T(8,128)(2,1)S(1)}, bf16[512,128]{1,0:T(8,128)(2,1)S(1)}, bf16[512,128]{1,0:T(8,128)(2,1)S(1)}, bf16[512,128]{1,0:T(8,128)(2,1)S(1)}) custom-call(s32[2]{0:T(128)S(1)} %pad_add_fusion.place_ref, f32[6,256,256]{2,1,0:T(8,128)S(1)} %shard_map.55.state_ref, bf16[16,256,128]{2,1,0:T(8,128)(2,1)S(1)} %get-tuple-element.26.plain, ...), custom_call_target="tpu_custom_call" | custom-call | flops 1073741824 | bytes 524288 | tf_op jit(solution)/shard_map/pallas_call | solution.py:422
  59.0 2.0 %collective-permute-start.6 = (bf16[512,128]{1,0:T(8,128)(2,1)S(1)}, bf16[512,128]{1,0:T(8,128)(2,1)S(1)}, u32[]{:S(2)}, u32[]{:S(2)}) collective-permute-start(bf16[512,128]{1,0:T(8,128)(2,1)S(1)} %get-tuple-element.28), channel_id=1, source_target_pairs={{0,2},{1,3},{2,0},{3,1},{4,6},{5,7},{6,4},{7,5},{8,10},{9,11},{10,... | collective-permute-start | bytes 393224 | tf_op jit(solution)/shard_map/ppermute | solution.py:438
  61.0 0.2 collective-permute-start.7
  61.2 1.4 %collective-permute-start.9 = (bf16[512,128]{1,0:T(8,128)(2,1)S(1)}, bf16[512,128]{1,0:T(8,128)(2,1)S(1)}, u32[]{:S(2)}, u32[]{:S(2)}) collective-permute-start(bf16[512,128]{1,0:T(8,128)(2,1)S(1)} %get-tuple-element.31), channel_id=1, source_target_pairs={{0,1},{1,0},{2,3},{3,2},{4,5},{5,4},{6,7},{7,6},{8,9},{9,8},{10,11... | collective-permute-start | bytes 393224 | tf_op jit(solution)/shard_map/ppermute | solution.py:438
  62.6 1.5 %collective-permute-start.3 = (bf16[512,128]{1,0:T(8,128)(2,1)S(1)}, bf16[512,128]{1,0:T(8,128)(2,1)S(1)}, u32[]{:S(2)}, u32[]{:S(2)}) collective-permute-start(bf16[512,128]{1,0:T(8,128)(2,1)S(1)} %get-tuple-element.23), channel_id=1, source_target_pairs={{0,4},{1,5},{2,6},{3,7},{4,0},{5,1},{6,2},{7,3},{8,12},{9,13},{10,... | collective-permute-start | bytes 393224 | tf_op jit(solution)/shard_map/ppermute | solution.py:438
  64.1 1.5 %collective-permute-start.4 = (bf16[512,128]{1,0:T(8,128)(2,1)S(1)}, bf16[512,128]{1,0:T(8,128)(2,1)S(1)}, u32[]{:S(2)}, u32[]{:S(2)}) collective-permute-start(bf16[512,128]{1,0:T(8,128)(2,1)S(1)} %get-tuple-element.24), channel_id=1, source_target_pairs={{0,5},{1,4},{2,7},{3,6},{4,1},{5,0},{6,3},{7,2},{8,13},{9,12},{10,... | collective-permute-start | bytes 393224 | tf_op jit(solution)/shard_map/ppermute | solution.py:438
  65.6 0.6 collective-permute-done.6.refs_3_
  66.2 0.0 collective-permute-start.5
  66.2 2.2 %collective-permute-done.7.refs_4_ = bf16[512,128]{1,0:T(8,128)(2,1)S(1)} collective-permute-done((bf16[512,128]{1,0:T(8,128)(2,1)S(1)}, bf16[512,128]{1,0:T(8,128)(2,1)S(1)}, u32[]{:S(2)}, u32[]{:S(2)}) %collective-permute-start.7) | collective-permute-done | bytes 131104 | tf_op jit(solution)/shard_map/ppermute | solution.py:438
  68.4 1.4 %collective-permute-start.8 = (bf16[512,128]{1,0:T(8,128)(2,1)S(1)}, bf16[512,128]{1,0:T(8,128)(2,1)S(1)}, u32[]{:S(2)}, u32[]{:S(2)}) collective-permute-start(bf16[512,128]{1,0:T(8,128)(2,1)S(1)} %get-tuple-element.30), channel_id=1, source_target_pairs={{0,7},{1,6},{2,5},{3,4},{4,3},{5,2},{6,1},{7,0},{8,15},{9,14},{10,... | collective-permute-start | bytes 393224 | tf_op jit(solution)/shard_map/ppermute | solution.py:438
  69.8 0.0 collective-permute-done.9.refs_6_
  69.8 9.5 %collective-permute-done.3.refs_0_ = bf16[512,128]{1,0:T(8,128)(2,1)S(1)} collective-permute-done((bf16[512,128]{1,0:T(8,128)(2,1)S(1)}, bf16[512,128]{1,0:T(8,128)(2,1)S(1)}, u32[]{:S(2)}, u32[]{:S(2)}) %collective-permute-start.3) | collective-permute-done | bytes 131104 | tf_op jit(solution)/shard_map/ppermute | solution.py:438
  79.2 2.8 %collective-permute-done.4.refs_1_ = bf16[512,128]{1,0:T(8,128)(2,1)S(1)} collective-permute-done((bf16[512,128]{1,0:T(8,128)(2,1)S(1)}, bf16[512,128]{1,0:T(8,128)(2,1)S(1)}, u32[]{:S(2)}, u32[]{:S(2)}) %collective-permute-start.4) | collective-permute-done | bytes 131104 | tf_op jit(solution)/shard_map/ppermute | solution.py:438
  82.1 4.4 %collective-permute-done.5.refs_2_ = bf16[512,128]{1,0:T(8,128)(2,1)S(1)} collective-permute-done((bf16[512,128]{1,0:T(8,128)(2,1)S(1)}, bf16[512,128]{1,0:T(8,128)(2,1)S(1)}, u32[]{:S(2)}, u32[]{:S(2)}) %collective-permute-start.5) | collective-permute-done | bytes 131104 | tf_op jit(solution)/shard_map/ppermute | solution.py:438
  86.5 2.0 %collective-permute-done.8.refs_5_ = bf16[512,128]{1,0:T(8,128)(2,1)S(1)} collective-permute-done((bf16[512,128]{1,0:T(8,128)(2,1)S(1)}, bf16[512,128]{1,0:T(8,128)(2,1)S(1)}, u32[]{:S(2)}, u32[]{:S(2)}) %collective-permute-start.8) | collective-permute-done | bytes 131104 | tf_op jit(solution)/shard_map/ppermute | solution.py:438
  88.5 2.1 %shard_map.61 = f32[32,64,256]{2,1,0:T(8,128)} custom-call(s32[2]{0:T(128)S(1)} %pad_add_fusion.place_ref, bf16[512,128]{1,0:T(8,128)(2,1)S(1)} %collective-permute-done.3.refs_0_, bf16[512,128]{1,0:T(8,128)(2,1)S(1)} %collective-permute-done.4.refs_1_, bf16[512,128]{1,0:T(8,128)(2,1)S(1)} %collective-permute-done.5.refs_2_, ...), custom_call_target="tpu_custom_call" | custom-call | tf_op jit(solution)/shard_map/pallas_call | solution.py:472
  (3 shorter events, 0.0 us)
Async XLA Ops:
  0.7 1.2 %copy-start.2 = (bf16[1024,512]{1,0:T(8,128)(2,1)S(1)}, bf16[1024,512]{1,0:T(8,128)(2,1)}, u32[]{:S(2)}) copy-start(bf16[1024,512]{1,0:T(8,128)(2,1)} %raw_ref.1) | copy-start | bytes 3145732
  3.9 1.9 %collective-permute-start = (bf16[256,512]{1,0:T(8,128)(2,1)S(1)}, bf16[256,512]{1,0:T(8,128)(2,1)S(1)}, u32[]{:S(2)}, u32[]{:S(2)}) collective-permute-start(bf16[256,512]{1,0:T(8,128)(2,1)S(1)} %get-tuple-element.20), channel_id=1, source_target_pairs={{0,8},{8,0},{16,24},{24,16},{1,9},{9,1},{17,25},{25,17},{2,10},{10... | collective-permute-start | bytes 786440 | tf_op jit(solution)/shard_map/ppermute | solution.py:528
  4.0 9.2 %collective-permute-start.1 = (bf16[256,512]{1,0:T(8,128)(2,1)S(1)}, bf16[256,512]{1,0:T(8,128)(2,1)S(1)}, u32[]{:S(2)}, u32[]{:S(2)}) collective-permute-start(bf16[256,512]{1,0:T(8,128)(2,1)S(1)} %get-tuple-element.21), channel_id=1, source_target_pairs={{0,16},{8,24},{16,0},{24,8},{1,17},{9,25},{17,1},{25,9},{2,18},{10... | collective-permute-start | bytes 786440 | tf_op jit(solution)/shard_map/ppermute | solution.py:528
  5.6 12.3 %collective-permute-start.2 = (bf16[256,512]{1,0:T(8,128)(2,1)S(1)}, bf16[256,512]{1,0:T(8,128)(2,1)S(1)}, u32[]{:S(2)}, u32[]{:S(2)}) collective-permute-start(bf16[256,512]{1,0:T(8,128)(2,1)S(1)} %get-tuple-element.22), channel_id=1, source_target_pairs={{0,24},{8,16},{16,8},{24,0},{1,25},{9,17},{17,9},{25,1},{2,26},{10... | collective-permute-start | bytes 786440 | tf_op jit(solution)/shard_map/ppermute | solution.py:528
  5.9 2.2 %copy-start = (bf16[1024,2048]{1,0:T(8,128)(2,1)S(1)}, bf16[1024,2048]{1,0:T(8,128)(2,1)}, u32[]{:S(2)}) copy-start(bf16[1024,2048]{1,0:T(8,128)(2,1)} %constant.34.clone.table_ref) | copy-start | bytes 12582916
  8.1 9.8 %copy-start.1 = (bf16[1024,2048]{1,0:T(8,128)(2,1)S(1)}, bf16[1024,2048]{1,0:T(8,128)(2,1)}, u32[]{:S(2)}) copy-start(bf16[1024,2048]{1,0:T(8,128)(2,1)} %constant.34.clone.table_ref) | copy-start | bytes 12582916
  20.1 6.1 %copy-start.3 = (s32[256]{0:T(256)S(1)}, s32[256]{0:T(256)}, u32[]{:S(2)}) copy-start(s32[256]{0:T(256)} %param.8) | copy-start | bytes 3076
  20.1 6.2 %copy-start.4 = (s32[256]{0:T(256)S(1)}, s32[256]{0:T(256)}, u32[]{:S(2)}) copy-start(s32[256]{0:T(256)} %param.7) | copy-start | bytes 3076
  20.1 32.0 %all-to-all-start = ((bf16[32,8,16,128]{3,2,1,0:T(8,128)(2,1)}), bf16[32,8,16,128]{3,2,1,0:T(8,128)(2,1)S(1)}, u32[]{:S(2)}, u32[]{:S(2)}) async-start(bf16[32,8,16,128]{3,2,1,0:T(8,128)(2,1)} %shard_map.58), calls=%async_computation | async-start | bytes 2097152 | tf_op jit(solution)/shard_map/all_to_all | solution.py:531
  59.0 7.2 %collective-permute-start.6 = (bf16[512,128]{1,0:T(8,128)(2,1)S(1)}, bf16[512,128]{1,0:T(8,128)(2,1)S(1)}, u32[]{:S(2)}, u32[]{:S(2)}) collective-permute-start(bf16[512,128]{1,0:T(8,128)(2,1)S(1)} %get-tuple-element.28), channel_id=1, source_target_pairs={{0,2},{1,3},{2,0},{3,1},{4,6},{5,7},{6,4},{7,5},{8,10},{9,11},{10,... | collective-permute-start | bytes 393224 | tf_op jit(solution)/shard_map/ppermute | solution.py:438
  61.0 7.4 %collective-permute-start.7 = (bf16[512,128]{1,0:T(8,128)(2,1)S(1)}, bf16[512,128]{1,0:T(8,128)(2,1)S(1)}, u32[]{:S(2)}, u32[]{:S(2)}) collective-permute-start(bf16[512,128]{1,0:T(8,128)(2,1)S(1)} %get-tuple-element.29), channel_id=1, source_target_pairs={{0,3},{1,2},{2,1},{3,0},{4,7},{5,6},{6,5},{7,4},{8,11},{9,10},{10,... | collective-permute-start | bytes 393224 | tf_op jit(solution)/shard_map/ppermute | solution.py:438
  61.2 8.6 %collective-permute-start.9 = (bf16[512,128]{1,0:T(8,128)(2,1)S(1)}, bf16[512,128]{1,0:T(8,128)(2,1)S(1)}, u32[]{:S(2)}, u32[]{:S(2)}) collective-permute-start(bf16[512,128]{1,0:T(8,128)(2,1)S(1)} %get-tuple-element.31), channel_id=1, source_target_pairs={{0,1},{1,0},{2,3},{3,2},{4,5},{5,4},{6,7},{7,6},{8,9},{9,8},{10,11... | collective-permute-start | bytes 393224 | tf_op jit(solution)/shard_map/ppermute | solution.py:438
  62.6 16.6 %collective-permute-start.3 = (bf16[512,128]{1,0:T(8,128)(2,1)S(1)}, bf16[512,128]{1,0:T(8,128)(2,1)S(1)}, u32[]{:S(2)}, u32[]{:S(2)}) collective-permute-start(bf16[512,128]{1,0:T(8,128)(2,1)S(1)} %get-tuple-element.23), channel_id=1, source_target_pairs={{0,4},{1,5},{2,6},{3,7},{4,0},{5,1},{6,2},{7,3},{8,12},{9,13},{10,... | collective-permute-start | bytes 393224 | tf_op jit(solution)/shard_map/ppermute | solution.py:438
  64.1 17.9 %collective-permute-start.4 = (bf16[512,128]{1,0:T(8,128)(2,1)S(1)}, bf16[512,128]{1,0:T(8,128)(2,1)S(1)}, u32[]{:S(2)}, u32[]{:S(2)}) collective-permute-start(bf16[512,128]{1,0:T(8,128)(2,1)S(1)} %get-tuple-element.24), channel_id=1, source_target_pairs={{0,5},{1,4},{2,7},{3,6},{4,1},{5,0},{6,3},{7,2},{8,13},{9,12},{10,... | collective-permute-start | bytes 393224 | tf_op jit(solution)/shard_map/ppermute | solution.py:438
  66.2 20.2 %collective-permute-start.5 = (bf16[512,128]{1,0:T(8,128)(2,1)S(1)}, bf16[512,128]{1,0:T(8,128)(2,1)S(1)}, u32[]{:S(2)}, u32[]{:S(2)}) collective-permute-start(bf16[512,128]{1,0:T(8,128)(2,1)S(1)} %get-tuple-element.25), channel_id=1, source_target_pairs={{0,6},{1,7},{2,4},{3,5},{4,2},{5,3},{6,0},{7,1},{8,14},{9,15},{10,... | collective-permute-start | bytes 393224 | tf_op jit(solution)/shard_map/ppermute | solution.py:438
  68.4 20.1 %collective-permute-start.8 = (bf16[512,128]{1,0:T(8,128)(2,1)S(1)}, bf16[512,128]{1,0:T(8,128)(2,1)S(1)}, u32[]{:S(2)}, u32[]{:S(2)}) collective-permute-start(bf16[512,128]{1,0:T(8,128)(2,1)S(1)} %get-tuple-element.30), channel_id=1, source_target_pairs={{0,7},{1,6},{2,5},{3,4},{4,3},{5,2},{6,1},{7,0},{8,15},{9,14},{10,... | collective-permute-start | bytes 393224 | tf_op jit(solution)/shard_map/ppermute | solution.py:438

commit v13 on v12

--- a/solution.py
+++ b/solution.py
@@ -376,16 +376,17 @@
         deal(held, remainder(me ^ (first + s), half) * each, out_ref)
 
 
-def far_kernel(gathers, half, place_ref, state_ref, data_ref, plain, turned, *refs):
+def far_kernel(gathers, half, place_ref, state_ref, data_ref, plain, turned, sign_ref, *refs):
     *out_refs, turns, held = refs
     me = place_ref[1]
     prepare(gathers, place_ref[0], data_ref, plain, turned)
+    sign_ref[...] = plain[0, :TILE]
     other = (1 - quotient(me, half)) * held.shape[1]
     sum_offsets(gathers, other, state_ref, plain, turned, turns, held)
     deal_half(held, me, half, out_refs)
 
 
-def near_kernel(gathers, half, place_ref, state_ref, plain, turned, *refs):
+def near_kernel(gathers, half, place_ref, state_ref, plain, turned, _, *refs):
     *out_refs, turns, held = refs
     me = place_ref[1]
     own = quotient(me, half) * held.shape[1]
@@ -410,33 +411,33 @@
         bytes_accessed=8 * count * offsets,
         transcendentals=0,
     )
-    plain, turned, *far = pl.pallas_call(
+    sign = jax.ShapeDtypeStruct((TILE, lanes), jnp.bfloat16)
+    plain, turned, sign, *far = pl.pallas_call(
         functools.partial(far_kernel, gathers, half),
         in_specs=[smem, vmem, vmem],
-        out_specs=[vmem] * (2 + half),
-        out_shape=[spectra, spectra] + [block] * half,
+        out_specs=[vmem] * (3 + half),
+        out_shape=[spectra, spectra, sign] + [block] * half,
         scratch_shapes=scratch,
         compiler_params=pltpu.CompilerParams(vmem_limit_bytes=20 * MIB),
         cost_estimate=cost,
     )(place, state, data)
+    def swapped(part, s):
+        swaps = [(o, o ^ s) for o in range(offset_devices)]
+        return lax.ppermute(part, "offset", swaps)
+
+    far = [swapped(part, half + s) for s, part in enumerate(far)]
+    sign = swapped(sign, 1)
     near = pl.pallas_call(
         functools.partial(near_kernel, gathers, half),
-        in_specs=[smem, vmem, vmem, vmem],
+        in_specs=[smem, vmem, vmem, vmem, vmem],
         out_specs=[vmem] * half,
         out_shape=[block] * half,
         scratch_shapes=scratch,
         compiler_params=pltpu.CompilerParams(vmem_limit_bytes=20 * MIB),
         cost_estimate=cost,
-    )(place, state, plain, turned)
-    crossing = list(range(half, offset_devices))
-    order = crossing[:-1] + list(range(2, half)) + crossing[-1:] + list(range(min(2, half)))[::-1]
-    parts = list(near) + list(far)
-    blocks = []
-    for s in order:
-        part = parts[s]
-        swaps = [(o, o ^ s) for o in range(offset_devices)]
-        blocks.append(lax.ppermute(part, "offset", swaps) if s else part)
-    return order, blocks
+    )(place, state, plain, turned, sign)
+    near = [swapped(part, s) if s else part for s, part in enumerate(near)]
+    return list(range(half, offset_devices)) + list(range(half)), far + near
 
 
 def join_kernel(scale, order, place_ref, *refs):

time: 90.9 us -> 86.7 us (0.954)
  the two profiles are of different devices: /device:TPU:8 before, /device:TPU:0 now
where the time goes in v13:
time: 86.7 us; the launch traced here: 86.4 us
  waiting for transfers between devices  45 us (52%)
  starting transfers between devices  19 us (22%)
  Pallas kernels  17.6 us (20%)
  local copies, waits for them, and re-layouts  3.74 us (4%)
    all_to_all x1, waiting for transfers between devices, local(): data = lax.all_to_all(spectrum, ('freq', 'offset'), 0, 0, tiled=True)  23.6 us
    ppermute x8, waiting for transfers between devices, swapped(): return lax.ppermute(part, 'offset', swaps)  12.3 us
    ppermute x8, starting transfers between devices, swapped(): return lax.ppermute(part, 'offset', swaps)  9.98 us
    ppermute x3, waiting for transfers between devices, local(): series[s] = lax.ppermute(series[s], 'freq', swaps)  9.08 us
    all_to_all x1, starting transfers between devices, local(): data = lax.all_to_all(spectrum, ('freq', 'offset'), 0, 0, tiled=True)  5.88 us
    pallas_call x1, Pallas kernels, radon_swapped(): pl.pallas_call(functools.partial(far_kernel, gathers, half), in_specs=[sm...  3.99 us
    pallas_call x1, Pallas kernels, moveout(): pl.pallas_call(functools.partial(moveout_kernel, shift, total_time), grid...  3.43 us
    unnamed x10, local copies, waits for them, and re-layouts  3.42 us
  transfers between devices with their start and end apart: 12, of which 8 were waited for; matrix products, arithmetic and copies ran while one was open for 0% of the time, Pallas kernels for 8%

profile of v13, /device:TPU:0, one launch (start us, length us, event | category | flops | bytes accessed | tf_op | source)
XLA Modules:
  0.0 86.4 jit_solution(7095854229505304598)
XLA Ops:
  0.0 0.7 convert_element_type.24.slot_ref
  0.7 0.0 copy-start.2
  0.7 1.2 %copy-done.2 = bf16[1024,512]{1,0:T(8,128)(2,1)S(1)} copy-done((bf16[1024,512]{1,0:T(8,128)(2,1)S(1)}, bf16[1024,512]{1,0:T(8,128)(2,1)}, u32[]{:S(2)}) %copy-start.2) | copy-done | bytes 1048600
  1.9 2.0 %shard_map.56 = (bf16[256,512]{1,0:T(8,128)(2,1)S(1)}, bf16[256,512]{1,0:T(8,128)(2,1)S(1)}, bf16[256,512]{1,0:T(8,128)(2,1)S(1)}, bf16[256,512]{1,0:T(8,128)(2,1)S(1)}) custom-call(s32[1]{0:T(128)} %bitcast.5.me_ref, f32[32,32]{1,0:T(8,128)S(1)} %convert_element_type.24.slot_ref, bf16[1024,512]{1,0:T(8,128)(2,1)S(1)} %copy-done.2), custom_call_target="tpu_custom_call" | custom-call | tf_op jit(solution)/shard_map/pallas_call | solution.py:68
  3.9 0.5 collective-permute-start
  4.4 2.6 %collective-permute-start.1 = (bf16[256,512]{1,0:T(8,128)(2,1)S(1)}, bf16[256,512]{1,0:T(8,128)(2,1)S(1)}, u32[]{:S(2)}, u32[]{:S(2)}) collective-permute-start(bf16[256,512]{1,0:T(8,128)(2,1)S(1)} %get-tuple-element.22), channel_id=1, source_target_pairs={{0,16},{8,24},{16,0},{24,8},{1,17},{9,25},{17,1},{25,9},{2,18},{10... | collective-permute-start | bytes 786440 | tf_op jit(solution)/shard_map/ppermute | solution.py:529
  7.0 0.1 collective-permute-start.2
  7.1 0.0 collective-permute-done.refs_1_
  7.1 0.0 copy-start
  7.1 2.2 %copy-done = bf16[1024,2048]{1,0:T(8,128)(2,1)S(1)} copy-done((bf16[1024,2048]{1,0:T(8,128)(2,1)S(1)}, bf16[1024,2048]{1,0:T(8,128)(2,1)}, u32[]{:S(2)}) %copy-start) | copy-done | bytes 4194328
  9.3 0.0 copy-start.1
  9.3 0.9 %shard_map.57.begun_ref = f32[2,1024,256]{2,1,0:T(8,128)S(1)} custom-call(s32[1]{0:T(128)} %bitcast.5.me_ref, bf16[1024,2048]{1,0:T(8,128)(2,1)S(1)} %copy-done, bf16[256,512]{1,0:T(8,128)(2,1)S(1)} %get-tuple-element.20.refs_0_, bf16[256,512]{1,0:T(8,128)(2,1)S(1)} %collective-permute-done.refs_1_), custom_call_target="tpu_custom_call" | custom-call | flops 536870912 | bytes 4194304 | tf_op jit(solution)/shard_map/pallas_call | solution.py:185
  10.2 4.0 %collective-permute-done.1.refs_0_ = bf16[256,512]{1,0:T(8,128)(2,1)S(1)} collective-permute-done((bf16[256,512]{1,0:T(8,128)(2,1)S(1)}, bf16[256,512]{1,0:T(8,128)(2,1)S(1)}, u32[]{:S(2)}, u32[]{:S(2)}) %collective-permute-start.1) | collective-permute-done | bytes 262176 | tf_op jit(solution)/shard_map/ppermute | solution.py:529
  14.2 5.1 %collective-permute-done.2.refs_1_ = bf16[256,512]{1,0:T(8,128)(2,1)S(1)} collective-permute-done((bf16[256,512]{1,0:T(8,128)(2,1)S(1)}, bf16[256,512]{1,0:T(8,128)(2,1)S(1)}, u32[]{:S(2)}, u32[]{:S(2)}) %collective-permute-start.2) | collective-permute-done | bytes 262176 | tf_op jit(solution)/shard_map/ppermute | solution.py:529
  19.3 0.0 copy-done.1
  19.3 2.2 %shard_map.58 = bf16[32,8,16,128]{3,2,1,0:T(8,128)(2,1)} custom-call(s32[1]{0:T(128)} %bitcast.5.me_ref, bf16[1024,2048]{1,0:T(8,128)(2,1)S(1)} %copy-done.1, f32[2,1024,256]{2,1,0:T(8,128)S(1)} %shard_map.57.begun_ref, bf16[256,512]{1,0:T(8,128)(2,1)S(1)} %collective-permute-done.1.refs_0_, bf16[256,512]{1,0:T(8,128)(2,1)S(1)} %collective-permute-done.2.refs_1_), custom_call_target="tpu_custom_call" | custom-call | tf_op jit(solution)/shard_map/pallas_call | solution.py:198
  21.5 0.0 copy-start.3
  21.5 0.0 copy-start.4
  21.5 5.9 %all-to-all-start = ((bf16[32,8,16,128]{3,2,1,0:T(8,128)(2,1)}), bf16[32,8,16,128]{3,2,1,0:T(8,128)(2,1)S(1)}, u32[]{:S(2)}, u32[]{:S(2)}) async-start(bf16[32,8,16,128]{3,2,1,0:T(8,128)(2,1)} %shard_map.58), calls=%async_computation | async-start | bytes 2097152 | tf_op jit(solution)/shard_map/all_to_all | solution.py:532
  27.5 0.0 copy-done.3
  27.5 0.0 copy-done.4
  27.5 0.1 convert_element_type.21
  27.6 0.1 convert_element_type.23.offs_ref
  27.7 0.1 copy.7.slow_ref
  27.9 3.4 %shard_map.55.state_ref = f32[6,256,256]{2,1,0:T(8,128)S(1)} custom-call(f32[1]{0:T(128)} %bitcast.2.base_ref, f32[256,1]{1,0:T(8,128)S(1)} %copy.7.slow_ref, f32[1,256]{1,0:T(1,128)S(1)} %convert_element_type.23.offs_ref), custom_call_target="tpu_custom_call" | custom-call | flops 19660800 | bytes 1572864 | tf_op jit(solution)/shard_map/pallas_call | solution.py:235
  31.3 0.1 pad_add_fusion.place_ref
  31.4 23.6 %all-to-all-done.data_ref = bf16[32,8,16,128]{3,2,1,0:T(8,128)(2,1)S(1)} async-done(((bf16[32,8,16,128]{3,2,1,0:T(8,128)(2,1)}), bf16[32,8,16,128]{3,2,1,0:T(8,128)(2,1)S(1)}, u32[]{:S(2)}, u32[]{:S(2)}) %all-to-all-start) | async-done | bytes 1048608 | tf_op jit(solution)/shard_map/all_to_all | solution.py:532
  55.0 4.0 %shard_map.59 = (bf16[16,256,128]{2,1,0:T(8,128)(2,1)S(1)}, bf16[16,256,128]{2,1,0:T(8,128)(2,1)S(1)}, bf16[16,128]{1,0:T(8,128)(2,1)S(1)}, bf16[512,128]{1,0:T(...) custom-call(s32[2]{0:T(128)S(1)} %pad_add_fusion.place_ref, ...), custom_call_target="tpu_custom_call" | custom-call | flops 1073741824 | bytes 524288 | tf_op jit(solution)/shard_map/pallas_call | solution.py:415
  59.0 0.1 collective-permute-start.3
  59.1 3.0 %collective-permute-start.4 = (bf16[512,128]{1,0:T(8,128)(2,1)S(1)}, bf16[512,128]{1,0:T(8,128)(2,1)S(1)}, u32[]{:S(2)}, u32[]{:S(2)}) collective-permute-start(bf16[512,128]{1,0:T(8,128)(2,1)S(1)} %get-tuple-element.25), channel_id=1, source_target_pairs={{0,5},{1,4},{2,7},{3,6},{4,1},{5,0},{6,3},{7,2},{8,13},{9,12},{10,... | collective-permute-start | bytes 393224 | tf_op jit(solution)/shard_map/ppermute | solution.py:426
  62.1 1.4 %collective-permute-start.7 = (bf16[16,128]{1,0:T(8,128)(2,1)S(1)}, bf16[16,128]{1,0:T(8,128)(2,1)S(1)}, u32[]{:S(2)}, u32[]{:S(2)}) collective-permute-start(bf16[16,128]{1,0:T(8,128)(2,1)S(1)} %get-tuple-element.30), channel_id=1, source_target_pairs={{0,1},{1,0},{2,3},{3,2},{4,5},{5,4},{6,7},{7,6},{8,9},{9,8},{10,11... | collective-permute-start | bytes 12296 | tf_op jit(solution)/shard_map/ppermute | solution.py:426
  63.5 1.1 %collective-permute-start.5 = (bf16[512,128]{1,0:T(8,128)(2,1)S(1)}, bf16[512,128]{1,0:T(8,128)(2,1)S(1)}, u32[]{:S(2)}, u32[]{:S(2)}) collective-permute-start(bf16[512,128]{1,0:T(8,128)(2,1)S(1)} %get-tuple-element.26), channel_id=1, source_target_pairs={{0,6},{1,7},{2,4},{3,5},{4,2},{5,3},{6,0},{7,1},{8,14},{9,15},{10,... | collective-permute-start | bytes 393224 | tf_op jit(solution)/shard_map/ppermute | solution.py:426
  64.5 2.9 %collective-permute-start.6 = (bf16[512,128]{1,0:T(8,128)(2,1)S(1)}, bf16[512,128]{1,0:T(8,128)(2,1)S(1)}, u32[]{:S(2)}, u32[]{:S(2)}) collective-permute-start(bf16[512,128]{1,0:T(8,128)(2,1)S(1)} %get-tuple-element.27), channel_id=1, source_target_pairs={{0,7},{1,6},{2,5},{3,4},{4,3},{5,2},{6,1},{7,0},{8,15},{9,14},{10,... | collective-permute-start | bytes 393224 | tf_op jit(solution)/shard_map/ppermute | solution.py:426
  67.4 0.0 collective-permute-done.7._
  67.4 3.0 %shard_map.60 = (bf16[512,128]{1,0:T(8,128)(2,1)S(1)}, bf16[512,128]{1,0:T(8,128)(2,1)S(1)}, bf16[512,128]{1,0:T(8,128)(2,1)S(1)}, bf16[512,128]{1,0:T(8,128)(2,1)S(1)}) custom-call(s32[2]{0:T(128)S(1)} %pad_add_fusion.place_ref, f32[6,256,256]{2,1,0:T(8,128)S(1)} %shard_map.55.state_ref, bf16[16,256,128]{2,1,0:T(8,128)(2,1)S(1)} %get-tuple-element.28.plain, ...), custom_call_target="tpu_custom_call" | custom-call | flops 1073741824 | bytes 524288 | tf_op jit(solution)/shard_map/pallas_call | solution.py:430
  70.4 1.4 %collective-permute-start.8 = (bf16[512,128]{1,0:T(8,128)(2,1)S(1)}, bf16[512,128]{1,0:T(8,128)(2,1)S(1)}, u32[]{:S(2)}, u32[]{:S(2)}) collective-permute-start(bf16[512,128]{1,0:T(8,128)(2,1)S(1)} %get-tuple-element.32), channel_id=1, source_target_pairs={{0,1},{1,0},{2,3},{3,2},{4,5},{5,4},{6,7},{7,6},{8,9},{9,8},{10,11... | collective-permute-start | bytes 393224 | tf_op jit(solution)/shard_map/ppermute | solution.py:426
  71.8 5.0 %collective-permute-done.3.refs_0_ = bf16[512,128]{1,0:T(8,128)(2,1)S(1)} collective-permute-done((bf16[512,128]{1,0:T(8,128)(2,1)S(1)}, bf16[512,128]{1,0:T(8,128)(2,1)S(1)}, u32[]{:S(2)}, u32[]{:S(2)}) %collective-permute-start.3) | collective-permute-done | bytes 131104 | tf_op jit(solution)/shard_map/ppermute | solution.py:426
  76.8 0.0 collective-permute-start.9
  76.8 1.3 %collective-permute-done.4.refs_1_ = bf16[512,128]{1,0:T(8,128)(2,1)S(1)} collective-permute-done((bf16[512,128]{1,0:T(8,128)(2,1)S(1)}, bf16[512,128]{1,0:T(8,128)(2,1)S(1)}, u32[]{:S(2)}, u32[]{:S(2)}) %collective-permute-start.4) | collective-permute-done | bytes 131104 | tf_op jit(solution)/shard_map/ppermute | solution.py:426
  78.0 0.2 collective-permute-start.10
  78.2 0.0 collective-permute-done.5.refs_2_
  78.2 0.0 collective-permute-done.6.refs_3_
  78.2 0.4 collective-permute-done.8.refs_5_
  78.6 3.4 %collective-permute-done.9.refs_6_ = bf16[512,128]{1,0:T(8,128)(2,1)S(1)} collective-permute-done((bf16[512,128]{1,0:T(8,128)(2,1)S(1)}, bf16[512,128]{1,0:T(8,128)(2,1)S(1)}, u32[]{:S(2)}, u32[]{:S(2)}) %collective-permute-start.9) | collective-permute-done | bytes 131104 | tf_op jit(solution)/shard_map/ppermute | solution.py:426
  82.0 2.3 %collective-permute-done.10.refs_7_ = bf16[512,128]{1,0:T(8,128)(2,1)S(1)} collective-permute-done((bf16[512,128]{1,0:T(8,128)(2,1)S(1)}, bf16[512,128]{1,0:T(8,128)(2,1)S(1)}, u32[]{:S(2)}, u32[]{:S(2)}) %collective-permute-start.10) | collective-permute-done | bytes 131104 | tf_op jit(solution)/shard_map/ppermute | solution.py:426
  84.3 2.1 %shard_map.61 = f32[32,64,256]{2,1,0:T(8,128)} custom-call(s32[2]{0:T(128)S(1)} %pad_add_fusion.place_ref, bf16[512,128]{1,0:T(8,128)(2,1)S(1)} %collective-permute-done.3.refs_0_, bf16[512,128]{1,0:T(8,128)(2,1)S(1)} %collective-permute-done.4.refs_1_, bf16[512,128]{1,0:T(8,128)(2,1)S(1)} %collective-permute-done.5.refs_2_, ...), custom_call_target="tpu_custom_call" | custom-call | tf_op jit(solution)/shard_map/pallas_call | solution.py:473
  (3 shorter events, 0.0 us)
Async XLA Ops:
  0.7 1.2 %copy-start.2 = (bf16[1024,512]{1,0:T(8,128)(2,1)S(1)}, bf16[1024,512]{1,0:T(8,128)(2,1)}, u32[]{:S(2)}) copy-start(bf16[1024,512]{1,0:T(8,128)(2,1)} %raw_ref.1) | copy-start | bytes 3145732
  3.9 3.2 %collective-permute-start = (bf16[256,512]{1,0:T(8,128)(2,1)S(1)}, bf16[256,512]{1,0:T(8,128)(2,1)S(1)}, u32[]{:S(2)}, u32[]{:S(2)}) collective-permute-start(bf16[256,512]{1,0:T(8,128)(2,1)S(1)} %get-tuple-element.21), channel_id=1, source_target_pairs={{0,8},{8,0},{16,24},{24,16},{1,9},{9,1},{17,25},{25,17},{2,10},{10... | collective-permute-start | bytes 786440 | tf_op jit(solution)/shard_map/ppermute | solution.py:529
  4.4 9.8 %collective-permute-start.1 = (bf16[256,512]{1,0:T(8,128)(2,1)S(1)}, bf16[256,512]{1,0:T(8,128)(2,1)S(1)}, u32[]{:S(2)}, u32[]{:S(2)}) collective-permute-start(bf16[256,512]{1,0:T(8,128)(2,1)S(1)} %get-tuple-element.22), channel_id=1, source_target_pairs={{0,16},{8,24},{16,0},{24,8},{1,17},{9,25},{17,1},{25,9},{2,18},{10... | collective-permute-start | bytes 786440 | tf_op jit(solution)/shard_map/ppermute | solution.py:529
  7.0 12.3 %collective-permute-start.2 = (bf16[256,512]{1,0:T(8,128)(2,1)S(1)}, bf16[256,512]{1,0:T(8,128)(2,1)S(1)}, u32[]{:S(2)}, u32[]{:S(2)}) collective-permute-start(bf16[256,512]{1,0:T(8,128)(2,1)S(1)} %get-tuple-element.23), channel_id=1, source_target_pairs={{0,24},{8,16},{16,8},{24,0},{1,25},{9,17},{17,9},{25,1},{2,26},{10... | collective-permute-start | bytes 786440 | tf_op jit(solution)/shard_map/ppermute | solution.py:529
  7.1 2.2 %copy-start = (bf16[1024,2048]{1,0:T(8,128)(2,1)S(1)}, bf16[1024,2048]{1,0:T(8,128)(2,1)}, u32[]{:S(2)}) copy-start(bf16[1024,2048]{1,0:T(8,128)(2,1)} %constant.34.clone.table_ref) | copy-start | bytes 12582916
  9.3 10.0 %copy-start.1 = (bf16[1024,2048]{1,0:T(8,128)(2,1)S(1)}, bf16[1024,2048]{1,0:T(8,128)(2,1)}, u32[]{:S(2)}) copy-start(bf16[1024,2048]{1,0:T(8,128)(2,1)} %constant.34.clone.table_ref) | copy-start | bytes 12582916
  21.5 5.9 %copy-start.3 = (s32[256]{0:T(256)S(1)}, s32[256]{0:T(256)}, u32[]{:S(2)}) copy-start(s32[256]{0:T(256)} %param.7) | copy-start | bytes 3076
  21.5 5.9 %copy-start.4 = (s32[256]{0:T(256)S(1)}, s32[256]{0:T(256)}, u32[]{:S(2)}) copy-start(s32[256]{0:T(256)} %param.8) | copy-start | bytes 3076
  21.5 33.5 %all-to-all-start = ((bf16[32,8,16,128]{3,2,1,0:T(8,128)(2,1)}), bf16[32,8,16,128]{3,2,1,0:T(8,128)(2,1)S(1)}, u32[]{:S(2)}, u32[]{:S(2)}) async-start(bf16[32,8,16,128]{3,2,1,0:T(8,128)(2,1)} %shard_map.58), calls=%async_computation | async-start | bytes 2097152 | tf_op jit(solution)/shard_map/all_to_all | solution.py:532
  59.0 17.8 %collective-permute-start.3 = (bf16[512,128]{1,0:T(8,128)(2,1)S(1)}, bf16[512,128]{1,0:T(8,128)(2,1)S(1)}, u32[]{:S(2)}, u32[]{:S(2)}) collective-permute-start(bf16[512,128]{1,0:T(8,128)(2,1)S(1)} %get-tuple-element.24), channel_id=1, source_target_pairs={{0,4},{1,5},{2,6},{3,7},{4,0},{5,1},{6,2},{7,3},{8,12},{9,13},{10,... | collective-permute-start | bytes 393224 | tf_op jit(solution)/shard_map/ppermute | solution.py:426
  59.1 18.9 %collective-permute-start.4 = (bf16[512,128]{1,0:T(8,128)(2,1)S(1)}, bf16[512,128]{1,0:T(8,128)(2,1)S(1)}, u32[]{:S(2)}, u32[]{:S(2)}) collective-permute-start(bf16[512,128]{1,0:T(8,128)(2,1)S(1)} %get-tuple-element.25), channel_id=1, source_target_pairs={{0,5},{1,4},{2,7},{3,6},{4,1},{5,0},{6,3},{7,2},{8,13},{9,12},{10,... | collective-permute-start | bytes 393224 | tf_op jit(solution)/shard_map/ppermute | solution.py:426
  62.1 5.3 %collective-permute-start.7 = (bf16[16,128]{1,0:T(8,128)(2,1)S(1)}, bf16[16,128]{1,0:T(8,128)(2,1)S(1)}, u32[]{:S(2)}, u32[]{:S(2)}) collective-permute-start(bf16[16,128]{1,0:T(8,128)(2,1)S(1)} %get-tuple-element.30), channel_id=1, source_target_pairs={{0,1},{1,0},{2,3},{3,2},{4,5},{5,4},{6,7},{7,6},{8,9},{9,8},{10,11... | collective-permute-start | bytes 12296 | tf_op jit(solution)/shard_map/ppermute | solution.py:426
  63.5 14.7 %collective-permute-start.5 = (bf16[512,128]{1,0:T(8,128)(2,1)S(1)}, bf16[512,128]{1,0:T(8,128)(2,1)S(1)}, u32[]{:S(2)}, u32[]{:S(2)}) collective-permute-start(bf16[512,128]{1,0:T(8,128)(2,1)S(1)} %get-tuple-element.26), channel_id=1, source_target_pairs={{0,6},{1,7},{2,4},{3,5},{4,2},{5,3},{6,0},{7,1},{8,14},{9,15},{10,... | collective-permute-start | bytes 393224 | tf_op jit(solution)/shard_map/ppermute | solution.py:426
  64.5 13.7 %collective-permute-start.6 = (bf16[512,128]{1,0:T(8,128)(2,1)S(1)}, bf16[512,128]{1,0:T(8,128)(2,1)S(1)}, u32[]{:S(2)}, u32[]{:S(2)}) collective-permute-start(bf16[512,128]{1,0:T(8,128)(2,1)S(1)} %get-tuple-element.27), channel_id=1, source_target_pairs={{0,7},{1,6},{2,5},{3,4},{4,3},{5,2},{6,1},{7,0},{8,15},{9,14},{10,... | collective-permute-start | bytes 393224 | tf_op jit(solution)/shard_map/ppermute | solution.py:426
  70.4 8.2 %collective-permute-start.8 = (bf16[512,128]{1,0:T(8,128)(2,1)S(1)}, bf16[512,128]{1,0:T(8,128)(2,1)S(1)}, u32[]{:S(2)}, u32[]{:S(2)}) collective-permute-start(bf16[512,128]{1,0:T(8,128)(2,1)S(1)} %get-tuple-element.32), channel_id=1, source_target_pairs={{0,1},{1,0},{2,3},{3,2},{4,5},{5,4},{6,7},{7,6},{8,9},{9,8},{10,11... | collective-permute-start | bytes 393224 | tf_op jit(solution)/shard_map/ppermute | solution.py:426
  76.8 5.2 %collective-permute-start.9 = (bf16[512,128]{1,0:T(8,128)(2,1)S(1)}, bf16[512,128]{1,0:T(8,128)(2,1)S(1)}, u32[]{:S(2)}, u32[]{:S(2)}) collective-permute-start(bf16[512,128]{1,0:T(8,128)(2,1)S(1)} %get-tuple-element.33), channel_id=1, source_target_pairs={{0,2},{1,3},{2,0},{3,1},{4,6},{5,7},{6,4},{7,5},{8,10},{9,11},{10,... | collective-permute-start | bytes 393224 | tf_op jit(solution)/shard_map/ppermute | solution.py:426
  78.0 6.2 %collective-permute-start.10 = (bf16[512,128]{1,0:T(8,128)(2,1)S(1)}, bf16[512,128]{1,0:T(8,128)(2,1)S(1)}, u32[]{:S(2)}, u32[]{:S(2)}) collective-permute-start(bf16[512,128]{1,0:T(8,128)(2,1)S(1)} %get-tuple-element.34), channel_id=1, source_target_pairs={{0,3},{1,2},{2,1},{3,0},{4,7},{5,6},{6,5},{7,4},{8,11},{9,10},{10,... | collective-permute-start | bytes 393224 | tf_op jit(solution)/shard_map/ppermute | solution.py:426

commit v14 on v13

--- a/solution.py
+++ b/solution.py
@@ -425,7 +425,7 @@
         swaps = [(o, o ^ s) for o in range(offset_devices)]
         return lax.ppermute(part, "offset", swaps)
 
-    far = [swapped(part, half + s) for s, part in enumerate(far)]
+    far[:-1] = [swapped(part, half + s) for s, part in enumerate(far[:-1])]
     sign = swapped(sign, 1)
     near = pl.pallas_call(
         functools.partial(near_kernel, gathers, half),
@@ -436,8 +436,12 @@
         compiler_params=pltpu.CompilerParams(vmem_limit_bytes=20 * MIB),
         cost_estimate=cost,
     )(place, state, plain, turned, sign)
+    near = list(near)
+    last, far[0] = lax.optimization_barrier((far[-1], far[0]))
     near = [swapped(part, s) if s else part for s, part in enumerate(near)]
-    return list(range(half, offset_devices)) + list(range(half)), far + near
+    far[-1] = swapped(last, offset_devices - 1)
+    parts = near + far
+    return list(range(half, offset_devices - 1)) + list(range(half))[::-1] + [offset_devices - 1], [parts[s] for s in list(range(half, offset_devices - 1)) + list(range(half))[::-1] + [offset_devices - 1]]
 
 
 def join_kernel(scale, order, place_ref, *refs):

time: 86.7 us -> 87.2 us (level)
  starting transfers between devices: 19 us -> 20.8 us
  waiting for transfers between devices: 45 us -> 43.7 us
    ppermute x8, starting transfers between devices: 9.98 us -> 11.8 us  [swapped(): return lax.ppermute(part, 'offset', swaps)]
    ppermute x8, waiting for transfers between devices: 12.3 us -> 11 us  [swapped(): return lax.ppermute(part, 'offset', swaps)]
  transfers between devices with their start and end apart: 12 -> 12, of which waited for: 8 -> 7; matrix products, arithmetic and copies ran while one was open for 0% -> 0% of each run, Pallas kernels for 8% -> 8%
where the time goes in v14:
time: 87.2 us; the launch traced here: 86.9 us
  waiting for transfers between devices  43.7 us (50%)
  starting transfers between devices  20.8 us (24%)
  Pallas kernels  17.6 us (20%)
  local copies, waits for them, and re-layouts  3.74 us (4%)
    all_to_all x1, waiting for transfers between devices, local(): data = lax.all_to_all(spectrum, ('freq', 'offset'), 0, 0, tiled=True)  23.6 us
    ppermute x8, starting transfers between devices, swapped(): return lax.ppermute(part, 'offset', swaps)  11.8 us
    ppermute x8, waiting for transfers between devices, swapped(): return lax.ppermute(part, 'offset', swaps)  11 us
    ppermute x3, waiting for transfers between devices, local(): series[s] = lax.ppermute(series[s], 'freq', swaps)  9.08 us
    all_to_all x1, starting transfers between devices, local(): data = lax.all_to_all(spectrum, ('freq', 'offset'), 0, 0, tiled=True)  5.88 us
    pallas_call x1, Pallas kernels, radon_swapped(): pl.pallas_call(functools.partial(far_kernel, gathers, half), in_specs=[sm...  3.99 us
    pallas_call x1, Pallas kernels, moveout(): pl.pallas_call(functools.partial(moveout_kernel, shift, total_time), grid...  3.43 us
    unnamed x10, local copies, waits for them, and re-layouts  3.42 us
  transfers between devices with their start and end apart: 12, of which 7 were waited for; matrix products, arithmetic and copies ran while one was open for 0% of the time, Pallas kernels for 8%

profile of v14, /device:TPU:0, one launch (start us, length us, event | category | flops | bytes accessed | tf_op | source)
XLA Modules:
  0.0 86.9 jit_solution(10605095668238038432)
XLA Ops:
  0.0 0.7 convert_element_type.24.slot_ref
  0.7 0.0 copy-start.2
  0.7 1.2 %copy-done.2 = bf16[1024,512]{1,0:T(8,128)(2,1)S(1)} copy-done((bf16[1024,512]{1,0:T(8,128)(2,1)S(1)}, bf16[1024,512]{1,0:T(8,128)(2,1)}, u32[]{:S(2)}) %copy-start.2) | copy-done | bytes 1048600
  1.9 2.0 %shard_map.56 = (bf16[256,512]{1,0:T(8,128)(2,1)S(1)}, bf16[256,512]{1,0:T(8,128)(2,1)S(1)}, bf16[256,512]{1,0:T(8,128)(2,1)S(1)}, bf16[256,512]{1,0:T(8,128)(2,1)S(1)}) custom-call(s32[1]{0:T(128)} %bitcast.5.me_ref, f32[32,32]{1,0:T(8,128)S(1)} %convert_element_type.24.slot_ref, bf16[1024,512]{1,0:T(8,128)(2,1)S(1)} %copy-done.2), custom_call_target="tpu_custom_call" | custom-call | tf_op jit(solution)/shard_map/pallas_call | solution.py:68
  3.9 0.5 collective-permute-start
  4.4 2.6 %collective-permute-start.1 = (bf16[256,512]{1,0:T(8,128)(2,1)S(1)}, bf16[256,512]{1,0:T(8,128)(2,1)S(1)}, u32[]{:S(2)}, u32[]{:S(2)}) collective-permute-start(bf16[256,512]{1,0:T(8,128)(2,1)S(1)} %get-tuple-element.24), channel_id=1, source_target_pairs={{0,16},{8,24},{16,0},{24,8},{1,17},{9,25},{17,1},{25,9},{2,18},{10... | collective-permute-start | bytes 786440 | tf_op jit(solution)/shard_map/ppermute | solution.py:533
  7.0 0.1 collective-permute-start.2
  7.1 0.0 collective-permute-done.refs_1_
  7.1 0.0 copy-start
  7.1 2.2 %copy-done = bf16[1024,2048]{1,0:T(8,128)(2,1)S(1)} copy-done((bf16[1024,2048]{1,0:T(8,128)(2,1)S(1)}, bf16[1024,2048]{1,0:T(8,128)(2,1)}, u32[]{:S(2)}) %copy-start) | copy-done | bytes 4194328
  9.3 0.0 copy-start.1
  9.3 0.9 %shard_map.57.begun_ref = f32[2,1024,256]{2,1,0:T(8,128)S(1)} custom-call(s32[1]{0:T(128)} %bitcast.5.me_ref, bf16[1024,2048]{1,0:T(8,128)(2,1)S(1)} %copy-done, bf16[256,512]{1,0:T(8,128)(2,1)S(1)} %get-tuple-element.22.refs_0_, bf16[256,512]{1,0:T(8,128)(2,1)S(1)} %collective-permute-done.refs_1_), custom_call_target="tpu_custom_call" | custom-call | flops 536870912 | bytes 4194304 | tf_op jit(solution)/shard_map/pallas_call | solution.py:185
  10.2 4.0 %collective-permute-done.1.refs_0_ = bf16[256,512]{1,0:T(8,128)(2,1)S(1)} collective-permute-done((bf16[256,512]{1,0:T(8,128)(2,1)S(1)}, bf16[256,512]{1,0:T(8,128)(2,1)S(1)}, u32[]{:S(2)}, u32[]{:S(2)}) %collective-permute-start.1) | collective-permute-done | bytes 262176 | tf_op jit(solution)/shard_map/ppermute | solution.py:533
  14.2 5.1 %collective-permute-done.2.refs_1_ = bf16[256,512]{1,0:T(8,128)(2,1)S(1)} collective-permute-done((bf16[256,512]{1,0:T(8,128)(2,1)S(1)}, bf16[256,512]{1,0:T(8,128)(2,1)S(1)}, u32[]{:S(2)}, u32[]{:S(2)}) %collective-permute-start.2) | collective-permute-done | bytes 262176 | tf_op jit(solution)/shard_map/ppermute | solution.py:533
  19.3 0.0 copy-done.1
  19.3 2.2 %shard_map.58 = bf16[32,8,16,128]{3,2,1,0:T(8,128)(2,1)} custom-call(s32[1]{0:T(128)} %bitcast.5.me_ref, bf16[1024,2048]{1,0:T(8,128)(2,1)S(1)} %copy-done.1, f32[2,1024,256]{2,1,0:T(8,128)S(1)} %shard_map.57.begun_ref, bf16[256,512]{1,0:T(8,128)(2,1)S(1)} %collective-permute-done.1.refs_0_, bf16[256,512]{1,0:T(8,128)(2,1)S(1)} %collective-permute-done.2.refs_1_), custom_call_target="tpu_custom_call" | custom-call | tf_op jit(solution)/shard_map/pallas_call | solution.py:198
  21.5 0.0 copy-start.3
  21.5 0.0 copy-start.4
  21.5 5.9 %all-to-all-start = ((bf16[32,8,16,128]{3,2,1,0:T(8,128)(2,1)}), bf16[32,8,16,128]{3,2,1,0:T(8,128)(2,1)S(1)}, u32[]{:S(2)}, u32[]{:S(2)}) async-start(bf16[32,8,16,128]{3,2,1,0:T(8,128)(2,1)} %shard_map.58), calls=%async_computation | async-start | bytes 2097152 | tf_op jit(solution)/shard_map/all_to_all | solution.py:536
  27.5 0.0 copy-done.3
  27.5 0.0 copy-done.4
  27.5 0.1 convert_element_type.21
  27.6 0.1 convert_element_type.23.offs_ref
  27.7 0.1 copy.7.slow_ref
  27.9 3.4 %shard_map.55.state_ref = f32[6,256,256]{2,1,0:T(8,128)S(1)} custom-call(f32[1]{0:T(128)} %bitcast.2.base_ref, f32[256,1]{1,0:T(8,128)S(1)} %copy.7.slow_ref, f32[1,256]{1,0:T(1,128)S(1)} %convert_element_type.23.offs_ref), custom_call_target="tpu_custom_call" | custom-call | flops 19660800 | bytes 1572864 | tf_op jit(solution)/shard_map/pallas_call | solution.py:235
  31.3 0.1 pad_add_fusion.place_ref
  31.4 23.6 %all-to-all-done.data_ref = bf16[32,8,16,128]{3,2,1,0:T(8,128)(2,1)S(1)} async-done(((bf16[32,8,16,128]{3,2,1,0:T(8,128)(2,1)}), bf16[32,8,16,128]{3,2,1,0:T(8,128)(2,1)S(1)}, u32[]{:S(2)}, u32[]{:S(2)}) %all-to-all-start) | async-done | bytes 1048608 | tf_op jit(solution)/shard_map/all_to_all | solution.py:536
  55.0 4.0 %shard_map.59 = (bf16[16,256,128]{2,1,0:T(8,128)(2,1)S(1)}, bf16[16,256,128]{2,1,0:T(8,128)(2,1)S(1)}, bf16[16,128]{1,0:T(8,128)(2,1)S(1)}, bf16[512,128]{1,0:T(...) custom-call(s32[2]{0:T(128)S(1)} %pad_add_fusion.place_ref, ...), custom_call_target="tpu_custom_call" | custom-call | flops 1073741824 | bytes 524288 | tf_op jit(solution)/shard_map/pallas_call | solution.py:415
  59.0 0.1 collective-permute-start.3
  59.1 3.0 %collective-permute-start.4 = (bf16[512,128]{1,0:T(8,128)(2,1)S(1)}, bf16[512,128]{1,0:T(8,128)(2,1)S(1)}, u32[]{:S(2)}, u32[]{:S(2)}) collective-permute-start(bf16[512,128]{1,0:T(8,128)(2,1)S(1)} %get-tuple-element.29), channel_id=1, source_target_pairs={{0,5},{1,4},{2,7},{3,6},{4,1},{5,0},{6,3},{7,2},{8,13},{9,12},{10,... | collective-permute-start | bytes 393224 | tf_op jit(solution)/shard_map/ppermute | solution.py:426
  62.1 1.4 %collective-permute-start.6 = (bf16[16,128]{1,0:T(8,128)(2,1)S(1)}, bf16[16,128]{1,0:T(8,128)(2,1)S(1)}, u32[]{:S(2)}, u32[]{:S(2)}) collective-permute-start(bf16[16,128]{1,0:T(8,128)(2,1)S(1)} %get-tuple-element.33), channel_id=1, source_target_pairs={{0,1},{1,0},{2,3},{3,2},{4,5},{5,4},{6,7},{7,6},{8,9},{9,8},{10,11... | collective-permute-start | bytes 12296 | tf_op jit(solution)/shard_map/ppermute | solution.py:426
  63.5 1.1 %collective-permute-start.5 = (bf16[512,128]{1,0:T(8,128)(2,1)S(1)}, bf16[512,128]{1,0:T(8,128)(2,1)S(1)}, u32[]{:S(2)}, u32[]{:S(2)}) collective-permute-start(bf16[512,128]{1,0:T(8,128)(2,1)S(1)} %get-tuple-element.30), channel_id=1, source_target_pairs={{0,6},{1,7},{2,4},{3,5},{4,2},{5,3},{6,0},{7,1},{8,14},{9,15},{10,... | collective-permute-start | bytes 393224 | tf_op jit(solution)/shard_map/ppermute | solution.py:426
  64.5 1.2 %collective-permute-done.6._ = bf16[16,128]{1,0:T(8,128)(2,1)S(1)} collective-permute-done((bf16[16,128]{1,0:T(8,128)(2,1)S(1)}, bf16[16,128]{1,0:T(8,128)(2,1)S(1)}, u32[]{:S(2)}, u32[]{:S(2)}) %collective-permute-start.6) | collective-permute-done | bytes 4128 | tf_op jit(solution)/shard_map/ppermute | solution.py:426
  65.7 3.0 %shard_map.60 = (bf16[512,128]{1,0:T(8,128)(2,1)S(1)}, bf16[512,128]{1,0:T(8,128)(2,1)S(1)}, bf16[512,128]{1,0:T(8,128)(2,1)S(1)}, bf16[512,128]{1,0:T(8,128)(2,1)S(1)}) custom-call(s32[2]{0:T(128)S(1)} %pad_add_fusion.place_ref, f32[6,256,256]{2,1,0:T(8,128)S(1)} %shard_map.55.state_ref, bf16[16,256,128]{2,1,0:T(8,128)(2,1)S(1)} %get-tuple-element.31.plain, ...), custom_call_target="tpu_custom_call" | custom-call | flops 1073741824 | bytes 524288 | tf_op jit(solution)/shard_map/pallas_call | solution.py:430
  68.7 1.0 %collective-permute-start.7 = (bf16[512,128]{1,0:T(8,128)(2,1)S(1)}, bf16[512,128]{1,0:T(8,128)(2,1)S(1)}, u32[]{:S(2)}, u32[]{:S(2)}) collective-permute-start(bf16[512,128]{1,0:T(8,128)(2,1)S(1)} %get-tuple-element.34), channel_id=1, source_target_pairs={{0,3},{1,2},{2,1},{3,0},{4,7},{5,6},{6,5},{7,4},{8,11},{9,10},{10,... | collective-permute-start | bytes 393224 | tf_op jit(solution)/shard_map/ppermute | solution.py:426
  69.7 1.9 %collective-permute-start.8 = (bf16[512,128]{1,0:T(8,128)(2,1)S(1)}, bf16[512,128]{1,0:T(8,128)(2,1)S(1)}, u32[]{:S(2)}, u32[]{:S(2)}) collective-permute-start(bf16[512,128]{1,0:T(8,128)(2,1)S(1)} %get-tuple-element.35), channel_id=1, source_target_pairs={{0,2},{1,3},{2,0},{3,1},{4,6},{5,7},{6,4},{7,5},{8,10},{9,11},{10,... | collective-permute-start | bytes 393224 | tf_op jit(solution)/shard_map/ppermute | solution.py:426
  71.6 2.4 %collective-permute-done.3.refs_0_ = bf16[512,128]{1,0:T(8,128)(2,1)S(1)} collective-permute-done((bf16[512,128]{1,0:T(8,128)(2,1)S(1)}, bf16[512,128]{1,0:T(8,128)(2,1)S(1)}, u32[]{:S(2)}, u32[]{:S(2)}) %collective-permute-start.3) | collective-permute-done | bytes 131104 | tf_op jit(solution)/shard_map/ppermute | solution.py:426
  74.0 0.0 collective-permute-start.9
  74.0 1.2 %collective-permute-done.4.refs_1_ = bf16[512,128]{1,0:T(8,128)(2,1)S(1)} collective-permute-done((bf16[512,128]{1,0:T(8,128)(2,1)S(1)}, bf16[512,128]{1,0:T(8,128)(2,1)S(1)}, u32[]{:S(2)}, u32[]{:S(2)}) %collective-permute-start.4) | collective-permute-done | bytes 131104 | tf_op jit(solution)/shard_map/ppermute | solution.py:426
  75.2 3.4 %collective-permute-start.10 = (bf16[512,128]{1,0:T(8,128)(2,1)S(1)}, bf16[512,128]{1,0:T(8,128)(2,1)S(1)}, u32[]{:S(2)}, u32[]{:S(2)}) collective-permute-start(bf16[512,128]{1,0:T(8,128)(2,1)S(1)} %get-tuple-element.38), channel_id=1, source_target_pairs={{0,7},{1,6},{2,5},{3,4},{4,3},{5,2},{6,1},{7,0},{8,15},{9,14},{10,... | collective-permute-start | bytes 393224 | tf_op jit(solution)/shard_map/ppermute | solution.py:426
  78.6 0.0 collective-permute-done.5.refs_2_
  78.6 0.0 collective-permute-done.7.refs_3_
  78.6 6.2 %collective-permute-done.8.refs_4_ = bf16[512,128]{1,0:T(8,128)(2,1)S(1)} collective-permute-done((bf16[512,128]{1,0:T(8,128)(2,1)S(1)}, bf16[512,128]{1,0:T(8,128)(2,1)S(1)}, u32[]{:S(2)}, u32[]{:S(2)}) %collective-permute-start.8) | collective-permute-done | bytes 131104 | tf_op jit(solution)/shard_map/ppermute | solution.py:426
  84.8 0.0 collective-permute-done.9.refs_5_
  84.8 0.0 collective-permute-done.10.refs_7_
  84.8 2.1 %shard_map.61 = f32[32,64,256]{2,1,0:T(8,128)} custom-call(s32[2]{0:T(128)S(1)} %pad_add_fusion.place_ref, bf16[512,128]{1,0:T(8,128)(2,1)S(1)} %collective-permute-done.3.refs_0_, bf16[512,128]{1,0:T(8,128)(2,1)S(1)} %collective-permute-done.4.refs_1_, bf16[512,128]{1,0:T(8,128)(2,1)S(1)} %collective-permute-done.5.refs_2_, ...), custom_call_target="tpu_custom_call" | custom-call | tf_op jit(solution)/shard_map/pallas_call | solution.py:477
  (3 shorter events, 0.0 us)
Async XLA Ops:
  0.7 1.2 %copy-start.2 = (bf16[1024,512]{1,0:T(8,128)(2,1)S(1)}, bf16[1024,512]{1,0:T(8,128)(2,1)}, u32[]{:S(2)}) copy-start(bf16[1024,512]{1,0:T(8,128)(2,1)} %raw_ref.1) | copy-start | bytes 3145732
  3.9 3.2 %collective-permute-start = (bf16[256,512]{1,0:T(8,128)(2,1)S(1)}, bf16[256,512]{1,0:T(8,128)(2,1)S(1)}, u32[]{:S(2)}, u32[]{:S(2)}) collective-permute-start(bf16[256,512]{1,0:T(8,128)(2,1)S(1)} %get-tuple-element.23), channel_id=1, source_target_pairs={{0,8},{8,0},{16,24},{24,16},{1,9},{9,1},{17,25},{25,17},{2,10},{10... | collective-permute-start | bytes 786440 | tf_op jit(solution)/shard_map/ppermute | solution.py:533
  4.4 9.8 %collective-permute-start.1 = (bf16[256,512]{1,0:T(8,128)(2,1)S(1)}, bf16[256,512]{1,0:T(8,128)(2,1)S(1)}, u32[]{:S(2)}, u32[]{:S(2)}) collective-permute-start(bf16[256,512]{1,0:T(8,128)(2,1)S(1)} %get-tuple-element.24), channel_id=1, source_target_pairs={{0,16},{8,24},{16,0},{24,8},{1,17},{9,25},{17,1},{25,9},{2,18},{10... | collective-permute-start | bytes 786440 | tf_op jit(solution)/shard_map/ppermute | solution.py:533
  7.0 12.3 %collective-permute-start.2 = (bf16[256,512]{1,0:T(8,128)(2,1)S(1)}, bf16[256,512]{1,0:T(8,128)(2,1)S(1)}, u32[]{:S(2)}, u32[]{:S(2)}) collective-permute-start(bf16[256,512]{1,0:T(8,128)(2,1)S(1)} %get-tuple-element.25), channel_id=1, source_target_pairs={{0,24},{8,16},{16,8},{24,0},{1,25},{9,17},{17,9},{25,1},{2,26},{10... | collective-permute-start | bytes 786440 | tf_op jit(solution)/shard_map/ppermute | solution.py:533
  7.1 2.2 %copy-start = (bf16[1024,2048]{1,0:T(8,128)(2,1)S(1)}, bf16[1024,2048]{1,0:T(8,128)(2,1)}, u32[]{:S(2)}) copy-start(bf16[1024,2048]{1,0:T(8,128)(2,1)} %constant.34.clone.table_ref) | copy-start | bytes 12582916
  9.3 10.0 %copy-start.1 = (bf16[1024,2048]{1,0:T(8,128)(2,1)S(1)}, bf16[1024,2048]{1,0:T(8,128)(2,1)}, u32[]{:S(2)}) copy-start(bf16[1024,2048]{1,0:T(8,128)(2,1)} %constant.34.clone.table_ref) | copy-start | bytes 12582916
  21.5 5.9 %copy-start.3 = (s32[256]{0:T(256)S(1)}, s32[256]{0:T(256)}, u32[]{:S(2)}) copy-start(s32[256]{0:T(256)} %param.7) | copy-start | bytes 3076
  21.5 5.9 %copy-start.4 = (s32[256]{0:T(256)S(1)}, s32[256]{0:T(256)}, u32[]{:S(2)}) copy-start(s32[256]{0:T(256)} %param.8) | copy-start | bytes 3076
  21.5 33.5 %all-to-all-start = ((bf16[32,8,16,128]{3,2,1,0:T(8,128)(2,1)}), bf16[32,8,16,128]{3,2,1,0:T(8,128)(2,1)S(1)}, u32[]{:S(2)}, u32[]{:S(2)}) async-start(bf16[32,8,16,128]{3,2,1,0:T(8,128)(2,1)} %shard_map.58), calls=%async_computation | async-start | bytes 2097152 | tf_op jit(solution)/shard_map/all_to_all | solution.py:536
  59.0 15.0 %collective-permute-start.3 = (bf16[512,128]{1,0:T(8,128)(2,1)S(1)}, bf16[512,128]{1,0:T(8,128)(2,1)S(1)}, u32[]{:S(2)}, u32[]{:S(2)}) collective-permute-start(bf16[512,128]{1,0:T(8,128)(2,1)S(1)} %get-tuple-element.27), channel_id=1, source_target_pairs={{0,4},{1,5},{2,6},{3,7},{4,0},{5,1},{6,2},{7,3},{8,12},{9,13},{10,... | collective-permute-start | bytes 393224 | tf_op jit(solution)/shard_map/ppermute | solution.py:426
  59.1 16.1 %collective-permute-start.4 = (bf16[512,128]{1,0:T(8,128)(2,1)S(1)}, bf16[512,128]{1,0:T(8,128)(2,1)S(1)}, u32[]{:S(2)}, u32[]{:S(2)}) collective-permute-start(bf16[512,128]{1,0:T(8,128)(2,1)S(1)} %get-tuple-element.29), channel_id=1, source_target_pairs={{0,5},{1,4},{2,7},{3,6},{4,1},{5,0},{6,3},{7,2},{8,13},{9,12},{10,... | collective-permute-start | bytes 393224 | tf_op jit(solution)/shard_map/ppermute | solution.py:426
  62.1 3.6 %collective-permute-start.6 = (bf16[16,128]{1,0:T(8,128)(2,1)S(1)}, bf16[16,128]{1,0:T(8,128)(2,1)S(1)}, u32[]{:S(2)}, u32[]{:S(2)}) collective-permute-start(bf16[16,128]{1,0:T(8,128)(2,1)S(1)} %get-tuple-element.33), channel_id=1, source_target_pairs={{0,1},{1,0},{2,3},{3,2},{4,5},{5,4},{6,7},{7,6},{8,9},{9,8},{10,11... | collective-permute-start | bytes 12296 | tf_op jit(solution)/shard_map/ppermute | solution.py:426
  63.5 15.1 %collective-permute-start.5 = (bf16[512,128]{1,0:T(8,128)(2,1)S(1)}, bf16[512,128]{1,0:T(8,128)(2,1)S(1)}, u32[]{:S(2)}, u32[]{:S(2)}) collective-permute-start(bf16[512,128]{1,0:T(8,128)(2,1)S(1)} %get-tuple-element.30), channel_id=1, source_target_pairs={{0,6},{1,7},{2,4},{3,5},{4,2},{5,3},{6,0},{7,1},{8,14},{9,15},{10,... | collective-permute-start | bytes 393224 | tf_op jit(solution)/shard_map/ppermute | solution.py:426
  68.7 9.9 %collective-permute-start.7 = (bf16[512,128]{1,0:T(8,128)(2,1)S(1)}, bf16[512,128]{1,0:T(8,128)(2,1)S(1)}, u32[]{:S(2)}, u32[]{:S(2)}) collective-permute-start(bf16[512,128]{1,0:T(8,128)(2,1)S(1)} %get-tuple-element.34), channel_id=1, source_target_pairs={{0,3},{1,2},{2,1},{3,0},{4,7},{5,6},{6,5},{7,4},{8,11},{9,10},{10,... | collective-permute-start | bytes 393224 | tf_op jit(solution)/shard_map/ppermute | solution.py:426
  69.7 15.1 %collective-permute-start.8 = (bf16[512,128]{1,0:T(8,128)(2,1)S(1)}, bf16[512,128]{1,0:T(8,128)(2,1)S(1)}, u32[]{:S(2)}, u32[]{:S(2)}) collective-permute-start(bf16[512,128]{1,0:T(8,128)(2,1)S(1)} %get-tuple-element.35), channel_id=1, source_target_pairs={{0,2},{1,3},{2,0},{3,1},{4,6},{5,7},{6,4},{7,5},{8,10},{9,11},{10,... | collective-permute-start | bytes 393224 | tf_op jit(solution)/shard_map/ppermute | solution.py:426
  74.0 10.7 %collective-permute-start.9 = (bf16[512,128]{1,0:T(8,128)(2,1)S(1)}, bf16[512,128]{1,0:T(8,128)(2,1)S(1)}, u32[]{:S(2)}, u32[]{:S(2)}) collective-permute-start(bf16[512,128]{1,0:T(8,128)(2,1)S(1)} %get-tuple-element.36), channel_id=1, source_target_pairs={{0,1},{1,0},{2,3},{3,2},{4,5},{5,4},{6,7},{7,6},{8,9},{9,8},{10,11... | collective-permute-start | bytes 393224 | tf_op jit(solution)/shard_map/ppermute | solution.py:426
  75.2 9.5 %collective-permute-start.10 = (bf16[512,128]{1,0:T(8,128)(2,1)S(1)}, bf16[512,128]{1,0:T(8,128)(2,1)S(1)}, u32[]{:S(2)}, u32[]{:S(2)}) collective-permute-start(bf16[512,128]{1,0:T(8,128)(2,1)S(1)} %get-tuple-element.38), channel_id=1, source_target_pairs={{0,7},{1,6},{2,5},{3,4},{4,3},{5,2},{6,1},{7,0},{8,15},{9,14},{10,... | collective-permute-start | bytes 393224 | tf_op jit(solution)/shard_map/ppermute | solution.py:426

commit v15 on v13

--- a/solution.py
+++ b/solution.py
@@ -19,9 +19,9 @@
 
 def table_rows(total_time, freq_devices, offset_devices, halves, pairs):
     band = NF // freq_devices
-    f, o, a, k = np.meshgrid(
-        np.arange(freq_devices // 2),
-        np.arange(offset_devices),
+    o, f, a, k = np.meshgrid(
+        np.arange(offset_devices // 2),
+        np.arange(freq_devices),
         np.arange(halves),
         np.arange(pairs),
         indexing="ij",
@@ -529,15 +529,14 @@
         series[s] = lax.ppermute(series[s], "freq", swaps)
     table = jnp.asarray(table_rows(total_time, freq_devices, offset_devices, halves, pairs))
     spectrum = transform(me, table, series, pairs, gathers)
-    data = lax.all_to_all(spectrum, ("freq", "offset"), 0, 0, tiled=True)
-
-    offs = offset_index.reshape(offset_devices, freq_devices, own_offsets)
-    offs = offs.transpose(1, 0, 2).reshape(1, offsets).astype(jnp.float32)
+    data = lax.all_to_all(spectrum, ("offset", "freq"), 0, 0, tiled=True)
+
+    offs = offset_index.reshape(1, offsets).astype(jnp.float32)
     slows = slowness_index.astype(jnp.float32)[:, None]
     first = lax.axis_index("freq") * band + lax.axis_index("offset") * pairs
     base = (2 * first + 1).astype(jnp.float32) * (math.pi / total_time)
     state = moveout(base.reshape(1), slows, offs, band // halves, total_time)
-    down = (2 * lax.axis_index("freq") // freq_devices).astype(jnp.int32)
+    down = (2 * lax.axis_index("offset") // offset_devices).astype(jnp.int32)
     place = jnp.stack([down, lax.axis_index("offset").astype(jnp.int32)])
     slows_each = NP // offset_devices
     scale = 1.0 / math.sqrt(offsets)

time: 86.7 us -> 86.9 us (level)
    ppermute x8, waiting for transfers between devices: 12.3 us -> 14 us  [swapped(): return lax.ppermute(part, 'offset', swaps)]
    all_to_all x1, waiting for transfers between devices: 23.6 us -> 22.5 us  [local(): data = lax.all_to_all(spectrum, ('offset', 'freq'), 0, 0, tiled=True)]
  transfers between devices with their start and end apart: 12 -> 12, of which waited for: 8 -> 7; matrix products, arithmetic and copies ran while one was open for 0% -> 0% of each run, Pallas kernels for 8% -> 8%
where the time goes in v15:
time: 86.9 us; the launch traced here: 86.6 us
  waiting for transfers between devices  45.6 us (52%)
  starting transfers between devices  18.9 us (22%)
  Pallas kernels  17.6 us (20%)
  local copies, waits for them, and re-layouts  3.56 us (4%)
    all_to_all x1, waiting for transfers between devices, local(): data = lax.all_to_all(spectrum, ('offset', 'freq'), 0, 0, tiled=True)  22.5 us
    ppermute x8, waiting for transfers between devices, swapped(): return lax.ppermute(part, 'offset', swaps)  14 us
    ppermute x8, starting transfers between devices, swapped(): return lax.ppermute(part, 'offset', swaps)  9.81 us
    ppermute x3, waiting for transfers between devices, local(): series[s] = lax.ppermute(series[s], 'freq', swaps)  9.08 us
    all_to_all x1, starting transfers between devices, local(): data = lax.all_to_all(spectrum, ('offset', 'freq'), 0, 0, tiled=True)  5.88 us
    pallas_call x1, Pallas kernels, radon_swapped(): pl.pallas_call(functools.partial(far_kernel, gathers, half), in_specs=[sm...  3.99 us
    pallas_call x1, Pallas kernels, moveout(): pl.pallas_call(functools.partial(moveout_kernel, shift, total_time), grid...  3.43 us
    unnamed x10, local copies, waits for them, and re-layouts  3.42 us
  transfers between devices with their start and end apart: 12, of which 7 were waited for; matrix products, arithmetic and copies ran while one was open for 0% of the time, Pallas kernels for 8%

profile of v15, /device:TPU:0, one launch (start us, length us, event | category | flops | bytes accessed | tf_op | source)
XLA Modules:
  0.0 86.6 jit_solution(17325617659701621045)
XLA Ops:
  0.0 0.7 convert_element_type.18.slot_ref
  0.7 0.0 copy-start.2
  0.7 1.2 %copy-done.2 = bf16[1024,512]{1,0:T(8,128)(2,1)S(1)} copy-done((bf16[1024,512]{1,0:T(8,128)(2,1)S(1)}, bf16[1024,512]{1,0:T(8,128)(2,1)}, u32[]{:S(2)}) %copy-start.2) | copy-done | bytes 1048600
  1.9 2.0 %shard_map.56 = (bf16[256,512]{1,0:T(8,128)(2,1)S(1)}, bf16[256,512]{1,0:T(8,128)(2,1)S(1)}, bf16[256,512]{1,0:T(8,128)(2,1)S(1)}, bf16[256,512]{1,0:T(8,128)(2,1)S(1)}) custom-call(s32[1]{0:T(128)} %bitcast.5.me_ref, f32[32,32]{1,0:T(8,128)S(1)} %convert_element_type.18.slot_ref, bf16[1024,512]{1,0:T(8,128)(2,1)S(1)} %copy-done.2), custom_call_target="tpu_custom_call" | custom-call | tf_op jit(solution)/shard_map/pallas_call | solution.py:68
  3.9 0.5 collective-permute-start
  4.4 2.6 %collective-permute-start.1 = (bf16[256,512]{1,0:T(8,128)(2,1)S(1)}, bf16[256,512]{1,0:T(8,128)(2,1)S(1)}, u32[]{:S(2)}, u32[]{:S(2)}) collective-permute-start(bf16[256,512]{1,0:T(8,128)(2,1)S(1)} %get-tuple-element.22), channel_id=1, source_target_pairs={{0,16},{8,24},{16,0},{24,8},{1,17},{9,25},{17,1},{25,9},{2,18},{10... | collective-permute-start | bytes 786440 | tf_op jit(solution)/shard_map/ppermute | solution.py:529
  7.0 0.1 collective-permute-start.2
  7.1 0.0 collective-permute-done.refs_1_
  7.1 0.0 copy-start
  7.1 2.2 %copy-done = bf16[1024,2048]{1,0:T(8,128)(2,1)S(1)} copy-done((bf16[1024,2048]{1,0:T(8,128)(2,1)S(1)}, bf16[1024,2048]{1,0:T(8,128)(2,1)}, u32[]{:S(2)}) %copy-start) | copy-done | bytes 4194328
  9.3 0.0 copy-start.1
  9.3 0.9 %shard_map.57.begun_ref = f32[2,1024,256]{2,1,0:T(8,128)S(1)} custom-call(s32[1]{0:T(128)} %bitcast.5.me_ref, bf16[1024,2048]{1,0:T(8,128)(2,1)S(1)} %copy-done, bf16[256,512]{1,0:T(8,128)(2,1)S(1)} %get-tuple-element.20.refs_0_, bf16[256,512]{1,0:T(8,128)(2,1)S(1)} %collective-permute-done.refs_1_), custom_call_target="tpu_custom_call" | custom-call | flops 536870912 | bytes 4194304 | tf_op jit(solution)/shard_map/pallas_call | solution.py:185
  10.2 4.0 %collective-permute-done.1.refs_0_ = bf16[256,512]{1,0:T(8,128)(2,1)S(1)} collective-permute-done((bf16[256,512]{1,0:T(8,128)(2,1)S(1)}, bf16[256,512]{1,0:T(8,128)(2,1)S(1)}, u32[]{:S(2)}, u32[]{:S(2)}) %collective-permute-start.1) | collective-permute-done | bytes 262176 | tf_op jit(solution)/shard_map/ppermute | solution.py:529
  14.2 5.1 %collective-permute-done.2.refs_1_ = bf16[256,512]{1,0:T(8,128)(2,1)S(1)} collective-permute-done((bf16[256,512]{1,0:T(8,128)(2,1)S(1)}, bf16[256,512]{1,0:T(8,128)(2,1)S(1)}, u32[]{:S(2)}, u32[]{:S(2)}) %collective-permute-start.2) | collective-permute-done | bytes 262176 | tf_op jit(solution)/shard_map/ppermute | solution.py:529
  19.3 0.0 copy-done.1
  19.3 2.2 %shard_map.58 = bf16[32,8,16,128]{3,2,1,0:T(8,128)(2,1)} custom-call(s32[1]{0:T(128)} %bitcast.5.me_ref, bf16[1024,2048]{1,0:T(8,128)(2,1)S(1)} %copy-done.1, f32[2,1024,256]{2,1,0:T(8,128)S(1)} %shard_map.57.begun_ref, bf16[256,512]{1,0:T(8,128)(2,1)S(1)} %collective-permute-done.1.refs_0_, bf16[256,512]{1,0:T(8,128)(2,1)S(1)} %collective-permute-done.2.refs_1_), custom_call_target="tpu_custom_call" | custom-call | tf_op jit(solution)/shard_map/pallas_call | solution.py:198
  21.5 0.0 copy-start.3
  21.5 0.0 copy-start.4
  21.5 5.9 %all-to-all-start = ((bf16[32,8,16,128]{3,2,1,0:T(8,128)(2,1)}), bf16[32,8,16,128]{3,2,1,0:T(8,128)(2,1)S(1)}, u32[]{:S(2)}, u32[]{:S(2)}) async-start(bf16[32,8,16,128]{3,2,1,0:T(8,128)(2,1)} %shard_map.58), calls=%async_computation | async-start | bytes 2097152 | tf_op jit(solution)/shard_map/all_to_all | solution.py:532
  27.5 0.0 copy-done.3
  27.5 0.0 copy-done.4
  27.5 0.1 copy.6.slow_ref
  27.7 3.4 %shard_map.55.state_ref = f32[6,256,256]{2,1,0:T(8,128)S(1)} custom-call(f32[1]{0:T(128)} %bitcast.2.base_ref, f32[256,1]{1,0:T(8,128)S(1)} %copy.6.slow_ref, f32[1,256]{1,0:T(1,128)S(1)} %bitcast.7), custom_call_target="tpu_custom_call" | custom-call | flops 19660800 | bytes 1572864 | tf_op jit(solution)/shard_map/pallas_call | solution.py:235
  31.1 0.1 pad_add_fusion.place_ref
  31.2 22.5 %all-to-all-done.data_ref = bf16[32,8,16,128]{3,2,1,0:T(8,128)(2,1)S(1)} async-done(((bf16[32,8,16,128]{3,2,1,0:T(8,128)(2,1)}), bf16[32,8,16,128]{3,2,1,0:T(8,128)(2,1)S(1)}, u32[]{:S(2)}, u32[]{:S(2)}) %all-to-all-start) | async-done | bytes 1048608 | tf_op jit(solution)/shard_map/all_to_all | solution.py:532
  53.7 4.0 %shard_map.59 = (bf16[16,256,128]{2,1,0:T(8,128)(2,1)S(1)}, bf16[16,256,128]{2,1,0:T(8,128)(2,1)S(1)}, bf16[16,128]{1,0:T(8,128)(2,1)S(1)}, bf16[512,128]{1,0:T(...) custom-call(s32[2]{0:T(128)S(1)} %pad_add_fusion.place_ref, ...), custom_call_target="tpu_custom_call" | custom-call | flops 1073741824 | bytes 524288 | tf_op jit(solution)/shard_map/pallas_call | solution.py:415
  57.7 0.8 collective-permute-start.3
  58.5 3.1 %collective-permute-start.4 = (bf16[512,128]{1,0:T(8,128)(2,1)S(1)}, bf16[512,128]{1,0:T(8,128)(2,1)S(1)}, u32[]{:S(2)}, u32[]{:S(2)}) collective-permute-start(bf16[512,128]{1,0:T(8,128)(2,1)S(1)} %get-tuple-element.25), channel_id=1, source_target_pairs={{0,5},{1,4},{2,7},{3,6},{4,1},{5,0},{6,3},{7,2},{8,13},{9,12},{10,... | collective-permute-start | bytes 393224 | tf_op jit(solution)/shard_map/ppermute | solution.py:426
  61.6 0.6 collective-permute-start.7
  62.1 1.3 %collective-permute-start.5 = (bf16[512,128]{1,0:T(8,128)(2,1)S(1)}, bf16[512,128]{1,0:T(8,128)(2,1)S(1)}, u32[]{:S(2)}, u32[]{:S(2)}) collective-permute-start(bf16[512,128]{1,0:T(8,128)(2,1)S(1)} %get-tuple-element.26), channel_id=1, source_target_pairs={{0,6},{1,7},{2,4},{3,5},{4,2},{5,3},{6,0},{7,1},{8,14},{9,15},{10,... | collective-permute-start | bytes 393224 | tf_op jit(solution)/shard_map/ppermute | solution.py:426
  63.4 3.4 %collective-permute-start.6 = (bf16[512,128]{1,0:T(8,128)(2,1)S(1)}, bf16[512,128]{1,0:T(8,128)(2,1)S(1)}, u32[]{:S(2)}, u32[]{:S(2)}) collective-permute-start(bf16[512,128]{1,0:T(8,128)(2,1)S(1)} %get-tuple-element.27), channel_id=1, source_target_pairs={{0,7},{1,6},{2,5},{3,4},{4,3},{5,2},{6,1},{7,0},{8,15},{9,14},{10,... | collective-permute-start | bytes 393224 | tf_op jit(solution)/shard_map/ppermute | solution.py:426
  66.9 0.0 collective-permute-done.7._
  66.9 3.0 %shard_map.60 = (bf16[512,128]{1,0:T(8,128)(2,1)S(1)}, bf16[512,128]{1,0:T(8,128)(2,1)S(1)}, bf16[512,128]{1,0:T(8,128)(2,1)S(1)}, bf16[512,128]{1,0:T(8,128)(2,1)S(1)}) custom-call(s32[2]{0:T(128)S(1)} %pad_add_fusion.place_ref, f32[6,256,256]{2,1,0:T(8,128)S(1)} %shard_map.55.state_ref, bf16[16,256,128]{2,1,0:T(8,128)(2,1)S(1)} %get-tuple-element.28.plain, ...), custom_call_target="tpu_custom_call" | custom-call | flops 1073741824 | bytes 524288 | tf_op jit(solution)/shard_map/pallas_call | solution.py:430
  69.8 0.6 collective-permute-start.8
  70.4 5.4 %collective-permute-done.3.refs_0_ = bf16[512,128]{1,0:T(8,128)(2,1)S(1)} collective-permute-done((bf16[512,128]{1,0:T(8,128)(2,1)S(1)}, bf16[512,128]{1,0:T(8,128)(2,1)S(1)}, u32[]{:S(2)}, u32[]{:S(2)}) %collective-permute-start.3) | collective-permute-done | bytes 131104 | tf_op jit(solution)/shard_map/ppermute | solution.py:426
  75.8 0.0 collective-permute-start.9
  75.9 2.8 %collective-permute-done.4.refs_1_ = bf16[512,128]{1,0:T(8,128)(2,1)S(1)} collective-permute-done((bf16[512,128]{1,0:T(8,128)(2,1)S(1)}, bf16[512,128]{1,0:T(8,128)(2,1)S(1)}, u32[]{:S(2)}, u32[]{:S(2)}) %collective-permute-start.4) | collective-permute-done | bytes 131104 | tf_op jit(solution)/shard_map/ppermute | solution.py:426
  78.6 0.0 collective-permute-start.10
  78.6 0.0 collective-permute-done.5.refs_2_
  78.6 0.0 collective-permute-done.6.refs_3_
  78.6 0.0 collective-permute-done.8.refs_5_
  78.6 3.2 %collective-permute-done.9.refs_6_ = bf16[512,128]{1,0:T(8,128)(2,1)S(1)} collective-permute-done((bf16[512,128]{1,0:T(8,128)(2,1)S(1)}, bf16[512,128]{1,0:T(8,128)(2,1)S(1)}, u32[]{:S(2)}, u32[]{:S(2)}) %collective-permute-start.9) | collective-permute-done | bytes 131104 | tf_op jit(solution)/shard_map/ppermute | solution.py:426
  81.9 2.6 %collective-permute-done.10.refs_7_ = bf16[512,128]{1,0:T(8,128)(2,1)S(1)} collective-permute-done((bf16[512,128]{1,0:T(8,128)(2,1)S(1)}, bf16[512,128]{1,0:T(8,128)(2,1)S(1)}, u32[]{:S(2)}, u32[]{:S(2)}) %collective-permute-start.10) | collective-permute-done | bytes 131104 | tf_op jit(solution)/shard_map/ppermute | solution.py:426
  84.5 2.1 %shard_map.61 = f32[32,64,256]{2,1,0:T(8,128)} custom-call(s32[2]{0:T(128)S(1)} %pad_add_fusion.place_ref, bf16[512,128]{1,0:T(8,128)(2,1)S(1)} %collective-permute-done.3.refs_0_, bf16[512,128]{1,0:T(8,128)(2,1)S(1)} %collective-permute-done.4.refs_1_, bf16[512,128]{1,0:T(8,128)(2,1)S(1)} %collective-permute-done.5.refs_2_, ...), custom_call_target="tpu_custom_call" | custom-call | tf_op jit(solution)/shard_map/pallas_call | solution.py:473
  (2 shorter events, 0.0 us)
Async XLA Ops:
  0.7 1.2 %copy-start.2 = (bf16[1024,512]{1,0:T(8,128)(2,1)S(1)}, bf16[1024,512]{1,0:T(8,128)(2,1)}, u32[]{:S(2)}) copy-start(bf16[1024,512]{1,0:T(8,128)(2,1)} %raw_ref.1) | copy-start | bytes 3145732
  3.9 3.2 %collective-permute-start = (bf16[256,512]{1,0:T(8,128)(2,1)S(1)}, bf16[256,512]{1,0:T(8,128)(2,1)S(1)}, u32[]{:S(2)}, u32[]{:S(2)}) collective-permute-start(bf16[256,512]{1,0:T(8,128)(2,1)S(1)} %get-tuple-element.21), channel_id=1, source_target_pairs={{0,8},{8,0},{16,24},{24,16},{1,9},{9,1},{17,25},{25,17},{2,10},{10... | collective-permute-start | bytes 786440 | tf_op jit(solution)/shard_map/ppermute | solution.py:529
  4.4 9.8 %collective-permute-start.1 = (bf16[256,512]{1,0:T(8,128)(2,1)S(1)}, bf16[256,512]{1,0:T(8,128)(2,1)S(1)}, u32[]{:S(2)}, u32[]{:S(2)}) collective-permute-start(bf16[256,512]{1,0:T(8,128)(2,1)S(1)} %get-tuple-element.22), channel_id=1, source_target_pairs={{0,16},{8,24},{16,0},{24,8},{1,17},{9,25},{17,1},{25,9},{2,18},{10... | collective-permute-start | bytes 786440 | tf_op jit(solution)/shard_map/ppermute | solution.py:529
  7.0 12.3 %collective-permute-start.2 = (bf16[256,512]{1,0:T(8,128)(2,1)S(1)}, bf16[256,512]{1,0:T(8,128)(2,1)S(1)}, u32[]{:S(2)}, u32[]{:S(2)}) collective-permute-start(bf16[256,512]{1,0:T(8,128)(2,1)S(1)} %get-tuple-element.23), channel_id=1, source_target_pairs={{0,24},{8,16},{16,8},{24,0},{1,25},{9,17},{17,9},{25,1},{2,26},{10... | collective-permute-start | bytes 786440 | tf_op jit(solution)/shard_map/ppermute | solution.py:529
  7.1 2.2 %copy-start = (bf16[1024,2048]{1,0:T(8,128)(2,1)S(1)}, bf16[1024,2048]{1,0:T(8,128)(2,1)}, u32[]{:S(2)}) copy-start(bf16[1024,2048]{1,0:T(8,128)(2,1)} %constant.35.clone.table_ref) | copy-start | bytes 12582916
  9.3 10.0 %copy-start.1 = (bf16[1024,2048]{1,0:T(8,128)(2,1)S(1)}, bf16[1024,2048]{1,0:T(8,128)(2,1)}, u32[]{:S(2)}) copy-start(bf16[1024,2048]{1,0:T(8,128)(2,1)} %constant.35.clone.table_ref) | copy-start | bytes 12582916
  21.5 5.9 %copy-start.3 = (s32[256]{0:T(256)S(1)}, s32[256]{0:T(256)}, u32[]{:S(2)}) copy-start(s32[256]{0:T(256)} %param.7) | copy-start | bytes 3076
  21.5 5.9 %copy-start.4 = (s32[256]{0:T(256)S(1)}, s32[256]{0:T(256)}, u32[]{:S(2)}) copy-start(s32[256]{0:T(256)} %param.8) | copy-start | bytes 3076
  21.5 32.1 %all-to-all-start = ((bf16[32,8,16,128]{3,2,1,0:T(8,128)(2,1)}), bf16[32,8,16,128]{3,2,1,0:T(8,128)(2,1)S(1)}, u32[]{:S(2)}, u32[]{:S(2)}) async-start(bf16[32,8,16,128]{3,2,1,0:T(8,128)(2,1)} %shard_map.58), calls=%async_computation | async-start | bytes 2097152 | tf_op jit(solution)/shard_map/all_to_all | solution.py:532
  57.7 18.2 %collective-permute-start.3 = (bf16[512,128]{1,0:T(8,128)(2,1)S(1)}, bf16[512,128]{1,0:T(8,128)(2,1)S(1)}, u32[]{:S(2)}, u32[]{:S(2)}) collective-permute-start(bf16[512,128]{1,0:T(8,128)(2,1)S(1)} %get-tuple-element.24), channel_id=1, source_target_pairs={{0,4},{1,5},{2,6},{3,7},{4,0},{5,1},{6,2},{7,3},{8,12},{9,13},{10,... | collective-permute-start | bytes 393224 | tf_op jit(solution)/shard_map/ppermute | solution.py:426
  58.5 20.1 %collective-permute-start.4 = (bf16[512,128]{1,0:T(8,128)(2,1)S(1)}, bf16[512,128]{1,0:T(8,128)(2,1)S(1)}, u32[]{:S(2)}, u32[]{:S(2)}) collective-permute-start(bf16[512,128]{1,0:T(8,128)(2,1)S(1)} %get-tuple-element.25), channel_id=1, source_target_pairs={{0,5},{1,4},{2,7},{3,6},{4,1},{5,0},{6,3},{7,2},{8,13},{9,12},{10,... | collective-permute-start | bytes 393224 | tf_op jit(solution)/shard_map/ppermute | solution.py:426
  61.6 5.3 %collective-permute-start.7 = (bf16[16,128]{1,0:T(8,128)(2,1)S(1)}, bf16[16,128]{1,0:T(8,128)(2,1)S(1)}, u32[]{:S(2)}, u32[]{:S(2)}) collective-permute-start(bf16[16,128]{1,0:T(8,128)(2,1)S(1)} %get-tuple-element.30), channel_id=1, source_target_pairs={{0,1},{1,0},{2,3},{3,2},{4,5},{5,4},{6,7},{7,6},{8,9},{9,8},{10,11... | collective-permute-start | bytes 12296 | tf_op jit(solution)/shard_map/ppermute | solution.py:426
  62.1 16.5 %collective-permute-start.5 = (bf16[512,128]{1,0:T(8,128)(2,1)S(1)}, bf16[512,128]{1,0:T(8,128)(2,1)S(1)}, u32[]{:S(2)}, u32[]{:S(2)}) collective-permute-start(bf16[512,128]{1,0:T(8,128)(2,1)S(1)} %get-tuple-element.26), channel_id=1, source_target_pairs={{0,6},{1,7},{2,4},{3,5},{4,2},{5,3},{6,0},{7,1},{8,14},{9,15},{10,... | collective-permute-start | bytes 393224 | tf_op jit(solution)/shard_map/ppermute | solution.py:426
  63.4 15.2 %collective-permute-start.6 = (bf16[512,128]{1,0:T(8,128)(2,1)S(1)}, bf16[512,128]{1,0:T(8,128)(2,1)S(1)}, u32[]{:S(2)}, u32[]{:S(2)}) collective-permute-start(bf16[512,128]{1,0:T(8,128)(2,1)S(1)} %get-tuple-element.27), channel_id=1, source_target_pairs={{0,7},{1,6},{2,5},{3,4},{4,3},{5,2},{6,1},{7,0},{8,15},{9,14},{10,... | collective-permute-start | bytes 393224 | tf_op jit(solution)/shard_map/ppermute | solution.py:426
  69.8 8.8 %collective-permute-start.8 = (bf16[512,128]{1,0:T(8,128)(2,1)S(1)}, bf16[512,128]{1,0:T(8,128)(2,1)S(1)}, u32[]{:S(2)}, u32[]{:S(2)}) collective-permute-start(bf16[512,128]{1,0:T(8,128)(2,1)S(1)} %get-tuple-element.32), channel_id=1, source_target_pairs={{0,1},{1,0},{2,3},{3,2},{4,5},{5,4},{6,7},{7,6},{8,9},{9,8},{10,11... | collective-permute-start | bytes 393224 | tf_op jit(solution)/shard_map/ppermute | solution.py:426
  75.8 6.0 %collective-permute-start.9 = (bf16[512,128]{1,0:T(8,128)(2,1)S(1)}, bf16[512,128]{1,0:T(8,128)(2,1)S(1)}, u32[]{:S(2)}, u32[]{:S(2)}) collective-permute-start(bf16[512,128]{1,0:T(8,128)(2,1)S(1)} %get-tuple-element.33), channel_id=1, source_target_pairs={{0,2},{1,3},{2,0},{3,1},{4,6},{5,7},{6,4},{7,5},{8,10},{9,11},{10,... | collective-permute-start | bytes 393224 | tf_op jit(solution)/shard_map/ppermute | solution.py:426
  78.6 5.9 %collective-permute-start.10 = (bf16[512,128]{1,0:T(8,128)(2,1)S(1)}, bf16[512,128]{1,0:T(8,128)(2,1)S(1)}, u32[]{:S(2)}, u32[]{:S(2)}) collective-permute-start(bf16[512,128]{1,0:T(8,128)(2,1)S(1)} %get-tuple-element.34), channel_id=1, source_target_pairs={{0,3},{1,2},{2,1},{3,0},{4,7},{5,6},{6,5},{7,4},{8,11},{9,10},{10,... | collective-permute-start | bytes 393224 | tf_op jit(solution)/shard_map/ppermute | solution.py:426

commit v16 on v15

--- a/solution.py
+++ b/solution.py
@@ -330,10 +330,14 @@
         held[k] = jnp.where(first_half, both[:slows], both[slows:]).astype(jnp.bfloat16)
 
 
-def deal(held, first, out_ref):
+def dealing(pairs):
+    size = TILE * pairs
+    return one_hot(size, size, lambda r: remainder(r, pairs) * TILE + quotient(r, pairs))
+
+
+def deal(swap, held, first, out_ref):
     pairs, _, lanes = held.shape
     size = TILE * pairs
-    swap = one_hot(size, size, lambda r: remainder(r, pairs) * TILE + quotient(r, pairs))
     for p in range(out_ref.shape[0] // size):
         start = first + p * TILE
         if not isinstance(start, int):
@@ -347,7 +351,7 @@
 def radon_kernel(gathers, down_ref, state_ref, data_ref, out_ref, turns, plain, turned, held):
     prepare(gathers, down_ref[0], data_ref, plain, turned)
     sum_offsets(gathers, 0, state_ref, plain, turned, turns, held)
-    deal(held, 0, out_ref)
+    deal(dealing(held.shape[0]), held, 0, out_ref)
 
 
 def radon(down, state, data, gathers):
@@ -370,10 +374,11 @@
 
 
 def deal_half(held, me, first, out_refs):
+    swap = dealing(held.shape[0])
     half = len(out_refs)
     each = held.shape[1] // half
     for s, out_ref in enumerate(out_refs):
-        deal(held, remainder(me ^ (first + s), half) * each, out_ref)
+        deal(swap, held, remainder(me ^ (first + s), half) * each, out_ref)
 
 
 def far_kernel(gathers, half, place_ref, state_ref, data_ref, plain, turned, sign_ref, *refs):
@@ -425,7 +430,7 @@
         swaps = [(o, o ^ s) for o in range(offset_devices)]
         return lax.ppermute(part, "offset", swaps)
 
-    far = [swapped(part, half + s) for s, part in enumerate(far)]
+    far[:-1] = [swapped(part, half + s) for s, part in enumerate(far[:-1])]
     sign = swapped(sign, 1)
     near = pl.pallas_call(
         functools.partial(near_kernel, gathers, half),
@@ -436,8 +441,12 @@
         compiler_params=pltpu.CompilerParams(vmem_limit_bytes=20 * MIB),
         cost_estimate=cost,
     )(place, state, plain, turned, sign)
+    near = list(near)
+    last, far[0] = lax.optimization_barrier((far[-1], far[0]))
     near = [swapped(part, s) if s else part for s, part in enumerate(near)]
-    return list(range(half, offset_devices)) + list(range(half)), far + near
+    far[-1] = swapped(last, offset_devices - 1)
+    parts = near + far
+    return list(range(half, offset_devices - 1)) + list(range(half))[::-1] + [offset_devices - 1], [parts[s] for s in list(range(half, offset_devices - 1)) + list(range(half))[::-1] + [offset_devices - 1]]
 
 
 def join_kernel(scale, order, place_ref, *refs):

time: 86.9 us -> 86 us (0.990)
  waiting for transfers between devices: 45.6 us -> 43.5 us
  starting transfers between devices: 18.9 us -> 20.1 us
    ppermute x8, waiting for transfers between devices: 14 us -> 11.9 us  [swapped(): return lax.ppermute(part, 'offset', swaps)]
    ppermute x8, starting transfers between devices: 9.81 us -> 11 us  [swapped(): return lax.ppermute(part, 'offset', swaps)]
  transfers between devices with their start and end apart: 12 -> 12, of which waited for: 7 -> 9; matrix products, arithmetic and copies ran while one was open for 0% -> 0% of each run, Pallas kernels for 8% -> 9%
where the time goes in v16:
time: 86 us; the launch traced here: 85.7 us
  waiting for transfers between devices  43.5 us (51%)
  starting transfers between devices  20.1 us (23%)
  Pallas kernels  17.6 us (20%)
  local copies, waits for them, and re-layouts  3.56 us (4%)
    all_to_all x1, waiting for transfers between devices, local(): data = lax.all_to_all(spectrum, ('offset', 'freq'), 0, 0, tiled=True)  22.5 us
    ppermute x8, waiting for transfers between devices, swapped(): return lax.ppermute(part, 'offset', swaps)  11.9 us
    ppermute x8, starting transfers between devices, swapped(): return lax.ppermute(part, 'offset', swaps)  11 us
    ppermute x3, waiting for transfers between devices, local(): series[s] = lax.ppermute(series[s], 'freq', swaps)  9.08 us
    all_to_all x1, starting transfers between devices, local(): data = lax.all_to_all(spectrum, ('offset', 'freq'), 0, 0, tiled=True)  5.88 us
    pallas_call x1, Pallas kernels, radon_swapped(): pl.pallas_call(functools.partial(far_kernel, gathers, half), in_specs=[sm...  3.99 us
    pallas_call x1, Pallas kernels, moveout(): pl.pallas_call(functools.partial(moveout_kernel, shift, total_time), grid...  3.43 us
    unnamed x10, local copies, waits for them, and re-layouts  3.42 us
  transfers between devices with their start and end apart: 12, of which 9 were waited for; matrix products, arithmetic and copies ran while one was open for 0% of the time, Pallas kernels for 9%

profile of v16, /device:TPU:0, one launch (start us, length us, event | category | flops | bytes accessed | tf_op | source)
XLA Modules:
  0.0 85.7 jit_solution(14521569385150826009)
XLA Ops:
  0.0 0.7 convert_element_type.18.slot_ref
  0.7 0.0 copy-start.2
  0.7 1.2 %copy-done.2 = bf16[1024,512]{1,0:T(8,128)(2,1)S(1)} copy-done((bf16[1024,512]{1,0:T(8,128)(2,1)S(1)}, bf16[1024,512]{1,0:T(8,128)(2,1)}, u32[]{:S(2)}) %copy-start.2) | copy-done | bytes 1048600
  1.9 2.0 %shard_map.56 = (bf16[256,512]{1,0:T(8,128)(2,1)S(1)}, bf16[256,512]{1,0:T(8,128)(2,1)S(1)}, bf16[256,512]{1,0:T(8,128)(2,1)S(1)}, bf16[256,512]{1,0:T(8,128)(2,1)S(1)}) custom-call(s32[1]{0:T(128)} %bitcast.5.me_ref, f32[32,32]{1,0:T(8,128)S(1)} %convert_element_type.18.slot_ref, bf16[1024,512]{1,0:T(8,128)(2,1)S(1)} %copy-done.2), custom_call_target="tpu_custom_call" | custom-call | tf_op jit(solution)/shard_map/pallas_call | solution.py:68
  3.9 0.5 collective-permute-start
  4.4 2.6 %collective-permute-start.1 = (bf16[256,512]{1,0:T(8,128)(2,1)S(1)}, bf16[256,512]{1,0:T(8,128)(2,1)S(1)}, u32[]{:S(2)}, u32[]{:S(2)}) collective-permute-start(bf16[256,512]{1,0:T(8,128)(2,1)S(1)} %get-tuple-element.24), channel_id=1, source_target_pairs={{0,16},{8,24},{16,0},{24,8},{1,17},{9,25},{17,1},{25,9},{2,18},{10... | collective-permute-start | bytes 786440 | tf_op jit(solution)/shard_map/ppermute | solution.py:538
  7.0 0.1 collective-permute-start.2
  7.1 0.0 collective-permute-done.refs_1_
  7.1 0.0 copy-start
  7.1 2.2 %copy-done = bf16[1024,2048]{1,0:T(8,128)(2,1)S(1)} copy-done((bf16[1024,2048]{1,0:T(8,128)(2,1)S(1)}, bf16[1024,2048]{1,0:T(8,128)(2,1)}, u32[]{:S(2)}) %copy-start) | copy-done | bytes 4194328
  9.3 0.0 copy-start.1
  9.3 0.9 %shard_map.57.begun_ref = f32[2,1024,256]{2,1,0:T(8,128)S(1)} custom-call(s32[1]{0:T(128)} %bitcast.5.me_ref, bf16[1024,2048]{1,0:T(8,128)(2,1)S(1)} %copy-done, bf16[256,512]{1,0:T(8,128)(2,1)S(1)} %get-tuple-element.22.refs_0_, bf16[256,512]{1,0:T(8,128)(2,1)S(1)} %collective-permute-done.refs_1_), custom_call_target="tpu_custom_call" | custom-call | flops 536870912 | bytes 4194304 | tf_op jit(solution)/shard_map/pallas_call | solution.py:185
  10.2 4.0 %collective-permute-done.1.refs_0_ = bf16[256,512]{1,0:T(8,128)(2,1)S(1)} collective-permute-done((bf16[256,512]{1,0:T(8,128)(2,1)S(1)}, bf16[256,512]{1,0:T(8,128)(2,1)S(1)}, u32[]{:S(2)}, u32[]{:S(2)}) %collective-permute-start.1) | collective-permute-done | bytes 262176 | tf_op jit(solution)/shard_map/ppermute | solution.py:538
  14.2 5.1 %collective-permute-done.2.refs_1_ = bf16[256,512]{1,0:T(8,128)(2,1)S(1)} collective-permute-done((bf16[256,512]{1,0:T(8,128)(2,1)S(1)}, bf16[256,512]{1,0:T(8,128)(2,1)S(1)}, u32[]{:S(2)}, u32[]{:S(2)}) %collective-permute-start.2) | collective-permute-done | bytes 262176 | tf_op jit(solution)/shard_map/ppermute | solution.py:538
  19.3 0.0 copy-done.1
  19.3 2.2 %shard_map.58 = bf16[32,8,16,128]{3,2,1,0:T(8,128)(2,1)} custom-call(s32[1]{0:T(128)} %bitcast.5.me_ref, bf16[1024,2048]{1,0:T(8,128)(2,1)S(1)} %copy-done.1, f32[2,1024,256]{2,1,0:T(8,128)S(1)} %shard_map.57.begun_ref, bf16[256,512]{1,0:T(8,128)(2,1)S(1)} %collective-permute-done.1.refs_0_, bf16[256,512]{1,0:T(8,128)(2,1)S(1)} %collective-permute-done.2.refs_1_), custom_call_target="tpu_custom_call" | custom-call | tf_op jit(solution)/shard_map/pallas_call | solution.py:198
  21.5 0.0 copy-start.3
  21.5 0.0 copy-start.4
  21.5 5.9 %all-to-all-start = ((bf16[32,8,16,128]{3,2,1,0:T(8,128)(2,1)}), bf16[32,8,16,128]{3,2,1,0:T(8,128)(2,1)S(1)}, u32[]{:S(2)}, u32[]{:S(2)}) async-start(bf16[32,8,16,128]{3,2,1,0:T(8,128)(2,1)} %shard_map.58), calls=%async_computation | async-start | bytes 2097152 | tf_op jit(solution)/shard_map/all_to_all | solution.py:541
  27.5 0.0 copy-done.3
  27.5 0.0 copy-done.4
  27.5 0.1 copy.6.slow_ref
  27.7 3.4 %shard_map.55.state_ref = f32[6,256,256]{2,1,0:T(8,128)S(1)} custom-call(f32[1]{0:T(128)} %bitcast.2.base_ref, f32[256,1]{1,0:T(8,128)S(1)} %copy.6.slow_ref, f32[1,256]{1,0:T(1,128)S(1)} %bitcast.7), custom_call_target="tpu_custom_call" | custom-call | flops 19660800 | bytes 1572864 | tf_op jit(solution)/shard_map/pallas_call | solution.py:235
  31.1 0.1 pad_add_fusion.place_ref
  31.2 22.5 %all-to-all-done.data_ref = bf16[32,8,16,128]{3,2,1,0:T(8,128)(2,1)S(1)} async-done(((bf16[32,8,16,128]{3,2,1,0:T(8,128)(2,1)}), bf16[32,8,16,128]{3,2,1,0:T(8,128)(2,1)S(1)}, u32[]{:S(2)}, u32[]{:S(2)}) %all-to-all-start) | async-done | bytes 1048608 | tf_op jit(solution)/shard_map/all_to_all | solution.py:541
  53.7 4.0 %shard_map.59 = (bf16[16,256,128]{2,1,0:T(8,128)(2,1)S(1)}, bf16[16,256,128]{2,1,0:T(8,128)(2,1)S(1)}, bf16[16,128]{1,0:T(8,128)(2,1)S(1)}, bf16[512,128]{1,0:T(...) custom-call(s32[2]{0:T(128)S(1)} %pad_add_fusion.place_ref, ...), custom_call_target="tpu_custom_call" | custom-call | flops 1073741824 | bytes 524288 | tf_op jit(solution)/shard_map/pallas_call | solution.py:420
  57.7 0.8 collective-permute-start.3
  58.5 3.1 %collective-permute-start.4 = (bf16[512,128]{1,0:T(8,128)(2,1)S(1)}, bf16[512,128]{1,0:T(8,128)(2,1)S(1)}, u32[]{:S(2)}, u32[]{:S(2)}) collective-permute-start(bf16[512,128]{1,0:T(8,128)(2,1)S(1)} %get-tuple-element.29), channel_id=1, source_target_pairs={{0,5},{1,4},{2,7},{3,6},{4,1},{5,0},{6,3},{7,2},{8,13},{9,12},{10,... | collective-permute-start | bytes 393224 | tf_op jit(solution)/shard_map/ppermute | solution.py:431
  61.6 0.6 collective-permute-start.6
  62.1 1.3 %collective-permute-start.5 = (bf16[512,128]{1,0:T(8,128)(2,1)S(1)}, bf16[512,128]{1,0:T(8,128)(2,1)S(1)}, u32[]{:S(2)}, u32[]{:S(2)}) collective-permute-start(bf16[512,128]{1,0:T(8,128)(2,1)S(1)} %get-tuple-element.30), channel_id=1, source_target_pairs={{0,6},{1,7},{2,4},{3,5},{4,2},{5,3},{6,0},{7,1},{8,14},{9,15},{10,... | collective-permute-start | bytes 393224 | tf_op jit(solution)/shard_map/ppermute | solution.py:431
  63.4 1.8 %collective-permute-done.6._ = bf16[16,128]{1,0:T(8,128)(2,1)S(1)} collective-permute-done((bf16[16,128]{1,0:T(8,128)(2,1)S(1)}, bf16[16,128]{1,0:T(8,128)(2,1)S(1)}, u32[]{:S(2)}, u32[]{:S(2)}) %collective-permute-start.6) | collective-permute-done | bytes 4128 | tf_op jit(solution)/shard_map/ppermute | solution.py:431
  65.2 3.0 %shard_map.60 = (bf16[512,128]{1,0:T(8,128)(2,1)S(1)}, bf16[512,128]{1,0:T(8,128)(2,1)S(1)}, bf16[512,128]{1,0:T(8,128)(2,1)S(1)}, bf16[512,128]{1,0:T(8,128)(2,1)S(1)}) custom-call(s32[2]{0:T(128)S(1)} %pad_add_fusion.place_ref, f32[6,256,256]{2,1,0:T(8,128)S(1)} %shard_map.55.state_ref, bf16[16,256,128]{2,1,0:T(8,128)(2,1)S(1)} %get-tuple-element.31.plain, ...), custom_call_target="tpu_custom_call" | custom-call | flops 1073741824 | bytes 524288 | tf_op jit(solution)/shard_map/pallas_call | solution.py:435
  68.1 0.9 %collective-permute-start.7 = (bf16[512,128]{1,0:T(8,128)(2,1)S(1)}, bf16[512,128]{1,0:T(8,128)(2,1)S(1)}, u32[]{:S(2)}, u32[]{:S(2)}) collective-permute-start(bf16[512,128]{1,0:T(8,128)(2,1)S(1)} %get-tuple-element.34), channel_id=1, source_target_pairs={{0,3},{1,2},{2,1},{3,0},{4,7},{5,6},{6,5},{7,4},{8,11},{9,10},{10,... | collective-permute-start | bytes 393224 | tf_op jit(solution)/shard_map/ppermute | solution.py:431
  69.0 1.2 %collective-permute-start.8 = (bf16[512,128]{1,0:T(8,128)(2,1)S(1)}, bf16[512,128]{1,0:T(8,128)(2,1)S(1)}, u32[]{:S(2)}, u32[]{:S(2)}) collective-permute-start(bf16[512,128]{1,0:T(8,128)(2,1)S(1)} %get-tuple-element.35), channel_id=1, source_target_pairs={{0,2},{1,3},{2,0},{3,1},{4,6},{5,7},{6,4},{7,5},{8,10},{9,11},{10,... | collective-permute-start | bytes 393224 | tf_op jit(solution)/shard_map/ppermute | solution.py:431
  70.2 2.9 %collective-permute-done.3.refs_0_ = bf16[512,128]{1,0:T(8,128)(2,1)S(1)} collective-permute-done((bf16[512,128]{1,0:T(8,128)(2,1)S(1)}, bf16[512,128]{1,0:T(8,128)(2,1)S(1)}, u32[]{:S(2)}, u32[]{:S(2)}) %collective-permute-start.3) | collective-permute-done | bytes 131104 | tf_op jit(solution)/shard_map/ppermute | solution.py:431
  73.1 0.6 collective-permute-start.9
  73.6 2.2 %collective-permute-done.4.refs_1_ = bf16[512,128]{1,0:T(8,128)(2,1)S(1)} collective-permute-done((bf16[512,128]{1,0:T(8,128)(2,1)S(1)}, bf16[512,128]{1,0:T(8,128)(2,1)S(1)}, u32[]{:S(2)}, u32[]{:S(2)}) %collective-permute-start.4) | collective-permute-done | bytes 131104 | tf_op jit(solution)/shard_map/ppermute | solution.py:431
  75.9 2.7 %collective-permute-start.10 = (bf16[512,128]{1,0:T(8,128)(2,1)S(1)}, bf16[512,128]{1,0:T(8,128)(2,1)S(1)}, u32[]{:S(2)}, u32[]{:S(2)}) collective-permute-start(bf16[512,128]{1,0:T(8,128)(2,1)S(1)} %get-tuple-element.38), channel_id=1, source_target_pairs={{0,7},{1,6},{2,5},{3,4},{4,3},{5,2},{6,1},{7,0},{8,15},{9,14},{10,... | collective-permute-start | bytes 393224 | tf_op jit(solution)/shard_map/ppermute | solution.py:431
  78.5 0.0 collective-permute-done.5.refs_2_
  78.5 0.0 collective-permute-done.7.refs_3_
  78.6 3.1 %collective-permute-done.8.refs_4_ = bf16[512,128]{1,0:T(8,128)(2,1)S(1)} collective-permute-done((bf16[512,128]{1,0:T(8,128)(2,1)S(1)}, bf16[512,128]{1,0:T(8,128)(2,1)S(1)}, u32[]{:S(2)}, u32[]{:S(2)}) %collective-permute-start.8) | collective-permute-done | bytes 131104 | tf_op jit(solution)/shard_map/ppermute | solution.py:431
  81.7 0.4 collective-permute-done.9.refs_5_
  82.1 1.4 %collective-permute-done.10.refs_7_ = bf16[512,128]{1,0:T(8,128)(2,1)S(1)} collective-permute-done((bf16[512,128]{1,0:T(8,128)(2,1)S(1)}, bf16[512,128]{1,0:T(8,128)(2,1)S(1)}, u32[]{:S(2)}, u32[]{:S(2)}) %collective-permute-start.10) | collective-permute-done | bytes 131104 | tf_op jit(solution)/shard_map/ppermute | solution.py:431
  83.6 2.1 %shard_map.61 = f32[32,64,256]{2,1,0:T(8,128)} custom-call(s32[2]{0:T(128)S(1)} %pad_add_fusion.place_ref, bf16[512,128]{1,0:T(8,128)(2,1)S(1)} %collective-permute-done.3.refs_0_, bf16[512,128]{1,0:T(8,128)(2,1)S(1)} %collective-permute-done.4.refs_1_, bf16[512,128]{1,0:T(8,128)(2,1)S(1)} %collective-permute-done.5.refs_2_, ...), custom_call_target="tpu_custom_call" | custom-call | tf_op jit(solution)/shard_map/pallas_call | solution.py:482
  (2 shorter events, 0.0 us)
Async XLA Ops:
  0.7 1.2 %copy-start.2 = (bf16[1024,512]{1,0:T(8,128)(2,1)S(1)}, bf16[1024,512]{1,0:T(8,128)(2,1)}, u32[]{:S(2)}) copy-start(bf16[1024,512]{1,0:T(8,128)(2,1)} %raw_ref.1) | copy-start | bytes 3145732
  3.9 3.2 %collective-permute-start = (bf16[256,512]{1,0:T(8,128)(2,1)S(1)}, bf16[256,512]{1,0:T(8,128)(2,1)S(1)}, u32[]{:S(2)}, u32[]{:S(2)}) collective-permute-start(bf16[256,512]{1,0:T(8,128)(2,1)S(1)} %get-tuple-element.23), channel_id=1, source_target_pairs={{0,8},{8,0},{16,24},{24,16},{1,9},{9,1},{17,25},{25,17},{2,10},{10... | collective-permute-start | bytes 786440 | tf_op jit(solution)/shard_map/ppermute | solution.py:538
  4.4 9.8 %collective-permute-start.1 = (bf16[256,512]{1,0:T(8,128)(2,1)S(1)}, bf16[256,512]{1,0:T(8,128)(2,1)S(1)}, u32[]{:S(2)}, u32[]{:S(2)}) collective-permute-start(bf16[256,512]{1,0:T(8,128)(2,1)S(1)} %get-tuple-element.24), channel_id=1, source_target_pairs={{0,16},{8,24},{16,0},{24,8},{1,17},{9,25},{17,1},{25,9},{2,18},{10... | collective-permute-start | bytes 786440 | tf_op jit(solution)/shard_map/ppermute | solution.py:538
  7.0 12.3 %collective-permute-start.2 = (bf16[256,512]{1,0:T(8,128)(2,1)S(1)}, bf16[256,512]{1,0:T(8,128)(2,1)S(1)}, u32[]{:S(2)}, u32[]{:S(2)}) collective-permute-start(bf16[256,512]{1,0:T(8,128)(2,1)S(1)} %get-tuple-element.25), channel_id=1, source_target_pairs={{0,24},{8,16},{16,8},{24,0},{1,25},{9,17},{17,9},{25,1},{2,26},{10... | collective-permute-start | bytes 786440 | tf_op jit(solution)/shard_map/ppermute | solution.py:538
  7.1 2.2 %copy-start = (bf16[1024,2048]{1,0:T(8,128)(2,1)S(1)}, bf16[1024,2048]{1,0:T(8,128)(2,1)}, u32[]{:S(2)}) copy-start(bf16[1024,2048]{1,0:T(8,128)(2,1)} %constant.35.clone.table_ref) | copy-start | bytes 12582916
  9.3 10.0 %copy-start.1 = (bf16[1024,2048]{1,0:T(8,128)(2,1)S(1)}, bf16[1024,2048]{1,0:T(8,128)(2,1)}, u32[]{:S(2)}) copy-start(bf16[1024,2048]{1,0:T(8,128)(2,1)} %constant.35.clone.table_ref) | copy-start | bytes 12582916
  21.5 5.9 %copy-start.3 = (s32[256]{0:T(256)S(1)}, s32[256]{0:T(256)}, u32[]{:S(2)}) copy-start(s32[256]{0:T(256)} %param.7) | copy-start | bytes 3076
  21.5 5.9 %copy-start.4 = (s32[256]{0:T(256)S(1)}, s32[256]{0:T(256)}, u32[]{:S(2)}) copy-start(s32[256]{0:T(256)} %param.8) | copy-start | bytes 3076
  21.5 32.1 %all-to-all-start = ((bf16[32,8,16,128]{3,2,1,0:T(8,128)(2,1)}), bf16[32,8,16,128]{3,2,1,0:T(8,128)(2,1)S(1)}, u32[]{:S(2)}, u32[]{:S(2)}) async-start(bf16[32,8,16,128]{3,2,1,0:T(8,128)(2,1)} %shard_map.58), calls=%async_computation | async-start | bytes 2097152 | tf_op jit(solution)/shard_map/all_to_all | solution.py:541
  57.7 15.4 %collective-permute-start.3 = (bf16[512,128]{1,0:T(8,128)(2,1)S(1)}, bf16[512,128]{1,0:T(8,128)(2,1)S(1)}, u32[]{:S(2)}, u32[]{:S(2)}) collective-permute-start(bf16[512,128]{1,0:T(8,128)(2,1)S(1)} %get-tuple-element.27), channel_id=1, source_target_pairs={{0,4},{1,5},{2,6},{3,7},{4,0},{5,1},{6,2},{7,3},{8,12},{9,13},{10,... | collective-permute-start | bytes 393224 | tf_op jit(solution)/shard_map/ppermute | solution.py:431
  58.5 17.4 %collective-permute-start.4 = (bf16[512,128]{1,0:T(8,128)(2,1)S(1)}, bf16[512,128]{1,0:T(8,128)(2,1)S(1)}, u32[]{:S(2)}, u32[]{:S(2)}) collective-permute-start(bf16[512,128]{1,0:T(8,128)(2,1)S(1)} %get-tuple-element.29), channel_id=1, source_target_pairs={{0,5},{1,4},{2,7},{3,6},{4,1},{5,0},{6,3},{7,2},{8,13},{9,12},{10,... | collective-permute-start | bytes 393224 | tf_op jit(solution)/shard_map/ppermute | solution.py:431
  61.6 3.6 %collective-permute-start.6 = (bf16[16,128]{1,0:T(8,128)(2,1)S(1)}, bf16[16,128]{1,0:T(8,128)(2,1)S(1)}, u32[]{:S(2)}, u32[]{:S(2)}) collective-permute-start(bf16[16,128]{1,0:T(8,128)(2,1)S(1)} %get-tuple-element.33), channel_id=1, source_target_pairs={{0,1},{1,0},{2,3},{3,2},{4,5},{5,4},{6,7},{7,6},{8,9},{9,8},{10,11... | collective-permute-start | bytes 12296 | tf_op jit(solution)/shard_map/ppermute | solution.py:431
  62.1 16.4 %collective-permute-start.5 = (bf16[512,128]{1,0:T(8,128)(2,1)S(1)}, bf16[512,128]{1,0:T(8,128)(2,1)S(1)}, u32[]{:S(2)}, u32[]{:S(2)}) collective-permute-start(bf16[512,128]{1,0:T(8,128)(2,1)S(1)} %get-tuple-element.30), channel_id=1, source_target_pairs={{0,6},{1,7},{2,4},{3,5},{4,2},{5,3},{6,0},{7,1},{8,14},{9,15},{10,... | collective-permute-start | bytes 393224 | tf_op jit(solution)/shard_map/ppermute | solution.py:431
  68.1 10.4 %collective-permute-start.7 = (bf16[512,128]{1,0:T(8,128)(2,1)S(1)}, bf16[512,128]{1,0:T(8,128)(2,1)S(1)}, u32[]{:S(2)}, u32[]{:S(2)}) collective-permute-start(bf16[512,128]{1,0:T(8,128)(2,1)S(1)} %get-tuple-element.34), channel_id=1, source_target_pairs={{0,3},{1,2},{2,1},{3,0},{4,7},{5,6},{6,5},{7,4},{8,11},{9,10},{10,... | collective-permute-start | bytes 393224 | tf_op jit(solution)/shard_map/ppermute | solution.py:431
  69.0 12.7 %collective-permute-start.8 = (bf16[512,128]{1,0:T(8,128)(2,1)S(1)}, bf16[512,128]{1,0:T(8,128)(2,1)S(1)}, u32[]{:S(2)}, u32[]{:S(2)}) collective-permute-start(bf16[512,128]{1,0:T(8,128)(2,1)S(1)} %get-tuple-element.35), channel_id=1, source_target_pairs={{0,2},{1,3},{2,0},{3,1},{4,6},{5,7},{6,4},{7,5},{8,10},{9,11},{10,... | collective-permute-start | bytes 393224 | tf_op jit(solution)/shard_map/ppermute | solution.py:431
  73.1 9.0 %collective-permute-start.9 = (bf16[512,128]{1,0:T(8,128)(2,1)S(1)}, bf16[512,128]{1,0:T(8,128)(2,1)S(1)}, u32[]{:S(2)}, u32[]{:S(2)}) collective-permute-start(bf16[512,128]{1,0:T(8,128)(2,1)S(1)} %get-tuple-element.36), channel_id=1, source_target_pairs={{0,1},{1,0},{2,3},{3,2},{4,5},{5,4},{6,7},{7,6},{8,9},{9,8},{10,11... | collective-permute-start | bytes 393224 | tf_op jit(solution)/shard_map/ppermute | solution.py:431
  75.9 7.7 %collective-permute-start.10 = (bf16[512,128]{1,0:T(8,128)(2,1)S(1)}, bf16[512,128]{1,0:T(8,128)(2,1)S(1)}, u32[]{:S(2)}, u32[]{:S(2)}) collective-permute-start(bf16[512,128]{1,0:T(8,128)(2,1)S(1)} %get-tuple-element.38), channel_id=1, source_target_pairs={{0,7},{1,6},{2,5},{3,4},{4,3},{5,2},{6,1},{7,0},{8,15},{9,14},{10,... | collective-permute-start | bytes 393224 | tf_op jit(solution)/shard_map/ppermute | solution.py:431

commit v17 on v16

--- a/solution.py
+++ b/solution.py
@@ -460,9 +460,9 @@
             own = pl.ds(pl.multiple_of((place_ref[1] ^ s) * pairs, pairs), pairs)
             for i in range(step):
                 p = g * step + i
-                wide[p, own] = part[p * pairs : (p + 1) * pairs].astype(jnp.float32) * scale
+                wide[p, own] = part[p * pairs : (p + 1) * pairs]
         for i in range(step):
-            block = wide[g * step + i].T
+            block = wide[g * step + i].T.astype(jnp.float32) * scale
             ready[g, i, :, :rows] = block[:half_lanes]
             ready[g, i, :, rows:] = block[half_lanes:]
         copies.append(
@@ -485,7 +485,7 @@
         out_specs=pl.BlockSpec(memory_space=pl.ANY),
         out_shape=jax.ShapeDtypeStruct((slows, lanes // 2, 2 * rows), jnp.float32),
         scratch_shapes=[
-            pltpu.VMEM((slows, rows, lanes), jnp.float32),
+            pltpu.VMEM((slows, rows, lanes), jnp.bfloat16),
             pltpu.VMEM((slows // step, step, lanes // 2, 2 * rows), jnp.float32),
             pltpu.SemaphoreType.DMA((slows // step,)),
         ],

time: 86 us -> 85.9 us (level)
  no operation moved by 1% of the time
where the time goes in v17:
time: 85.9 us; the launch traced here: 85.6 us
  waiting for transfers between devices  43.5 us (51%)
  starting transfers between devices  20.1 us (23%)
  Pallas kernels  17.5 us (20%)
  local copies, waits for them, and re-layouts  3.56 us (4%)
    all_to_all x1, waiting for transfers between devices, local(): data = lax.all_to_all(spectrum, ('offset', 'freq'), 0, 0, tiled=True)  22.5 us
    ppermute x8, waiting for transfers between devices, swapped(): return lax.ppermute(part, 'offset', swaps)  11.9 us
    ppermute x8, starting transfers between devices, swapped(): return lax.ppermute(part, 'offset', swaps)  11 us
    ppermute x3, waiting for transfers between devices, local(): series[s] = lax.ppermute(series[s], 'freq', swaps)  9.08 us
    all_to_all x1, starting transfers between devices, local(): data = lax.all_to_all(spectrum, ('offset', 'freq'), 0, 0, tiled=True)  5.88 us
    pallas_call x1, Pallas kernels, radon_swapped(): pl.pallas_call(functools.partial(far_kernel, gathers, half), in_specs=[sm...  3.99 us
    pallas_call x1, Pallas kernels, moveout(): pl.pallas_call(functools.partial(moveout_kernel, shift, total_time), grid...  3.43 us
    unnamed x10, local copies, waits for them, and re-layouts  3.42 us
  transfers between devices with their start and end apart: 12, of which 9 were waited for; matrix products, arithmetic and copies ran while one was open for 0% of the time, Pallas kernels for 9%

profile of v17, /device:TPU:0, one launch (start us, length us, event | category | flops | bytes accessed | tf_op | source)
XLA Modules:
  0.0 85.6 jit_solution(342335735875982950)
XLA Ops:
  0.0 0.7 convert_element_type.18.slot_ref
  0.7 0.0 copy-start.2
  0.7 1.2 %copy-done.2 = bf16[1024,512]{1,0:T(8,128)(2,1)S(1)} copy-done((bf16[1024,512]{1,0:T(8,128)(2,1)S(1)}, bf16[1024,512]{1,0:T(8,128)(2,1)}, u32[]{:S(2)}) %copy-start.2) | copy-done | bytes 1048600
  1.9 2.0 %shard_map.56 = (bf16[256,512]{1,0:T(8,128)(2,1)S(1)}, bf16[256,512]{1,0:T(8,128)(2,1)S(1)}, bf16[256,512]{1,0:T(8,128)(2,1)S(1)}, bf16[256,512]{1,0:T(8,128)(2,1)S(1)}) custom-call(s32[1]{0:T(128)} %bitcast.5.me_ref, f32[32,32]{1,0:T(8,128)S(1)} %convert_element_type.18.slot_ref, bf16[1024,512]{1,0:T(8,128)(2,1)S(1)} %copy-done.2), custom_call_target="tpu_custom_call" | custom-call | tf_op jit(solution)/shard_map/pallas_call | solution.py:68
  3.9 0.5 collective-permute-start
  4.4 2.6 %collective-permute-start.1 = (bf16[256,512]{1,0:T(8,128)(2,1)S(1)}, bf16[256,512]{1,0:T(8,128)(2,1)S(1)}, u32[]{:S(2)}, u32[]{:S(2)}) collective-permute-start(bf16[256,512]{1,0:T(8,128)(2,1)S(1)} %get-tuple-element.24), channel_id=1, source_target_pairs={{0,16},{8,24},{16,0},{24,8},{1,17},{9,25},{17,1},{25,9},{2,18},{10... | collective-permute-start | bytes 786440 | tf_op jit(solution)/shard_map/ppermute | solution.py:538
  7.0 0.1 collective-permute-start.2
  7.1 0.0 collective-permute-done.refs_1_
  7.1 0.0 copy-start
  7.1 2.2 %copy-done = bf16[1024,2048]{1,0:T(8,128)(2,1)S(1)} copy-done((bf16[1024,2048]{1,0:T(8,128)(2,1)S(1)}, bf16[1024,2048]{1,0:T(8,128)(2,1)}, u32[]{:S(2)}) %copy-start) | copy-done | bytes 4194328
  9.3 0.0 copy-start.1
  9.3 0.9 %shard_map.57.begun_ref = f32[2,1024,256]{2,1,0:T(8,128)S(1)} custom-call(s32[1]{0:T(128)} %bitcast.5.me_ref, bf16[1024,2048]{1,0:T(8,128)(2,1)S(1)} %copy-done, bf16[256,512]{1,0:T(8,128)(2,1)S(1)} %get-tuple-element.22.refs_0_, bf16[256,512]{1,0:T(8,128)(2,1)S(1)} %collective-permute-done.refs_1_), custom_call_target="tpu_custom_call" | custom-call | flops 536870912 | bytes 4194304 | tf_op jit(solution)/shard_map/pallas_call | solution.py:185
  10.2 4.0 %collective-permute-done.1.refs_0_ = bf16[256,512]{1,0:T(8,128)(2,1)S(1)} collective-permute-done((bf16[256,512]{1,0:T(8,128)(2,1)S(1)}, bf16[256,512]{1,0:T(8,128)(2,1)S(1)}, u32[]{:S(2)}, u32[]{:S(2)}) %collective-permute-start.1) | collective-permute-done | bytes 262176 | tf_op jit(solution)/shard_map/ppermute | solution.py:538
  14.2 5.1 %collective-permute-done.2.refs_1_ = bf16[256,512]{1,0:T(8,128)(2,1)S(1)} collective-permute-done((bf16[256,512]{1,0:T(8,128)(2,1)S(1)}, bf16[256,512]{1,0:T(8,128)(2,1)S(1)}, u32[]{:S(2)}, u32[]{:S(2)}) %collective-permute-start.2) | collective-permute-done | bytes 262176 | tf_op jit(solution)/shard_map/ppermute | solution.py:538
  19.3 0.0 copy-done.1
  19.3 2.2 %shard_map.58 = bf16[32,8,16,128]{3,2,1,0:T(8,128)(2,1)} custom-call(s32[1]{0:T(128)} %bitcast.5.me_ref, bf16[1024,2048]{1,0:T(8,128)(2,1)S(1)} %copy-done.1, f32[2,1024,256]{2,1,0:T(8,128)S(1)} %shard_map.57.begun_ref, bf16[256,512]{1,0:T(8,128)(2,1)S(1)} %collective-permute-done.1.refs_0_, bf16[256,512]{1,0:T(8,128)(2,1)S(1)} %collective-permute-done.2.refs_1_), custom_call_target="tpu_custom_call" | custom-call | tf_op jit(solution)/shard_map/pallas_call | solution.py:198
  21.5 0.0 copy-start.3
  21.5 0.0 copy-start.4
  21.5 5.9 %all-to-all-start = ((bf16[32,8,16,128]{3,2,1,0:T(8,128)(2,1)}), bf16[32,8,16,128]{3,2,1,0:T(8,128)(2,1)S(1)}, u32[]{:S(2)}, u32[]{:S(2)}) async-start(bf16[32,8,16,128]{3,2,1,0:T(8,128)(2,1)} %shard_map.58), calls=%async_computation | async-start | bytes 2097152 | tf_op jit(solution)/shard_map/all_to_all | solution.py:541
  27.5 0.0 copy-done.3
  27.5 0.0 copy-done.4
  27.5 0.1 copy.6.slow_ref
  27.7 3.4 %shard_map.55.state_ref = f32[6,256,256]{2,1,0:T(8,128)S(1)} custom-call(f32[1]{0:T(128)} %bitcast.2.base_ref, f32[256,1]{1,0:T(8,128)S(1)} %copy.6.slow_ref, f32[1,256]{1,0:T(1,128)S(1)} %bitcast.7), custom_call_target="tpu_custom_call" | custom-call | flops 19660800 | bytes 1572864 | tf_op jit(solution)/shard_map/pallas_call | solution.py:235
  31.1 0.1 pad_add_fusion.place_ref
  31.2 22.5 %all-to-all-done.data_ref = bf16[32,8,16,128]{3,2,1,0:T(8,128)(2,1)S(1)} async-done(((bf16[32,8,16,128]{3,2,1,0:T(8,128)(2,1)}), bf16[32,8,16,128]{3,2,1,0:T(8,128)(2,1)S(1)}, u32[]{:S(2)}, u32[]{:S(2)}) %all-to-all-start) | async-done | bytes 1048608 | tf_op jit(solution)/shard_map/all_to_all | solution.py:541
  53.7 4.0 %shard_map.59 = (bf16[16,256,128]{2,1,0:T(8,128)(2,1)S(1)}, bf16[16,256,128]{2,1,0:T(8,128)(2,1)S(1)}, bf16[16,128]{1,0:T(8,128)(2,1)S(1)}, bf16[512,128]{1,0:T(...) custom-call(s32[2]{0:T(128)S(1)} %pad_add_fusion.place_ref, ...), custom_call_target="tpu_custom_call" | custom-call | flops 1073741824 | bytes 524288 | tf_op jit(solution)/shard_map/pallas_call | solution.py:420
  57.7 0.8 collective-permute-start.3
  58.5 3.1 %collective-permute-start.4 = (bf16[512,128]{1,0:T(8,128)(2,1)S(1)}, bf16[512,128]{1,0:T(8,128)(2,1)S(1)}, u32[]{:S(2)}, u32[]{:S(2)}) collective-permute-start(bf16[512,128]{1,0:T(8,128)(2,1)S(1)} %get-tuple-element.29), channel_id=1, source_target_pairs={{0,5},{1,4},{2,7},{3,6},{4,1},{5,0},{6,3},{7,2},{8,13},{9,12},{10,... | collective-permute-start | bytes 393224 | tf_op jit(solution)/shard_map/ppermute | solution.py:431
  61.6 0.6 collective-permute-start.6
  62.1 1.3 %collective-permute-start.5 = (bf16[512,128]{1,0:T(8,128)(2,1)S(1)}, bf16[512,128]{1,0:T(8,128)(2,1)S(1)}, u32[]{:S(2)}, u32[]{:S(2)}) collective-permute-start(bf16[512,128]{1,0:T(8,128)(2,1)S(1)} %get-tuple-element.30), channel_id=1, source_target_pairs={{0,6},{1,7},{2,4},{3,5},{4,2},{5,3},{6,0},{7,1},{8,14},{9,15},{10,... | collective-permute-start | bytes 393224 | tf_op jit(solution)/shard_map/ppermute | solution.py:431
  63.4 1.8 %collective-permute-done.6._ = bf16[16,128]{1,0:T(8,128)(2,1)S(1)} collective-permute-done((bf16[16,128]{1,0:T(8,128)(2,1)S(1)}, bf16[16,128]{1,0:T(8,128)(2,1)S(1)}, u32[]{:S(2)}, u32[]{:S(2)}) %collective-permute-start.6) | collective-permute-done | bytes 4128 | tf_op jit(solution)/shard_map/ppermute | solution.py:431
  65.2 3.0 %shard_map.60 = (bf16[512,128]{1,0:T(8,128)(2,1)S(1)}, bf16[512,128]{1,0:T(8,128)(2,1)S(1)}, bf16[512,128]{1,0:T(8,128)(2,1)S(1)}, bf16[512,128]{1,0:T(8,128)(2,1)S(1)}) custom-call(s32[2]{0:T(128)S(1)} %pad_add_fusion.place_ref, f32[6,256,256]{2,1,0:T(8,128)S(1)} %shard_map.55.state_ref, bf16[16,256,128]{2,1,0:T(8,128)(2,1)S(1)} %get-tuple-element.31.plain, ...), custom_call_target="tpu_custom_call" | custom-call | flops 1073741824 | bytes 524288 | tf_op jit(solution)/shard_map/pallas_call | solution.py:435
  68.1 0.9 %collective-permute-start.7 = (bf16[512,128]{1,0:T(8,128)(2,1)S(1)}, bf16[512,128]{1,0:T(8,128)(2,1)S(1)}, u32[]{:S(2)}, u32[]{:S(2)}) collective-permute-start(bf16[512,128]{1,0:T(8,128)(2,1)S(1)} %get-tuple-element.34), channel_id=1, source_target_pairs={{0,3},{1,2},{2,1},{3,0},{4,7},{5,6},{6,5},{7,4},{8,11},{9,10},{10,... | collective-permute-start | bytes 393224 | tf_op jit(solution)/shard_map/ppermute | solution.py:431
  69.0 1.2 %collective-permute-start.8 = (bf16[512,128]{1,0:T(8,128)(2,1)S(1)}, bf16[512,128]{1,0:T(8,128)(2,1)S(1)}, u32[]{:S(2)}, u32[]{:S(2)}) collective-permute-start(bf16[512,128]{1,0:T(8,128)(2,1)S(1)} %get-tuple-element.35), channel_id=1, source_target_pairs={{0,2},{1,3},{2,0},{3,1},{4,6},{5,7},{6,4},{7,5},{8,10},{9,11},{10,... | collective-permute-start | bytes 393224 | tf_op jit(solution)/shard_map/ppermute | solution.py:431
  70.2 2.9 %collective-permute-done.3.refs_0_ = bf16[512,128]{1,0:T(8,128)(2,1)S(1)} collective-permute-done((bf16[512,128]{1,0:T(8,128)(2,1)S(1)}, bf16[512,128]{1,0:T(8,128)(2,1)S(1)}, u32[]{:S(2)}, u32[]{:S(2)}) %collective-permute-start.3) | collective-permute-done | bytes 131104 | tf_op jit(solution)/shard_map/ppermute | solution.py:431
  73.1 0.6 collective-permute-start.9
  73.6 2.2 %collective-permute-done.4.refs_1_ = bf16[512,128]{1,0:T(8,128)(2,1)S(1)} collective-permute-done((bf16[512,128]{1,0:T(8,128)(2,1)S(1)}, bf16[512,128]{1,0:T(8,128)(2,1)S(1)}, u32[]{:S(2)}, u32[]{:S(2)}) %collective-permute-start.4) | collective-permute-done | bytes 131104 | tf_op jit(solution)/shard_map/ppermute | solution.py:431
  75.9 2.7 %collective-permute-start.10 = (bf16[512,128]{1,0:T(8,128)(2,1)S(1)}, bf16[512,128]{1,0:T(8,128)(2,1)S(1)}, u32[]{:S(2)}, u32[]{:S(2)}) collective-permute-start(bf16[512,128]{1,0:T(8,128)(2,1)S(1)} %get-tuple-element.38), channel_id=1, source_target_pairs={{0,7},{1,6},{2,5},{3,4},{4,3},{5,2},{6,1},{7,0},{8,15},{9,14},{10,... | collective-permute-start | bytes 393224 | tf_op jit(solution)/shard_map/ppermute | solution.py:431
  78.5 0.0 collective-permute-done.5.refs_2_
  78.5 0.0 collective-permute-done.7.refs_3_
  78.6 3.1 %collective-permute-done.8.refs_4_ = bf16[512,128]{1,0:T(8,128)(2,1)S(1)} collective-permute-done((bf16[512,128]{1,0:T(8,128)(2,1)S(1)}, bf16[512,128]{1,0:T(8,128)(2,1)S(1)}, u32[]{:S(2)}, u32[]{:S(2)}) %collective-permute-start.8) | collective-permute-done | bytes 131104 | tf_op jit(solution)/shard_map/ppermute | solution.py:431
  81.7 0.4 collective-permute-done.9.refs_5_
  82.1 1.4 %collective-permute-done.10.refs_7_ = bf16[512,128]{1,0:T(8,128)(2,1)S(1)} collective-permute-done((bf16[512,128]{1,0:T(8,128)(2,1)S(1)}, bf16[512,128]{1,0:T(8,128)(2,1)S(1)}, u32[]{:S(2)}, u32[]{:S(2)}) %collective-permute-start.10) | collective-permute-done | bytes 131104 | tf_op jit(solution)/shard_map/ppermute | solution.py:431
  83.6 2.0 %shard_map.61 = f32[32,64,256]{2,1,0:T(8,128)} custom-call(s32[2]{0:T(128)S(1)} %pad_add_fusion.place_ref, bf16[512,128]{1,0:T(8,128)(2,1)S(1)} %collective-permute-done.3.refs_0_, bf16[512,128]{1,0:T(8,128)(2,1)S(1)} %collective-permute-done.4.refs_1_, bf16[512,128]{1,0:T(8,128)(2,1)S(1)} %collective-permute-done.5.refs_2_, ...), custom_call_target="tpu_custom_call" | custom-call | tf_op jit(solution)/shard_map/pallas_call | solution.py:482
  (2 shorter events, 0.0 us)
Async XLA Ops:
  0.7 1.2 %copy-start.2 = (bf16[1024,512]{1,0:T(8,128)(2,1)S(1)}, bf16[1024,512]{1,0:T(8,128)(2,1)}, u32[]{:S(2)}) copy-start(bf16[1024,512]{1,0:T(8,128)(2,1)} %raw_ref.1) | copy-start | bytes 3145732
  3.9 3.2 %collective-permute-start = (bf16[256,512]{1,0:T(8,128)(2,1)S(1)}, bf16[256,512]{1,0:T(8,128)(2,1)S(1)}, u32[]{:S(2)}, u32[]{:S(2)}) collective-permute-start(bf16[256,512]{1,0:T(8,128)(2,1)S(1)} %get-tuple-element.23), channel_id=1, source_target_pairs={{0,8},{8,0},{16,24},{24,16},{1,9},{9,1},{17,25},{25,17},{2,10},{10... | collective-permute-start | bytes 786440 | tf_op jit(solution)/shard_map/ppermute | solution.py:538
  4.4 9.8 %collective-permute-start.1 = (bf16[256,512]{1,0:T(8,128)(2,1)S(1)}, bf16[256,512]{1,0:T(8,128)(2,1)S(1)}, u32[]{:S(2)}, u32[]{:S(2)}) collective-permute-start(bf16[256,512]{1,0:T(8,128)(2,1)S(1)} %get-tuple-element.24), channel_id=1, source_target_pairs={{0,16},{8,24},{16,0},{24,8},{1,17},{9,25},{17,1},{25,9},{2,18},{10... | collective-permute-start | bytes 786440 | tf_op jit(solution)/shard_map/ppermute | solution.py:538
  7.0 12.3 %collective-permute-start.2 = (bf16[256,512]{1,0:T(8,128)(2,1)S(1)}, bf16[256,512]{1,0:T(8,128)(2,1)S(1)}, u32[]{:S(2)}, u32[]{:S(2)}) collective-permute-start(bf16[256,512]{1,0:T(8,128)(2,1)S(1)} %get-tuple-element.25), channel_id=1, source_target_pairs={{0,24},{8,16},{16,8},{24,0},{1,25},{9,17},{17,9},{25,1},{2,26},{10... | collective-permute-start | bytes 786440 | tf_op jit(solution)/shard_map/ppermute | solution.py:538
  7.1 2.2 %copy-start = (bf16[1024,2048]{1,0:T(8,128)(2,1)S(1)}, bf16[1024,2048]{1,0:T(8,128)(2,1)}, u32[]{:S(2)}) copy-start(bf16[1024,2048]{1,0:T(8,128)(2,1)} %constant.35.clone.table_ref) | copy-start | bytes 12582916
  9.3 10.0 %copy-start.1 = (bf16[1024,2048]{1,0:T(8,128)(2,1)S(1)}, bf16[1024,2048]{1,0:T(8,128)(2,1)}, u32[]{:S(2)}) copy-start(bf16[1024,2048]{1,0:T(8,128)(2,1)} %constant.35.clone.table_ref) | copy-start | bytes 12582916
  21.5 5.9 %copy-start.3 = (s32[256]{0:T(256)S(1)}, s32[256]{0:T(256)}, u32[]{:S(2)}) copy-start(s32[256]{0:T(256)} %param.7) | copy-start | bytes 3076
  21.5 5.9 %copy-start.4 = (s32[256]{0:T(256)S(1)}, s32[256]{0:T(256)}, u32[]{:S(2)}) copy-start(s32[256]{0:T(256)} %param.8) | copy-start | bytes 3076
  21.5 32.1 %all-to-all-start = ((bf16[32,8,16,128]{3,2,1,0:T(8,128)(2,1)}), bf16[32,8,16,128]{3,2,1,0:T(8,128)(2,1)S(1)}, u32[]{:S(2)}, u32[]{:S(2)}) async-start(bf16[32,8,16,128]{3,2,1,0:T(8,128)(2,1)} %shard_map.58), calls=%async_computation | async-start | bytes 2097152 | tf_op jit(solution)/shard_map/all_to_all | solution.py:541
  57.7 15.4 %collective-permute-start.3 = (bf16[512,128]{1,0:T(8,128)(2,1)S(1)}, bf16[512,128]{1,0:T(8,128)(2,1)S(1)}, u32[]{:S(2)}, u32[]{:S(2)}) collective-permute-start(bf16[512,128]{1,0:T(8,128)(2,1)S(1)} %get-tuple-element.27), channel_id=1, source_target_pairs={{0,4},{1,5},{2,6},{3,7},{4,0},{5,1},{6,2},{7,3},{8,12},{9,13},{10,... | collective-permute-start | bytes 393224 | tf_op jit(solution)/shard_map/ppermute | solution.py:431
  58.5 17.4 %collective-permute-start.4 = (bf16[512,128]{1,0:T(8,128)(2,1)S(1)}, bf16[512,128]{1,0:T(8,128)(2,1)S(1)}, u32[]{:S(2)}, u32[]{:S(2)}) collective-permute-start(bf16[512,128]{1,0:T(8,128)(2,1)S(1)} %get-tuple-element.29), channel_id=1, source_target_pairs={{0,5},{1,4},{2,7},{3,6},{4,1},{5,0},{6,3},{7,2},{8,13},{9,12},{10,... | collective-permute-start | bytes 393224 | tf_op jit(solution)/shard_map/ppermute | solution.py:431
  61.6 3.6 %collective-permute-start.6 = (bf16[16,128]{1,0:T(8,128)(2,1)S(1)}, bf16[16,128]{1,0:T(8,128)(2,1)S(1)}, u32[]{:S(2)}, u32[]{:S(2)}) collective-permute-start(bf16[16,128]{1,0:T(8,128)(2,1)S(1)} %get-tuple-element.33), channel_id=1, source_target_pairs={{0,1},{1,0},{2,3},{3,2},{4,5},{5,4},{6,7},{7,6},{8,9},{9,8},{10,11... | collective-permute-start | bytes 12296 | tf_op jit(solution)/shard_map/ppermute | solution.py:431
  62.1 16.4 %collective-permute-start.5 = (bf16[512,128]{1,0:T(8,128)(2,1)S(1)}, bf16[512,128]{1,0:T(8,128)(2,1)S(1)}, u32[]{:S(2)}, u32[]{:S(2)}) collective-permute-start(bf16[512,128]{1,0:T(8,128)(2,1)S(1)} %get-tuple-element.30), channel_id=1, source_target_pairs={{0,6},{1,7},{2,4},{3,5},{4,2},{5,3},{6,0},{7,1},{8,14},{9,15},{10,... | collective-permute-start | bytes 393224 | tf_op jit(solution)/shard_map/ppermute | solution.py:431
  68.1 10.4 %collective-permute-start.7 = (bf16[512,128]{1,0:T(8,128)(2,1)S(1)}, bf16[512,128]{1,0:T(8,128)(2,1)S(1)}, u32[]{:S(2)}, u32[]{:S(2)}) collective-permute-start(bf16[512,128]{1,0:T(8,128)(2,1)S(1)} %get-tuple-element.34), channel_id=1, source_target_pairs={{0,3},{1,2},{2,1},{3,0},{4,7},{5,6},{6,5},{7,4},{8,11},{9,10},{10,... | collective-permute-start | bytes 393224 | tf_op jit(solution)/shard_map/ppermute | solution.py:431
  69.0 12.7 %collective-permute-start.8 = (bf16[512,128]{1,0:T(8,128)(2,1)S(1)}, bf16[512,128]{1,0:T(8,128)(2,1)S(1)}, u32[]{:S(2)}, u32[]{:S(2)}) collective-permute-start(bf16[512,128]{1,0:T(8,128)(2,1)S(1)} %get-tuple-element.35), channel_id=1, source_target_pairs={{0,2},{1,3},{2,0},{3,1},{4,6},{5,7},{6,4},{7,5},{8,10},{9,11},{10,... | collective-permute-start | bytes 393224 | tf_op jit(solution)/shard_map/ppermute | solution.py:431
  73.1 9.0 %collective-permute-start.9 = (bf16[512,128]{1,0:T(8,128)(2,1)S(1)}, bf16[512,128]{1,0:T(8,128)(2,1)S(1)}, u32[]{:S(2)}, u32[]{:S(2)}) collective-permute-start(bf16[512,128]{1,0:T(8,128)(2,1)S(1)} %get-tuple-element.36), channel_id=1, source_target_pairs={{0,1},{1,0},{2,3},{3,2},{4,5},{5,4},{6,7},{7,6},{8,9},{9,8},{10,11... | collective-permute-start | bytes 393224 | tf_op jit(solution)/shard_map/ppermute | solution.py:431
  75.9 7.7 %collective-permute-start.10 = (bf16[512,128]{1,0:T(8,128)(2,1)S(1)}, bf16[512,128]{1,0:T(8,128)(2,1)S(1)}, u32[]{:S(2)}, u32[]{:S(2)}) collective-permute-start(bf16[512,128]{1,0:T(8,128)(2,1)S(1)} %get-tuple-element.38), channel_id=1, source_target_pairs={{0,7},{1,6},{2,5},{3,4},{4,3},{5,2},{6,1},{7,0},{8,15},{9,14},{10,... | collective-permute-start | bytes 393224 | tf_op jit(solution)/shard_map/ppermute | solution.py:431

commit v18 on v17

--- a/solution.py
+++ b/solution.py
@@ -477,7 +477,7 @@
     pairs = parts[0].shape[0] // slows
     lanes = parts[0].shape[1]
     rows = len(parts) * pairs
-    step = 4
+    step = 2
     vmem = pl.BlockSpec(memory_space=pltpu.VMEM)
     return pl.pallas_call(
         functools.partial(join_kernel, scale, order),

time: 85.9 us -> 86 us (level)
  no operation moved by 1% of the time
where the time goes in v18:
time: 86 us; the launch traced here: 85.6 us
  waiting for transfers between devices  43.5 us (51%)
  starting transfers between devices  20.1 us (23%)
  Pallas kernels  17.6 us (20%)
  local copies, waits for them, and re-layouts  3.56 us (4%)
    all_to_all x1, waiting for transfers between devices, local(): data = lax.all_to_all(spectrum, ('offset', 'freq'), 0, 0, tiled=True)  22.5 us
    ppermute x8, waiting for transfers between devices, swapped(): return lax.ppermute(part, 'offset', swaps)  11.9 us
    ppermute x8, starting transfers between devices, swapped(): return lax.ppermute(part, 'offset', swaps)  11 us
    ppermute x3, waiting for transfers between devices, local(): series[s] = lax.ppermute(series[s], 'freq', swaps)  9.08 us
    all_to_all x1, starting transfers between devices, local(): data = lax.all_to_all(spectrum, ('offset', 'freq'), 0, 0, tiled=True)  5.88 us
    pallas_call x1, Pallas kernels, radon_swapped(): pl.pallas_call(functools.partial(far_kernel, gathers, half), in_specs=[sm...  3.99 us
    pallas_call x1, Pallas kernels, moveout(): pl.pallas_call(functools.partial(moveout_kernel, shift, total_time), grid...  3.43 us
    unnamed x10, local copies, waits for them, and re-layouts  3.42 us
  transfers between devices with their start and end apart: 12, of which 9 were waited for; matrix products, arithmetic and copies ran while one was open for 0% of the time, Pallas kernels for 9%

profile of v18, /device:TPU:0, one launch (start us, length us, event | category | flops | bytes accessed | tf_op | source)
XLA Modules:
  0.0 85.6 jit_solution(14172832915151200255)
XLA Ops:
  0.0 0.7 convert_element_type.18.slot_ref
  0.7 0.0 copy-start.2
  0.7 1.2 %copy-done.2 = bf16[1024,512]{1,0:T(8,128)(2,1)S(1)} copy-done((bf16[1024,512]{1,0:T(8,128)(2,1)S(1)}, bf16[1024,512]{1,0:T(8,128)(2,1)}, u32[]{:S(2)}) %copy-start.2) | copy-done | bytes 1048600
  1.9 2.0 %shard_map.56 = (bf16[256,512]{1,0:T(8,128)(2,1)S(1)}, bf16[256,512]{1,0:T(8,128)(2,1)S(1)}, bf16[256,512]{1,0:T(8,128)(2,1)S(1)}, bf16[256,512]{1,0:T(8,128)(2,1)S(1)}) custom-call(s32[1]{0:T(128)} %bitcast.5.me_ref, f32[32,32]{1,0:T(8,128)S(1)} %convert_element_type.18.slot_ref, bf16[1024,512]{1,0:T(8,128)(2,1)S(1)} %copy-done.2), custom_call_target="tpu_custom_call" | custom-call | tf_op jit(solution)/shard_map/pallas_call | solution.py:68
  3.9 0.5 collective-permute-start
  4.4 2.6 %collective-permute-start.1 = (bf16[256,512]{1,0:T(8,128)(2,1)S(1)}, bf16[256,512]{1,0:T(8,128)(2,1)S(1)}, u32[]{:S(2)}, u32[]{:S(2)}) collective-permute-start(bf16[256,512]{1,0:T(8,128)(2,1)S(1)} %get-tuple-element.24), channel_id=1, source_target_pairs={{0,16},{8,24},{16,0},{24,8},{1,17},{9,25},{17,1},{25,9},{2,18},{10... | collective-permute-start | bytes 786440 | tf_op jit(solution)/shard_map/ppermute | solution.py:538
  7.0 0.1 collective-permute-start.2
  7.1 0.0 collective-permute-done.refs_1_
  7.1 0.0 copy-start
  7.1 2.2 %copy-done = bf16[1024,2048]{1,0:T(8,128)(2,1)S(1)} copy-done((bf16[1024,2048]{1,0:T(8,128)(2,1)S(1)}, bf16[1024,2048]{1,0:T(8,128)(2,1)}, u32[]{:S(2)}) %copy-start) | copy-done | bytes 4194328
  9.3 0.0 copy-start.1
  9.3 0.9 %shard_map.57.begun_ref = f32[2,1024,256]{2,1,0:T(8,128)S(1)} custom-call(s32[1]{0:T(128)} %bitcast.5.me_ref, bf16[1024,2048]{1,0:T(8,128)(2,1)S(1)} %copy-done, bf16[256,512]{1,0:T(8,128)(2,1)S(1)} %get-tuple-element.22.refs_0_, bf16[256,512]{1,0:T(8,128)(2,1)S(1)} %collective-permute-done.refs_1_), custom_call_target="tpu_custom_call" | custom-call | flops 536870912 | bytes 4194304 | tf_op jit(solution)/shard_map/pallas_call | solution.py:185
  10.2 4.0 %collective-permute-done.1.refs_0_ = bf16[256,512]{1,0:T(8,128)(2,1)S(1)} collective-permute-done((bf16[256,512]{1,0:T(8,128)(2,1)S(1)}, bf16[256,512]{1,0:T(8,128)(2,1)S(1)}, u32[]{:S(2)}, u32[]{:S(2)}) %collective-permute-start.1) | collective-permute-done | bytes 262176 | tf_op jit(solution)/shard_map/ppermute | solution.py:538
  14.2 5.1 %collective-permute-done.2.refs_1_ = bf16[256,512]{1,0:T(8,128)(2,1)S(1)} collective-permute-done((bf16[256,512]{1,0:T(8,128)(2,1)S(1)}, bf16[256,512]{1,0:T(8,128)(2,1)S(1)}, u32[]{:S(2)}, u32[]{:S(2)}) %collective-permute-start.2) | collective-permute-done | bytes 262176 | tf_op jit(solution)/shard_map/ppermute | solution.py:538
  19.3 0.0 copy-done.1
  19.3 2.2 %shard_map.58 = bf16[32,8,16,128]{3,2,1,0:T(8,128)(2,1)} custom-call(s32[1]{0:T(128)} %bitcast.5.me_ref, bf16[1024,2048]{1,0:T(8,128)(2,1)S(1)} %copy-done.1, f32[2,1024,256]{2,1,0:T(8,128)S(1)} %shard_map.57.begun_ref, bf16[256,512]{1,0:T(8,128)(2,1)S(1)} %collective-permute-done.1.refs_0_, bf16[256,512]{1,0:T(8,128)(2,1)S(1)} %collective-permute-done.2.refs_1_), custom_call_target="tpu_custom_call" | custom-call | tf_op jit(solution)/shard_map/pallas_call | solution.py:198
  21.5 0.0 copy-start.3
  21.5 0.0 copy-start.4
  21.5 5.9 %all-to-all-start = ((bf16[32,8,16,128]{3,2,1,0:T(8,128)(2,1)}), bf16[32,8,16,128]{3,2,1,0:T(8,128)(2,1)S(1)}, u32[]{:S(2)}, u32[]{:S(2)}) async-start(bf16[32,8,16,128]{3,2,1,0:T(8,128)(2,1)} %shard_map.58), calls=%async_computation | async-start | bytes 2097152 | tf_op jit(solution)/shard_map/all_to_all | solution.py:541
  27.5 0.0 copy-done.3
  27.5 0.0 copy-done.4
  27.5 0.1 copy.6.slow_ref
  27.7 3.4 %shard_map.55.state_ref = f32[6,256,256]{2,1,0:T(8,128)S(1)} custom-call(f32[1]{0:T(128)} %bitcast.2.base_ref, f32[256,1]{1,0:T(8,128)S(1)} %copy.6.slow_ref, f32[1,256]{1,0:T(1,128)S(1)} %bitcast.7), custom_call_target="tpu_custom_call" | custom-call | flops 19660800 | bytes 1572864 | tf_op jit(solution)/shard_map/pallas_call | solution.py:235
  31.1 0.1 pad_add_fusion.place_ref
  31.2 22.5 %all-to-all-done.data_ref = bf16[32,8,16,128]{3,2,1,0:T(8,128)(2,1)S(1)} async-done(((bf16[32,8,16,128]{3,2,1,0:T(8,128)(2,1)}), bf16[32,8,16,128]{3,2,1,0:T(8,128)(2,1)S(1)}, u32[]{:S(2)}, u32[]{:S(2)}) %all-to-all-start) | async-done | bytes 1048608 | tf_op jit(solution)/shard_map/all_to_all | solution.py:541
  53.7 4.0 %shard_map.59 = (bf16[16,256,128]{2,1,0:T(8,128)(2,1)S(1)}, bf16[16,256,128]{2,1,0:T(8,128)(2,1)S(1)}, bf16[16,128]{1,0:T(8,128)(2,1)S(1)}, bf16[512,128]{1,0:T(...) custom-call(s32[2]{0:T(128)S(1)} %pad_add_fusion.place_ref, ...), custom_call_target="tpu_custom_call" | custom-call | flops 1073741824 | bytes 524288 | tf_op jit(solution)/shard_map/pallas_call | solution.py:420
  57.7 0.8 collective-permute-start.3
  58.5 3.1 %collective-permute-start.4 = (bf16[512,128]{1,0:T(8,128)(2,1)S(1)}, bf16[512,128]{1,0:T(8,128)(2,1)S(1)}, u32[]{:S(2)}, u32[]{:S(2)}) collective-permute-start(bf16[512,128]{1,0:T(8,128)(2,1)S(1)} %get-tuple-element.29), channel_id=1, source_target_pairs={{0,5},{1,4},{2,7},{3,6},{4,1},{5,0},{6,3},{7,2},{8,13},{9,12},{10,... | collective-permute-start | bytes 393224 | tf_op jit(solution)/shard_map/ppermute | solution.py:431
  61.6 0.6 collective-permute-start.6
  62.1 1.3 %collective-permute-start.5 = (bf16[512,128]{1,0:T(8,128)(2,1)S(1)}, bf16[512,128]{1,0:T(8,128)(2,1)S(1)}, u32[]{:S(2)}, u32[]{:S(2)}) collective-permute-start(bf16[512,128]{1,0:T(8,128)(2,1)S(1)} %get-tuple-element.30), channel_id=1, source_target_pairs={{0,6},{1,7},{2,4},{3,5},{4,2},{5,3},{6,0},{7,1},{8,14},{9,15},{10,... | collective-permute-start | bytes 393224 | tf_op jit(solution)/shard_map/ppermute | solution.py:431
  63.4 1.8 %collective-permute-done.6._ = bf16[16,128]{1,0:T(8,128)(2,1)S(1)} collective-permute-done((bf16[16,128]{1,0:T(8,128)(2,1)S(1)}, bf16[16,128]{1,0:T(8,128)(2,1)S(1)}, u32[]{:S(2)}, u32[]{:S(2)}) %collective-permute-start.6) | collective-permute-done | bytes 4128 | tf_op jit(solution)/shard_map/ppermute | solution.py:431
  65.2 3.0 %shard_map.60 = (bf16[512,128]{1,0:T(8,128)(2,1)S(1)}, bf16[512,128]{1,0:T(8,128)(2,1)S(1)}, bf16[512,128]{1,0:T(8,128)(2,1)S(1)}, bf16[512,128]{1,0:T(8,128)(2,1)S(1)}) custom-call(s32[2]{0:T(128)S(1)} %pad_add_fusion.place_ref, f32[6,256,256]{2,1,0:T(8,128)S(1)} %shard_map.55.state_ref, bf16[16,256,128]{2,1,0:T(8,128)(2,1)S(1)} %get-tuple-element.31.plain, ...), custom_call_target="tpu_custom_call" | custom-call | flops 1073741824 | bytes 524288 | tf_op jit(solution)/shard_map/pallas_call | solution.py:435
  68.1 0.9 %collective-permute-start.7 = (bf16[512,128]{1,0:T(8,128)(2,1)S(1)}, bf16[512,128]{1,0:T(8,128)(2,1)S(1)}, u32[]{:S(2)}, u32[]{:S(2)}) collective-permute-start(bf16[512,128]{1,0:T(8,128)(2,1)S(1)} %get-tuple-element.34), channel_id=1, source_target_pairs={{0,3},{1,2},{2,1},{3,0},{4,7},{5,6},{6,5},{7,4},{8,11},{9,10},{10,... | collective-permute-start | bytes 393224 | tf_op jit(solution)/shard_map/ppermute | solution.py:431
  69.0 1.2 %collective-permute-start.8 = (bf16[512,128]{1,0:T(8,128)(2,1)S(1)}, bf16[512,128]{1,0:T(8,128)(2,1)S(1)}, u32[]{:S(2)}, u32[]{:S(2)}) collective-permute-start(bf16[512,128]{1,0:T(8,128)(2,1)S(1)} %get-tuple-element.35), channel_id=1, source_target_pairs={{0,2},{1,3},{2,0},{3,1},{4,6},{5,7},{6,4},{7,5},{8,10},{9,11},{10,... | collective-permute-start | bytes 393224 | tf_op jit(solution)/shard_map/ppermute | solution.py:431
  70.2 2.9 %collective-permute-done.3.refs_0_ = bf16[512,128]{1,0:T(8,128)(2,1)S(1)} collective-permute-done((bf16[512,128]{1,0:T(8,128)(2,1)S(1)}, bf16[512,128]{1,0:T(8,128)(2,1)S(1)}, u32[]{:S(2)}, u32[]{:S(2)}) %collective-permute-start.3) | collective-permute-done | bytes 131104 | tf_op jit(solution)/shard_map/ppermute | solution.py:431
  73.1 0.6 collective-permute-start.9
  73.6 2.2 %collective-permute-done.4.refs_1_ = bf16[512,128]{1,0:T(8,128)(2,1)S(1)} collective-permute-done((bf16[512,128]{1,0:T(8,128)(2,1)S(1)}, bf16[512,128]{1,0:T(8,128)(2,1)S(1)}, u32[]{:S(2)}, u32[]{:S(2)}) %collective-permute-start.4) | collective-permute-done | bytes 131104 | tf_op jit(solution)/shard_map/ppermute | solution.py:431
  75.9 2.7 %collective-permute-start.10 = (bf16[512,128]{1,0:T(8,128)(2,1)S(1)}, bf16[512,128]{1,0:T(8,128)(2,1)S(1)}, u32[]{:S(2)}, u32[]{:S(2)}) collective-permute-start(bf16[512,128]{1,0:T(8,128)(2,1)S(1)} %get-tuple-element.38), channel_id=1, source_target_pairs={{0,7},{1,6},{2,5},{3,4},{4,3},{5,2},{6,1},{7,0},{8,15},{9,14},{10,... | collective-permute-start | bytes 393224 | tf_op jit(solution)/shard_map/ppermute | solution.py:431
  78.5 0.0 collective-permute-done.5.refs_2_
  78.5 0.0 collective-permute-done.7.refs_3_
  78.6 3.1 %collective-permute-done.8.refs_4_ = bf16[512,128]{1,0:T(8,128)(2,1)S(1)} collective-permute-done((bf16[512,128]{1,0:T(8,128)(2,1)S(1)}, bf16[512,128]{1,0:T(8,128)(2,1)S(1)}, u32[]{:S(2)}, u32[]{:S(2)}) %collective-permute-start.8) | collective-permute-done | bytes 131104 | tf_op jit(solution)/shard_map/ppermute | solution.py:431
  81.7 0.4 collective-permute-done.9.refs_5_
  82.1 1.4 %collective-permute-done.10.refs_7_ = bf16[512,128]{1,0:T(8,128)(2,1)S(1)} collective-permute-done((bf16[512,128]{1,0:T(8,128)(2,1)S(1)}, bf16[512,128]{1,0:T(8,128)(2,1)S(1)}, u32[]{:S(2)}, u32[]{:S(2)}) %collective-permute-start.10) | collective-permute-done | bytes 131104 | tf_op jit(solution)/shard_map/ppermute | solution.py:431
  83.6 2.1 %shard_map.61 = f32[32,64,256]{2,1,0:T(8,128)} custom-call(s32[2]{0:T(128)S(1)} %pad_add_fusion.place_ref, bf16[512,128]{1,0:T(8,128)(2,1)S(1)} %collective-permute-done.3.refs_0_, bf16[512,128]{1,0:T(8,128)(2,1)S(1)} %collective-permute-done.4.refs_1_, bf16[512,128]{1,0:T(8,128)(2,1)S(1)} %collective-permute-done.5.refs_2_, ...), custom_call_target="tpu_custom_call" | custom-call | tf_op jit(solution)/shard_map/pallas_call | solution.py:482
  (2 shorter events, 0.0 us)
Async XLA Ops:
  0.7 1.2 %copy-start.2 = (bf16[1024,512]{1,0:T(8,128)(2,1)S(1)}, bf16[1024,512]{1,0:T(8,128)(2,1)}, u32[]{:S(2)}) copy-start(bf16[1024,512]{1,0:T(8,128)(2,1)} %raw_ref.1) | copy-start | bytes 3145732
  3.9 3.2 %collective-permute-start = (bf16[256,512]{1,0:T(8,128)(2,1)S(1)}, bf16[256,512]{1,0:T(8,128)(2,1)S(1)}, u32[]{:S(2)}, u32[]{:S(2)}) collective-permute-start(bf16[256,512]{1,0:T(8,128)(2,1)S(1)} %get-tuple-element.23), channel_id=1, source_target_pairs={{0,8},{8,0},{16,24},{24,16},{1,9},{9,1},{17,25},{25,17},{2,10},{10... | collective-permute-start | bytes 786440 | tf_op jit(solution)/shard_map/ppermute | solution.py:538
  4.4 9.8 %collective-permute-start.1 = (bf16[256,512]{1,0:T(8,128)(2,1)S(1)}, bf16[256,512]{1,0:T(8,128)(2,1)S(1)}, u32[]{:S(2)}, u32[]{:S(2)}) collective-permute-start(bf16[256,512]{1,0:T(8,128)(2,1)S(1)} %get-tuple-element.24), channel_id=1, source_target_pairs={{0,16},{8,24},{16,0},{24,8},{1,17},{9,25},{17,1},{25,9},{2,18},{10... | collective-permute-start | bytes 786440 | tf_op jit(solution)/shard_map/ppermute | solution.py:538
  7.0 12.3 %collective-permute-start.2 = (bf16[256,512]{1,0:T(8,128)(2,1)S(1)}, bf16[256,512]{1,0:T(8,128)(2,1)S(1)}, u32[]{:S(2)}, u32[]{:S(2)}) collective-permute-start(bf16[256,512]{1,0:T(8,128)(2,1)S(1)} %get-tuple-element.25), channel_id=1, source_target_pairs={{0,24},{8,16},{16,8},{24,0},{1,25},{9,17},{17,9},{25,1},{2,26},{10... | collective-permute-start | bytes 786440 | tf_op jit(solution)/shard_map/ppermute | solution.py:538
  7.1 2.2 %copy-start = (bf16[1024,2048]{1,0:T(8,128)(2,1)S(1)}, bf16[1024,2048]{1,0:T(8,128)(2,1)}, u32[]{:S(2)}) copy-start(bf16[1024,2048]{1,0:T(8,128)(2,1)} %constant.35.clone.table_ref) | copy-start | bytes 12582916
  9.3 10.0 %copy-start.1 = (bf16[1024,2048]{1,0:T(8,128)(2,1)S(1)}, bf16[1024,2048]{1,0:T(8,128)(2,1)}, u32[]{:S(2)}) copy-start(bf16[1024,2048]{1,0:T(8,128)(2,1)} %constant.35.clone.table_ref) | copy-start | bytes 12582916
  21.5 5.9 %copy-start.3 = (s32[256]{0:T(256)S(1)}, s32[256]{0:T(256)}, u32[]{:S(2)}) copy-start(s32[256]{0:T(256)} %param.7) | copy-start | bytes 3076
  21.5 5.9 %copy-start.4 = (s32[256]{0:T(256)S(1)}, s32[256]{0:T(256)}, u32[]{:S(2)}) copy-start(s32[256]{0:T(256)} %param.8) | copy-start | bytes 3076
  21.5 32.1 %all-to-all-start = ((bf16[32,8,16,128]{3,2,1,0:T(8,128)(2,1)}), bf16[32,8,16,128]{3,2,1,0:T(8,128)(2,1)S(1)}, u32[]{:S(2)}, u32[]{:S(2)}) async-start(bf16[32,8,16,128]{3,2,1,0:T(8,128)(2,1)} %shard_map.58), calls=%async_computation | async-start | bytes 2097152 | tf_op jit(solution)/shard_map/all_to_all | solution.py:541
  57.7 15.4 %collective-permute-start.3 = (bf16[512,128]{1,0:T(8,128)(2,1)S(1)}, bf16[512,128]{1,0:T(8,128)(2,1)S(1)}, u32[]{:S(2)}, u32[]{:S(2)}) collective-permute-start(bf16[512,128]{1,0:T(8,128)(2,1)S(1)} %get-tuple-element.27), channel_id=1, source_target_pairs={{0,4},{1,5},{2,6},{3,7},{4,0},{5,1},{6,2},{7,3},{8,12},{9,13},{10,... | collective-permute-start | bytes 393224 | tf_op jit(solution)/shard_map/ppermute | solution.py:431
  58.5 17.4 %collective-permute-start.4 = (bf16[512,128]{1,0:T(8,128)(2,1)S(1)}, bf16[512,128]{1,0:T(8,128)(2,1)S(1)}, u32[]{:S(2)}, u32[]{:S(2)}) collective-permute-start(bf16[512,128]{1,0:T(8,128)(2,1)S(1)} %get-tuple-element.29), channel_id=1, source_target_pairs={{0,5},{1,4},{2,7},{3,6},{4,1},{5,0},{6,3},{7,2},{8,13},{9,12},{10,... | collective-permute-start | bytes 393224 | tf_op jit(solution)/shard_map/ppermute | solution.py:431
  61.6 3.6 %collective-permute-start.6 = (bf16[16,128]{1,0:T(8,128)(2,1)S(1)}, bf16[16,128]{1,0:T(8,128)(2,1)S(1)}, u32[]{:S(2)}, u32[]{:S(2)}) collective-permute-start(bf16[16,128]{1,0:T(8,128)(2,1)S(1)} %get-tuple-element.33), channel_id=1, source_target_pairs={{0,1},{1,0},{2,3},{3,2},{4,5},{5,4},{6,7},{7,6},{8,9},{9,8},{10,11... | collective-permute-start | bytes 12296 | tf_op jit(solution)/shard_map/ppermute | solution.py:431
  62.1 16.4 %collective-permute-start.5 = (bf16[512,128]{1,0:T(8,128)(2,1)S(1)}, bf16[512,128]{1,0:T(8,128)(2,1)S(1)}, u32[]{:S(2)}, u32[]{:S(2)}) collective-permute-start(bf16[512,128]{1,0:T(8,128)(2,1)S(1)} %get-tuple-element.30), channel_id=1, source_target_pairs={{0,6},{1,7},{2,4},{3,5},{4,2},{5,3},{6,0},{7,1},{8,14},{9,15},{10,... | collective-permute-start | bytes 393224 | tf_op jit(solution)/shard_map/ppermute | solution.py:431
  68.1 10.4 %collective-permute-start.7 = (bf16[512,128]{1,0:T(8,128)(2,1)S(1)}, bf16[512,128]{1,0:T(8,128)(2,1)S(1)}, u32[]{:S(2)}, u32[]{:S(2)}) collective-permute-start(bf16[512,128]{1,0:T(8,128)(2,1)S(1)} %get-tuple-element.34), channel_id=1, source_target_pairs={{0,3},{1,2},{2,1},{3,0},{4,7},{5,6},{6,5},{7,4},{8,11},{9,10},{10,... | collective-permute-start | bytes 393224 | tf_op jit(solution)/shard_map/ppermute | solution.py:431
  69.0 12.7 %collective-permute-start.8 = (bf16[512,128]{1,0:T(8,128)(2,1)S(1)}, bf16[512,128]{1,0:T(8,128)(2,1)S(1)}, u32[]{:S(2)}, u32[]{:S(2)}) collective-permute-start(bf16[512,128]{1,0:T(8,128)(2,1)S(1)} %get-tuple-element.35), channel_id=1, source_target_pairs={{0,2},{1,3},{2,0},{3,1},{4,6},{5,7},{6,4},{7,5},{8,10},{9,11},{10,... | collective-permute-start | bytes 393224 | tf_op jit(solution)/shard_map/ppermute | solution.py:431
  73.1 9.0 %collective-permute-start.9 = (bf16[512,128]{1,0:T(8,128)(2,1)S(1)}, bf16[512,128]{1,0:T(8,128)(2,1)S(1)}, u32[]{:S(2)}, u32[]{:S(2)}) collective-permute-start(bf16[512,128]{1,0:T(8,128)(2,1)S(1)} %get-tuple-element.36), channel_id=1, source_target_pairs={{0,1},{1,0},{2,3},{3,2},{4,5},{5,4},{6,7},{7,6},{8,9},{9,8},{10,11... | collective-permute-start | bytes 393224 | tf_op jit(solution)/shard_map/ppermute | solution.py:431
  75.9 7.7 %collective-permute-start.10 = (bf16[512,128]{1,0:T(8,128)(2,1)S(1)}, bf16[512,128]{1,0:T(8,128)(2,1)S(1)}, u32[]{:S(2)}, u32[]{:S(2)}) collective-permute-start(bf16[512,128]{1,0:T(8,128)(2,1)S(1)} %get-tuple-element.38), channel_id=1, source_target_pairs={{0,7},{1,6},{2,5},{3,4},{4,3},{5,2},{6,1},{7,0},{8,15},{9,14},{10,... | collective-permute-start | bytes 393224 | tf_op jit(solution)/shard_map/ppermute | solution.py:431
